TPU v7x, 32 devices: a whole 2x2x4 slice. The times are simulated.
32 devices in a mesh: dp: 4 (over y, core), zero: 8 (over z, x).
Axes of the slice: x: 2, y: 2, z: 4, core: 2. Of those that a mesh axis runs over, the one named last changes fastest.
Arguments:
- tokens: bfloat16 [32768, 1024], P(('dp', 'zero')), may hold values from -40 to 40
- segments: int32 [32768], P(('dp', 'zero')), may hold values from 0 to 32767, as said below
- cotangent: bfloat16 [32768, 1024], P(('dp', 'zero')), may hold values from -6 to 6
- w_qkv: float32 [1024, 3072], P('zero'), may hold values from -0.1875 to 0.1875
- w_out: float32 [1024, 1024], P('zero'), may hold values from -0.75 to 0.75
- w_up: float32 [1024, 4096], P('zero'), may hold values from -0.1875 to 0.1875
- w_down: float32 [4096, 1024], P('zero'), may hold values from -0.09375 to 0.09375
- vectors: float32 [13, 1024], P(None, 'zero'), may hold values from -0.8 to 1.6
- m_qkv: float32 [1024, 3072], P('zero'), may hold values from -108.6116 to 108.6116
- m_out: float32 [1024, 1024], P('zero'), may hold values from -36.20387 to 36.20387
- m_up: float32 [1024, 4096], P('zero'), may hold values from -72.40774 to 72.40774
- m_down: float32 [4096, 1024], P('zero'), may hold values from -72.40774 to 72.40774
- m_vectors: float32 [13, 1024], P(None, 'zero'), may hold values from -108.6116 to 108.6116
- v_qkv: float32 [1024, 3072], P('zero'), may hold values from 32.768 to 131.072
- v_out: float32 [1024, 1024], P('zero'), may hold values from 2.94912 to 11.79648
- v_up: float32 [1024, 4096], P('zero'), may hold values from 11.79648 to 47.18592
- v_down: float32 [4096, 1024], P('zero'), may hold values from 11.79648 to 47.18592
- v_vectors: float32 [13, 1024], P(None, 'zero'), may hold values from 32.768 to 131.072
Outputs:
- layer_out: bfloat16 [32768, 1024], P(('dp', 'zero'))
- tokens_grad: float32 [32768, 1024], P(('dp', 'zero'))
- first_qkv: float32 [1024, 3072], P('zero')
- first_out: float32 [1024, 1024], P('zero')
- first_up: float32 [1024, 4096], P('zero')
- first_down: float32 [4096, 1024], P('zero')
- first_vectors: float32 [13, 1024], P(None, 'zero')
- second_qkv: float32 [1024, 3072], P('zero')
- second_out: float32 [1024, 1024], P('zero')
- second_up: float32 [1024, 4096], P('zero')
- second_down: float32 [4096, 1024], P('zero')
- second_vectors: float32 [13, 1024], P(None, 'zero')
- new_qkv: float32 [1024, 3072], P('zero')
- new_out: float32 [1024, 1024], P('zero')
- new_up: float32 [1024, 4096], P('zero')
- new_down: float32 [4096, 1024], P('zero')
- new_vectors: float32 [13, 1024], P(None, 'zero')
Inputs may be any that keep to these rules, and one draw needn't show every extreme that they name: The rows of one device (1024 rows) hold whole segments: no segment crosses from one device's rows to another's, an id's rows are consecutive, and no id occurs on two devices. In every draw at least one device holds a single segment of 1024 rows.
All inputs are finite; a program needn't handle non-finite values.
Results may differ from a plain program's by a relative error of at most 0.011.
Values may be sent and summed in bfloat16 or wider, within the bound.
No kernel may reach another device: no remote copies, remote signals or barrier semaphores. Data moves between devices by JAX's collectives and lax.ppermute only.
A program may use at most 384 MiB of HBM per device.

v0:
```python
import jax
import jax.numpy as jnp
from jax import lax
from jax.sharding import PartitionSpec as P

HEAD_DIM = 64
ROT_DIM = 16
STEP = 10


EPS_NORM = 1e-05
BETA_ONE = 0.9
BETA_TWO = 0.999
ADAM_EPS = 1e-08
RATE_MATRIX = 0.05
RATE_VECTOR = 0.2
DECAY_MATRIX = 0.1
ROPE_BASE = 10000.0
INV_ROOT_TWO = 0.7071067811865476
INV_ROOT_TAU = 0.3989422804014327
MASKED = -1e30


def layer_norm(inputs):
    row_mean = jnp.mean(inputs, axis=-1, keepdims=True)
    centred = inputs - row_mean
    variance = jnp.mean(centred * centred, axis=-1, keepdims=True)
    inv_std = lax.rsqrt(variance + EPS_NORM)
    return (centred * inv_std, inv_std)


def norm_back(upstream, normed, inv_std, gain):
    scaled = upstream * gain
    return inv_std * (
        scaled
        - jnp.mean(scaled, axis=-1, keepdims=True)
        - normed * jnp.mean(scaled * normed, axis=-1, keepdims=True)
    )


def rotary_tables(segments):
    row_count = segments.shape[0]
    row_index = jnp.arange(row_count, dtype=jnp.int32)
    earlier = jnp.concatenate([jnp.full((1,), -1, jnp.int32), segments[:-1]])
    starts = jnp.where(segments != earlier, row_index, 0)
    position = (row_index - lax.cummax(starts, axis=0)).astype(jnp.float32)
    frequency = ROPE_BASE ** (-2.0 * jnp.arange(ROT_DIM // 2, dtype=jnp.float32) / ROT_DIM)
    angles = position[:, None] * frequency[None, :]
    return (jnp.cos(angles), jnp.sin(angles))


def rotate(head_rows, cosine_table, sine_table, direction):
    half_dim = ROT_DIM // 2
    front_half = head_rows[..., :half_dim]
    back_half = head_rows[..., half_dim:ROT_DIM]
    cos_rows = cosine_table[:, None, :]
    sin_rows = direction * sine_table[:, None, :]
    return jnp.concatenate(
        [
            front_half * cos_rows - back_half * sin_rows,
            back_half * cos_rows + front_half * sin_rows,
            head_rows[..., ROT_DIM:],
        ],
        axis=-1,
    )


def inner_rows(left, right):
    return lax.dot_general(
        left, right, (((0,), (0,)), ((), ())), preferred_element_type=jnp.float32
    )


def times_transposed(left, right):
    return lax.dot_general(
        left, right, (((1,), (1,)), ((), ())), preferred_element_type=jnp.float32
    )


def block_scores(queries, key_rows, segments, first_row, last_row):
    scores = jnp.einsum(
        "qhd,khd->hqk",
        queries[first_row:last_row],
        key_rows[:last_row],
        preferred_element_type=jnp.float32,
    ) * HEAD_DIM ** (-0.5)
    row_index = jnp.arange(last_row)
    allowed = (segments[first_row:last_row, None] == segments[None, :last_row]) & (
        row_index[first_row:last_row, None] >= row_index[None, :]
    )
    return jnp.where(allowed[None], scores, MASKED)


def regroup(gradient, dimension, owners, replicas):
    full_shape = gradient.shape
    split_shape = (
        full_shape[:dimension]
        + (owners, replicas, full_shape[dimension] // (owners * replicas))
        + full_shape[dimension + 1 :]
    )
    return jnp.swapaxes(gradient.reshape(split_shape), dimension, dimension + 1).reshape(full_shape)


def adam_step(weight, first, second, gradient, rate, decay):
    first_new = BETA_ONE * first + (1.0 - BETA_ONE) * gradient
    second_new = BETA_TWO * second + (1.0 - BETA_TWO) * gradient * gradient
    first_hat = first_new / (1.0 - BETA_ONE**STEP)
    second_hat = second_new / (1.0 - BETA_TWO**STEP)
    weight_new = weight - rate * (first_hat / (jnp.sqrt(second_hat) + ADAM_EPS) + decay * weight)
    return (first_new, second_new, weight_new)


def on_device(
    tokens,
    segments,
    cotangent,
    w_qkv,
    w_out,
    w_up,
    w_down,
    vectors,
    m_qkv,
    m_out,
    m_up,
    m_down,
    m_vectors,
    v_qkv,
    v_out,
    v_up,
    v_down,
    v_vectors,
):
    full_qkv, full_out, full_up, full_down, full_vectors = (
        lax.all_gather(w_qkv.astype(jnp.bfloat16), "zero", axis=0, tiled=True),
        lax.all_gather(w_out.astype(jnp.bfloat16), "zero", axis=0, tiled=True),
        lax.all_gather(w_up.astype(jnp.bfloat16), "zero", axis=0, tiled=True),
        lax.all_gather(w_down.astype(jnp.bfloat16), "zero", axis=0, tiled=True),
        lax.all_gather(vectors.astype(jnp.bfloat16), "zero", axis=1, tiled=True),
    )
    inputs = tokens.astype(jnp.float32)
    row_count = inputs.shape[0]
    model_width = inputs.shape[1]
    head_count = model_width // HEAD_DIM
    vector_rows = full_vectors.astype(jnp.float32)
    gain_attn = vector_rows[0]
    gain_mlp = vector_rows[2]
    normed, inv_std = layer_norm(inputs)
    attn_in = (normed * gain_attn + vector_rows[1]).astype(jnp.bfloat16)
    mlp_in = (normed * gain_mlp + vector_rows[3]).astype(jnp.bfloat16)
    qkv = jnp.dot(attn_in, full_qkv, preferred_element_type=jnp.float32) + vector_rows[4:7].reshape(
        -1
    )
    cosine_table, sine_table = rotary_tables(segments)
    queries = rotate(
        qkv[:, :model_width].reshape(row_count, head_count, HEAD_DIM), cosine_table, sine_table, 1.0
    ).astype(jnp.bfloat16)
    key_rows = rotate(
        qkv[:, model_width : 2 * model_width].reshape(row_count, head_count, HEAD_DIM),
        cosine_table,
        sine_table,
        1.0,
    ).astype(jnp.bfloat16)
    values = qkv[:, 2 * model_width :].reshape(row_count, head_count, HEAD_DIM).astype(jnp.bfloat16)
    block_rows = min(512, row_count)
    bounds = [(first_row, first_row + block_rows) for first_row in range(0, row_count, block_rows)]
    attended_parts = []
    log_sums = []
    for first_row, last_row in bounds:
        scores = block_scores(queries, key_rows, segments, first_row, last_row)
        row_max = jnp.max(scores, axis=-1, keepdims=True)
        exp_scores = jnp.exp(scores - row_max)
        row_total = jnp.sum(exp_scores, axis=-1, keepdims=True)
        attn_probs = (exp_scores / row_total).astype(jnp.bfloat16)
        attended_parts.append(
            jnp.einsum(
                "hqk,khd->qhd", attn_probs, values[:last_row], preferred_element_type=jnp.float32
            )
        )
        log_sums.append(row_max + jnp.log(row_total))
    attended = (
        jnp.concatenate(attended_parts, axis=0).reshape(row_count, model_width).astype(jnp.bfloat16)
    )
    attn_branch = jnp.dot(attended, full_out, preferred_element_type=jnp.float32) + vector_rows[7]
    pre_up = jnp.dot(mlp_in, full_up, preferred_element_type=jnp.float32) + vector_rows[
        8:12
    ].reshape(-1)
    hidden = jax.nn.gelu(pre_up, approximate=False).astype(jnp.bfloat16)
    mlp_branch = jnp.dot(hidden, full_down, preferred_element_type=jnp.float32) + vector_rows[12]
    layer_out = (inputs + attn_branch + mlp_branch).astype(jnp.bfloat16)
    upstream = cotangent.astype(jnp.float32)
    grad_w_down = inner_rows(hidden, cotangent)
    grad_w_out = inner_rows(attended, cotangent)
    grad_bias = jnp.sum(upstream, axis=0)
    grad_hidden = times_transposed(cotangent, full_down)
    normal_cdf = 0.5 * (1.0 + lax.erf(pre_up * INV_ROOT_TWO))
    normal_pdf = jnp.exp(-0.5 * pre_up * pre_up) * INV_ROOT_TAU
    grad_pre = (grad_hidden * (normal_cdf + pre_up * normal_pdf)).astype(jnp.bfloat16)
    grad_w_up = inner_rows(mlp_in, grad_pre)
    grad_bias_up = jnp.sum(grad_pre.astype(jnp.float32), axis=0)
    grad_mlp_in = times_transposed(grad_pre, full_up)
    grad_attended = (
        times_transposed(cotangent, full_out)
        .reshape(row_count, head_count, HEAD_DIM)
        .astype(jnp.bfloat16)
    )
    query_parts = []
    grad_keys = jnp.zeros((row_count, head_count, HEAD_DIM), jnp.float32)
    grad_values = jnp.zeros((row_count, head_count, HEAD_DIM), jnp.float32)
    for pair_index, (first_row, last_row) in enumerate(bounds):
        scores = block_scores(queries, key_rows, segments, first_row, last_row)
        attn_probs = jnp.exp(scores - log_sums[pair_index])
        grad_probs = jnp.einsum(
            "qhd,khd->hqk",
            grad_attended[first_row:last_row],
            values[:last_row],
            preferred_element_type=jnp.float32,
        )
        row_delta = jnp.sum(grad_probs * attn_probs, axis=-1, keepdims=True)
        grad_scores = (attn_probs * (grad_probs - row_delta)).astype(jnp.bfloat16)
        query_parts.append(
            jnp.einsum(
                "hqk,khd->qhd", grad_scores, key_rows[:last_row], preferred_element_type=jnp.float32
            )
            * HEAD_DIM ** (-0.5)
        )
        grad_keys = grad_keys.at[:last_row].add(
            jnp.einsum(
                "hqk,qhd->khd",
                grad_scores,
                queries[first_row:last_row],
                preferred_element_type=jnp.float32,
            )
            * HEAD_DIM ** (-0.5)
        )
        grad_values = grad_values.at[:last_row].add(
            jnp.einsum(
                "hqk,qhd->khd",
                attn_probs.astype(jnp.bfloat16),
                grad_attended[first_row:last_row],
                preferred_element_type=jnp.float32,
            )
        )
    grad_queries = rotate(jnp.concatenate(query_parts, axis=0), cosine_table, sine_table, -1.0)
    grad_keys = rotate(grad_keys, cosine_table, sine_table, -1.0)
    grad_qkv = jnp.concatenate(
        [
            grad_queries.reshape(row_count, model_width),
            grad_keys.reshape(row_count, model_width),
            grad_values.reshape(row_count, model_width),
        ],
        axis=1,
    ).astype(jnp.bfloat16)
    grad_w_qkv = inner_rows(attn_in, grad_qkv)
    grad_bias_qkv = jnp.sum(grad_qkv.astype(jnp.float32), axis=0)
    grad_attn_in = times_transposed(grad_qkv, full_qkv)
    tokens_grad = (
        upstream
        + norm_back(grad_attn_in, normed, inv_std, gain_attn)
        + norm_back(grad_mlp_in, normed, inv_std, gain_mlp)
    )
    grad_vectors = jnp.concatenate(
        [
            jnp.stack(
                [
                    jnp.sum(grad_attn_in * normed, axis=0),
                    jnp.sum(grad_attn_in, axis=0),
                    jnp.sum(grad_mlp_in * normed, axis=0),
                    jnp.sum(grad_mlp_in, axis=0),
                ]
            ),
            grad_bias_qkv.reshape(3, model_width),
            grad_bias[None, :],
            grad_bias_up.reshape(-1, model_width),
            grad_bias[None, :],
        ],
        axis=0,
    )
    owners = lax.axis_size("zero")
    replicas = lax.axis_size("dp")
    summed = (
        lax.psum_scatter(
            regroup(grad_w_qkv, 0, owners, replicas),
            ("dp", "zero"),
            scatter_dimension=0,
            tiled=True,
        ),
        lax.psum_scatter(
            regroup(grad_w_out, 0, owners, replicas),
            ("dp", "zero"),
            scatter_dimension=0,
            tiled=True,
        ),
        lax.psum_scatter(
            regroup(grad_w_up, 0, owners, replicas), ("dp", "zero"), scatter_dimension=0, tiled=True
        ),
        lax.psum_scatter(
            regroup(grad_w_down, 0, owners, replicas),
            ("dp", "zero"),
            scatter_dimension=0,
            tiled=True,
        ),
        lax.psum_scatter(
            regroup(grad_vectors, 1, owners, replicas),
            ("dp", "zero"),
            scatter_dimension=1,
            tiled=True,
        ),
    )
    shares = (
        lax.all_gather(summed[0], "dp", axis=0, tiled=True),
        lax.all_gather(summed[1], "dp", axis=0, tiled=True),
        lax.all_gather(summed[2], "dp", axis=0, tiled=True),
        lax.all_gather(summed[3], "dp", axis=0, tiled=True),
        lax.all_gather(summed[4], "dp", axis=1, tiled=True),
    )
    first_qkv, second_qkv, new_qkv = adam_step(
        w_qkv, m_qkv, v_qkv, shares[0], RATE_MATRIX, DECAY_MATRIX
    )
    first_out, second_out, new_out = adam_step(
        w_out, m_out, v_out, shares[1], RATE_MATRIX, DECAY_MATRIX
    )
    first_up, second_up, new_up = adam_step(w_up, m_up, v_up, shares[2], RATE_MATRIX, DECAY_MATRIX)
    first_down, second_down, new_down = adam_step(
        w_down, m_down, v_down, shares[3], RATE_MATRIX, DECAY_MATRIX
    )
    first_vectors, second_vectors, new_vectors = adam_step(
        vectors, m_vectors, v_vectors, shares[4], RATE_VECTOR, 0.0
    )
    return (
        layer_out,
        tokens_grad,
        first_qkv,
        first_out,
        first_up,
        first_down,
        first_vectors,
        second_qkv,
        second_out,
        second_up,
        second_down,
        second_vectors,
        new_qkv,
        new_out,
        new_up,
        new_down,
        new_vectors,
    )


def solution(mesh):
    return jax.shard_map(
        on_device,
        mesh=mesh,
        in_specs=(
            P(("dp", "zero"), None),
            P(("dp", "zero")),
            P(("dp", "zero"), None),
            P("zero", None),
            P("zero", None),
            P("zero", None),
            P("zero", None),
            P(None, "zero"),
            P("zero", None),
            P("zero", None),
            P("zero", None),
            P("zero", None),
            P(None, "zero"),
            P("zero", None),
            P("zero", None),
            P("zero", None),
            P("zero", None),
            P(None, "zero"),
        ),
        out_specs=(
            P(("dp", "zero"), None),
            P(("dp", "zero"), None),
            P("zero", None),
            P("zero", None),
            P("zero", None),
            P("zero", None),
            P(None, "zero"),
            P("zero", None),
            P("zero", None),
            P("zero", None),
            P("zero", None),
            P(None, "zero"),
            P("zero", None),
            P("zero", None),
            P("zero", None),
            P("zero", None),
            P(None, "zero"),
        ),
        check_vma=False,
    )
```

profile of v0, /device:TPU:0, one launch (start us, length us, event | category | flops | bytes accessed | tf_op | source)
XLA Modules:
  0.0 1683.2 jit_solution(13092512565764872475)
XLA Ops:
  12.7 28.4 %all_gather.30 = bf16[13,1024]{1,0:T(8,128)(2,1)S(1)} all-gather(bf16[13,128]{1,0:T(8,128)(2,1)S(1)} %convert_element_type.86), channel_id=1, replica_groups=mesh['dp'=4,'zero'=8] {'zero'}, dimensions={1}, use_global_device_ids=true | all-gather | bytes 29952 | tf_op jit(solution)/shard_map/all_gather | solution.py:138
  47.2 65.7 %all-gather.9.cloned.1.call-done = bf16[1024,3072]{1,0:T(8,128)(2,1)} async-done(((bf16[128,3072]{1,0:T(8,128)(2,1)}), bf16[1024,3072]{1,0:T(8,128)(2,1)}) %all-gather.9.cloned.1.call-update) | async-done | bytes 6291472 | tf_op jit(solution)/shard_map/all_gather | solution.py:134
  113.0 9.6 fusion.101
  129.3 5.4 copy.93
  143.7 5.3 copy.92
  153.5 7.4 fusion.103
  160.9 9.2 fusion.22
  170.2 15.7 fusion.102
  185.8 14.4 fusion
  200.3 7.8 fusion.69
  208.1 13.1 fusion.68
  228.3 10.5 all-gather.13.cloned.1.call-done
  238.8 50.2 %fusion.4 = (bf16[1024,4096]{1,0:T(8,128)(2,1)}, f32[1024,4096]{1,0:T(8,128)}) fusion(f32[4096]{0:T(1024)S(1)} %bitcast.159, bf16[1024,4096]{1,0:T(8,128)(2,1)} %all-gather.13.cloned.1.call-done, bf16[1024,1024]{1,0:T(8,128)(2,1)S(1)} %copy-done.2, f32[1024]{0:T(1024)S(1)} %bitcast.163, f32[1024]{0:T(1024)S(1)} %bitcast.150, f32[1024]{0:T(1024)S(1)} %add_rsqrt_fusion, ...), kind=kOutput, calls=%fused_computation.12 | convolution fusion | flops 8873050112 | bytes 35684352 | tf_op jit(solution)/shard_map/dot_general | solution.py:184
  289.1 11.8 fusion.106
  300.9 6.6 copy.102
  307.6 75.8 %reduce-scatter.10.cloned.1.call-done = f32[32,1024]{1,0:T(8,128)} async-done(((f32[1024,1024]{1,0:T(8,128)}), f32[32,1024]{1,0:T(8,128)}) %reduce-scatter.10.cloned.1.call-update) | async-done | bytes 131088 | tf_op jit(solution)/shard_map/reduce_scatter | solution.py:287
  383.5 6.7 all_gather.36
  392.8 348.7 %reduce-scatter.14.cloned.1.call-done = f32[128,1024]{1,0:T(8,128)} async-done(((f32[4096,1024]{1,0:T(8,128)}), f32[128,1024]{1,0:T(8,128)}) %reduce-scatter.14.cloned.1.call-update) | async-done | bytes 524304 | tf_op jit(solution)/shard_map/reduce_scatter | solution.py:296
  741.6 51.0 %all-gather.11.cloned.1.call-done = bf16[1024,1024]{1,0:T(8,128)(2,1)} async-done(((bf16[128,1024]{1,0:T(8,128)(2,1)}), bf16[1024,1024]{1,0:T(8,128)(2,1)}) %all-gather.11.cloned.1.call-update) | async-done | bytes 2097168 | tf_op jit(solution)/shard_map/all_gather | solution.py:135
  798.2 11.8 multiply_reduce_fusion.1
  809.9 5.2 all-gather.21.cloned.1.call-done
  815.2 7.3 multiply_subtract_fusion
  822.6 13.0 multiply_convert_fusion.1
  839.8 22.3 %multiply_reduce_fusion = (f32[16,512]{1,0:T(8,128)S(1)}, f32[16,512,1024]{2,1,0:T(8,128)}) fusion(f32[16,512,1024]{2,1,0:T(8,128)} %get-tuple-element.142, f32[16,512]{1,0:T(8,128)S(1)} %log_add_fusion, bf16[512,16,64]{0,2,1:T(8,128)(2,1)S(1)} %bitcast.124, bf16[1024,16,64]{0,2,1:T(8,128)(2,1)S(1)} %bitcast.123), kind=kOutput, calls=%fused_computation.1 | convolution fusion | flops 1098899456 | bytes 70320128 | tf_op jit(solution)/shard_map/qhd,khd->hqk/dot_general | solution.py:212
  862.1 28.6 %multiply_convert_fusion = bf16[16,512,1024]{2,1,0:T(8,128)(2,1)} fusion(f32[16,512,1024]{2,1,0:T(8,128)} %get-tuple-element.150, f32[16,512,1024]{2,1,0:T(8,128)} %get-tuple-element.142, f32[16,512]{1,0:T(8,128)S(1)} %get-tuple-element.149, f32[16,512]{1,0:T(8,128)S(1)} %log_add_fusion), kind=kLoop, calls=%fused_computation | loop fusion | flops 33554432 | bytes 83951616 | tf_op jit(solution)/shard_map/convert_element_type | solution.py:219
  890.7 9.5 bitcast_add_fusion.1
  905.6 12.9 multiply_bitcast_fusion.1
  924.5 9.8 fusion.62
  934.3 15.5 fusion.54
  949.9 14.7 fusion.87
  964.5 10.7 copy.99
  976.0 20.1 %convert_reduce_fusion = (f32[4096]{0:T(1024)S(1)}, bf16[1024,4096]{1,0:T(8,128)(2,1)}) fusion(f32[1024,4096]{1,0:T(8,128)} %get-tuple-element.146, f32[4096]{0:T(1024)S(1)} %bitcast.160, bf16[1024,1024]{1,0:T(8,128)(2,1)} %param.32, bf16[4096,1024]{1,0:T(8,128)(2,1)} %all-gather.15.cloned.1.call-done), kind=kOutput, calls=%fused_computation.20 | convolution fusion | flops 8644456448 | bytes 35684352 | tf_op jit(solution)/shard_map/dot_general | solution.py:75
  996.1 12.1 fusion.83
  1008.2 6.5 copy.101
  1014.7 4.6 convert_reduce_fusion.1
  1019.4 112.0 %reduce-scatter.8.cloned.1.call-done = f32[32,3072]{1,0:T(8,128)} async-done(((f32[1024,3072]{1,0:T(8,128)}), f32[32,3072]{1,0:T(8,128)}) %reduce-scatter.8.cloned.1.call-update) | async-done | bytes 393232 | tf_op jit(solution)/shard_map/reduce_scatter | solution.py:281
  1131.6 15.4 fusion.105
  1147.0 14.1 fusion.49
  1161.2 6.8 convert_reduce_fusion.3
  1169.8 6.6 fusion.104
  1176.4 314.6 %reduce-scatter.12.cloned.1.call-done = f32[32,4096]{1,0:T(8,128)} async-done(((f32[1024,4096]{1,0:T(8,128)}), f32[32,4096]{1,0:T(8,128)}) %reduce-scatter.12.cloned.1.call-update) | async-done | bytes 524304 | tf_op jit(solution)/shard_map/reduce_scatter | solution.py:293
  1491.0 20.4 %all-gather.17.cloned.1.call-done = f32[128,3072]{1,0:T(8,128)} async-done(((f32[32,3072]{1,0:T(8,128)}), f32[128,3072]{1,0:T(8,128)}) %all-gather.17.cloned.1.call-update) | async-done | bytes 1572880 | tf_op jit(solution)/shard_map/all_gather | solution.py:310
  1511.4 6.0 multiply_subtract_fusion.2
  1517.5 14.8 fusion.53
  1532.4 116.0 %reduce-scatter.16.cloned.1.call-done = f32[32,13]{1,0:T(8,128)} async-done(((f32[1024,13]{1,0:T(8,128)}), f32[32,13]{1,0:T(8,128)}) %reduce-scatter.16.cloned.1.call-update) | async-done | bytes 1680
  1649.1 5.2 all-gather
  1655.0 13.7 all-gather.19.cloned.1.call-done
  1668.8 7.4 multiply_subtract_fusion.1
  (228 shorter events, 67.0 us)
Async XLA Ops:
  7.2 34.5 %copy-start.43 = (s32[1024]{0:T(1024)S(1)}, s32[1024]{0:T(1024)}, u32[]{:S(2)}) copy-start(s32[1024]{0:T(1024)} %param.31) | copy-start | bytes 12292
  7.2 35.2 %copy-start.2 = (bf16[1024,1024]{1,0:T(8,128)(2,1)S(1)}, bf16[1024,1024]{1,0:T(8,128)(2,1)}, u32[]{:S(2)}) copy-start(bf16[1024,1024]{1,0:T(8,128)(2,1)} %param.30) | copy-start | bytes 6291460
  7.2 105.7 %all-gather.9.cloned.1.call-start = ((), (), s32[]{:S(2)}) async-start(), calls=%async_computation.5 | async-start | bytes 7077888 | tf_op jit(solution)/shard_map/all_gather | solution.py:134
  9.8 229.0 %all-gather.13.cloned.1.call-start = ((), (), s32[]{:S(2)}) async-start(), calls=%async_computation.7 | async-start | bytes 9437184 | tf_op jit(solution)/shard_map/all_gather | solution.py:136
  12.6 370.9 %reduce-scatter.10.cloned.1.call-start = ((), (), s32[]{:S(2)}) async-start(), calls=%async_computation.11 | async-start | bytes 4325376 | tf_op jit(solution)/shard_map/reduce_scatter | solution.py:287
  41.7 80.8 %copy-start.50 = (f32[1,1024]{1,0:T(1,128)}, f32[1,1024]{1,0:T(1,128)S(1)}, u32[]{:S(2)}) copy-start(f32[1,1024]{1,0:T(1,128)S(1)} %get-tuple-element.132) | copy-start | bytes 12292
  41.7 80.8 %copy-start.62 = (f32[1,1024]{1,0:T(1,128)}, f32[1,1024]{1,0:T(1,128)S(1)}, u32[]{:S(2)}) copy-start(f32[1,1024]{1,0:T(1,128)S(1)} %get-tuple-element.133) | copy-start | bytes 12292
  42.7 196.1 %copy-start.44 = (f32[1024]{0:T(1024)}, f32[1024]{0:T(1024)S(1)}, u32[]{:S(2)}) copy-start(f32[1024]{0:T(1024)S(1)} %broadcast_multiply_fusion.5) | copy-start | bytes 12292
  43.5 195.4 %copy-start.52 = (f32[1024]{0:T(1024)}, f32[1024]{0:T(1024)S(1)}, u32[]{:S(2)}) copy-start(f32[1024]{0:T(1024)S(1)} %add_rsqrt_fusion) | copy-start | bytes 12292
  45.8 105.4 %copy-start.31 = (f32[1024,8]{0,1:T(8,128)}, f32[1024,8]{0,1:T(8,128)S(1)}, u32[]{:S(2)}) copy-start(f32[1024,8]{0,1:T(8,128)S(1)} %get-tuple-element.136) | copy-start | bytes 98308
  140.1 60.2 %copy-start.18 = (bf16[512,1024]{0,1:T(8,128)(2,1)}, bf16[512,1024]{0,1:T(8,128)(2,1)S(1)}, u32[]{:S(2)}) copy-start(bf16[512,1024]{0,1:T(8,128)(2,1)S(1)} %copy.91) | copy-start | bytes 3145732
  153.2 16.9 %copy-start.20 = (bf16[1024,16,8]{0,2,1:T(8,128)(2,1)}, bf16[1024,16,8]{0,2,1:T(8,128)(2,1)S(1)}, u32[]{:S(2)}) copy-start(bf16[1024,16,8]{0,2,1:T(8,128)(2,1)S(1)} %get-tuple-element.114) | copy-start | bytes 786436
  160.9 39.3 %copy-start.35 = (f32[16,512]{1,0:T(8,128)}, f32[16,512]{1,0:T(8,128)S(1)}, u32[]{:S(2)}) copy-start(f32[16,512]{1,0:T(8,128)S(1)} %get-tuple-element.143) | copy-start | bytes 98308
  170.1 30.1 %copy-start.37 = (f32[16,512]{1,0:T(8,128)}, f32[16,512]{1,0:T(8,128)S(1)}, u32[]{:S(2)}) copy-start(f32[16,512]{1,0:T(8,128)S(1)} %fusion.22) | copy-start | bytes 98308
  185.8 22.2 %copy-start.39 = (f32[16,512]{1,0:T(8,128)}, f32[16,512]{1,0:T(8,128)S(1)}, u32[]{:S(2)}) copy-start(f32[16,512]{1,0:T(8,128)S(1)} %get-tuple-element.141) | copy-start | bytes 98308
  228.2 513.3 %reduce-scatter.14.cloned.1.call-start = ((), (), s32[]{:S(2)}) async-start(), calls=%async_computation.14 | async-start | bytes 17301504 | tf_op jit(solution)/shard_map/reduce_scatter | solution.py:296
  238.8 50.2 %copy-start.26 = (bf16[1024,1024]{1,0:T(8,128)(2,1)S(1)}, bf16[1024,1024]{1,0:T(8,128)(2,1)}, u32[]{:S(2)}) copy-start(bf16[1024,1024]{1,0:T(8,128)(2,1)} %param.32) | copy-start | bytes 6291460
  307.5 82.7 %copy-start.29 = (f32[128,1024]{1,0:T(8,128)S(1)}, f32[128,1024]{1,0:T(8,128)}, u32[]{:S(2)}) copy-start(f32[128,1024]{1,0:T(8,128)} %param.34) | copy-start | bytes 1572868
  307.5 82.7 %copy-start.30 = (f32[128,1024]{1,0:T(8,128)S(1)}, f32[128,1024]{1,0:T(8,128)}, u32[]{:S(2)}) copy-start(f32[128,1024]{1,0:T(8,128)} %param.44) | copy-start | bytes 1572868
  307.5 434.0 %copy-start.36 = (f32[16,512]{1,0:T(8,128)S(1)}, f32[16,512]{1,0:T(8,128)}, u32[]{:S(2)}) copy-start(f32[16,512]{1,0:T(8,128)} %copy-done.35) | copy-start | bytes 98308
  307.5 434.0 %copy-start.38 = (f32[16,512]{1,0:T(8,128)S(1)}, f32[16,512]{1,0:T(8,128)}, u32[]{:S(2)}) copy-start(f32[16,512]{1,0:T(8,128)} %copy-done.37) | copy-start | bytes 98308
  307.6 434.0 %copy-start.40 = (f32[16,512]{1,0:T(8,128)S(1)}, f32[16,512]{1,0:T(8,128)}, u32[]{:S(2)}) copy-start(f32[16,512]{1,0:T(8,128)} %copy-done.39) | copy-start | bytes 98308
  307.6 434.0 %copy-start.42 = (f32[16,512]{1,0:T(8,128)S(1)}, f32[16,512]{1,0:T(8,128)}, u32[]{:S(2)}) copy-start(f32[16,512]{1,0:T(8,128)} %copy-done.41) | copy-start | bytes 98308
  307.6 485.1 %copy-start.27 = (bf16[1024,1024]{1,0:T(8,128)(2,1)S(1)}, bf16[1024,1024]{1,0:T(8,128)(2,1)}, u32[]{:S(2)}) copy-start(bf16[1024,1024]{1,0:T(8,128)(2,1)} %param.32) | copy-start | bytes 6291460
  307.6 485.0 %all-gather.11.cloned.1.call-start = ((), (), s32[]{:S(2)}) async-start(), calls=%async_computation.6 | async-start | bytes 2359296 | tf_op jit(solution)/shard_map/all_gather | solution.py:135
  392.8 422.4 %all-gather.21.cloned.1.call-start = ((), (), s32[]{:S(2)}) async-start(), calls=%async_computation.15 | async-start | bytes 2621440 | tf_op jit(solution)/shard_map/all_gather | solution.py:313
  741.5 233.8 %all-gather.15.cloned.1.call-start = ((), (), s32[]{:S(2)}) async-start(), calls=%async_computation.8 | async-start | bytes 9437184 | tf_op jit(solution)/shard_map/all_gather | solution.py:137
  798.2 17.0 %copy-start.24 = (f32[512,1024]{1,0:T(8,128)S(1)}, f32[512,1024]{1,0:T(8,128)}, u32[]{:S(2)}) copy-start(f32[512,1024]{1,0:T(8,128)} %param.36) | copy-start | bytes 6291460
  822.5 308.9 %reduce-scatter.8.cloned.1.call-start = ((), (), s32[]{:S(2)}) async-start(), calls=%async_computation.9 | async-start | bytes 12976128 | tf_op jit(solution)/shard_map/reduce_scatter | solution.py:281
  934.3 15.5 copy-start.3
  934.3 15.5 copy-start.45
  934.3 15.5 copy-start.51
  934.3 15.5 copy-start.53
  934.3 15.5 copy-start.63
  975.3 515.7 %reduce-scatter.12.cloned.1.call-start = ((), (), s32[]{:S(2)}) async-start(), calls=%async_computation.12 | async-start | bytes 17301504 | tf_op jit(solution)/shard_map/reduce_scatter | solution.py:293
  976.0 20.1 %copy-start.49 = (f32[1,1024]{1,0:T(1,128)S(1)}, f32[1,1024]{1,0:T(1,128)}, u32[]{:S(2)}) copy-start(f32[1,1024]{1,0:T(1,128)} %get-tuple-element.128) | copy-start | bytes 12292
  976.0 20.1 %copy-start.61 = (f32[1,1024]{1,0:T(1,128)S(1)}, f32[1,1024]{1,0:T(1,128)}, u32[]{:S(2)}) copy-start(f32[1,1024]{1,0:T(1,128)} %get-tuple-element.129) | copy-start | bytes 12292
  1014.7 496.7 %all-gather.17.cloned.1.call-start = ((), (), s32[]{:S(2)}) async-start(), calls=%async_computation.10 | async-start | bytes 1966080 | tf_op jit(solution)/shard_map/all_gather | solution.py:310
  1131.5 516.9 %reduce-scatter.16.cloned.1.call-start = ((), (), s32[]{:S(2)}) async-start(), calls=%async_computation.16 | async-start | bytes 540672
  1131.6 15.4 copy-start.14
  1131.6 15.4 copy-start.15
  1131.6 15.4 copy-start.16
  1169.5 499.3 %all-gather.19.cloned.1.call-start = ((), (), s32[]{:S(2)}) async-start(), calls=%async_computation.13 | async-start | bytes 2621440 | tf_op jit(solution)/shard_map/all_gather | solution.py:312
  1491.0 26.5 %copy-start.58 = (f32[1,1024]{1,0:T(1,128)S(1)}, f32[1,1024]{1,0:T(1,128)}, u32[]{:S(2)}) copy-start(f32[1,1024]{1,0:T(1,128)} %get-tuple-element.130) | copy-start | bytes 12292
  1491.0 26.5 %copy-start.59 = (f32[1,1024]{1,0:T(1,128)S(1)}, f32[1,1024]{1,0:T(1,128)}, u32[]{:S(2)}) copy-start(f32[1,1024]{1,0:T(1,128)} %get-tuple-element.131) | copy-start | bytes 12292
  1517.5 136.9 %copy-start.47 = (f32[13,128]{1,0:T(8,128)S(1)}, f32[13,128]{1,0:T(8,128)}, u32[]{:S(2)}) copy-start(f32[13,128]{1,0:T(8,128)} %param.37) | copy-start | bytes 19972
  1517.5 136.9 %copy-start.56 = (f32[13,128]{1,0:T(8,128)S(1)}, f32[13,128]{1,0:T(8,128)}, u32[]{:S(2)}) copy-start(f32[13,128]{1,0:T(8,128)} %param.47) | copy-start | bytes 19972
  1517.5 136.9 %copy-start.57 = (f32[13,128]{1,0:T(8,128)S(1)}, f32[13,128]{1,0:T(8,128)}, u32[]{:S(2)}) copy-start(f32[13,128]{1,0:T(8,128)} %param.42) | copy-start | bytes 19972
  (29 other events, 163.4 us)
Sparse Core Ops, SparseCore 0:
  10.8 102.0 all-gather.8
  115.7 123.1 all-gather.12
  241.7 141.7 reduce-scatter.9
  385.6 355.8 reduce-scatter.13
  744.0 48.5 all-gather.10
  794.0 21.0 all-gather.20
  822.6 124.9 all-gather.14
  975.4 155.9 reduce-scatter.7
  1133.8 357.1 reduce-scatter.11
  1492.5 18.9 all-gather.16
  1514.3 133.9 reduce-scatter.15
  1649.7 18.9 all-gather.18
where the time goes:
time: 1690 us; the launch traced here: 1680 us
  waiting for transfers between devices  1130 us (67%)
  matrix products  307 us (18%)
  other arithmetic  118 us (7%)
  local copies, waits for them, and re-layouts  67.7 us (4%)
  blocking collectives  40.3 us (2%)
    reduce_scatter x1, waiting for transfers between devices, on_device(): lax.psum_scatter(regroup(grad_w_down, 0, owners, replicas), ('dp', 'zero'...  349 us
    reduce_scatter x1, waiting for transfers between devices, on_device(): lax.psum_scatter(regroup(grad_w_up, 0, owners, replicas), ('dp', 'zero'),...  315 us
    unnamed x13, waiting for transfers between devices  116 us
    reduce_scatter x1, waiting for transfers between devices, on_device(): lax.psum_scatter(regroup(grad_w_qkv, 0, owners, replicas), ('dp', 'zero')...  112 us
    reduce_scatter x1, waiting for transfers between devices, on_device(): lax.psum_scatter(regroup(grad_w_out, 0, owners, replicas), ('dp', 'zero')...  75.8 us
    all_gather x1, waiting for transfers between devices, on_device(): lax.all_gather(w_qkv.astype(jnp.bfloat16), 'zero', axis=0, tiled=True)  65.7 us
    dot_general x4, matrix products, times_transposed(): lax.dot_general(left, right, (((1,), (1,)), ((), ())), preferred_element_...  53.6 us
    all_gather x1, waiting for transfers between devices, on_device(): lax.all_gather(w_out.astype(jnp.bfloat16), 'zero', axis=0, tiled=True)  51 us
  transfers between devices with their start and end apart: 12, of which 11 were waited for; matrix products, arithmetic and copies ran while one was open for 28% of the time, Pallas kernels for 0%

commit v1 on v0

v1 whole, which is shorter than its diff:
```python
import functools

import jax
import jax.numpy as jnp
from jax import lax
from jax.experimental import pallas as pl
from jax.experimental.pallas import tpu as pltpu
from jax.sharding import PartitionSpec as P

HEAD_DIM = 64
ROT_DIM = 16
STEP = 10
EPS_NORM = 1e-05
BETA_ONE = 0.9
BETA_TWO = 0.999
ADAM_EPS = 1e-08
RATE_MATRIX = 0.05
RATE_VECTOR = 0.2
DECAY_MATRIX = 0.1
ROPE_BASE = 10000.0
INV_ROOT_TWO = 0.7071067811865476
INV_ROOT_TAU = 0.3989422804014327
MASKED = -1e30
LANES = 128
AXES = ("dp", "zero")
F32 = jnp.float32
BF16 = jnp.bfloat16
VMEM_LIMIT = 58 * 1024 * 1024


def spec(block, index, single=False):
    if single:
        return pl.BlockSpec(block, index, pipeline_mode=pl.Buffered(1))
    return pl.BlockSpec(block, index)


def whole(shape):
    return spec(shape, lambda *_: (0,) * len(shape), single=True)


def scalars():
    return pl.BlockSpec(memory_space=pltpu.SMEM)


def kernel_call(body, grid, in_specs, out_specs, out_shape, flops, moved, scratch=(), name=None):
    return pl.pallas_call(
        body,
        grid=grid,
        in_specs=in_specs,
        out_specs=out_specs,
        out_shape=out_shape,
        scratch_shapes=list(scratch),
        cost_estimate=pl.CostEstimate(flops=int(flops), bytes_accessed=int(moved), transcendentals=0),
        compiler_params=pltpu.CompilerParams(
            vmem_limit_bytes=VMEM_LIMIT, dimension_semantics=("arbitrary",) * len(grid)
        ),
        name=name,
    )


def nn(left, right):
    return lax.dot_general(left, right, (((1,), (0,)), ((), ())), preferred_element_type=F32)


def nt(left, right):
    return lax.dot_general(left, right, (((1,), (1,)), ((), ())), preferred_element_type=F32)


def tn(left, right):
    return lax.dot_general(left, right, (((0,), (0,)), ((), ())), preferred_element_type=F32)


def offset_of(place):
    return 2 * (place % 4) + place // 4


def low_lanes():
    return lax.broadcasted_iota(jnp.int32, (1, LANES), 1) < HEAD_DIM


def pick_parity(core, tile_a, tile_b):
    low = low_lanes()
    even = jnp.where(low, tile_a, pltpu.roll(tile_b, HEAD_DIM, 1))
    odd = jnp.where(low, pltpu.roll(tile_a, HEAD_DIM, 1), tile_b)
    return jnp.where(core == 0, even, odd)


def prep_attn_body(ids, w_qkv, w_out, vec, out):
    core = ids[1]
    for part in range(3):
        for tile in range(4):
            base = part * 1024 + tile * 256
            out[part * 128 : (part + 1) * 128, tile * 128 : (tile + 1) * 128] = pick_parity(
                core, w_qkv[:, base : base + 128], w_qkv[:, base + 128 : base + 256]
            ).astype(BF16)
    rows = w_out[pl.ds(pl.multiple_of(core * 64, 64), 64), :].astype(BF16)
    out[384:448, :] = rows[:, :512]
    out[448:512, :] = rows[:, 512:]
    out[512:528, :] = vec[...].astype(BF16)


def prep_mlp_body(ids, w_up, w_down, out_a, out_b):
    core = ids[1]
    for part, out in enumerate((out_a, out_b)):
        for owner in range(8):
            start = pl.multiple_of(owner * 512 + core * 256 + part * 128, 128)
            out[0:128, owner * 128 : (owner + 1) * 128] = w_up[:, pl.ds(start, 128)].astype(BF16)
        out[128:256, :] = w_down[pl.ds(pl.multiple_of(core * 256 + part * 128, 128), 128), :].astype(BF16)


def join_attn_body(ids, *refs):
    pieces, (w_qkv, w_out, vec, bias) = refs[:8], refs[8:]
    me, core = ids[0], ids[1]
    for place, piece in enumerate(pieces):
        owner = jnp.bitwise_xor(me, offset_of(place))
        at = pl.ds(pl.multiple_of(owner * 128, 128), 128)
        at_half = pl.ds(pl.multiple_of(owner * 64, 64), 64)
        for part in range(3):
            w_qkv[at, part * 512 : (part + 1) * 512] = piece[part * 128 : (part + 1) * 128, :]
        w_out[at_half, 0:512] = piece[384:448, :]
        w_out[at_half, 512:1024] = piece[448:512, :]
        vec[:, at] = piece[512:528, 0:128].astype(F32)
    for part in range(3):
        for tile in range(4):
            base = tile * 256
            row = slice(4 + part, 5 + part)
            bias[:, part * 512 + tile * 128 : part * 512 + (tile + 1) * 128] = pick_parity(
                core, vec[row, base : base + 128], vec[row, base + 128 : base + 256]
            )


def normalize(inputs):
    centred = inputs - jnp.mean(inputs, axis=-1, keepdims=True)
    variance = jnp.mean(centred * centred, axis=-1, keepdims=True)
    inv_std = lax.rsqrt(variance + EPS_NORM)
    return centred * inv_std, inv_std


def norm_body(tok, dy, vec, attn_in, mlp_in, attn_t, mlp_t, dy_t, dy_sum):
    normed, _ = normalize(tok[...].astype(F32))
    attn = (normed * vec[0:1, :] + vec[1:2, :]).astype(BF16)
    mlp = (normed * vec[2:3, :] + vec[3:4, :]).astype(BF16)
    attn_in[...] = attn
    mlp_in[...] = mlp
    attn_t[...] = attn.T
    mlp_t[...] = mlp.T
    grad = dy[...]
    dy_t[...] = grad.T

    @pl.when(pl.program_id(0) == 0)
    def _():
        dy_sum[...] = jnp.zeros_like(dy_sum)

    dy_sum[0:1, :] += jnp.sum(grad.astype(F32), axis=0, keepdims=True)


def qkv_body(attn_in, dy, w_qkv, w_out, bias, cos, sin_lo, sin_hi, q, k, v, d_att):
    rows = attn_in[...]
    for part, out in enumerate((q, k, v)):
        cols = slice(part * 512, (part + 1) * 512)
        acc = nn(rows, w_qkv[:, cols]) + bias[:, cols]
        if part == 2:
            out[...] = acc.astype(BF16)
            continue
        for tile in range(4):
            x = acc[:, tile * 128 : (tile + 1) * 128]
            x = x * cos[...] + pltpu.roll(x, 8, 1) * sin_hi[...] + pltpu.roll(x, 120, 1) * sin_lo[...]
            if part == 0:
                x = x * HEAD_DIM ** (-0.5)
            out[:, tile * 128 : (tile + 1) * 128] = x.astype(BF16)
    d_att[...] = nt(dy[...], w_out[...]).astype(BF16)


ATTN_ROWS = 256


def attn_body(q, k, v, d_att, seg_col, seg_row, cos, sin_lo, sin_hi, att, grad, dq_acc, dk_acc, dv_acc):
    row_count = q.shape[0]
    low = low_lanes()
    dk_acc[...] = jnp.zeros_like(dk_acc)
    dv_acc[...] = jnp.zeros_like(dv_acc)
    step = ATTN_ROWS
    causal = lax.broadcasted_iota(jnp.int32, (step, step), 0) >= lax.broadcasted_iota(
        jnp.int32, (step, step), 1
    )
    for first in range(0, row_count, step):
        rows = slice(first, first + step)
        ids = seg_col[rows, :]
        ranges = [(0, first), (first, first + step)] if first else [(0, step)]
        outs = []
        dqs = []
        for half in range(2):
            lanes = low if half == 0 else jnp.logical_not(low)
            q_h = jnp.where(lanes, q[rows, :], jnp.zeros((), BF16))
            da_h = jnp.where(lanes, d_att[rows, :], jnp.zeros((), BF16))
            scores = []
            for begin, end in ranges:
                allowed = ids == seg_row[0, :, begin:end]
                if begin == first:
                    allowed = allowed & causal
                scores.append(jnp.where(allowed, nt(q_h, k[begin:end, :]), MASKED))
            top = functools.reduce(jnp.maximum, [jnp.max(s, axis=-1, keepdims=True) for s in scores])
            scores = [jnp.exp(s - top) for s in scores]
            total = functools.reduce(jnp.add, [jnp.sum(s, axis=-1, keepdims=True) for s in scores])
            inv = 1.0 / total
            probs = [s * inv for s in scores]
            low_probs = [p.astype(BF16) for p in probs]
            outs.append(
                functools.reduce(jnp.add, [nn(p, v[b:e, :]) for p, (b, e) in zip(low_probs, ranges)])
            )
            grad_probs = [nt(da_h, v[b:e, :]) for b, e in ranges]
            delta = functools.reduce(
                jnp.add, [jnp.sum(g * p, axis=-1, keepdims=True) for g, p in zip(grad_probs, probs)]
            )
            grad_scores = [(p * (g - delta)).astype(BF16) for g, p in zip(grad_probs, probs)]
            dqs.append(
                functools.reduce(jnp.add, [nn(g, k[b:e, :]) for g, (b, e) in zip(grad_scores, ranges)])
            )
            for g, p, (b, e) in zip(grad_scores, low_probs, ranges):
                dk_acc[b:e, :] += tn(g, q_h)
                dv_acc[b:e, :] += tn(p, da_h)
        att[rows, :] = jnp.where(low, outs[0], outs[1]).astype(BF16)
        dq_acc[rows, :] = jnp.where(low, dqs[0], dqs[1]) * HEAD_DIM ** (-0.5)
    for part, acc in enumerate((dq_acc, dk_acc)):
        x = acc[...]
        x = x * cos[...] - pltpu.roll(x, 8, 1) * sin_hi[...] - pltpu.roll(x, 120, 1) * sin_lo[...]
        grad[part] = x.astype(BF16)
    grad[2] = dv_acc[...].astype(BF16)


def attn_weights_body(ids, attn_t, dy_t, grad, att, out_a, out_b, bias, result):
    me = ids[0]
    step = pl.program_id(0)

    @pl.when(step < 3)
    def _():
        rhs = grad[0]
        result[...] = nn(attn_t[...], rhs).astype(BF16)
        cols = pl.ds(pl.multiple_of(step * 512, 512), 512)
        bias[0:1, cols] = jnp.sum(rhs.astype(F32), axis=0, keepdims=True)
        for place in range(8):
            out = out_a if place < 4 else out_b
            owner = jnp.bitwise_xor(me, offset_of(place))
            out[place % 4, 0:128, cols] = result[pl.ds(pl.multiple_of(owner * 128, 128), 128), :]

    @pl.when(step == 3)
    def _():
        result[...] = nn(dy_t[...], att[...]).astype(BF16)
        for place in range(8):
            out = out_a if place < 4 else out_b
            out[place % 4, 128:192, 1024:1536] = jnp.zeros((64, 512), BF16)
        flipped = result[...].T
        result[0:512, :] = flipped[:, 0:512]
        result[512:1024, :] = flipped[:, 512:1024]
        for place in range(8):
            out = out_a if place < 4 else out_b
            owner = jnp.bitwise_xor(me, offset_of(place))
            base = pl.multiple_of(owner * 64, 64)
            out[place % 4, 128:192, 0:512] = result[pl.ds(base, 64), :]
            out[place % 4, 128:192, 512:1024] = result[pl.ds(pl.multiple_of(base + 512, 64), 64), :]


def attn_back_body(grad, att, w_qkv, w_out, tok, vec, out, scaled, sums):
    normed, _ = normalize(tok[...].astype(F32))
    upstream = nt(grad[0], w_qkv[:, 0:512]) + nt(grad[1], w_qkv[:, 512:1024]) + nt(grad[2], w_qkv[:, 1024:1536])
    out[...] = nn(att[...], w_out[...])
    scaled[...] = upstream * vec[0:1, :]

    @pl.when(pl.program_id(0) == 0)
    def _():
        sums[...] = jnp.zeros_like(sums)

    sums[0:1, :] += jnp.sum(upstream * normed, axis=0, keepdims=True)
    sums[1:2, :] += jnp.sum(upstream, axis=0, keepdims=True)


def mlp_body(part, steps, ids, *refs):
    pieces = refs[:8]
    if part == 0:
        (vec, mlp_in, dy, mlp_t, dy_t, out_in, out_a, out_b, out, back, bias_up) = refs[8:19]
        w_up, w_down, hidden, grad_pre, bias, result = refs[19:]
    else:
        (vec, mlp_in, dy, mlp_t, dy_t, out_in, back_in, scaled_in, tok) = refs[8:17]
        (out_a, out_b, out, scaled, bias_up, sums) = refs[17:23]
        w_up, w_down, hidden, grad_pre, bias, result = refs[23:]
    me, core = ids[0], ids[1]
    step = pl.program_id(0)

    @pl.when(step == 0)
    def _():
        for place, piece in enumerate(pieces):
            owner = jnp.bitwise_xor(me, offset_of(place))
            at = pl.ds(pl.multiple_of(owner * 128, 128), 128)
            w_up[at, :] = piece[0:128, :]
            w_down[at, :] = piece[128:256, :]
        for owner in range(8):
            start = pl.multiple_of((owner % 2) * 512 + core * 256 + part * 128, 128)
            row = 8 + owner // 2
            bias[0:1, owner * 128 : (owner + 1) * 128] = vec[row : row + 1, pl.ds(start, 128)]
        bias_up[...] = jnp.zeros_like(bias_up)
        if part:
            sums[...] = jnp.zeros_like(sums)

    rows = mlp_in[...]
    grads = dy[...]
    count = rows.shape[0]
    at = pl.ds(pl.multiple_of(step * count, count), count)
    for col in range(0, 1024, 256):
        cols = slice(col, col + 256)
        pre = nn(rows, w_up[:, cols]) + bias[0:1, cols]
        grad_hidden = nt(grads, w_down[cols, :])
        cdf = 0.5 + 0.5 * lax.erf(pre * INV_ROOT_TWO)
        pdf = jnp.exp(-0.5 * pre * pre) * INV_ROOT_TAU
        hidden[at, cols] = (pre * cdf).astype(BF16)
        gp = (grad_hidden * (cdf + pre * pdf)).astype(BF16)
        grad_pre[at, cols] = gp
        bias_up[0:1, cols] += jnp.sum(gp.astype(F32), axis=0, keepdims=True)
    out[...] = out_in[...] + nn(hidden[at, :], w_down[...])
    upstream = nt(grad_pre[at, :], w_up[...])
    if part == 0:
        back[...] = upstream
    else:
        upstream = back_in[...] + upstream
        scaled[...] = scaled_in[...] + upstream * vec[2:3, :]
        normed, _ = normalize(tok[...].astype(F32))
        sums[0:1, :] += jnp.sum(upstream * normed, axis=0, keepdims=True)
        sums[1:2, :] += jnp.sum(upstream, axis=0, keepdims=True)

    @pl.when(step == steps - 1)
    def _():
        for col in range(0, 1024, 512):
            cols = slice(col, col + 512)
            result[...] = nn(mlp_t[...], grad_pre[:, cols]).astype(BF16)
            for place in range(8):
                out_ref = out_a if place < 4 else out_b
                owner = jnp.bitwise_xor(me, offset_of(place))
                out_ref[place % 4, 0:128, cols] = result[pl.ds(pl.multiple_of(owner * 128, 128), 128), :]
        for col in range(0, 1024, 512):
            cols = slice(col, col + 512)
            flipped = nn(dy_t[...], hidden[:, cols]).astype(BF16).T
            w_down[cols, :] = flipped
        for place in range(8):
            out_ref = out_a if place < 4 else out_b
            owner = jnp.bitwise_xor(me, offset_of(place))
            out_ref[place % 4, 128:256, :] = w_down[pl.ds(pl.multiple_of(owner * 128, 128), 128), :]


def final_body(tok, dy, vec, out_own, out_other, scaled_own, scaled_other, out, grad):
    inputs = tok[...].astype(F32)
    normed, inv_std = normalize(inputs)
    branches = out_own[...] + out_other[...].astype(F32)
    out[...] = (inputs + branches + (vec[7:8, :] + vec[12:13, :])).astype(BF16)
    scaled = scaled_own[...] + scaled_other[...].astype(F32)
    grad[...] = dy[...].astype(F32) + inv_std * (
        scaled
        - jnp.mean(scaled, axis=-1, keepdims=True)
        - normed * jnp.mean(scaled * normed, axis=-1, keepdims=True)
    )


def adam_math(weight, first, second, gradient, rate, decay):
    first_new = BETA_ONE * first + (1.0 - BETA_ONE) * gradient
    second_new = BETA_TWO * second + (1.0 - BETA_TWO) * gradient * gradient
    first_hat = first_new / (1.0 - BETA_ONE**STEP)
    second_hat = second_new / (1.0 - BETA_TWO**STEP)
    weight_new = weight - rate * (first_hat / (jnp.sqrt(second_hat) + ADAM_EPS) + decay * weight)
    return (first_new, second_new, weight_new)


def adam_store(refs, at, gradient):
    w, m, v, m_out, v_out, w_out = refs
    first, second, weight = adam_math(w[at], m[at], v[at], gradient, RATE_MATRIX, DECAY_MATRIX)
    m_out[at] = first
    v_out[at] = second
    w_out[at] = weight


def parities(core, own, other):
    return jnp.where(core == 0, own, other), jnp.where(core == 0, other, own)


def adam_attn_body(ids, own, other, own_out, other_out, *refs):
    core = ids[1]
    step = pl.program_id(0)
    low = low_lanes()

    @pl.when(step < 3)
    def _():
        qkv_refs = refs[0:3] + refs[6:9]
        for tile in range(4):
            cols = slice(tile * 128, (tile + 1) * 128)
            even, odd = parities(core, own[:, cols].astype(F32), other[:, cols].astype(F32))
            first = jnp.where(low, even, pltpu.roll(odd, HEAD_DIM, 1))
            second = jnp.where(low, pltpu.roll(even, HEAD_DIM, 1), odd)
            adam_store(qkv_refs, (slice(None), slice(tile * 256, tile * 256 + 128)), first)
            adam_store(qkv_refs, (slice(None), slice(tile * 256 + 128, tile * 256 + 256)), second)

    @pl.when(step == 0)
    def _():
        out_refs = refs[3:6] + refs[9:12]
        even, odd = parities(core, own_out[:, 0:1024].astype(F32), other_out[:, 0:1024].astype(F32))
        adam_store(out_refs, (slice(0, 64), slice(None)), even)
        adam_store(out_refs, (slice(64, 128), slice(None)), odd)


def adam_mlp_body(ids, own_a, other_a, own_b, other_b, *refs):
    core = ids[1]
    step = pl.program_id(0)
    up_refs = refs[0:3] + refs[6:9]
    down_refs = refs[3:6] + refs[9:12]
    for half in range(2):
        cols = pl.ds(pl.multiple_of(step * 256 + half * 128, 128), 128)
        for part, (own, other) in enumerate(((own_a, other_a), (own_b, other_b))):
            even, odd = parities(core, own[0:128, cols].astype(F32), other[0:128, cols].astype(F32))
            for parity, grad in enumerate((even, odd)):
                base = half * 512 + parity * 256 + part * 128
                adam_store(up_refs, (slice(None), slice(base, base + 128)), grad)
    cols = pl.ds(pl.multiple_of(step * 256, 256), 256)
    for part, (own, other) in enumerate(((own_a, other_a), (own_b, other_b))):
        even, odd = parities(core, own[128:256, cols].astype(F32), other[128:256, cols].astype(F32))
        for parity, grad in enumerate((even, odd)):
            base = parity * 256 + part * 128
            adam_store(down_refs, (slice(base, base + 128), slice(None)), grad)


def rotary_tables(segments):
    row_count = segments.shape[0]
    row_index = jnp.arange(row_count, dtype=jnp.int32)
    earlier = jnp.concatenate([jnp.full((1,), -1, jnp.int32), segments[:-1]])
    starts = jnp.where(segments != earlier, row_index, 0)
    position = (row_index - lax.cummax(starts, axis=0)).astype(F32)
    half_dim = ROT_DIM // 2
    dims = jnp.arange(LANES, dtype=jnp.int32) % HEAD_DIM
    frequency = ROPE_BASE ** (-2.0 * (dims % half_dim).astype(F32) / ROT_DIM)
    turned = dims < ROT_DIM
    angles = position[:, None] * jnp.where(turned, frequency, 0.0)[None, :]
    cosine, sine = jnp.cos(angles), jnp.sin(angles)
    front = (dims < half_dim)[None, :]
    return cosine, jnp.where(front, -sine, 0.0), jnp.where(front, 0.0, sine)


def on_device(
    sizes,
    tokens,
    segments,
    cotangent,
    w_qkv,
    w_out,
    w_up,
    w_down,
    vectors,
    m_qkv,
    m_out,
    m_up,
    m_down,
    m_vectors,
    v_qkv,
    v_out,
    v_up,
    v_down,
    v_vectors,
):
    copies, owners = sizes
    me = lax.axis_index("zero")
    core = lax.axis_index("dp") % 2
    ids = jnp.stack([me, core]).astype(jnp.int32)

    def swap(value, dp_bits, zero_bits):
        pairs = [
            (d * owners + z, (d ^ dp_bits) * owners + (z ^ zero_bits))
            for d in range(copies)
            for z in range(owners)
        ]
        return lax.ppermute(value, AXES, pairs)

    def after(value, *others):
        return lax.optimization_barrier((value,) + others)[0]

    def gather(own):
        near = [own] + [swap(own, 0, 2 * k) for k in (1, 2, 3)]
        far = [swap(piece, 0, 1) for piece in near]
        return near + far

    def reduce(blocks_near, blocks_far):
        arrived = swap(blocks_far, 0, 1)
        parts = [
            (blocks_near[k].astype(F32) + arrived[k].astype(F32)).astype(BF16) for k in range(4)
        ]
        total = parts[0].astype(F32)
        for k in (1, 2, 3):
            total = total + swap(parts[k], 0, 2 * k).astype(F32)
        total = total.astype(BF16)
        bit = 2
        while bit < copies:
            total = (total.astype(F32) + swap(total, bit, 0).astype(F32)).astype(BF16)
            bit *= 2
        return total, swap(total, 1, 0)

    T, width = tokens.shape
    rows = 2 * T
    sds = jax.ShapeDtypeStruct

    with jax.named_scope("prep"):
        own_attn = kernel_call(
            prep_attn_body,
            (1,),
            [scalars(), whole((128, 3072)), whole((128, 1024)), whole((16, 512))],
            whole((528, 512)),
            sds((528, 512), BF16),
            0,
            3e6,
            name="prep_attn",
        )(ids, w_qkv, w_out, jnp.pad(vectors, ((0, 3), (0, 384))))
        own_mlp = kernel_call(
            prep_mlp_body,
            (1,),
            [scalars(), whole((128, 4096)), whole((512, 1024))],
            [whole((256, 1024))] * 2,
            [sds((256, 1024), BF16)] * 2,
            0,
            5e6,
            name="prep_mlp",
        )(ids, w_up, w_down)

    with jax.named_scope("gather"):
        attn_pieces = gather(own_attn)
        tok_other = swap(tokens, 1, 0)
        dy_other = swap(cotangent, 1, 0)
        seg_other = swap(segments, 1, 0)
        mlp_pieces = [gather(after(own_mlp[0], *attn_pieces[1:4]))]
        mlp_pieces.append(gather(after(own_mlp[1], *mlp_pieces[0][1:4])))

    with jax.named_scope("rows"):
        tok = jnp.concatenate([tokens, tok_other], axis=0)
        dy = jnp.concatenate([cotangent, dy_other], axis=0)
        tables = [
            jnp.concatenate(pair, axis=0)
            for pair in zip(rotary_tables(segments), rotary_tables(seg_other))
        ]
        seg_row = jnp.stack([segments, seg_other])[:, None, :]
        seg_col = jnp.concatenate([segments, seg_other])[:, None]

    with jax.named_scope("join"):
        full_qkv, full_out, vec, bias_qkv = kernel_call(
            join_attn_body,
            (1,),
            [scalars()] + [whole((528, 512))] * 8,
            [whole((1024, 1536)), whole((512, 1024)), whole((16, 1024)), whole((1, 1536))],
            [sds((1024, 1536), BF16), sds((512, 1024), BF16), sds((16, 1024), F32), sds((1, 1536), F32)],
            0,
            9e6,
            name="join_attn",
        )(ids, *attn_pieces)

    row_block = lambda n, c=width: spec((n, c), lambda i: (i, 0))
    col_block = lambda n: spec((width, n), lambda i: (0, i))
    with jax.named_scope("norm"):
        attn_in, mlp_in, attn_t, mlp_t, dy_t, dy_sum = kernel_call(
            norm_body,
            (rows // 256,),
            [row_block(256), row_block(256), whole((16, width))],
            [row_block(256), row_block(256), col_block(256), col_block(256), col_block(256), whole((8, width))],
            [sds((rows, width), BF16)] * 2 + [sds((width, rows), BF16)] * 3 + [sds((8, width), F32)],
            0,
            30e6,
            name="norm",
        )(tok, dy, vec)

    with jax.named_scope("qkv"):
        q, k, v, d_att = kernel_call(
            qkv_body,
            (rows // 512,),
            [row_block(512), row_block(512), whole((1024, 1536)), whole((512, 1024)), whole((1, 1536))]
            + [row_block(512, 128)] * 3,
            [row_block(512, 512)] * 4,
            [sds((rows, 512), BF16)] * 4,
            2 * rows * 1024 * 2048,
            25e6,
            name="qkv",
        )(attn_in, dy, full_qkv, full_out, bias_qkv, *tables)

    with jax.named_scope("attention"):
        head_block = spec((T, 128), lambda h, m: (h, m))
        att, grad_qkv = kernel_call(
            attn_body,
            (2, 4),
            [head_block] * 4
            + [spec((T, 1), lambda h, m: (h, 0)), spec((1, 1, T), lambda h, m: (h, 0, 0))]
            + [spec((T, 128), lambda h, m: (h, 0))] * 3,
            [head_block, spec((3, T, 128), lambda h, m: (0, h, m))],
            [sds((rows, 512), BF16), sds((3, rows, 512), BF16)],
            60e9,
            20e6,
            scratch=[pltpu.VMEM((T, 128), F32)] * 3,
            name="attention",
        )(q, k, v, d_att, seg_col, seg_row, *tables)

    with jax.named_scope("attn_weights"):
        grad_near, grad_far, bias_sum = kernel_call(
            attn_weights_body,
            (4,),
            [
                scalars(),
                whole((width, rows)),
                whole((width, rows)),
                spec((1, rows, 512), lambda n: (jnp.minimum(n, 2), 0, 0)),
                whole((rows, 512)),
            ],
            [whole((4, 192, 1536))] * 2 + [whole((8, 1536))],
            [sds((4, 192, 1536), BF16)] * 2 + [sds((8, 1536), F32)],
            2 * rows * 1024 * 2048,
            25e6,
            scratch=[pltpu.VMEM((1024, 512), BF16)],
            name="attn_weights",
        )(ids, attn_t, dy_t, grad_qkv, att)
        attn_total = reduce(grad_near, grad_far)

    with jax.named_scope("attn_back"):
        branch, scaled, attn_sums = kernel_call(
            attn_back_body,
            (rows // 512,),
            [spec((3, 512, 512), lambda i: (0, i, 0)), row_block(512, 512), whole((1024, 1536)), whole((512, 1024))]
            + [row_block(512), whole((16, width))],
            [row_block(512), row_block(512), whole((8, width))],
            [sds((rows, width), F32)] * 2 + [sds((8, width), F32)],
            2 * rows * 1024 * 2048,
            35e6,
            name="attn_back",
        )(grad_qkv, att, full_qkv, full_out, tok, vec)

    mlp_totals = []
    bias_ups = []
    back = None
    mlp_sums = None
    steps = rows // 256
    for part in range(2):
        with jax.named_scope("mlp"):
            ins = [ids] + mlp_pieces[part] + [vec, mlp_in, dy, mlp_t, dy_t, branch]
            in_specs = (
                [scalars()]
                + [whole((256, 1024))] * 8
                + [whole((16, width)), row_block(256), row_block(256), whole((width, rows)), whole((width, rows))]
                + [row_block(256)]
            )
            out_specs = [whole((4, 256, 1024))] * 2 + [row_block(256)] * 2 + [whole((8, 1024))]
            out_shape = (
                [sds((4, 256, 1024), BF16)] * 2 + [sds((rows, width), F32)] * 2 + [sds((8, 1024), F32)]
            )
            if part:
                ins += [back, scaled, tok]
                in_specs += [row_block(256)] * 3
                out_specs.append(whole((8, width)))
                out_shape.append(sds((8, width), F32))
            results = kernel_call(
                functools.partial(mlp_body, part, steps),
                (steps,),
                in_specs,
                out_specs,
                out_shape,
                2 * rows * 1024 * 1024 * 6,
                60e6,
                scratch=[pltpu.VMEM((1024, 1024), BF16)] * 2
                + [pltpu.VMEM((rows, 1024), BF16)] * 2
                + [pltpu.VMEM((8, 1024), F32), pltpu.VMEM((1024, 512), BF16)],
                name="mlp",
            )(*ins)
            mlp_totals.append(reduce(results[0], results[1]))
            branch = results[2]
            bias_ups.append(results[4][0])
            if part:
                scaled, mlp_sums = results[3], results[5]
            else:
                back = results[3]

    with jax.named_scope("vectors"):
        is_core = jnp.arange(2) == core
        grad_bias = jnp.where(core == 0, dy_sum[0:1], 0.0)
        grad_bias_qkv = jnp.where(
            is_core[None, None, :, None], bias_sum[0].reshape(3, 8, 1, 64), 0.0
        ).reshape(3, width)
        grad_bias_up = jnp.where(
            is_core[None, :, None, None],
            jnp.swapaxes(jnp.stack(bias_ups).reshape(2, 8, 128), 0, 1)[:, None],
            0.0,
        ).reshape(4, width)
        grad_vectors = jnp.concatenate(
            [attn_sums[0:2], mlp_sums[0:2], grad_bias_qkv, grad_bias, grad_bias_up, grad_bias], axis=0
        )
        share = lax.dynamic_slice_in_dim(lax.psum(grad_vectors, AXES), me * 128, 128, 1)
        first_vectors, second_vectors, new_vectors = adam_math(
            vectors, m_vectors, v_vectors, share, RATE_VECTOR, 0.0
        )

    with jax.named_scope("final"):
        out_other = swap(branch[T:].astype(BF16), 1, 0)
        scaled_other = swap(scaled[T:].astype(BF16), 1, 0)
        layer_out, tokens_grad = kernel_call(
            final_body,
            (T // 256,),
            [row_block(256), row_block(256), whole((16, width))] + [row_block(256)] * 4,
            [row_block(256)] * 2,
            [sds((T, width), BF16), sds((T, width), F32)],
            0,
            26e6,
            name="final",
        )(tokens, cotangent, vec, branch, out_other, scaled, scaled_other)

    with jax.named_scope("adam"):
        own, other = attn_total
        third = lambda n: (0, jnp.minimum(n, 2))
        wide = [spec((128, 1024), third)] * 3 + [whole((128, 1024))] * 3
        updated_attn = kernel_call(
            adam_attn_body,
            (3,),
            [scalars()]
            + [spec((128, 512), third)] * 2
            + [spec((64, 1536), lambda n: (2, 0), single=True)] * 2
            + wide,
            wide,
            [sds((128, 3072), F32)] * 3 + [sds((128, 1024), F32)] * 3,
            0,
            13e6,
            name="adam_attn",
        )(ids, own, other, own, other, w_qkv, m_qkv, v_qkv, w_out, m_out, v_out)
        wide = [spec((128, 1024), lambda n: (0, n))] * 3 + [spec((512, 256), lambda n: (0, n))] * 3
        updated_mlp = kernel_call(
            adam_mlp_body,
            (4,),
            [scalars()] + [whole((256, 1024))] * 4 + wide,
            wide,
            [sds((128, 4096), F32)] * 3 + [sds((512, 1024), F32)] * 3,
            0,
            27e6,
            name="adam_mlp",
        )(ids, *mlp_totals[0], *mlp_totals[1], w_up, m_up, v_up, w_down, m_down, v_down)
    first_qkv, second_qkv, new_qkv, first_out, second_out, new_out = updated_attn
    first_up, second_up, new_up, first_down, second_down, new_down = updated_mlp
    return (
        layer_out,
        tokens_grad,
        first_qkv,
        first_out,
        first_up,
        first_down,
        first_vectors,
        second_qkv,
        second_out,
        second_up,
        second_down,
        second_vectors,
        new_qkv,
        new_out,
        new_up,
        new_down,
        new_vectors,
    )


def solution(mesh):
    rows, owned, spread = P(AXES, None), P("zero", None), P(None, "zero")
    state = (owned, owned, owned, owned, spread)
    return jax.shard_map(
        functools.partial(on_device, (mesh.shape["dp"], mesh.shape["zero"])),
        mesh=mesh,
        in_specs=(rows, P(AXES), rows) + state * 3,
        out_specs=(rows, rows) + state * 3,
        check_vma=False,
    )
```

time: 1690 us -> 670 us (0.40)
  waiting for transfers between devices: 1130 us -> 248 us
  matrix products: 307 us -> 0 us
  Pallas kernels: 0 us -> 253 us
  other arithmetic: 118 us -> 18 us
  starting transfers between devices: 0.7 us -> 69.7 us
  local copies, waits for them, and re-layouts: 67.7 us -> 32.9 us
    reduce_scatter x4 -> x0, waiting for transfers between devices: 851 us -> none  [the longest x1 349 us: on_device(): lax.psum_scatter(regroup(grad_w_down, 0, owners, replicas), ('dp', 'zero'...]
    dot_general x24 -> x0, matrix products: 307 us -> none  [the longest x4 53.6 us: times_transposed(): lax.dot_general(left, right, (((1,), (1,)), ((), ())), preferred_element_...]
    pallas_call x0 -> x13, Pallas kernels: none -> 253 us  [the longest x2 80.9 us: on_device(): kernel_call(functools.partial(mlp_body, part, steps), (steps,), in_specs,...]
    ppermute x0 -> x44, waiting for transfers between devices: none -> 248 us  [swap(): return lax.ppermute(value, AXES, pairs)]
    all_gather x7 -> x0, waiting for transfers between devices: 167 us -> none  [the longest x1 65.7 us: on_device(): lax.all_gather(w_qkv.astype(jnp.bfloat16), 'zero', axis=0, tiled=True)]
    unnamed x13 -> x0, waiting for transfers between devices: 116 us -> none
    ppermute x0 -> x44, starting transfers between devices: none -> 69.7 us  [swap(): return lax.ppermute(value, AXES, pairs)]
    all_gather x3 -> x0, blocking collectives: 40.3 us -> none  [the longest x1 28.4 us: on_device(): lax.all_gather(vectors.astype(jnp.bfloat16), 'zero', axis=1, tiled=True)]
  transfers between devices with their start and end apart: 12 -> 44, of which waited for: 11 -> 15; matrix products, arithmetic and copies ran while one was open for 28% -> 6% of each run, Pallas kernels for 0% -> 37%
where the time goes in v1:
time: 670 us; the launch traced here: 663 us
  Pallas kernels  253 us (38%)
  waiting for transfers between devices  248 us (37%)
  starting transfers between devices  69.7 us (10%)
  blocking collectives  40.2 us (6%)
  local copies, waits for them, and re-layouts  32.9 us (5%)
  other arithmetic  18 us (3%)
    ppermute x44, waiting for transfers between devices, swap(): return lax.ppermute(value, AXES, pairs)  248 us
    pallas_call x2, Pallas kernels, on_device(): kernel_call(functools.partial(mlp_body, part, steps), (steps,), in_specs,...  80.9 us
    pallas_call x1, Pallas kernels, on_device(): kernel_call(attn_body, (2, 4), [head_block] * 4 + [spec((T, 1), lambda h,...  70 us
    ppermute x44, starting transfers between devices, swap(): return lax.ppermute(value, AXES, pairs)  69.7 us
    psum x1, blocking collectives, on_device(): lax.psum(grad_vectors, AXES)  40.2 us
    pallas_call x1, Pallas kernels, on_device(): kernel_call(attn_back_body, (rows // 512,), [spec((3, 512, 512), lambda i...  17.7 us
    pallas_call x1, Pallas kernels, on_device(): kernel_call(attn_weights_body, (4,), [scalars(), whole((width, rows)), wh...  16.7 us
    pallas_call x1, Pallas kernels, on_device(): kernel_call(norm_body, (rows // 256,), [row_block(256), row_block(256), w...  13.8 us
  transfers between devices with their start and end apart: 44, of which 15 were waited for; matrix products, arithmetic and copies ran while one was open for 6% of the time, Pallas kernels for 37%

profile of v1, /device:TPU:0, one launch (start us, length us, event | category | flops | bytes accessed | tf_op | source)
XLA Modules:
  0.0 663.0 jit_solution(12596388480491880023)
XLA Ops:
  2.6 2.7 prep_attn.1.refs_0_
  5.3 2.9 collective-permute-start.3
  8.3 3.6 collective-permute-start.2
  13.0 3.1 constant_dynamic-update-slice_fusion.1
  16.1 3.1 constant_dynamic-update-slice_fusion.3
  19.2 3.5 prep_mlp.1
  24.3 23.8 %collective-permute-start = (bf16[528,512]{1,0:T(8,128)(2,1)S(1)}, bf16[528,512]{1,0:T(8,128)(2,1)}, u32[]{:S(2)}, u32[]{:S(2)}) collective-permute-start(bf16[528,512]{1,0:T(8,128)(2,1)S(1)} %copy-done.5), channel_id=1, source_target_pairs={{0,2},{1,3},{2,0},{3,1},{4,6},{5,7},{6,4},{7,5},{8,10},{9,11},{10,... | collective-permute-start | bytes 1622024 | tf_op jit(solution)/shard_map/gather/ppermute | solution.py:474
  48.7 9.5 %collective-permute-done.1.refs_2_ = bf16[528,512]{1,0:T(8,128)(2,1)} collective-permute-done((bf16[528,512]{1,0:T(8,128)(2,1)S(1)}, bf16[528,512]{1,0:T(8,128)(2,1)}, u32[]{:S(2)}, u32[]{:S(2)}) %collective-permute-start.1) | collective-permute-done | bytes 540704 | tf_op jit(solution)/shard_map/gather/ppermute | solution.py:474
  58.2 11.3 %collective-permute-done.refs_1_ = bf16[528,512]{1,0:T(8,128)(2,1)} collective-permute-done((bf16[528,512]{1,0:T(8,128)(2,1)S(1)}, bf16[528,512]{1,0:T(8,128)(2,1)}, u32[]{:S(2)}, u32[]{:S(2)}) %collective-permute-start) | collective-permute-done | bytes 540704 | tf_op jit(solution)/shard_map/gather/ppermute | solution.py:474
  69.4 2.0 collective-permute-start.9
  71.5 2.3 collective-permute-start.7
  73.9 3.8 fusion.9
  77.7 8.7 %collective-permute-done.9.refs_3_ = bf16[256,1024]{1,0:T(8,128)(2,1)S(1)} collective-permute-done((bf16[256,1024]{1,0:T(8,128)(2,1)}, bf16[256,1024]{1,0:T(8,128)(2,1)S(1)}, u32[]{:S(2)}, u32[]{:S(2)}) %collective-permute-start.9) | collective-permute-done | bytes 524320 | tf_op jit(solution)/shard_map/gather/ppermute | solution.py:474
  86.9 29.0 %collective-permute-done.8.refs_2_ = bf16[256,1024]{1,0:T(8,128)(2,1)S(1)} collective-permute-done((bf16[256,1024]{1,0:T(8,128)(2,1)}, bf16[256,1024]{1,0:T(8,128)(2,1)S(1)}, u32[]{:S(2)}, u32[]{:S(2)}) %collective-permute-start.8) | collective-permute-done | bytes 524320 | tf_op jit(solution)/shard_map/gather/ppermute | solution.py:474
  122.9 8.5 %collective-permute-done.5.refs_6_ = bf16[528,512]{1,0:T(8,128)(2,1)} collective-permute-done((bf16[528,512]{1,0:T(8,128)(2,1)}, bf16[528,512]{1,0:T(8,128)(2,1)}, u32[]{:S(2)}, u32[]{:S(2)}) %collective-permute-start.5) | collective-permute-done | bytes 540704 | tf_op jit(solution)/shard_map/gather/ppermute | solution.py:474
  132.9 10.0 %collective-permute-done.4.refs_5_ = bf16[528,512]{1,0:T(8,128)(2,1)} collective-permute-done((bf16[528,512]{1,0:T(8,128)(2,1)}, bf16[528,512]{1,0:T(8,128)(2,1)}, u32[]{:S(2)}, u32[]{:S(2)}) %collective-permute-start.4) | collective-permute-done | bytes 540704 | tf_op jit(solution)/shard_map/gather/ppermute | solution.py:474
  143.0 4.4 join_attn.1
  147.4 2.2 collective-permute-start.10
  149.5 3.1 constant_dynamic-update-slice_fusion.tok.refs_16_
  153.2 1.8 constant_dynamic-update-slice_fusion.2.dy.refs_10_
  154.9 2.0 copy-done.1
  157.0 13.8 %norm.1 = (bf16[2048,1024]{1,0:T(8,128)(2,1)}, bf16[2048,1024]{1,0:T(8,128)(2,1)}, bf16[1024,2048]{1,0:T(8,128)(2,1)}, bf16[1024,2048]{1,0:T(8,128)(2,1)}, bf16[...) custom-call(bf16[2048,1024]{1,0:T(8,128)(2,1)} %constant_dynamic-update-slice_fusion.tok.refs_16_, bf16[2048,1024]{1,0:T(8,128)(2,1)} %copy-done.1, ...), custom_call_target="tpu_custom_call" | custom-call | bytes 30000000 | tf_op jit(solution)/shard_map/norm/norm/pallas_call | solution.py:558
  170.8 13.8 %qkv.1 = (bf16[2048,512]{1,0:T(8,128)(2,1)}, bf16[2048,512]{1,0:T(8,128)(2,1)}, bf16[2048,512]{1,0:T(8,128)(2,1)}, bf16[2048,512]{1,0:T(8,128)(2,1)}) custom-call(bf16[2048,1024]{1,0:T(8,128)(2,1)} %get-tuple-element.76.attn_in, bf16[2048,1024]{1,0:T(8,128)(2,1)} %copy-done.1, bf16[1024,1536]{1,0:T(8,128)(2,1)} %get-tuple-element.77.w_qkv, ...), custom_call_target="tpu_custom_call" | custom-call | flops 8589934592 | bytes 25000000 | tf_op jit(solution)/shard_map/qkv/qkv/pallas_call | solution.py:570
  184.6 70.0 %attention.1 = (bf16[2048,512]{1,0:T(8,128)(2,1)}, bf16[3,2048,512]{2,1,0:T(8,128)(2,1)}) custom-call(bf16[2048,512]{1,0:T(8,128)(2,1)} %get-tuple-element.80.q, bf16[2048,512]{1,0:T(8,128)(2,1)} %get-tuple-element.81.k, bf16[2048,512]{1,0:T(8,128)(2,1)} %get-tuple-element.82.v, bf16[2048,512]{1,0:T(8,128)(2,1)} %get-tuple-element.83.d_att, ...), custom_call_target="tpu_custom_call" | custom-call | flops 60000002048 | bytes 20000000 | tf_op jit(solution)/shard_map/attention/attention/pallas_call | solution.py:584
  254.6 17.7 %attn_back.1 = (f32[2048,1024]{1,0:T(8,128)}, f32[2048,1024]{1,0:T(8,128)}, f32[8,1024]{1,0:T(8,128)}) custom-call(bf16[3,2048,512]{2,1,0:T(8,128)(2,1)} %get-tuple-element.84.grad, bf16[2048,512]{1,0:T(8,128)(2,1)} %get-tuple-element.85.att, bf16[1024,1536]{1,0:T(8,128)(2,1)} %get-tuple-element.77.w_qkv, bf16[512,1024]{1,0:T(8,128)(2,1)} %get-tuple-element.78.w_out, ...), custom_call_target="tpu_custom_call" | custom-call | flops 8589934592 | bytes 35000000 | tf_op jit(solution)/shard_map/attn_back/attn_back/pallas_call | solution.py:619
  274.5 16.7 %attn_weights.1 = (bf16[4,192,1536]{2,1,0:T(8,128)(2,1)}, bf16[4,192,1536]{2,1,0:T(8,128)(2,1)}, f32[8,1536]{1,0:T(8,128)}) custom-call(s32[2]{0:T(128)} %pad_add_fusion.4.ids, bf16[1024,2048]{1,0:T(8,128)(2,1)} %get-tuple-element.94.attn_t, bf16[1024,2048]{1,0:T(8,128)(2,1)} %get-tuple-element.75.refs_12_.dy_t, ...), custom_call_target="tpu_custom_call" | custom-call | flops 8589934592 | bytes 25000000 | tf_op jit(solution)/shard_map/attn_weights/attn_weights/pallas_call | solution.py:599
  298.4 38.5 %mlp.2 = (bf16[4,256,1024]{2,1,0:T(8,128)(2,1)}, bf16[4,256,1024]{2,1,0:T(8,128)(2,1)}, f32[2048,1024]{1,0:T(8,128)}, f32[2048,1024]{1,0:T(8,128)}, f32[8,1024]{1,0:T(8,128)}) custom-call(s32[2]{0:T(128)} %pad_add_fusion.4.ids, bf16[256,1024]{1,0:T(8,128)(2,1)} %get-tuple-element.71.refs_0_, bf16[256,1024]{1,0:T(8,128)(2,1)} %copy-done.21, ...), custom_call_target="tpu_custom_call" | custom-call | flops 25769803776 | bytes 60000000 | tf_op jit(solution)/shard_map/mlp/mlp/pallas_call | solution.py:654
  337.6 3.5 collective-permute-done.14.refs_5_
  341.9 42.4 %mlp.3 = (bf16[4,256,1024]{2,1,0:T(8,128)(2,1)}, bf16[4,256,1024]{2,1,0:T(8,128)(2,1)}, f32[2048,1024]{1,0:T(8,128)}, f32[2048,1024]{1,0:T(8,128)}, f32[8,1024]{1,0:T(8,128)}, /*index=5*/f32[8,1024]{1,0:T(8,128)}) custom-call(s32[2]{0:T(128)} %pad_add_fusion.4.ids, bf16[256,1024]{1,0:T(8,128)(2,1)} %get-tuple-element.72.refs_0_, ...), custom_call_target="tpu_custom_call" | custom-call | flops 25769803776 | bytes 60000000 | tf_op jit(solution)/shard_map/mlp/mlp/pallas_call | solution.py:654
  387.7 3.8 slice.203
  391.6 4.0 slice.202
  395.6 41.1 %collective-permute-done.32 = bf16[4,256,1024]{2,1,0:T(8,128)(2,1)} collective-permute-done((bf16[4,256,1024]{2,1,0:T(8,128)(2,1)}, bf16[4,256,1024]{2,1,0:T(8,128)(2,1)}, u32[]{:S(2)}, u32[]{:S(2)}) %collective-permute-start.32) | collective-permute-done | bytes 2097184 | tf_op jit(solution)/shard_map/mlp/ppermute | solution.py:474
  436.7 2.2 fusion.20
  438.9 1.6 collective-permute-start.33
  440.5 1.7 collective-permute-start.35
  442.9 2.5 collective-permute-start.27
  445.4 32.2 %collective-permute-done.38 = bf16[4,256,1024]{2,1,0:T(8,128)(2,1)} collective-permute-done((bf16[4,256,1024]{2,1,0:T(8,128)(2,1)}, bf16[4,256,1024]{2,1,0:T(8,128)(2,1)}, u32[]{:S(2)}, u32[]{:S(2)}) %collective-permute-start.38) | collective-permute-done | bytes 2097184 | tf_op jit(solution)/shard_map/mlp/ppermute | solution.py:474
  477.6 2.7 collective-permute-start.29
  480.7 2.0 fusion.24
  482.8 24.9 %collective-permute-done.34 = bf16[256,1024]{1,0:T(8,128)(2,1)S(1)} collective-permute-done((bf16[256,1024]{1,0:T(8,128)(2,1)S(1)}, bf16[256,1024]{1,0:T(8,128)(2,1)S(1)}, u32[]{:S(2)}, u32[]{:S(2)}) %collective-permute-start.34) | collective-permute-done | bytes 524320 | tf_op jit(solution)/shard_map/mlp/ppermute | solution.py:474
  509.9 2.9 collective-permute-start.41
  512.8 37.0 %collective-permute-done.28 = bf16[192,1536]{1,0:T(8,128)(2,1)S(1)} collective-permute-done((bf16[192,1536]{1,0:T(8,128)(2,1)S(1)}, bf16[192,1536]{1,0:T(8,128)(2,1)S(1)}, u32[]{:S(2)}, u32[]{:S(2)}) %collective-permute-start.28) | collective-permute-done | bytes 589856 | tf_op jit(solution)/shard_map/attn_weights/ppermute | solution.py:474
  554.7 20.8 %collective-permute-done.40 = bf16[256,1024]{1,0:T(8,128)(2,1)S(1)} collective-permute-done((bf16[256,1024]{1,0:T(8,128)(2,1)S(1)}, bf16[256,1024]{1,0:T(8,128)(2,1)S(1)}, u32[]{:S(2)}, u32[]{:S(2)}) %collective-permute-start.40) | collective-permute-done | bytes 524320 | tf_op jit(solution)/shard_map/mlp/ppermute | solution.py:474
  579.6 8.9 %collective-permute-done.42 = bf16[256,1024]{1,0:T(8,128)(2,1)S(1)} collective-permute-done((bf16[256,1024]{1,0:T(8,128)(2,1)S(1)}, bf16[256,1024]{1,0:T(8,128)(2,1)S(1)}, u32[]{:S(2)}, u32[]{:S(2)}) %collective-permute-start.42) | collective-permute-done | bytes 524320 | tf_op jit(solution)/shard_map/mlp/ppermute | solution.py:474
  589.8 40.2 %psum.7 = f32[13,1024]{1,0:T(8,128)S(1)} all-reduce(f32[13,1024]{1,0:T(8,128)S(1)} %concatenate.35), channel_id=1, replica_groups=mesh['dp'=4,'zero'=8] {'dp','zero'}, use_global_device_ids=true, to_apply=%region_4.5 | all-reduce | flops 13312 | bytes 106496 | tf_op jit(solution)/shard_map/vectors/psum | solution.py:689
  630.6 9.8 %final.1 = (bf16[1024,1024]{1,0:T(8,128)(2,1)}, f32[1024,1024]{1,0:T(8,128)}) custom-call(bf16[1024,1024]{1,0:T(8,128)(2,1)} %tok.1, bf16[1024,1024]{1,0:T(8,128)(2,1)} %dy.1, f32[16,1024]{1,0:T(8,128)} %get-tuple-element.68.vec.refs_8_, f32[2048,1024]{1,0:T(8,128)} %get-tuple-element.90.out_own, bf16[1024,1024]{1,0:T(8,128)(2,1)} %collective-permute-done.24.out_other, ...), custom_call_target="tpu_custom_call" | custom-call | bytes 26000000 | tf_op jit(solution)/shard_map/final/final/pallas_call | solution.py:697
  642.0 11.5 %adam_mlp.1 = (f32[128,4096]{1,0:T(8,128)}, f32[128,4096]{1,0:T(8,128)}, f32[128,4096]{1,0:T(8,128)}, f32[512,1024]{1,0:T(8,128)}, f32[512,1024]{1,0:T(8,128)}, /*index=5*/f32[512,1024]{1,0:T(8,128)}) custom-call(s32[2]{0:T(128)} %pad_add_fusion.4.ids, bf16[256,1024]{1,0:T(8,128)(2,1)} %copy-done.6, bf16[256,1024]{1,0:T(8,128)(2,1)} %copy-done.11, ...), custom_call_target="tpu_custom_call" | custom-call | bytes 27000000 | tf_op jit(solution)/shard_map/adam/adam_mlp/pallas_call | solution.py:726
  654.4 8.2 %adam_attn.1 = (f32[128,3072]{1,0:T(8,128)}, f32[128,3072]{1,0:T(8,128)}, f32[128,3072]{1,0:T(8,128)}, f32[128,1024]{1,0:T(8,128)}, f32[128,1024]{1,0:T(8,128)}, /*index=5*/f32[128,1024]{1,0:T(8,128)}) custom-call(s32[2]{0:T(128)} %pad_add_fusion.4.ids, bf16[192,1536]{1,0:T(8,128)(2,1)} %copy-done.2, bf16[192,1536]{1,0:T(8,128)(2,1)} %copy-done.3, ...), custom_call_target="tpu_custom_call" | custom-call | bytes 13000000 | tf_op jit(solution)/shard_map/adam/adam_attn/pallas_call | solution.py:712
  (174 shorter events, 45.8 us)
Async XLA Ops:
  5.3 66.2 %collective-permute-start.3 = (bf16[528,512]{1,0:T(8,128)(2,1)}, bf16[528,512]{1,0:T(8,128)(2,1)S(1)}, u32[]{:S(2)}, u32[]{:S(2)}) collective-permute-start(bf16[528,512]{1,0:T(8,128)(2,1)} %prep_attn.1.refs_0_), channel_id=1, source_target_pairs={{0,1},{1,0},{2,3},{3,2},{4,5},{5,4},{6,7},{7,6},{8,9},{9,8},{10,11... | collective-permute-start | bytes 1622024 | tf_op jit(solution)/shard_map/gather/ppermute | solution.py:474
  8.3 16.1 %collective-permute-start.2 = (bf16[528,512]{1,0:T(8,128)(2,1)}, bf16[528,512]{1,0:T(8,128)(2,1)}, u32[]{:S(2)}, u32[]{:S(2)}) collective-permute-start(bf16[528,512]{1,0:T(8,128)(2,1)} %prep_attn.1.refs_0_), channel_id=1, source_target_pairs={{0,6},{1,7},{2,4},{3,5},{4,2},{5,3},{6,0},{7,1},{8,14},{9,15},{10,... | collective-permute-start | bytes 1622024 | tf_op jit(solution)/shard_map/gather/ppermute | solution.py:474
  11.9 10.8 %collective-permute-start.23 = (s32[1024]{0:T(1024)S(1)}, s32[1024]{0:T(1024)S(1)}, u32[]{:S(2)}, u32[]{:S(2)}) collective-permute-start(s32[1024]{0:T(1024)S(1)} %copy-done.13), channel_id=1, source_target_pairs={{0,8},{1,9},{2,10},{3,11},{4,12},{5,13},{6,14},{7,15},{8,0},{9,1},... | collective-permute-start | bytes 12296 | tf_op jit(solution)/shard_map/gather/ppermute | solution.py:474
  11.9 135.5 %collective-permute-start.17 = (bf16[1024,1024]{1,0:T(8,128)(2,1)}, bf16[1024,1024]{1,0:T(8,128)(2,1)}, u32[]{:S(2)}, u32[]{:S(2)}) collective-permute-start(bf16[1024,1024]{1,0:T(8,128)(2,1)} %tok.1), channel_id=1, source_target_pairs={{0,8},{1,9},{2,10},{3,11},{4,12},{5,13},{6,14},{7,15},{8,0},{9,1},... | collective-permute-start | bytes 6291464 | tf_op jit(solution)/shard_map/gather/ppermute | solution.py:474
  12.4 140.2 %collective-permute-start.18 = (bf16[1024,1024]{1,0:T(8,128)(2,1)}, bf16[1024,1024]{1,0:T(8,128)(2,1)}, u32[]{:S(2)}, u32[]{:S(2)}) collective-permute-start(bf16[1024,1024]{1,0:T(8,128)(2,1)} %dy.1), channel_id=1, source_target_pairs={{0,8},{1,9},{2,10},{3,11},{4,12},{5,13},{6,14},{7,15},{8,0},{9,1},... | collective-permute-start | bytes 6291464 | tf_op jit(solution)/shard_map/gather/ppermute | solution.py:474
  22.7 35.5 %collective-permute-start.1 = (bf16[528,512]{1,0:T(8,128)(2,1)S(1)}, bf16[528,512]{1,0:T(8,128)(2,1)}, u32[]{:S(2)}, u32[]{:S(2)}) collective-permute-start(bf16[528,512]{1,0:T(8,128)(2,1)S(1)} %copy-done.5), channel_id=1, source_target_pairs={{0,4},{1,5},{2,6},{3,7},{4,0},{5,1},{6,2},{7,3},{8,12},{9,13},{10,... | collective-permute-start | bytes 1622024 | tf_op jit(solution)/shard_map/gather/ppermute | solution.py:474
  24.3 45.1 %collective-permute-start = (bf16[528,512]{1,0:T(8,128)(2,1)S(1)}, bf16[528,512]{1,0:T(8,128)(2,1)}, u32[]{:S(2)}, u32[]{:S(2)}) collective-permute-start(bf16[528,512]{1,0:T(8,128)(2,1)S(1)} %copy-done.5), channel_id=1, source_target_pairs={{0,2},{1,3},{2,0},{3,1},{4,6},{5,7},{6,4},{7,5},{8,10},{9,11},{10,... | collective-permute-start | bytes 1622024 | tf_op jit(solution)/shard_map/gather/ppermute | solution.py:474
  69.4 16.9 %collective-permute-start.9 = (bf16[256,1024]{1,0:T(8,128)(2,1)}, bf16[256,1024]{1,0:T(8,128)(2,1)S(1)}, u32[]{:S(2)}, u32[]{:S(2)}) collective-permute-start(bf16[256,1024]{1,0:T(8,128)(2,1)} %get-tuple-element.71.refs_0_), channel_id=1, source_target_pairs={{0,6},{1,7},{2,4},{3,5},{4,2},{5,3},{6,0},{7,1},{8,14},{9,15},{10,... | collective-permute-start | bytes 1572872 | tf_op jit(solution)/shard_map/gather/ppermute | solution.py:474
  71.5 44.4 %collective-permute-start.8 = (bf16[256,1024]{1,0:T(8,128)(2,1)}, bf16[256,1024]{1,0:T(8,128)(2,1)S(1)}, u32[]{:S(2)}, u32[]{:S(2)}) collective-permute-start(bf16[256,1024]{1,0:T(8,128)(2,1)} %get-tuple-element.71.refs_0_), channel_id=1, source_target_pairs={{0,4},{1,5},{2,6},{3,7},{4,0},{5,1},{6,2},{7,3},{8,12},{9,13},{10,... | collective-permute-start | bytes 1572872 | tf_op jit(solution)/shard_map/gather/ppermute | solution.py:474
  71.5 44.9 %collective-permute-start.7 = (bf16[256,1024]{1,0:T(8,128)(2,1)}, bf16[256,1024]{1,0:T(8,128)(2,1)S(1)}, u32[]{:S(2)}, u32[]{:S(2)}) collective-permute-start(bf16[256,1024]{1,0:T(8,128)(2,1)} %get-tuple-element.71.refs_0_), channel_id=1, source_target_pairs={{0,2},{1,3},{2,0},{3,1},{4,6},{5,7},{6,4},{7,5},{8,10},{9,11},{10,... | collective-permute-start | bytes 1572872 | tf_op jit(solution)/shard_map/gather/ppermute | solution.py:474
  86.4 36.0 %collective-permute-start.6 = (bf16[528,512]{1,0:T(8,128)(2,1)}, bf16[528,512]{1,0:T(8,128)(2,1)}, u32[]{:S(2)}, u32[]{:S(2)}) collective-permute-start(bf16[528,512]{1,0:T(8,128)(2,1)} %collective-permute-done.2.refs_3_), channel_id=1, source_target_pairs={{0,1},{1,0},{2,3},{3,2},{4,5},{5,4},{6,7},{7,6},{8,9},{9,8},{10,11... | collective-permute-start | bytes 1622024 | tf_op jit(solution)/shard_map/gather/ppermute | solution.py:474
  115.9 15.5 %collective-permute-start.5 = (bf16[528,512]{1,0:T(8,128)(2,1)}, bf16[528,512]{1,0:T(8,128)(2,1)}, u32[]{:S(2)}, u32[]{:S(2)}) collective-permute-start(bf16[528,512]{1,0:T(8,128)(2,1)} %collective-permute-done.1.refs_2_), channel_id=1, source_target_pairs={{0,1},{1,0},{2,3},{3,2},{4,5},{5,4},{6,7},{7,6},{8,9},{9,8},{10,11... | collective-permute-start | bytes 1622024 | tf_op jit(solution)/shard_map/gather/ppermute | solution.py:474
  116.4 26.6 %collective-permute-start.4 = (bf16[528,512]{1,0:T(8,128)(2,1)}, bf16[528,512]{1,0:T(8,128)(2,1)}, u32[]{:S(2)}, u32[]{:S(2)}) collective-permute-start(bf16[528,512]{1,0:T(8,128)(2,1)} %collective-permute-done.refs_1_), channel_id=1, source_target_pairs={{0,1},{1,0},{2,3},{3,2},{4,5},{5,4},{6,7},{7,6},{8,9},{9,8},{10,11... | collective-permute-start | bytes 1622024 | tf_op jit(solution)/shard_map/gather/ppermute | solution.py:474
  122.3 150.0 %collective-permute-start.19 = (bf16[256,1024]{1,0:T(8,128)(2,1)}, bf16[256,1024]{1,0:T(8,128)(2,1)S(1)}, u32[]{:S(2)}, u32[]{:S(2)}) collective-permute-start(bf16[256,1024]{1,0:T(8,128)(2,1)} %get-tuple-element.71.refs_0_), channel_id=1, source_target_pairs={{0,1},{1,0},{2,3},{3,2},{4,5},{5,4},{6,7},{7,6},{8,9},{9,8},{10,11... | collective-permute-start | bytes 1572872 | tf_op jit(solution)/shard_map/gather/ppermute | solution.py:474
  131.4 161.3 %collective-permute-start.12 = (bf16[256,1024]{1,0:T(8,128)(2,1)}, bf16[256,1024]{1,0:T(8,128)(2,1)S(1)}, u32[]{:S(2)}, u32[]{:S(2)}) collective-permute-start(bf16[256,1024]{1,0:T(8,128)(2,1)} %get-tuple-element.72.refs_0_), channel_id=1, source_target_pairs={{0,6},{1,7},{2,4},{3,5},{4,2},{5,3},{6,0},{7,1},{8,14},{9,15},{10,... | collective-permute-start | bytes 1572872 | tf_op jit(solution)/shard_map/gather/ppermute | solution.py:474
  143.0 150.3 %collective-permute-start.11 = (bf16[256,1024]{1,0:T(8,128)(2,1)}, bf16[256,1024]{1,0:T(8,128)(2,1)}, u32[]{:S(2)}, u32[]{:S(2)}) collective-permute-start(bf16[256,1024]{1,0:T(8,128)(2,1)} %get-tuple-element.72.refs_0_), channel_id=1, source_target_pairs={{0,4},{1,5},{2,6},{3,7},{4,0},{5,1},{6,2},{7,3},{8,12},{9,13},{10,... | collective-permute-start | bytes 1572872 | tf_op jit(solution)/shard_map/gather/ppermute | solution.py:474
  147.4 147.4 %collective-permute-start.10 = (bf16[256,1024]{1,0:T(8,128)(2,1)}, bf16[256,1024]{1,0:T(8,128)(2,1)}, u32[]{:S(2)}, u32[]{:S(2)}) collective-permute-start(bf16[256,1024]{1,0:T(8,128)(2,1)} %get-tuple-element.72.refs_0_), channel_id=1, source_target_pairs={{0,2},{1,3},{2,0},{3,1},{4,6},{5,7},{6,4},{7,5},{8,10},{9,11},{10,... | collective-permute-start | bytes 1572872 | tf_op jit(solution)/shard_map/gather/ppermute | solution.py:474
  152.6 121.3 %collective-permute-start.22 = (bf16[256,1024]{1,0:T(8,128)(2,1)S(1)}, bf16[256,1024]{1,0:T(8,128)(2,1)}, u32[]{:S(2)}, u32[]{:S(2)}) collective-permute-start(bf16[256,1024]{1,0:T(8,128)(2,1)S(1)} %copy-done.18), channel_id=1, source_target_pairs={{0,1},{1,0},{2,3},{3,2},{4,5},{5,4},{6,7},{7,6},{8,9},{9,8},{10,11... | collective-permute-start | bytes 1572872 | tf_op jit(solution)/shard_map/gather/ppermute | solution.py:474
  272.4 18.8 %collective-permute-start.21 = (bf16[256,1024]{1,0:T(8,128)(2,1)S(1)}, bf16[256,1024]{1,0:T(8,128)(2,1)S(1)}, u32[]{:S(2)}, u32[]{:S(2)}) collective-permute-start(bf16[256,1024]{1,0:T(8,128)(2,1)S(1)} %copy-done.20), channel_id=1, source_target_pairs={{0,1},{1,0},{2,3},{3,2},{4,5},{5,4},{6,7},{7,6},{8,9},{9,8},{10,11... | collective-permute-start | bytes 1572872 | tf_op jit(solution)/shard_map/gather/ppermute | solution.py:474
  273.9 22.2 %collective-permute-start.20 = (bf16[256,1024]{1,0:T(8,128)(2,1)S(1)}, bf16[256,1024]{1,0:T(8,128)(2,1)S(1)}, u32[]{:S(2)}, u32[]{:S(2)}) collective-permute-start(bf16[256,1024]{1,0:T(8,128)(2,1)S(1)} %copy-done.22), channel_id=1, source_target_pairs={{0,1},{1,0},{2,3},{3,2},{4,5},{5,4},{6,7},{7,6},{8,9},{9,8},{10,11... | collective-permute-start | bytes 1572872 | tf_op jit(solution)/shard_map/gather/ppermute | solution.py:474
  291.1 45.8 %collective-permute-start.13 = (bf16[256,1024]{1,0:T(8,128)(2,1)}, bf16[256,1024]{1,0:T(8,128)(2,1)S(1)}, u32[]{:S(2)}, u32[]{:S(2)}) collective-permute-start(bf16[256,1024]{1,0:T(8,128)(2,1)} %get-tuple-element.72.refs_0_), channel_id=1, source_target_pairs={{0,1},{1,0},{2,3},{3,2},{4,5},{5,4},{6,7},{7,6},{8,9},{9,8},{10,11... | collective-permute-start | bytes 1572872 | tf_op jit(solution)/shard_map/gather/ppermute | solution.py:474
  292.7 44.9 %collective-permute-start.16 = (bf16[256,1024]{1,0:T(8,128)(2,1)S(1)}, bf16[256,1024]{1,0:T(8,128)(2,1)S(1)}, u32[]{:S(2)}, u32[]{:S(2)}) collective-permute-start(bf16[256,1024]{1,0:T(8,128)(2,1)S(1)} %collective-permute-done.12.refs_3_), channel_id=1, source_target_pairs={{0,1},{1,0},{2,3},{3,2},{4,5},{5,4},{6,7},{7,6},{8,9},{9,8},{10,11... | collective-permute-start | bytes 1572872 | tf_op jit(solution)/shard_map/gather/ppermute | solution.py:474
  293.2 44.3 %collective-permute-start.15 = (bf16[256,1024]{1,0:T(8,128)(2,1)}, bf16[256,1024]{1,0:T(8,128)(2,1)S(1)}, u32[]{:S(2)}, u32[]{:S(2)}) collective-permute-start(bf16[256,1024]{1,0:T(8,128)(2,1)} %collective-permute-done.11.refs_2_), channel_id=1, source_target_pairs={{0,1},{1,0},{2,3},{3,2},{4,5},{5,4},{6,7},{7,6},{8,9},{9,8},{10,11... | collective-permute-start | bytes 1572872 | tf_op jit(solution)/shard_map/gather/ppermute | solution.py:474
  294.7 46.3 %collective-permute-start.14 = (bf16[256,1024]{1,0:T(8,128)(2,1)}, bf16[256,1024]{1,0:T(8,128)(2,1)S(1)}, u32[]{:S(2)}, u32[]{:S(2)}) collective-permute-start(bf16[256,1024]{1,0:T(8,128)(2,1)} %collective-permute-done.10.refs_1_), channel_id=1, source_target_pairs={{0,1},{1,0},{2,3},{3,2},{4,5},{5,4},{6,7},{7,6},{8,9},{9,8},{10,11... | collective-permute-start | bytes 1572872 | tf_op jit(solution)/shard_map/gather/ppermute | solution.py:474
  296.9 145.5 %collective-permute-start.26 = (bf16[4,192,1536]{2,1,0:T(8,128)(2,1)}, bf16[4,192,1536]{2,1,0:T(8,128)(2,1)S(1)}, u32[]{:S(2)}, u32[]{:S(2)}) collective-permute-start(bf16[4,192,1536]{2,1,0:T(8,128)(2,1)} %get-tuple-element.96), channel_id=1, source_target_pairs={{0,1},{1,0},{2,3},{3,2},{4,5},{5,4},{6,7},{7,6},{8,9},{9,8},{10,11... | collective-permute-start | bytes 7077896 | tf_op jit(solution)/shard_map/attn_weights/ppermute | solution.py:474
  337.0 99.7 %collective-permute-start.32 = (bf16[4,256,1024]{2,1,0:T(8,128)(2,1)}, bf16[4,256,1024]{2,1,0:T(8,128)(2,1)}, u32[]{:S(2)}, u32[]{:S(2)}) collective-permute-start(bf16[4,256,1024]{2,1,0:T(8,128)(2,1)} %get-tuple-element.100), channel_id=1, source_target_pairs={{0,1},{1,0},{2,3},{3,2},{4,5},{5,4},{6,7},{7,6},{8,9},{9,8},{10,11... | collective-permute-start | bytes 6291464 | tf_op jit(solution)/shard_map/mlp/ppermute | solution.py:474
  384.2 93.4 %collective-permute-start.38 = (bf16[4,256,1024]{2,1,0:T(8,128)(2,1)}, bf16[4,256,1024]{2,1,0:T(8,128)(2,1)}, u32[]{:S(2)}, u32[]{:S(2)}) collective-permute-start(bf16[4,256,1024]{2,1,0:T(8,128)(2,1)} %get-tuple-element.102), channel_id=1, source_target_pairs={{0,1},{1,0},{2,3},{3,2},{4,5},{5,4},{6,7},{7,6},{8,9},{9,8},{10,11... | collective-permute-start | bytes 6291464 | tf_op jit(solution)/shard_map/mlp/ppermute | solution.py:474
  438.9 41.5 %collective-permute-start.33 = (bf16[256,1024]{1,0:T(8,128)(2,1)S(1)}, bf16[256,1024]{1,0:T(8,128)(2,1)S(1)}, u32[]{:S(2)}, u32[]{:S(2)}) collective-permute-start(bf16[256,1024]{1,0:T(8,128)(2,1)S(1)} %get-tuple-element.128), channel_id=1, source_target_pairs={{0,2},{1,3},{2,0},{3,1},{4,6},{5,7},{6,4},{7,5},{8,10},{9,11},{10,... | collective-permute-start | bytes 1572872 | tf_op jit(solution)/shard_map/mlp/ppermute | solution.py:474
  440.5 42.2 %collective-permute-start.35 = (bf16[256,1024]{1,0:T(8,128)(2,1)S(1)}, bf16[256,1024]{1,0:T(8,128)(2,1)S(1)}, u32[]{:S(2)}, u32[]{:S(2)}) collective-permute-start(bf16[256,1024]{1,0:T(8,128)(2,1)S(1)} %get-tuple-element.129), channel_id=1, source_target_pairs={{0,6},{1,7},{2,4},{3,5},{4,2},{5,3},{6,0},{7,1},{8,14},{9,15},{10,... | collective-permute-start | bytes 1572872 | tf_op jit(solution)/shard_map/mlp/ppermute | solution.py:474
  442.2 65.5 %collective-permute-start.34 = (bf16[256,1024]{1,0:T(8,128)(2,1)S(1)}, bf16[256,1024]{1,0:T(8,128)(2,1)S(1)}, u32[]{:S(2)}, u32[]{:S(2)}) collective-permute-start(bf16[256,1024]{1,0:T(8,128)(2,1)S(1)} %get-tuple-element.130), channel_id=1, source_target_pairs={{0,4},{1,5},{2,6},{3,7},{4,0},{5,1},{6,2},{7,3},{8,12},{9,13},{10,... | collective-permute-start | bytes 1572872 | tf_op jit(solution)/shard_map/mlp/ppermute | solution.py:474
  442.9 66.4 %collective-permute-start.27 = (bf16[192,1536]{1,0:T(8,128)(2,1)S(1)}, bf16[192,1536]{1,0:T(8,128)(2,1)S(1)}, u32[]{:S(2)}, u32[]{:S(2)}) collective-permute-start(bf16[192,1536]{1,0:T(8,128)(2,1)S(1)} %get-tuple-element.122), channel_id=1, source_target_pairs={{0,2},{1,3},{2,0},{3,1},{4,6},{5,7},{6,4},{7,5},{8,10},{9,11},{10,... | collective-permute-start | bytes 1769480 | tf_op jit(solution)/shard_map/attn_weights/ppermute | solution.py:474
  477.6 32.3 %collective-permute-start.29 = (bf16[192,1536]{1,0:T(8,128)(2,1)S(1)}, bf16[192,1536]{1,0:T(8,128)(2,1)S(1)}, u32[]{:S(2)}, u32[]{:S(2)}) collective-permute-start(bf16[192,1536]{1,0:T(8,128)(2,1)S(1)} %get-tuple-element.123), channel_id=1, source_target_pairs={{0,6},{1,7},{2,4},{3,5},{4,2},{5,3},{6,0},{7,1},{8,14},{9,15},{10,... | collective-permute-start | bytes 1769480 | tf_op jit(solution)/shard_map/attn_weights/ppermute | solution.py:474
  480.3 69.6 %collective-permute-start.28 = (bf16[192,1536]{1,0:T(8,128)(2,1)S(1)}, bf16[192,1536]{1,0:T(8,128)(2,1)S(1)}, u32[]{:S(2)}, u32[]{:S(2)}) collective-permute-start(bf16[192,1536]{1,0:T(8,128)(2,1)S(1)} %get-tuple-element.124), channel_id=1, source_target_pairs={{0,4},{1,5},{2,6},{3,7},{4,0},{5,1},{6,2},{7,3},{8,12},{9,13},{10,... | collective-permute-start | bytes 1769480 | tf_op jit(solution)/shard_map/attn_weights/ppermute | solution.py:474
  482.7 147.9 %collective-permute-start.25 = (bf16[1024,1024]{1,0:T(8,128)(2,1)}, bf16[1024,1024]{1,0:T(8,128)(2,1)}, u32[]{:S(2)}, u32[]{:S(2)}) collective-permute-start(bf16[1024,1024]{1,0:T(8,128)(2,1)} %slice.202), channel_id=1, source_target_pairs={{0,8},{1,9},{2,10},{3,11},{4,12},{5,13},{6,14},{7,15},{8,0},{9,1},... | collective-permute-start | bytes 6291464 | tf_op jit(solution)/shard_map/final/ppermute | solution.py:474
  507.7 122.9 %collective-permute-start.24 = (bf16[1024,1024]{1,0:T(8,128)(2,1)}, bf16[1024,1024]{1,0:T(8,128)(2,1)}, u32[]{:S(2)}, u32[]{:S(2)}) collective-permute-start(bf16[1024,1024]{1,0:T(8,128)(2,1)} %slice.203), channel_id=1, source_target_pairs={{0,8},{1,9},{2,10},{3,11},{4,12},{5,13},{6,14},{7,15},{8,0},{9,1},... | collective-permute-start | bytes 6291464 | tf_op jit(solution)/shard_map/final/ppermute | solution.py:474
  509.2 41.0 %collective-permute-start.39 = (bf16[256,1024]{1,0:T(8,128)(2,1)S(1)}, bf16[256,1024]{1,0:T(8,128)(2,1)S(1)}, u32[]{:S(2)}, u32[]{:S(2)}) collective-permute-start(bf16[256,1024]{1,0:T(8,128)(2,1)S(1)} %get-tuple-element.125), channel_id=1, source_target_pairs={{0,2},{1,3},{2,0},{3,1},{4,6},{5,7},{6,4},{7,5},{8,10},{9,11},{10,... | collective-permute-start | bytes 1572872 | tf_op jit(solution)/shard_map/mlp/ppermute | solution.py:474
  509.9 41.9 %collective-permute-start.41 = (bf16[256,1024]{1,0:T(8,128)(2,1)S(1)}, bf16[256,1024]{1,0:T(8,128)(2,1)S(1)}, u32[]{:S(2)}, u32[]{:S(2)}) collective-permute-start(bf16[256,1024]{1,0:T(8,128)(2,1)S(1)} %get-tuple-element.126), channel_id=1, source_target_pairs={{0,6},{1,7},{2,4},{3,5},{4,2},{5,3},{6,0},{7,1},{8,14},{9,15},{10,... | collective-permute-start | bytes 1572872 | tf_op jit(solution)/shard_map/mlp/ppermute | solution.py:474
  549.9 25.6 %collective-permute-start.40 = (bf16[256,1024]{1,0:T(8,128)(2,1)S(1)}, bf16[256,1024]{1,0:T(8,128)(2,1)S(1)}, u32[]{:S(2)}, u32[]{:S(2)}) collective-permute-start(bf16[256,1024]{1,0:T(8,128)(2,1)S(1)} %get-tuple-element.127), channel_id=1, source_target_pairs={{0,4},{1,5},{2,6},{3,7},{4,0},{5,1},{6,2},{7,3},{8,12},{9,13},{10,... | collective-permute-start | bytes 1572872 | tf_op jit(solution)/shard_map/mlp/ppermute | solution.py:474
  550.3 28.3 %collective-permute-start.36 = (bf16[256,1024]{1,0:T(8,128)(2,1)S(1)}, bf16[256,1024]{1,0:T(8,128)(2,1)S(1)}, u32[]{:S(2)}, u32[]{:S(2)}) collective-permute-start(bf16[256,1024]{1,0:T(8,128)(2,1)S(1)} %fusion.8), channel_id=1, source_target_pairs={{0,16},{1,17},{2,18},{3,19},{4,20},{5,21},{6,22},{7,23},{8,24},{9,... | collective-permute-start | bytes 1572872 | tf_op jit(solution)/shard_map/mlp/ppermute | solution.py:474
  551.9 27.1 %collective-permute-start.30 = (bf16[192,1536]{1,0:T(8,128)(2,1)S(1)}, bf16[192,1536]{1,0:T(8,128)(2,1)S(1)}, u32[]{:S(2)}, u32[]{:S(2)}) collective-permute-start(bf16[192,1536]{1,0:T(8,128)(2,1)S(1)} %fusion.2), channel_id=1, source_target_pairs={{0,16},{1,17},{2,18},{3,19},{4,20},{5,21},{6,22},{7,23},{8,24},{9,... | collective-permute-start | bytes 1769480 | tf_op jit(solution)/shard_map/attn_weights/ppermute | solution.py:474
  577.0 11.5 %collective-permute-start.42 = (bf16[256,1024]{1,0:T(8,128)(2,1)S(1)}, bf16[256,1024]{1,0:T(8,128)(2,1)S(1)}, u32[]{:S(2)}, u32[]{:S(2)}) collective-permute-start(bf16[256,1024]{1,0:T(8,128)(2,1)S(1)} %fusion.5), channel_id=1, source_target_pairs={{0,16},{1,17},{2,18},{3,19},{4,20},{5,21},{6,22},{7,23},{8,24},{9,... | collective-permute-start | bytes 1572872 | tf_op jit(solution)/shard_map/mlp/ppermute | solution.py:474
  578.8 61.6 %copy-start.6 = (bf16[256,1024]{1,0:T(8,128)(2,1)}, bf16[256,1024]{1,0:T(8,128)(2,1)S(1)}, u32[]{:S(2)}) copy-start(bf16[256,1024]{1,0:T(8,128)(2,1)S(1)} %add_convert_fusion.10.own_a) | copy-start | bytes 1572868
  578.8 51.1 %copy-start.14 = (f32[13,128]{1,0:T(8,128)S(1)}, f32[13,128]{1,0:T(8,128)}, u32[]{:S(2)}) copy-start(f32[13,128]{1,0:T(8,128)} %param.25) | copy-start | bytes 19972
  578.8 61.6 %collective-permute-start.37 = (bf16[256,1024]{1,0:T(8,128)(2,1)S(1)}, bf16[256,1024]{1,0:T(8,128)(2,1)S(1)}, u32[]{:S(2)}, u32[]{:S(2)}) collective-permute-start(bf16[256,1024]{1,0:T(8,128)(2,1)S(1)} %add_convert_fusion.10.own_a), channel_id=1, source_target_pairs={{0,8},{1,9},{2,10},{3,11},{4,12},{5,13},{6,14},{7,15},{8,0},{9,1},... | collective-permute-start | bytes 1572872 | tf_op jit(solution)/shard_map/mlp/ppermute | solution.py:474
  579.1 61.3 %copy-start.2 = (bf16[192,1536]{1,0:T(8,128)(2,1)}, bf16[192,1536]{1,0:T(8,128)(2,1)S(1)}, u32[]{:S(2)}) copy-start(bf16[192,1536]{1,0:T(8,128)(2,1)S(1)} %add_convert_fusion.own.own_out) | copy-start | bytes 1769476
  579.1 74.4 %collective-permute-start.31 = (bf16[192,1536]{1,0:T(8,128)(2,1)S(1)}, bf16[192,1536]{1,0:T(8,128)(2,1)S(1)}, u32[]{:S(2)}, u32[]{:S(2)}) collective-permute-start(bf16[192,1536]{1,0:T(8,128)(2,1)S(1)} %add_convert_fusion.own.own_out), channel_id=1, source_target_pairs={{0,8},{1,9},{2,10},{3,11},{4,12},{5,13},{6,14},{7,15},{8,0},{9,1},... | collective-permute-start | bytes 1769480 | tf_op jit(solution)/shard_map/attn_weights/ppermute | solution.py:474
  588.7 51.7 %copy-start.7 = (bf16[256,1024]{1,0:T(8,128)(2,1)}, bf16[256,1024]{1,0:T(8,128)(2,1)S(1)}, u32[]{:S(2)}) copy-start(bf16[256,1024]{1,0:T(8,128)(2,1)S(1)} %add_convert_fusion.5.own_b) | copy-start | bytes 1572868
  588.7 51.7 %collective-permute-start.43 = (bf16[256,1024]{1,0:T(8,128)(2,1)S(1)}, bf16[256,1024]{1,0:T(8,128)(2,1)S(1)}, u32[]{:S(2)}, u32[]{:S(2)}) collective-permute-start(bf16[256,1024]{1,0:T(8,128)(2,1)S(1)} %add_convert_fusion.5.own_b), channel_id=1, source_target_pairs={{0,8},{1,9},{2,10},{3,11},{4,12},{5,13},{6,14},{7,15},{8,0},{9,1},... | collective-permute-start | bytes 1572872 | tf_op jit(solution)/shard_map/mlp/ppermute | solution.py:474
  (27 other events, 385.2 us)

commit v2 on v1

v2 whole, which is shorter than its diff:
```python
import functools

import jax
import jax.numpy as jnp
from jax import lax
from jax.experimental import pallas as pl
from jax.experimental.pallas import tpu as pltpu
from jax.sharding import PartitionSpec as P

HEAD_DIM = 64
ROT_DIM = 16
STEP = 10
EPS_NORM = 1e-05
BETA_ONE = 0.9
BETA_TWO = 0.999
ADAM_EPS = 1e-08
RATE_MATRIX = 0.05
RATE_VECTOR = 0.2
DECAY_MATRIX = 0.1
ROPE_BASE = 10000.0
INV_ROOT_TWO = 0.7071067811865476
INV_ROOT_TAU = 0.3989422804014327
MASKED = -1e30
LANES = 128
AXES = ("dp", "zero")
F32 = jnp.float32
BF16 = jnp.bfloat16
VMEM_LIMIT = 58 * 1024 * 1024


def spec(block, index, single=False):
    if single:
        return pl.BlockSpec(block, index, pipeline_mode=pl.Buffered(1))
    return pl.BlockSpec(block, index)


def whole(shape):
    return spec(shape, lambda *_: (0,) * len(shape), single=True)


def scalars():
    return pl.BlockSpec(memory_space=pltpu.SMEM)


def kernel_call(body, grid, in_specs, out_specs, out_shape, flops, moved, scratch=(), name=None):
    return pl.pallas_call(
        body,
        grid=grid,
        in_specs=in_specs,
        out_specs=out_specs,
        out_shape=out_shape,
        scratch_shapes=list(scratch),
        cost_estimate=pl.CostEstimate(flops=int(flops), bytes_accessed=int(moved), transcendentals=0),
        compiler_params=pltpu.CompilerParams(
            vmem_limit_bytes=VMEM_LIMIT, dimension_semantics=("arbitrary",) * len(grid)
        ),
        name=name,
    )


def nn(left, right):
    return lax.dot_general(left, right, (((1,), (0,)), ((), ())), preferred_element_type=F32)


def nt(left, right):
    return lax.dot_general(left, right, (((1,), (1,)), ((), ())), preferred_element_type=F32)


def tn(left, right):
    return lax.dot_general(left, right, (((0,), (0,)), ((), ())), preferred_element_type=F32)


def piece_owner(ids, place):
    step = place % 4
    if step > 1:
        step = 2 + ids[2] if step == 2 else 3 - ids[2]
    return jnp.bitwise_xor(ids[0], 2 * step + place // 4)


SLOTS = ((0, 0), (1, 0), (2, 0), (2, 1), (0, 1), (1, 1), (3, 0), (3, 1))


def slot_owner(ids, slot):
    step, side = SLOTS[slot]
    if step > 1:
        step = 2 + ids[2] if step == 2 else 3 - ids[2]
    return jnp.bitwise_xor(ids[0], 2 * step + side)


def slot_ref(outs, slot):
    return (outs[0], slot) if slot < 4 else (outs[1], slot - 4) if slot < 6 else (outs[2], slot - 6)


def low_lanes():
    return lax.broadcasted_iota(jnp.int32, (1, LANES), 1) < HEAD_DIM


def pick_parity(core, tile_a, tile_b):
    low = low_lanes()
    even = jnp.where(low, tile_a, pltpu.roll(tile_b, HEAD_DIM, 1))
    odd = jnp.where(low, pltpu.roll(tile_a, HEAD_DIM, 1), tile_b)
    return jnp.where(core == 0, even, odd)


def prep_attn_body(ids, w_qkv, w_out, out_a, out_b):
    core = ids[1]
    for part in range(3):
        for tile in range(4):
            base = part * 1024 + tile * 256
            out = out_a if tile < 2 else out_b
            at = part * 256 + (tile % 2) * 128
            out[:, at : at + 128] = pick_parity(
                core, w_qkv[:, base : base + 128], w_qkv[:, base + 128 : base + 256]
            ).astype(BF16)
    rows = w_out[pl.ds(pl.multiple_of(core * 64, 64), 64), :].astype(BF16)
    for panel in range(4):
        at = 768 + 256 * (panel // 2)
        base = (panel % 2) * 64
        out_a[base : base + 64, at : at + 256] = rows[:, 256 * panel : 256 * panel + 256]


def prep_mlp_body(ids, w_up, w_down, out_a, out_b):
    core = ids[1]
    for part, out in enumerate((out_a, out_b)):
        for owner in range(8):
            start = pl.multiple_of(owner * 512 + part * 256 + core * 128, 128)
            out[0:128, owner * 128 : (owner + 1) * 128] = w_up[:, pl.ds(start, 128)].astype(BF16)
        out[128:256, :] = w_down[pl.ds(pl.multiple_of(part * 256 + core * 128, 128), 128), :].astype(BF16)


def join_vec_body(ids, pieces, vec, bias):
    for step in range(8):
        owner = jnp.bitwise_xor(ids[0], 2 * (step & 3) + step // 4)
        vec[:, pl.ds(pl.multiple_of(owner * 128, 128), 128)] = pieces[step].astype(F32)
    for part in range(3):
        for tile in range(4):
            base = tile * 256
            row = slice(4 + part, 5 + part)
            at = (tile // 2) * 768 + part * 256 + (tile % 2) * 128
            bias[:, at : at + 128] = pick_parity(
                ids[1], vec[row, base : base + 128], vec[row, base + 128 : base + 256]
            )


def normalize(inputs):
    centred = inputs - jnp.mean(inputs, axis=-1, keepdims=True)
    variance = jnp.mean(centred * centred, axis=-1, keepdims=True)
    inv_std = lax.rsqrt(variance + EPS_NORM)
    return centred * inv_std, inv_std


def norm_body(steps, tok_own, tok_other, dy_own, dy_other, vec, attn_in, mlp_in, dy, attn_t, mlp_t, dy_t, dy_sum):
    first = pl.program_id(0) < steps // 2
    normed, _ = normalize(jnp.where(first, tok_own[...], tok_other[...]).astype(F32))
    attn = (normed * vec[0:1, :] + vec[1:2, :]).astype(BF16)
    mlp = (normed * vec[2:3, :] + vec[3:4, :]).astype(BF16)
    attn_in[...] = attn
    mlp_in[...] = mlp
    attn_t[...] = attn.T
    mlp_t[...] = mlp.T
    grad = jnp.where(first, dy_own[...], dy_other[...])
    dy[...] = grad
    dy_t[...] = grad.T

    @pl.when(pl.program_id(0) == 0)
    def _():
        dy_sum[...] = jnp.zeros_like(dy_sum)

    dy_sum[0:1, :] += jnp.sum(grad.astype(F32), axis=0, keepdims=True)


def turned(x, cos, sin_lo, sin_hi, sign):
    return x * cos[...] + sign * (pltpu.roll(x, 8, 1) * sin_hi[...] + pltpu.roll(x, 120, 1) * sin_lo[...])


def project(group, attn_in, dy, w_qkv, w_out, bias, tables, outs):
    rows = attn_in[...]
    for part, out in enumerate(outs[:3]):
        cols = slice(part * 256, (part + 1) * 256)
        at = group * 768 + part * 256
        acc = nn(rows, w_qkv[:, cols]) + bias[:, at : at + 256]
        if part == 2:
            out[...] = acc.astype(BF16)
            continue
        for tile in range(2):
            x = turned(acc[:, tile * 128 : (tile + 1) * 128], *tables, 1.0)
            if part == 0:
                x = x * HEAD_DIM ** (-0.5)
            out[:, tile * 128 : (tile + 1) * 128] = x.astype(BF16)
    outs[3][...] = nt(dy[...], w_out[group * 256 : group * 256 + 256, :]).astype(BF16)


def qkv_first_body(ids, *refs):
    pieces, (attn_in, dy, bias, cos, sin_lo, sin_hi, q, k, v, d_att, w_qkv, w_out) = refs[:8], refs[8:]

    @pl.when(pl.program_id(0) == 0)
    def _():
        for place, piece in enumerate(pieces):
            owner = piece_owner(ids, place)
            w_qkv[pl.ds(pl.multiple_of(owner * 128, 128), 128), :] = piece[:, 0:768]
            for panel in range(4):
                at = 768 + 256 * (panel // 2)
                base = (panel % 2) * 64
                w_out[pl.ds(pl.multiple_of(owner * 64, 64), 64), 256 * panel : 256 * panel + 256] = piece[
                    base : base + 64, at : at + 256
                ]

    project(0, attn_in, dy, w_qkv, w_out, bias, (cos, sin_lo, sin_hi), (q, k, v, d_att))


def qkv_second_body(attn_in, dy, w_qkv, w_out, bias, cos, sin_lo, sin_hi, q, k, v, d_att):
    project(1, attn_in, dy, w_qkv, w_out, bias, (cos, sin_lo, sin_hi), (q, k, v, d_att))


ATTN_ROWS = 256


def attn_body(q, k, v, d_att, seg_col, seg_row, cos, sin_lo, sin_hi, att, grad, dq_acc, dk_acc, dv_acc):
    row_count = q.shape[0]
    low = low_lanes()
    dk_acc[...] = jnp.zeros_like(dk_acc)
    dv_acc[...] = jnp.zeros_like(dv_acc)
    step = ATTN_ROWS
    causal = lax.broadcasted_iota(jnp.int32, (step, step), 0) >= lax.broadcasted_iota(
        jnp.int32, (step, step), 1
    )
    for first in range(0, row_count, step):
        rows = slice(first, first + step)
        ids = seg_col[rows, :]
        ranges = [(0, first), (first, first + step)] if first else [(0, step)]
        outs = []
        dqs = []
        for half in range(2):
            lanes = low if half == 0 else jnp.logical_not(low)
            q_h = jnp.where(lanes, q[rows, :], jnp.zeros((), BF16))
            da_h = jnp.where(lanes, d_att[rows, :], jnp.zeros((), BF16))
            scores = []
            for begin, end in ranges:
                allowed = ids == seg_row[0, :, begin:end]
                if begin == first:
                    allowed = allowed & causal
                scores.append(jnp.where(allowed, nt(q_h, k[begin:end, :]), MASKED))
            top = functools.reduce(jnp.maximum, [jnp.max(s, axis=-1, keepdims=True) for s in scores])
            scores = [jnp.exp(s - top) for s in scores]
            total = functools.reduce(jnp.add, [jnp.sum(s, axis=-1, keepdims=True) for s in scores])
            inv = 1.0 / total
            probs = [s * inv for s in scores]
            low_probs = [p.astype(BF16) for p in probs]
            outs.append(
                functools.reduce(jnp.add, [nn(p, v[b:e, :]) for p, (b, e) in zip(low_probs, ranges)])
            )
            grad_probs = [nt(da_h, v[b:e, :]) for b, e in ranges]
            delta = functools.reduce(
                jnp.add, [jnp.sum(g * p, axis=-1, keepdims=True) for g, p in zip(grad_probs, probs)]
            )
            grad_scores = [(p * (g - delta)).astype(BF16) for g, p in zip(grad_probs, probs)]
            dqs.append(
                functools.reduce(jnp.add, [nn(g, k[b:e, :]) for g, (b, e) in zip(grad_scores, ranges)])
            )
            for g, p, (b, e) in zip(grad_scores, low_probs, ranges):
                dk_acc[b:e, :] += tn(g, q_h)
                dv_acc[b:e, :] += tn(p, da_h)
        att[rows, :] = jnp.where(low, outs[0], outs[1]).astype(BF16)
        dq_acc[rows, :] = jnp.where(low, dqs[0], dqs[1]) * HEAD_DIM ** (-0.5)
    for part, acc in enumerate((dq_acc, dk_acc)):
        x = acc[...]
        grad[part] = turned(x, cos, sin_lo, sin_hi, -1.0).astype(BF16)
    grad[2] = dv_acc[...].astype(BF16)


def attn_weights_body(last, ids, attn_t, grad, *refs):
    if last:
        dy_t, att_a, att_b, keep, send_x, send_y, bias, result, flipped = refs
    else:
        keep, send_x, send_y, bias, result = refs
    step = pl.program_id(0)
    outs = (keep, send_x, send_y)

    @pl.when(step < 3)
    def _():
        rhs = grad[0]
        result[...] = nn(attn_t[...], rhs).astype(BF16)
        cols = pl.ds(pl.multiple_of(step * 256, 256), 256)
        bias[0:1, cols] = jnp.sum(rhs.astype(F32), axis=0, keepdims=True)
        for slot in range(8):
            out, at = slot_ref(outs, slot)
            base = pl.multiple_of(slot_owner(ids, slot) * 128, 128)
            out[at, 0:128, cols] = result[pl.ds(base, 128), :]

    if not last:
        return

    @pl.when(step == 3)
    def _():
        flipped[0:256, :] = nn(dy_t[...], att_a[...]).astype(BF16).T
        flipped[256:512, :] = nn(dy_t[...], att_b[...]).astype(BF16).T
        for slot in range(8):
            out, at = slot_ref(outs, slot)
            rows = pl.ds(pl.multiple_of(slot_owner(ids, slot) * 64, 64), 64)
            for panel in range(4):
                col = 768 + 256 * (panel // 2)
                base = (panel % 2) * 64
                out[at, base : base + 64, col : col + 256] = flipped[rows, 256 * panel : 256 * panel + 256]


def mlp_body(part, steps, ids, *refs):
    count = 1 if part else 8
    pieces = refs[:count]
    vec, mlp_in, dy, mlp_t, dy_t, keep, send_x, send_y, hidden_out, grad_out, bias_up, w_up, w_down = refs[count:-5]
    hidden, grad_pre, bias, result, flipped = refs[-5:]
    outs = (keep, send_x, send_y)
    core = ids[1]
    step = pl.program_id(0)

    @pl.when(step == 0)
    def _():
        for owner in range(8):
            start = pl.multiple_of((owner % 2) * 512 + part * 256 + core * 128, 128)
            row = 8 + owner // 2
            bias[0:1, owner * 128 : (owner + 1) * 128] = vec[row : row + 1, pl.ds(start, 128)]
        bias_up[...] = jnp.zeros_like(bias_up)
        for place in range(8):
            if part:
                piece, at = pieces[0].at[place], slice(place * 128, place * 128 + 128)
            else:
                piece = pieces[place]
                at = pl.ds(pl.multiple_of(piece_owner(ids, place) * 128, 128), 128)
            w_up[at, :] = piece[0:128, :]
            w_down[at, :] = piece[128:256, :]

    rows = mlp_in[...]
    grads = dy[...]
    count = rows.shape[0]
    at = pl.ds(pl.multiple_of(step * count, count), count)
    for col in range(0, 1024, 256):
        cols = slice(col, col + 256)
        pre = nn(rows, w_up[:, cols]) + bias[0:1, cols]
        grad_hidden = nt(grads, w_down[cols, :])
        cdf = 0.5 + 0.5 * lax.erf(pre * INV_ROOT_TWO)
        pdf = jnp.exp(-0.5 * pre * pre) * INV_ROOT_TAU
        act = (pre * cdf).astype(BF16)
        hidden[at, cols] = act
        hidden_out[:, cols] = act
        gp = (grad_hidden * (cdf + pre * pdf)).astype(BF16)
        grad_pre[at, cols] = gp
        grad_out[:, cols] = gp
        bias_up[0:1, cols] += jnp.sum(gp.astype(F32), axis=0, keepdims=True)

    @pl.when(step == steps - 1)
    def _():
        for col in range(0, 1024, 512):
            cols = slice(col, col + 512)
            result[...] = nn(mlp_t[...], grad_pre[:, cols]).astype(BF16)
            for slot in range(8):
                out, place = slot_ref(outs, slot)
                base = pl.multiple_of(slot_owner(ids, slot) * 128, 128)
                out[place, 0:128, cols] = result[pl.ds(base, 128), :]
        for col in range(0, 1024, 512):
            cols = slice(col, col + 512)
            flipped[cols, :] = nn(dy_t[...], hidden[:, cols]).astype(BF16).T
        for slot in range(8):
            out, place = slot_ref(outs, slot)
            base = pl.multiple_of(slot_owner(ids, slot) * 128, 128)
            out[place, 128:256, :] = flipped[pl.ds(base, 128), :]


def back_body(own, grad_a, grad_b, att_a, att_b, hid_a, hid_b, gp_a, gp_b, wq_a, wq_b, w_out, up_a, up_b, down_a, down_b, tok, vec, *refs):
    if own:
        dy, out_other, scaled_other, out, result, sums = refs
    else:
        out, result, sums = refs
    inputs = tok[...].astype(F32)
    normed, inv_std = normalize(inputs)
    branch = nn(att_a[...], w_out[0:256, :]) + nn(att_b[...], w_out[256:512, :])
    back_mlp = None
    for hid, gp, up, down in ((hid_a, gp_a, up_a, down_a), (hid_b, gp_b, up_b, down_b)):
        branch = branch + nn(hid[...], down[...])
        term = nt(gp[...], up[...])
        back_mlp = term if back_mlp is None else back_mlp + term
    back_attn = None
    for grad, w in ((grad_a, wq_a), (grad_b, wq_b)):
        for part in range(3):
            term = nt(grad[part], w[:, part * 256 : part * 256 + 256])
            back_attn = term if back_attn is None else back_attn + term
    scaled = back_attn * vec[0:1, :] + back_mlp * vec[2:3, :]

    @pl.when(pl.program_id(0) == 0)
    def _():
        sums[...] = jnp.zeros_like(sums)

    for row, value in enumerate((back_attn * normed, back_attn, back_mlp * normed, back_mlp)):
        sums[row : row + 1, :] += jnp.sum(value, axis=0, keepdims=True)
    if not own:
        out[...] = branch.astype(BF16)
        result[...] = scaled.astype(BF16)
        return
    branch = branch + out_other[...].astype(F32)
    out[...] = (inputs + branch + (vec[7:8, :] + vec[12:13, :])).astype(BF16)
    scaled = scaled + scaled_other[...].astype(F32)
    result[...] = dy[...].astype(F32) + inv_std * (
        scaled
        - jnp.mean(scaled, axis=-1, keepdims=True)
        - normed * jnp.mean(scaled * normed, axis=-1, keepdims=True)
    )


def adam_math(weight, first, second, gradient, rate, decay):
    first_new = BETA_ONE * first + (1.0 - BETA_ONE) * gradient
    second_new = BETA_TWO * second + (1.0 - BETA_TWO) * gradient * gradient
    first_hat = first_new / (1.0 - BETA_ONE**STEP)
    second_hat = second_new / (1.0 - BETA_TWO**STEP)
    weight_new = weight - rate * (first_hat / (jnp.sqrt(second_hat) + ADAM_EPS) + decay * weight)
    return (first_new, second_new, weight_new)


def adam_store(refs, at, gradient):
    w, m, v, m_out, v_out, w_out = refs
    first, second, weight = adam_math(w[at], m[at], v[at], gradient, RATE_MATRIX, DECAY_MATRIX)
    m_out[at] = first
    v_out[at] = second
    w_out[at] = weight


def parities(core, own, other):
    return jnp.where(core == 0, own, other), jnp.where(core == 0, other, own)


def adam_attn_body(ids, own_a, other_a, own_b, other_b, own_out, other_out, *refs):
    core = ids[1]
    low = low_lanes()
    qkv_refs = refs[0:3] + refs[6:9]
    for tile in range(4):
        own, other = (own_a, other_a) if tile < 2 else (own_b, other_b)
        cols = slice((tile % 2) * 128, (tile % 2) * 128 + 128)
        even, odd = parities(core, own[:, cols].astype(F32), other[:, cols].astype(F32))
        first = jnp.where(low, even, pltpu.roll(odd, HEAD_DIM, 1))
        second = jnp.where(low, pltpu.roll(even, HEAD_DIM, 1), odd)
        adam_store(qkv_refs, (slice(None), slice(tile * 256, tile * 256 + 128)), first)
        adam_store(qkv_refs, (slice(None), slice(tile * 256 + 128, tile * 256 + 256)), second)

    @pl.when(pl.program_id(0) == 0)
    def _():
        out_refs = refs[3:6] + refs[9:12]
        for panel in range(4):
            rows = slice((panel % 2) * 64, (panel % 2) * 64 + 64)
            cols = slice(256 * (panel // 2), 256 * (panel // 2) + 256)
            span = slice(panel * 256, panel * 256 + 256)
            even, odd = parities(core, own_out[rows, cols].astype(F32), other_out[rows, cols].astype(F32))
            adam_store(out_refs, (slice(0, 64), span), even)
            adam_store(out_refs, (slice(64, 128), span), odd)


def adam_mlp_body(ids, own, other, *refs):
    core = ids[1]
    up_refs = refs[0:3] + refs[-6:-3]
    down_refs = refs[3:6] + refs[-3:]
    cols = pl.ds(pl.multiple_of(pl.program_id(0) * 128, 128), 128)
    for base, refs_of in ((0, up_refs), (128, down_refs)):
        rows = slice(base, base + 128)
        for parity, grad in enumerate(
            parities(core, own[rows, cols].astype(F32), other[rows, cols].astype(F32))
        ):
            span = slice(parity * 128, (parity + 1) * 128)
            adam_store(refs_of, (slice(None), span) if base == 0 else (span, slice(None)), grad)


def rotary_tables(segments):
    row_count = segments.shape[0]
    row_index = jnp.arange(row_count, dtype=jnp.int32)
    earlier = jnp.concatenate([jnp.full((1,), -1, jnp.int32), segments[:-1]])
    starts = jnp.where(segments != earlier, row_index, 0)
    position = (row_index - lax.cummax(starts, axis=0)).astype(F32)
    half_dim = ROT_DIM // 2
    dims = jnp.arange(LANES, dtype=jnp.int32) % HEAD_DIM
    frequency = ROPE_BASE ** (-2.0 * (dims % half_dim).astype(F32) / ROT_DIM)
    turned = dims < ROT_DIM
    angles = position[:, None] * jnp.where(turned, frequency, 0.0)[None, :]
    cosine, sine = jnp.cos(angles), jnp.sin(angles)
    front = (dims < half_dim)[None, :]
    return cosine, jnp.where(front, -sine, 0.0), jnp.where(front, 0.0, sine)


def on_device(
    sizes,
    tokens,
    segments,
    cotangent,
    w_qkv,
    w_out,
    w_up,
    w_down,
    vectors,
    m_qkv,
    m_out,
    m_up,
    m_down,
    m_vectors,
    v_qkv,
    v_out,
    v_up,
    v_down,
    v_vectors,
):
    copies, owners = sizes
    me = lax.axis_index("zero")
    plane = lax.axis_index("dp")
    core = plane % 2
    ids = jnp.stack([me, core, (plane // 2) % 2]).astype(jnp.int32)

    def move(value, target):
        pairs = []
        for d in range(copies):
            for z in range(owners):
                to_d, to_z = target(d, z)
                pairs.append((d * owners + z, to_d * owners + to_z))
        return lax.ppermute(value, AXES, pairs)

    def swap(value, dp_bits, zero_bits):
        return move(value, lambda d, z: (d ^ dp_bits, z ^ zero_bits))

    def swap_far(value):
        return move(value, lambda d, z: (d, z ^ (6 if d & 2 else 4)))

    def sync(*values):
        return lax.optimization_barrier(values)

    def gather_first(own):
        return [own, swap(own, 0, 2), swap_far(own), swap(own, 0, 1)]

    def gather_second(got):
        own, next_z, far_z, across = got
        return got + [swap(next_z, 0, 1), swap(far_z, 0, 1), swap(far_z, 2, 0)]

    def gather_third(got):
        own, next_z, far_z, across, next_across, far_across, rest_z = got
        return [own, next_z, far_z, rest_z, across, next_across, far_across, swap(far_across, 2, 0)]

    def add(*terms):
        return functools.reduce(jnp.add, [t.astype(F32) for t in terms])

    def reduce_first(keep, send_x, send_y):
        return keep, swap(send_x, 0, 1), swap(send_y, 2, 0)

    def reduce_second(state):
        keep, got_x, got_y = state
        far = add(keep[3], got_y[1]).astype(BF16)
        near = add(keep[1], got_x[1]).astype(BF16)
        return keep, got_x, got_y, far, near, swap(far, 0, 1), swap(near, 0, 2)

    def reduce_third(state):
        keep, got_x, got_y, _, _, got_far, got_near = state
        far = add(keep[2], got_y[0], got_far).astype(BF16)
        return add(keep[0], got_x[0], got_near), far, swap_far(far)

    def reduce_fourth(state):
        total = (state[0] + state[2].astype(F32)).astype(BF16)
        bit = 2
        while bit < copies:
            total = add(total, swap(total, bit, 0)).astype(BF16)
            bit *= 2
        return total, swap(total, 1, 0)

    T, width = tokens.shape
    rows = 2 * T
    sds = jax.ShapeDtypeStruct
    row_block = lambda n, c=width: spec((n, c), lambda i: (i, 0))
    col_block = lambda n: spec((width, n), lambda i: (0, i))

    def block_call(body, grid, ins, outs, flops, moved, scratch=(), name=None):
        return kernel_call(
            body,
            grid,
            [place for _, place in ins],
            [place for _, place in outs],
            [shape for shape, _ in outs],
            flops,
            moved,
            scratch=scratch,
            name=name,
        )(*[value for value, _ in ins])

    def const(value):
        return value, whole(value.shape)

    def kept(shape, dtype):
        return sds(shape, dtype), whole(shape)

    with jax.named_scope("exchange"):
        tok_other = swap(tokens, 1, 0)
        dy_other = swap(cotangent, 1, 0)
        seg_other = swap(segments, 1, 0)
        vec_pieces = jnp.pad(vectors, ((0, 3), (0, 0))).astype(BF16)[None]

    with jax.named_scope("prep"):
        own_a, own_q = block_call(
            prep_attn_body,
            (1,),
            [(ids, scalars()), const(w_qkv), const(w_out)],
            [kept((128, 1280), BF16), kept((128, 768), BF16)],
            0,
            3e6,
            name="prep_attn",
        )
        own_mlp = block_call(
            prep_mlp_body,
            (1,),
            [(ids, scalars()), const(w_up), const(w_down)],
            [kept((256, 1024), BF16)] * 2,
            0,
            5e6,
            name="prep_mlp",
        )

    with jax.named_scope("gather"):
        attn_pieces = gather_first(own_a)
        for bits in (2, 4, 1):
            vec_pieces = jnp.concatenate([vec_pieces, swap(vec_pieces, 0, bits)], axis=0)

    with jax.named_scope("rows"):
        tables = [
            jnp.concatenate(pair, axis=0)
            for pair in zip(rotary_tables(segments), rotary_tables(seg_other))
        ]
        seg_row = jnp.stack([segments, seg_other])[:, None, :]
        seg_col = jnp.concatenate([segments, seg_other])[:, None]

    attn_pieces, own_mlp, vec_pieces, tok_other, dy_other = sync(
        attn_pieces, own_mlp, vec_pieces, tok_other, dy_other
    )

    steps = rows // 256
    with jax.named_scope("gather"):
        attn_pieces = gather_second(attn_pieces)
        mlp_pieces = gather_first(own_mlp[0])

    with jax.named_scope("norm"):
        vec, bias_qkv = block_call(
            join_vec_body,
            (1,),
            [(ids, scalars()), const(vec_pieces)],
            [kept((16, 1024), F32), kept((1, 1536), F32)],
            0,
            1e5,
            name="join_vec",
        )
        first_half = spec((256, width), lambda i: (jnp.minimum(i, steps // 2 - 1), 0))
        second_half = spec((256, width), lambda i: (jnp.maximum(i - steps // 2, 0), 0))
        normed = block_call(
            functools.partial(norm_body, steps),
            (steps,),
            [(tokens, first_half), (tok_other, second_half), (cotangent, first_half), (dy_other, second_half)]
            + [const(vec)],
            [(sds((rows, width), BF16), row_block(256))] * 3
            + [(sds((width, rows), BF16), col_block(256))] * 3
            + [kept((8, width), F32)],
            0,
            34e6,
            name="norm",
        )

    attn_pieces, normed, tables, seg_row, seg_col = sync(attn_pieces, normed, tables, seg_row, seg_col)
    attn_in, mlp_in, dy, attn_t, mlp_t, dy_t, dy_sum = normed
    with jax.named_scope("gather"):
        attn_pieces = gather_third(attn_pieces)
        own_mlp_b, attn_pieces[0] = sync(own_mlp[1], attn_pieces[0])
        weights_b = lax.all_gather(own_mlp_b, "zero", axis=0, tiled=False)
        weights_q = lax.all_gather(sync(own_q, weights_b)[0], "zero", axis=0, tiled=False)

    def table_blocks(count):
        return [(t, row_block(count, 128)) for t in tables]

    def heads(value):
        return value, row_block(512, 256)

    def attention(group, projected):
        with jax.named_scope("attention"):
            head_block = spec((T, 128), lambda h, m: (h, m))
            return block_call(
                attn_body,
                (2, 2),
                [(value, head_block) for value in projected]
                + [(seg_col, spec((T, 1), lambda h, m: (h, 0)))]
                + [(seg_row, spec((1, 1, T), lambda h, m: (h, 0, 0)))]
                + [(t, spec((T, 128), lambda h, m: (h, 0))) for t in tables],
                [
                    (sds((rows, 256), BF16), head_block),
                    (sds((3, rows, 256), BF16), spec((3, T, 128), lambda h, m: (0, h, m))),
                ],
                30e9,
                10e6,
                scratch=[pltpu.VMEM((T, 128), F32)] * 3,
                name="attention",
            )

    def blocks_of(shape):
        return [kept((n,) + shape, BF16) for n in (4, 2, 2)]

    with jax.named_scope("qkv"):
        *projected, wq_a, full_out = block_call(
            qkv_first_body,
            (rows // 512,),
            [(ids, scalars())]
            + [const(piece) for piece in attn_pieces]
            + [(attn_in, row_block(512)), (dy, row_block(512)), const(bias_qkv)]
            + table_blocks(512),
            [(sds((rows, 256), BF16), row_block(512, 256))] * 4
            + [kept((1024, 768), BF16), kept((512, 1024), BF16)],
            2 * rows * 1024 * 1024,
            20e6,
            name="qkv",
        )
    projected, mlp_pieces = sync(projected, mlp_pieces)
    with jax.named_scope("gather"):
        mlp_pieces = gather_second(mlp_pieces)
    att_a, grad_a = attention(0, projected)
    att_a, grad_a, mlp_pieces, attn_t = sync(att_a, grad_a, mlp_pieces, attn_t)
    with jax.named_scope("gather"):
        mlp_pieces = gather_third(mlp_pieces)

    with jax.named_scope("attn_weights"):
        grad_block = spec((1, rows, 256), lambda n: (jnp.minimum(n, 2), 0, 0))
        *blocks, bias_sum_a = block_call(
            functools.partial(attn_weights_body, False),
            (3,),
            [(ids, scalars()), const(attn_t), (grad_a, grad_block)],
            blocks_of((128, 768)) + [kept((8, 768), F32)],
            2 * rows * 1024 * 768,
            12e6,
            scratch=[pltpu.VMEM((1024, 256), BF16)],
            name="attn_weights",
        )
    blocks, mlp_pieces, mlp_in = sync(blocks, mlp_pieces, mlp_in)
    reduce_q = reduce_first(*blocks)

    def mlp(part, weights, rows_in):
        with jax.named_scope("mlp"):
            *results, hid, gp, bias_up, w_up_full, w_down_full = block_call(
                functools.partial(mlp_body, part, steps),
                (steps,),
                [(ids, scalars())]
                + [const(w) for w in weights]
                + [const(vec), (rows_in, row_block(256)), (dy, row_block(256)), const(mlp_t), const(dy_t)],
                blocks_of((256, 1024))
                + [(sds((rows, width), BF16), row_block(256))] * 2
                + [kept((8, 1024), F32)]
                + [kept((1024, 1024), BF16)] * 2,
                2 * rows * 1024 * 1024 * 4,
                40e6,
                scratch=[pltpu.VMEM((rows, 1024), BF16)] * 2
                + [pltpu.VMEM((8, 1024), F32), pltpu.VMEM((1024, 512), BF16), pltpu.VMEM((1024, 1024), BF16)],
                name="mlp",
            )
            return results, hid, gp, bias_up[0], w_up_full, w_down_full

    mlp_a = mlp(0, mlp_pieces, mlp_in)
    mlp_a, reduce_q = sync(mlp_a, reduce_q)
    reduce_q = reduce_second(reduce_q)
    reduce_a = reduce_first(*mlp_a[0])
    mlp_in, *ready = sync(mlp_in, *reduce_q[3:5])
    mlp_b = mlp(1, [weights_b], mlp_in)
    mlp_b, reduce_q, reduce_a, attn_in = sync(mlp_b, reduce_q, reduce_a, attn_in)
    reduce_q = reduce_third(reduce_q)
    reduce_a = reduce_second(reduce_a)
    reduce_b = reduce_first(*mlp_b[0])
    attn_in, *ready = sync(attn_in, reduce_q[1], *reduce_a[3:5])

    with jax.named_scope("qkv"):
        wq_b = weights_q.reshape(1024, 768)
        projected = block_call(
            qkv_second_body,
            (rows // 512,),
            [(attn_in, row_block(512)), (dy, row_block(512)), const(wq_b), const(full_out), const(bias_qkv)]
            + table_blocks(512),
            [(sds((rows, 256), BF16), row_block(512, 256))] * 4,
            2 * rows * 1024 * 1024,
            20e6,
            name="qkv",
        )
    att_b, grad_b = attention(1, projected)
    att_b, grad_b, reduce_q, reduce_a, reduce_b = sync(att_b, grad_b, reduce_q, reduce_a, reduce_b)
    reduce_q = reduce_fourth(reduce_q)
    reduce_a = reduce_third(reduce_a)
    reduce_b = reduce_second(reduce_b)
    grad_b, *ready = sync(grad_b, reduce_a[1], *reduce_b[3:5])
    with jax.named_scope("attn_weights"):
        *blocks, bias_sum_b = block_call(
            functools.partial(attn_weights_body, True),
            (4,),
            [(ids, scalars()), const(attn_t), (grad_b, grad_block), const(dy_t), const(att_a), const(att_b)],
            blocks_of((128, 1280)) + [kept((8, 768), F32)],
            2 * rows * 1024 * 1280,
            20e6,
            scratch=[pltpu.VMEM((1024, 256), BF16), pltpu.VMEM((512, 1024), BF16)],
            name="attn_weights",
        )
    blocks, grad_b = sync(blocks, grad_b)
    reduce_o = reduce_first(*blocks)

    _, hid_a, gp_a, bias_up_a, up_a, down_a = mlp_a
    _, hid_b, gp_b, bias_up_b, up_b, down_b = mlp_b

    def back(own, grad, rows_tok, extra, outs):
        first = 0 if own else T // 256
        block = lambda c=width: spec((256, c), lambda i: (i + first, 0))
        lead = spec((3, 256, 256), lambda i: (0, i + first, 0))
        with jax.named_scope("back"):
            return block_call(
                functools.partial(back_body, own),
                (T // 256,),
                [(grad_a, lead), (grad, lead), (att_a, block(256)), (att_b, block(256))]
                + [(value, block()) for value in (hid_a, hid_b, gp_a, gp_b)]
                + [const(w) for w in (wq_a, wq_b, full_out, up_a, up_b, down_a, down_b)]
                + [(rows_tok, row_block(256)), const(vec)]
                + [(value, row_block(256)) for value in extra],
                [(sds((T, width), t), row_block(256)) for t in outs] + [kept((8, width), F32)],
                2 * T * 1024 * 6144,
                40e6,
                name="back",
            )

    out_part, scaled_part, sums_other = back(False, grad_b, tok_other, [], (BF16, BF16))
    out_part, scaled_part, sums_other, grad_b, reduce_q, reduce_a, reduce_b, reduce_o = sync(
        out_part, scaled_part, sums_other, grad_b, reduce_q, reduce_a, reduce_b, reduce_o
    )
    out_got, scaled_got = swap(out_part, 1, 0), swap(scaled_part, 1, 0)
    reduce_a = reduce_fourth(reduce_a)
    reduce_b = reduce_third(reduce_b)
    reduce_o = reduce_second(reduce_o)
    grad_b, *ready = sync(grad_b, reduce_a[0], reduce_b[1], *reduce_o[3:5])
    layer_out, tokens_grad, sums_own = back(
        True, grad_b, tokens, [cotangent, out_got, scaled_got], (BF16, F32)
    )
    sums_own, reduce_a, reduce_b, reduce_o = sync(sums_own, reduce_a, reduce_b, reduce_o)
    reduce_b = reduce_fourth(reduce_b)
    reduce_o = reduce_third(reduce_o)

    with jax.named_scope("vectors"):
        is_core = jnp.arange(2) == core
        grad_bias = jnp.where(core == 0, dy_sum[0:1], 0.0)
        bias_sum = jnp.concatenate([bias_sum_a[0].reshape(3, 256), bias_sum_b[0].reshape(3, 256)], axis=1)
        grad_bias_qkv = jnp.where(
            is_core[None, None, :, None], bias_sum.reshape(3, 8, 1, 64), 0.0
        ).reshape(3, width)
        grad_bias_up = jnp.where(
            is_core[None, None, :, None],
            jnp.swapaxes(jnp.stack([bias_up_a, bias_up_b]).reshape(2, 8, 128), 0, 1)[:, :, None],
            0.0,
        ).reshape(4, width)
        total = jnp.concatenate(
            [
                sums_own[0:4] + sums_other[0:4],
                grad_bias_qkv,
                grad_bias,
                grad_bias_up,
                grad_bias,
                jnp.zeros((3, width), F32),
            ],
            axis=0,
        )
        bits = [(0, b) for b in (1, 2, 4)]
        bit = 1
        while bit < copies:
            bits.append((bit, 0))
            bit *= 2
        for pair in bits:
            total = total + swap(total, *pair)
        share = lax.dynamic_slice_in_dim(total[0:13], me * 128, 128, 1)
        first_vectors, second_vectors, new_vectors = adam_math(
            vectors, m_vectors, v_vectors, share, RATE_VECTOR, 0.0
        )

    with jax.named_scope("adam"):

        def adam_mlp(part, totals, previous):
            wide = [spec((128, 256), lambda n: (0, 2 * n + part))] * 3
            wide += [spec((256, 128), lambda n: (part, n))] * 3
            return pl.pallas_call(
                adam_mlp_body,
                grid=(8,),
                in_specs=[scalars()]
                + [whole((256, 1024))] * 2
                + wide
                + [pl.BlockSpec(memory_space=pl.ANY)] * len(previous),
                out_specs=wide,
                out_shape=[sds((128, 4096), F32)] * 3 + [sds((512, 1024), F32)] * 3,
                input_output_aliases={9 + n: n for n in range(len(previous))},
                cost_estimate=pl.CostEstimate(flops=0, bytes_accessed=14000000, transcendentals=0),
                compiler_params=pltpu.CompilerParams(
                    vmem_limit_bytes=VMEM_LIMIT, dimension_semantics=("arbitrary",)
                ),
                name="adam_mlp",
            )(ids, *totals, w_up, m_up, v_up, w_down, m_down, v_down, *previous)

        updated_mlp = adam_mlp(0, reduce_a, [])
        updated_mlp, reduce_o, reduce_b = sync(updated_mlp, reduce_o, reduce_b)
        reduce_o = reduce_fourth(reduce_o)
        reduce_b, *ready = sync(reduce_b, reduce_o[0])
        updated_mlp = adam_mlp(1, reduce_b, updated_mlp)
        (own_b, other_b) = reduce_o
        (own_a, other_a) = reduce_q
        part_block = lambda n: (0, n)
        out_block = spec((128, 512), lambda n: (0, 0))
        wide = [spec((128, 1024), part_block)] * 3 + [whole((128, 1024))] * 3
        updated_attn = kernel_call(
            adam_attn_body,
            (3,),
            [scalars()] + [spec((128, 256), part_block)] * 4 + [whole((128, 512))] * 2 + wide,
            wide,
            [sds((128, 3072), F32)] * 3 + [sds((128, 1024), F32)] * 3,
            0,
            13e6,
            name="adam_attn",
        )(
            ids,
            own_a,
            other_a,
            own_b,
            other_b,
            own_b[:, 768:],
            other_b[:, 768:],
            w_qkv,
            m_qkv,
            v_qkv,
            w_out,
            m_out,
            v_out,
        )
    first_qkv, second_qkv, new_qkv, first_out, second_out, new_out = updated_attn
    first_up, second_up, new_up, first_down, second_down, new_down = updated_mlp
    return (
        layer_out,
        tokens_grad,
        first_qkv,
        first_out,
        first_up,
        first_down,
        first_vectors,
        second_qkv,
        second_out,
        second_up,
        second_down,
        second_vectors,
        new_qkv,
        new_out,
        new_up,
        new_down,
        new_vectors,
    )


def solution(mesh):
    rows, owned, spread = P(AXES, None), P("zero", None), P(None, "zero")
    state = (owned, owned, owned, owned, spread)
    return jax.shard_map(
        functools.partial(on_device, (mesh.shape["dp"], mesh.shape["zero"])),
        mesh=mesh,
        in_specs=(rows, P(AXES), rows) + state * 3,
        out_specs=(rows, rows) + state * 3,
        check_vma=False,
    )
```

time: 670 us -> 478 us (0.71)
  waiting for transfers between devices: 248 us -> 75.4 us
  blocking collectives: 40.2 us -> 0 us
  Pallas kernels: 253 us -> 273 us
  local copies, waits for them, and re-layouts: 32.9 us -> 14 us
  other arithmetic: 18 us -> 32.5 us
  between operations: 1.64 us -> 15.2 us
  starting transfers between devices: 69.7 us -> 61.7 us
    ppermute x44 -> x55, waiting for transfers between devices: 248 us -> 73.3 us  [move(): return lax.ppermute(value, AXES, pairs)]
    psum x1 -> x0, blocking collectives: 40.2 us -> none  [on_device(): lax.psum(grad_vectors, AXES)]
    pallas_call x13 -> x17, Pallas kernels: 253 us -> 273 us  [the longest x14 247 us: block_call(): kernel_call(body, grid, [place for _, place in ins], [place for _, place...]
    unnamed x65 -> x98, local copies, waits for them, and re-layouts: 12.3 us -> 3.02 us
    ppermute x44 -> x55, starting transfers between devices: 69.7 us -> 61.4 us  [move(): return lax.ppermute(value, AXES, pairs)]
  transfers between devices with their start and end apart: 44 -> 57, of which waited for: 15 -> 16; matrix products, arithmetic and copies ran while one was open for 6% -> 9% of each run, Pallas kernels for 37% -> 56%
where the time goes in v2:
time: 478 us; the launch traced here: 472 us
  Pallas kernels  273 us (57%)
  waiting for transfers between devices  75.4 us (16%)
  starting transfers between devices  61.7 us (13%)
  other arithmetic  32.5 us (7%)
  between operations  15.2 us (3%)
  local copies, waits for them, and re-layouts  14 us (3%)
    pallas_call x14, Pallas kernels, block_call(): kernel_call(body, grid, [place for _, place in ins], [place for _, place...  247 us
    ppermute x55, waiting for transfers between devices, move(): return lax.ppermute(value, AXES, pairs)  73.3 us
    ppermute x55, starting transfers between devices, move(): return lax.ppermute(value, AXES, pairs)  61.4 us
    pallas_call x2, Pallas kernels, adam_mlp(): pl.pallas_call(adam_mlp_body, grid=(8,), in_specs=[scalars()] + [whole((2...  18.1 us
  transfers between devices with their start and end apart: 57, of which 16 were waited for; matrix products, arithmetic and copies ran while one was open for 9% of the time, Pallas kernels for 56%

profile of v2, /device:TPU:0, one launch (start us, length us, event | category | flops | bytes accessed | tf_op | source)
XLA Modules:
  0.0 472.3 jit_solution(5911625109492959886)
XLA Ops:
  8.0 2.6 prep_attn.1
  10.5 3.0 collective-permute-start
  13.6 2.6 collective-permute-start.1
  17.9 3.4 prep_mlp.1
  21.3 7.2 %collective-permute-done.3 = bf16[1,16,128]{2,1,0:T(8,128)(2,1)S(1)} collective-permute-done((bf16[1,16,128]{2,1,0:T(8,128)(2,1)S(1)}, bf16[1,16,128]{2,1,0:T(8,128)(2,1)S(1)}, u32[]{:S(2)}, u32[]{:S(2)}) %collective-permute-start.3) | collective-permute-done | bytes 4128 | tf_op jit(solution)/shard_map/gather/ppermute | solution.py:516
  29.7 2.9 collective-permute-start.4
  33.2 4.9 %fusion.2 = (f32[1024,128]{1,0:T(8,128)S(1)}, f32[1024,128]{1,0:T(8,128)S(1)}, f32[1024,128]{1,0:T(8,128)S(1)}, f32[1024,128]{1,0:T(8,128)}, f32[1024,128]{1,0:T(8,128)}, /*index=5*/f32[1024,128]{1,0:T(8,128)S(1)}) fusion(f32[128]{0:T(128)S(1)} %compare_select_fusion.2, f32[1024]{0:T(1024)S(1)} %fusion.22, pred[128]{0:T(512)(128)(4,1)S(1)} %broadcast_compare_fusion, ...), kind=kLoop, calls=%fused_computation.21 | loop fusion | flops 1048576 | bytes 3154560 | tf_op jit(solution)/shard_map/rows/jit(_where)/select_n | solution.py:480
  39.7 2.2 collective-permute-done.5
  45.1 5.2 %collective-permute-done.2.refs_4_ = bf16[128,1280]{1,0:T(8,128)(2,1)S(1)} collective-permute-done((bf16[128,1280]{1,0:T(8,128)(2,1)S(1)}, bf16[128,1280]{1,0:T(8,128)(2,1)S(1)}, u32[]{:S(2)}, u32[]{:S(2)}) %collective-permute-start.2) | collective-permute-done | bytes 327712 | tf_op jit(solution)/shard_map/gather/ppermute | solution.py:516
  55.2 2.6 pad_maximum_fusion
  59.3 14.4 %norm.1 = (bf16[2048,1024]{1,0:T(8,128)(2,1)}, bf16[2048,1024]{1,0:T(8,128)(2,1)}, bf16[2048,1024]{1,0:T(8,128)(2,1)}, bf16[1024,2048]{1,0:T(8,128)(2,1)}, bf16[...) custom-call(bf16[1024,1024]{1,0:T(8,128)(2,1)} %tok.1, ...), custom_call_target="tpu_custom_call" | custom-call | bytes 34000000 | tf_op jit(solution)/shard_map/norm/norm/pallas_call | solution.py:570
  79.8 2.0 collective-permute-done.12.refs_7_
  82.5 11.0 %qkv.2 = (bf16[2048,256]{1,0:T(8,128)(2,1)}, bf16[2048,256]{1,0:T(8,128)(2,1)}, bf16[2048,256]{1,0:T(8,128)(2,1)}, bf16[2048,256]{1,0:T(8,128)(2,1)}, bf16[1024,...) custom-call(s32[3]{0:T(128)} %pad_add_fusion.4.ids, bf16[128,1280]{1,0:T(8,128)(2,1)} %get-tuple-element.259.refs_0_, ...), custom_call_target="tpu_custom_call" | custom-call | flops 4294967296 | bytes 20000000 | tf_op jit(solution)/shard_map/qkv/qkv/pallas_call | solution.py:570
  93.5 16.6 %collective-permute-done.13.refs_1_ = bf16[256,1024]{1,0:T(8,128)(2,1)S(1)} collective-permute-done((bf16[256,1024]{1,0:T(8,128)(2,1)S(1)}, bf16[256,1024]{1,0:T(8,128)(2,1)S(1)}, u32[]{:S(2)}, u32[]{:S(2)}) %collective-permute-start.13) | collective-permute-done | bytes 524320 | tf_op jit(solution)/shard_map/gather/ppermute | solution.py:516
  110.1 5.5 %collective-permute-done.14.refs_2_ = bf16[256,1024]{1,0:T(8,128)(2,1)S(1)} collective-permute-done((bf16[256,1024]{1,0:T(8,128)(2,1)S(1)}, bf16[256,1024]{1,0:T(8,128)(2,1)S(1)}, u32[]{:S(2)}, u32[]{:S(2)}) %collective-permute-start.14) | collective-permute-done | bytes 524320 | tf_op jit(solution)/shard_map/gather/ppermute | solution.py:516
  117.8 36.9 %attention.2 = (bf16[2048,256]{1,0:T(8,128)(2,1)}, bf16[3,2048,256]{2,1,0:T(8,128)(2,1)}) custom-call(bf16[2048,256]{1,0:T(8,128)(2,1)} %get-tuple-element.277.q, bf16[2048,256]{1,0:T(8,128)(2,1)} %get-tuple-element.278.k, bf16[2048,256]{1,0:T(8,128)(2,1)} %get-tuple-element.279.v, bf16[2048,256]{1,0:T(8,128)(2,1)} %get-tuple-element.280.d_att, ...), custom_call_target="tpu_custom_call" | custom-call | flops 30000001024 | bytes 10000000 | tf_op jit(solution)/shard_map/attention/attention/pallas_call | solution.py:570
  154.8 2.1 collective-permute-start.19
  156.9 7.6 %attn_weights.2 = (bf16[4,128,768]{2,1,0:T(8,128)(2,1)}, bf16[2,128,768]{2,1,0:T(8,128)(2,1)}, bf16[2,128,768]{2,1,0:T(8,128)(2,1)}, f32[8,768]{1,0:T(8,128)}) custom-call(s32[3]{0:T(128)} %pad_add_fusion.4.ids, bf16[1024,2048]{1,0:T(8,128)(2,1)} %get-tuple-element.291.attn_t, bf16[3,2048,256]{2,1,0:T(8,128)(2,1)} %get-tuple-element.290.grad.grad_a), custom_call_target="tpu_custom_call" | custom-call | flops 3221225472 | bytes 12000000 | tf_op jit(solution)/shard_map/attn_weights/attn_weights/pallas_call | solution.py:570
  167.6 2.1 all-gather.5.cloned.1.call-done
  169.8 31.0 %mlp.2 = (bf16[4,256,1024]{2,1,0:T(8,128)(2,1)}, bf16[2,256,1024]{2,1,0:T(8,128)(2,1)}, bf16[2,256,1024]{2,1,0:T(8,128)(2,1)}, bf16[2048,1024]{1,0:T(8,128)(2,1)...) custom-call(s32[3]{0:T(128)} %pad_add_fusion.4.ids, ...), custom_call_target="tpu_custom_call" | custom-call | flops 17179869184 | bytes 40000000 | tf_op jit(solution)/shard_map/mlp/mlp/pallas_call | solution.py:570
  204.1 3.5 collective-permute-start.23
  208.0 31.1 %mlp.3 = (bf16[4,256,1024]{2,1,0:T(8,128)(2,1)}, bf16[2,256,1024]{2,1,0:T(8,128)(2,1)}, bf16[2,256,1024]{2,1,0:T(8,128)(2,1)}, bf16[2048,1024]{1,0:T(8,128)(2,1)...) custom-call(s32[3]{0:T(128)} %pad_add_fusion.4.ids, ...), custom_call_target="tpu_custom_call" | custom-call | flops 17179869184 | bytes 40000000 | tf_op jit(solution)/shard_map/mlp/mlp/pallas_call | solution.py:570
  243.3 1.8 bitcast_add_fusion.6
  245.2 3.0 collective-permute-start.26
  249.9 10.0 %qkv.3 = (bf16[2048,256]{1,0:T(8,128)(2,1)}, bf16[2048,256]{1,0:T(8,128)(2,1)}, bf16[2048,256]{1,0:T(8,128)(2,1)}, bf16[2048,256]{1,0:T(8,128)(2,1)}) custom-call(bf16[2048,1024]{1,0:T(8,128)(2,1)} %get-tuple-element.348.refs_8_.attn_in, bf16[2048,1024]{1,0:T(8,128)(2,1)} %get-tuple-element.267.refs_9_.refs_10_.refs_3_.dy, ...), custom_call_target="tpu_custom_call" | custom-call | flops 4294967296 | bytes 20000000 | tf_op jit(solution)/shard_map/qkv/qkv/pallas_call | solution.py:570
  260.0 36.8 %attention.3 = (bf16[2048,256]{1,0:T(8,128)(2,1)}, bf16[3,2048,256]{2,1,0:T(8,128)(2,1)}) custom-call(bf16[2048,256]{1,0:T(8,128)(2,1)} %get-tuple-element.352.q, bf16[2048,256]{1,0:T(8,128)(2,1)} %get-tuple-element.353.k, bf16[2048,256]{1,0:T(8,128)(2,1)} %get-tuple-element.354.v, bf16[2048,256]{1,0:T(8,128)(2,1)} %get-tuple-element.355.d_att, ...), custom_call_target="tpu_custom_call" | custom-call | flops 30000001024 | bytes 10000000 | tf_op jit(solution)/shard_map/attention/attention/pallas_call | solution.py:570
  298.8 2.4 fusion.12
  306.9 12.3 %attn_weights.3 = (bf16[4,128,1280]{2,1,0:T(8,128)(2,1)}, bf16[2,128,1280]{2,1,0:T(8,128)(2,1)}, bf16[2,128,1280]{2,1,0:T(8,128)(2,1)}, f32[8,768]{1,0:T(8,128)}) custom-call(s32[3]{0:T(128)} %pad_add_fusion.4.ids, bf16[1024,2048]{1,0:T(8,128)(2,1)} %get-tuple-element.291.attn_t, bf16[3,2048,256]{2,1,0:T(8,128)(2,1)} %get-tuple-element.405.grad.grad_b, ...), custom_call_target="tpu_custom_call" | custom-call | flops 5368709120 | bytes 20000000 | tf_op jit(solution)/shard_map/attn_weights/attn_weights/pallas_call | solution.py:570
  319.6 2.0 collective-permute-start.37
  321.6 23.1 %back.2 = (bf16[1024,1024]{1,0:T(8,128)(2,1)}, bf16[1024,1024]{1,0:T(8,128)(2,1)}, f32[8,1024]{1,0:T(8,128)}) custom-call(bf16[3,2048,256]{2,1,0:T(8,128)(2,1)} %get-tuple-element.290.grad.grad_a, bf16[3,2048,256]{2,1,0:T(8,128)(2,1)} %get-tuple-element.405.grad.grad_b, bf16[2048,256]{1,0:T(8,128)(2,1)} %get-tuple-element.371.refs_1_.att_a, ...), custom_call_target="tpu_custom_call" | custom-call | flops 12884901888 | bytes 40000000 | tf_op jit(solution)/shard_map/back/back/pallas_call | solution.py:570
  349.6 2.1 fusion.15
  353.9 2.0 bitcast_add_fusion
  355.9 7.6 %collective-permute-done.38 = bf16[256,1024]{1,0:T(8,128)(2,1)S(1)} collective-permute-done((bf16[256,1024]{1,0:T(8,128)(2,1)S(1)}, bf16[256,1024]{1,0:T(8,128)(2,1)S(1)}, u32[]{:S(2)}, u32[]{:S(2)}) %collective-permute-start.38) | collective-permute-done | bytes 524320 | tf_op jit(solution)/shard_map/ppermute | solution.py:516
  364.8 25.7 %back.3 = (bf16[1024,1024]{1,0:T(8,128)(2,1)}, f32[1024,1024]{1,0:T(8,128)}, f32[8,1024]{1,0:T(8,128)}) custom-call(bf16[3,2048,256]{2,1,0:T(8,128)(2,1)} %get-tuple-element.290.grad.grad_a, bf16[3,2048,256]{2,1,0:T(8,128)(2,1)} %get-tuple-element.405.grad.grad_b, bf16[2048,256]{1,0:T(8,128)(2,1)} %get-tuple-element.371.refs_1_.att_a, ...), custom_call_target="tpu_custom_call" | custom-call | flops 12884901888 | bytes 40000000 | tf_op jit(solution)/shard_map/back/back/pallas_call | solution.py:570
  390.7 1.8 collective-permute-start.46
  398.1 7.0 %collective-permute-done.46 = bf16[256,1024]{1,0:T(8,128)(2,1)S(1)} collective-permute-done((bf16[256,1024]{1,0:T(8,128)(2,1)S(1)}, bf16[256,1024]{1,0:T(8,128)(2,1)S(1)}, u32[]{:S(2)}, u32[]{:S(2)}) %collective-permute-start.46) | collective-permute-done | bytes 524320 | tf_op jit(solution)/shard_map/ppermute | solution.py:516
  405.3 2.3 fusion.6
  407.7 1.9 collective-permute-start.45
  410.4 9.0 %adam_mlp.2 = (f32[128,4096]{1,0:T(8,128)}, f32[128,4096]{1,0:T(8,128)}, f32[128,4096]{1,0:T(8,128)}, f32[512,1024]{1,0:T(8,128)}, f32[512,1024]{1,0:T(8,128)}, /*index=5*/f32[512,1024]{1,0:T(8,128)}) custom-call(s32[3]{0:T(128)} %pad_add_fusion.4.ids, bf16[256,1024]{1,0:T(8,128)(2,1)} %copy-done.5, bf16[256,1024]{1,0:T(8,128)(2,1)} %copy-done.20, ...), custom_call_target="tpu_custom_call" | custom-call | bytes 14000000 | tf_op jit(solution)/shard_map/adam/adam_mlp/pallas_call | solution.py:877
  419.4 6.4 %collective-permute-done.45 = bf16[128,1280]{1,0:T(8,128)(2,1)S(1)} collective-permute-done((bf16[128,1280]{1,0:T(8,128)(2,1)}, bf16[128,1280]{1,0:T(8,128)(2,1)S(1)}, u32[]{:S(2)}, u32[]{:S(2)}) %collective-permute-start.45) | collective-permute-done | bytes 327712 | tf_op jit(solution)/shard_map/ppermute | solution.py:516
  426.0 1.8 collective-permute-start.50
  427.9 2.5 collective-permute-done.50
  431.8 2.9 collective-permute-done.51
  436.1 3.9 collective-permute-done.52
  441.3 2.2 collective-permute-start.54
  443.5 2.4 collective-permute-done.54
  447.2 9.0 %adam_mlp.3 = (f32[128,4096]{1,0:T(8,128)}, f32[128,4096]{1,0:T(8,128)}, f32[128,4096]{1,0:T(8,128)}, f32[512,1024]{1,0:T(8,128)}, f32[512,1024]{1,0:T(8,128)}, /*index=5*/f32[512,1024]{1,0:T(8,128)}) custom-call(s32[3]{0:T(128)} %pad_add_fusion.4.ids, ...), custom_call_target="tpu_custom_call", output_to_operand_aliasing={{0}: (9, {}), {1}: (10, {}), {2}: (11, {}), {3}: (12, {}), ... | custom-call | bytes 14000000 | tf_op jit(solution)/shard_map/adam/adam_mlp/pallas_call | solution.py:877
  457.1 8.1 %adam_attn.1 = (f32[128,3072]{1,0:T(8,128)}, f32[128,3072]{1,0:T(8,128)}, f32[128,3072]{1,0:T(8,128)}, f32[128,1024]{1,0:T(8,128)}, f32[128,1024]{1,0:T(8,128)}, /*index=5*/f32[128,1024]{1,0:T(8,128)}) custom-call(s32[3]{0:T(128)} %pad_add_fusion.4.ids, bf16[128,768]{1,0:T(8,128)(2,1)} %copy-done.16, bf16[128,768]{1,0:T(8,128)(2,1)} %copy-done.25, ...), custom_call_target="tpu_custom_call" | custom-call | bytes 13000000 | tf_op jit(solution)/shard_map/adam/adam_attn/pallas_call | solution.py:904
  (253 shorter events, 66.4 us)
Async XLA Ops:
  7.2 162.5 %all-gather.5.cloned.1.call-start = ((), (), s32[]{:S(2)}) async-start(), calls=%async_computation | async-start | bytes 4718592 | tf_op jit(solution)/shard_map/gather/all_gather | solution.py:666
  10.5 34.5 %collective-permute-start = (bf16[128,1280]{1,0:T(8,128)(2,1)}, bf16[128,1280]{1,0:T(8,128)(2,1)}, u32[]{:S(2)}, u32[]{:S(2)}) collective-permute-start(bf16[128,1280]{1,0:T(8,128)(2,1)} %get-tuple-element.259.refs_0_), channel_id=1, source_target_pairs={{0,2},{1,3},{2,0},{3,1},{4,6},{5,7},{6,4},{7,5},{8,10},{9,11},{10,... | collective-permute-start | bytes 983048 | tf_op jit(solution)/shard_map/gather/ppermute | solution.py:516
  13.6 31.5 %collective-permute-start.1 = (bf16[128,1280]{1,0:T(8,128)(2,1)}, bf16[128,1280]{1,0:T(8,128)(2,1)}, u32[]{:S(2)}, u32[]{:S(2)}) collective-permute-start(bf16[128,1280]{1,0:T(8,128)(2,1)} %get-tuple-element.259.refs_0_), channel_id=1, source_target_pairs={{0,4},{1,5},{2,6},{3,7},{4,0},{5,1},{6,2},{7,3},{8,12},{9,13},{10,... | collective-permute-start | bytes 983048 | tf_op jit(solution)/shard_map/gather/ppermute | solution.py:516
  16.2 12.4 %collective-permute-start.3 = (bf16[1,16,128]{2,1,0:T(8,128)(2,1)S(1)}, bf16[1,16,128]{2,1,0:T(8,128)(2,1)S(1)}, u32[]{:S(2)}, u32[]{:S(2)}) collective-permute-start(bf16[1,16,128]{2,1,0:T(8,128)(2,1)S(1)} %pad_bitcast_fusion), channel_id=1, source_target_pairs={{0,2},{1,3},{2,0},{3,1},{4,6},{5,7},{6,4},{7,5},{8,10},{9,11},{10,... | collective-permute-start | bytes 12296 | tf_op jit(solution)/shard_map/gather/ppermute | solution.py:516
  16.7 33.6 %collective-permute-start.6 = (bf16[1024,1024]{1,0:T(8,128)(2,1)S(1)}, bf16[1024,1024]{1,0:T(8,128)(2,1)}, u32[]{:S(2)}, u32[]{:S(2)}) collective-permute-start(bf16[1024,1024]{1,0:T(8,128)(2,1)S(1)} %copy-done.4), channel_id=1, source_target_pairs={{0,8},{1,9},{2,10},{3,11},{4,12},{5,13},{6,14},{7,15},{8,0},{9,1},... | collective-permute-start | bytes 6291464 | tf_op jit(solution)/shard_map/exchange/ppermute | solution.py:516
  16.7 34.3 %collective-permute-start.7 = (bf16[1024,1024]{1,0:T(8,128)(2,1)}, bf16[1024,1024]{1,0:T(8,128)(2,1)}, u32[]{:S(2)}, u32[]{:S(2)}) collective-permute-start(bf16[1024,1024]{1,0:T(8,128)(2,1)} %refs_0_.4), channel_id=1, source_target_pairs={{0,8},{1,9},{2,10},{3,11},{4,12},{5,13},{6,14},{7,15},{8,0},{9,1},... | collective-permute-start | bytes 6291464 | tf_op jit(solution)/shard_map/exchange/ppermute | solution.py:516
  29.7 8.4 %collective-permute-start.4 = (bf16[2,16,128]{2,1,0:T(8,128)(2,1)S(1)}, bf16[2,16,128]{2,1,0:T(8,128)(2,1)S(1)}, u32[]{:S(2)}, u32[]{:S(2)}) collective-permute-start(bf16[2,16,128]{2,1,0:T(8,128)(2,1)S(1)} %pad_maximum_fusion.5), channel_id=1, source_target_pairs={{0,4},{1,5},{2,6},{3,7},{4,0},{5,1},{6,2},{7,3},{8,12},{9,13},{10,... | collective-permute-start | bytes 24584 | tf_op jit(solution)/shard_map/gather/ppermute | solution.py:516
  51.0 22.7 %collective-permute-start.10 = (bf16[128,1280]{1,0:T(8,128)(2,1)}, bf16[128,1280]{1,0:T(8,128)(2,1)S(1)}, u32[]{:S(2)}, u32[]{:S(2)}) collective-permute-start(bf16[128,1280]{1,0:T(8,128)(2,1)} %collective-permute-done.1.refs_2_), channel_id=1, source_target_pairs={{0,16},{1,17},{2,18},{3,19},{4,20},{5,21},{6,22},{7,23},{8,24},{9,... | collective-permute-start | bytes 983048 | tf_op jit(solution)/shard_map/gather/ppermute | solution.py:516
  52.5 21.2 %collective-permute-start.9 = (bf16[128,1280]{1,0:T(8,128)(2,1)}, bf16[128,1280]{1,0:T(8,128)(2,1)}, u32[]{:S(2)}, u32[]{:S(2)}) collective-permute-start(bf16[128,1280]{1,0:T(8,128)(2,1)} %collective-permute-done.1.refs_2_), channel_id=1, source_target_pairs={{0,1},{1,0},{2,3},{3,2},{4,5},{5,4},{6,7},{7,6},{8,9},{9,8},{10,11... | collective-permute-start | bytes 983048 | tf_op jit(solution)/shard_map/gather/ppermute | solution.py:516
  54.0 19.7 %collective-permute-start.8 = (bf16[128,1280]{1,0:T(8,128)(2,1)}, bf16[128,1280]{1,0:T(8,128)(2,1)S(1)}, u32[]{:S(2)}, u32[]{:S(2)}) collective-permute-start(bf16[128,1280]{1,0:T(8,128)(2,1)} %collective-permute-done.refs_1_), channel_id=1, source_target_pairs={{0,1},{1,0},{2,3},{3,2},{4,5},{5,4},{6,7},{7,6},{8,9},{9,8},{10,11... | collective-permute-start | bytes 983048 | tf_op jit(solution)/shard_map/gather/ppermute | solution.py:516
  73.8 176.2 %all-gather.7.cloned.1.call-start = ((), (), s32[]{:S(2)}) async-start(), calls=%async_computation.1 | async-start | bytes 1769472 | tf_op jit(solution)/shard_map/gather/all_gather | solution.py:667
  75.0 35.1 %collective-permute-start.13 = (bf16[256,1024]{1,0:T(8,128)(2,1)S(1)}, bf16[256,1024]{1,0:T(8,128)(2,1)S(1)}, u32[]{:S(2)}, u32[]{:S(2)}) collective-permute-start(bf16[256,1024]{1,0:T(8,128)(2,1)S(1)} %copy-done.36), channel_id=1, source_target_pairs={{0,2},{1,3},{2,0},{3,1},{4,6},{5,7},{6,4},{7,5},{8,10},{9,11},{10,... | collective-permute-start | bytes 1572872 | tf_op jit(solution)/shard_map/gather/ppermute | solution.py:516
  76.1 39.6 %collective-permute-start.14 = (bf16[256,1024]{1,0:T(8,128)(2,1)S(1)}, bf16[256,1024]{1,0:T(8,128)(2,1)S(1)}, u32[]{:S(2)}, u32[]{:S(2)}) collective-permute-start(bf16[256,1024]{1,0:T(8,128)(2,1)S(1)} %copy-done.36), channel_id=1, source_target_pairs={{0,4},{1,5},{2,6},{3,7},{4,0},{5,1},{6,2},{7,3},{8,12},{9,13},{10,... | collective-permute-start | bytes 1572872 | tf_op jit(solution)/shard_map/gather/ppermute | solution.py:516
  76.9 38.7 %collective-permute-start.15 = (bf16[256,1024]{1,0:T(8,128)(2,1)S(1)}, bf16[256,1024]{1,0:T(8,128)(2,1)S(1)}, u32[]{:S(2)}, u32[]{:S(2)}) collective-permute-start(bf16[256,1024]{1,0:T(8,128)(2,1)S(1)} %copy-done.36), channel_id=1, source_target_pairs={{0,1},{1,0},{2,3},{3,2},{4,5},{5,4},{6,7},{7,6},{8,9},{9,8},{10,11... | collective-permute-start | bytes 1572872 | tf_op jit(solution)/shard_map/gather/ppermute | solution.py:516
  115.7 39.1 %collective-permute-start.17 = (bf16[256,1024]{1,0:T(8,128)(2,1)S(1)}, bf16[256,1024]{1,0:T(8,128)(2,1)S(1)}, u32[]{:S(2)}, u32[]{:S(2)}) collective-permute-start(bf16[256,1024]{1,0:T(8,128)(2,1)S(1)} %collective-permute-done.14.refs_2_), channel_id=1, source_target_pairs={{0,1},{1,0},{2,3},{3,2},{4,5},{5,4},{6,7},{7,6},{8,9},{9,8},{10,11... | collective-permute-start | bytes 1572872 | tf_op jit(solution)/shard_map/gather/ppermute | solution.py:516
  117.2 37.5 %collective-permute-start.18 = (bf16[256,1024]{1,0:T(8,128)(2,1)S(1)}, bf16[256,1024]{1,0:T(8,128)(2,1)S(1)}, u32[]{:S(2)}, u32[]{:S(2)}) collective-permute-start(bf16[256,1024]{1,0:T(8,128)(2,1)S(1)} %collective-permute-done.14.refs_2_), channel_id=1, source_target_pairs={{0,16},{1,17},{2,18},{3,19},{4,20},{5,21},{6,22},{7,23},{8,24},{9,... | collective-permute-start | bytes 1572872 | tf_op jit(solution)/shard_map/gather/ppermute | solution.py:516
  117.2 37.5 %collective-permute-start.16 = (bf16[256,1024]{1,0:T(8,128)(2,1)S(1)}, bf16[256,1024]{1,0:T(8,128)(2,1)S(1)}, u32[]{:S(2)}, u32[]{:S(2)}) collective-permute-start(bf16[256,1024]{1,0:T(8,128)(2,1)S(1)} %collective-permute-done.13.refs_1_), channel_id=1, source_target_pairs={{0,1},{1,0},{2,3},{3,2},{4,5},{5,4},{6,7},{7,6},{8,9},{9,8},{10,11... | collective-permute-start | bytes 1572872 | tf_op jit(solution)/shard_map/gather/ppermute | solution.py:516
  154.8 9.8 %collective-permute-start.19 = (bf16[256,1024]{1,0:T(8,128)(2,1)S(1)}, bf16[256,1024]{1,0:T(8,128)(2,1)S(1)}, u32[]{:S(2)}, u32[]{:S(2)}) collective-permute-start(bf16[256,1024]{1,0:T(8,128)(2,1)S(1)} %collective-permute-done.17.refs_6_), channel_id=1, source_target_pairs={{0,16},{1,17},{2,18},{3,19},{4,20},{5,21},{6,22},{7,23},{8,24},{9,... | collective-permute-start | bytes 1572872 | tf_op jit(solution)/shard_map/gather/ppermute | solution.py:516
  164.5 37.0 %collective-permute-start.20 = (bf16[2,128,768]{2,1,0:T(8,128)(2,1)}, bf16[2,128,768]{2,1,0:T(8,128)(2,1)S(1)}, u32[]{:S(2)}, u32[]{:S(2)}) collective-permute-start(bf16[2,128,768]{2,1,0:T(8,128)(2,1)} %get-tuple-element.324), channel_id=1, source_target_pairs={{0,1},{1,0},{2,3},{3,2},{4,5},{5,4},{6,7},{7,6},{8,9},{9,8},{10,11... | collective-permute-start | bytes 1179656 | tf_op jit(solution)/shard_map/ppermute | solution.py:516
  166.1 35.4 %collective-permute-start.21 = (bf16[2,128,768]{2,1,0:T(8,128)(2,1)}, bf16[2,128,768]{2,1,0:T(8,128)(2,1)S(1)}, u32[]{:S(2)}, u32[]{:S(2)}) collective-permute-start(bf16[2,128,768]{2,1,0:T(8,128)(2,1)} %get-tuple-element.325), channel_id=1, source_target_pairs={{0,16},{1,17},{2,18},{3,19},{4,20},{5,21},{6,22},{7,23},{8,24},{9,... | collective-permute-start | bytes 1179656 | tf_op jit(solution)/shard_map/ppermute | solution.py:516
  202.4 37.4 %collective-permute-start.22 = (bf16[128,768]{1,0:T(8,128)(2,1)}, bf16[128,768]{1,0:T(8,128)(2,1)S(1)}, u32[]{:S(2)}, u32[]{:S(2)}) collective-permute-start(bf16[128,768]{1,0:T(8,128)(2,1)} %get-tuple-element.479), channel_id=1, source_target_pairs={{0,1},{1,0},{2,3},{3,2},{4,5},{5,4},{6,7},{7,6},{8,9},{9,8},{10,11... | collective-permute-start | bytes 589832 | tf_op jit(solution)/shard_map/ppermute | solution.py:516
  204.1 35.7 %collective-permute-start.23 = (bf16[128,768]{1,0:T(8,128)(2,1)}, bf16[128,768]{1,0:T(8,128)(2,1)S(1)}, u32[]{:S(2)}, u32[]{:S(2)}) collective-permute-start(bf16[128,768]{1,0:T(8,128)(2,1)} %get-tuple-element.478), channel_id=1, source_target_pairs={{0,2},{1,3},{2,0},{3,1},{4,6},{5,7},{6,4},{7,5},{8,10},{9,11},{10,... | collective-permute-start | bytes 589832 | tf_op jit(solution)/shard_map/ppermute | solution.py:516
  207.7 32.2 %collective-permute-start.24 = (bf16[2,256,1024]{2,1,0:T(8,128)(2,1)}, bf16[2,256,1024]{2,1,0:T(8,128)(2,1)S(1)}, u32[]{:S(2)}, u32[]{:S(2)}) collective-permute-start(bf16[2,256,1024]{2,1,0:T(8,128)(2,1)} %get-tuple-element.339), channel_id=1, source_target_pairs={{0,1},{1,0},{2,3},{3,2},{4,5},{5,4},{6,7},{7,6},{8,9},{9,8},{10,11... | collective-permute-start | bytes 3145736 | tf_op jit(solution)/shard_map/ppermute | solution.py:516
  207.9 31.9 %collective-permute-start.25 = (bf16[2,256,1024]{2,1,0:T(8,128)(2,1)}, bf16[2,256,1024]{2,1,0:T(8,128)(2,1)S(1)}, u32[]{:S(2)}, u32[]{:S(2)}) collective-permute-start(bf16[2,256,1024]{2,1,0:T(8,128)(2,1)} %get-tuple-element.340), channel_id=1, source_target_pairs={{0,16},{1,17},{2,18},{3,19},{4,20},{5,21},{6,22},{7,23},{8,24},{9,... | collective-permute-start | bytes 3145736 | tf_op jit(solution)/shard_map/ppermute | solution.py:516
  241.6 55.2 %collective-permute-start.27 = (bf16[256,1024]{1,0:T(8,128)(2,1)}, bf16[256,1024]{1,0:T(8,128)(2,1)}, u32[]{:S(2)}, u32[]{:S(2)}) collective-permute-start(bf16[256,1024]{1,0:T(8,128)(2,1)} %get-tuple-element.471), channel_id=1, source_target_pairs={{0,1},{1,0},{2,3},{3,2},{4,5},{5,4},{6,7},{7,6},{8,9},{9,8},{10,11... | collective-permute-start | bytes 1572872 | tf_op jit(solution)/shard_map/ppermute | solution.py:516
  243.3 53.5 %collective-permute-start.28 = (bf16[256,1024]{1,0:T(8,128)(2,1)}, bf16[256,1024]{1,0:T(8,128)(2,1)}, u32[]{:S(2)}, u32[]{:S(2)}) collective-permute-start(bf16[256,1024]{1,0:T(8,128)(2,1)} %get-tuple-element.470), channel_id=1, source_target_pairs={{0,2},{1,3},{2,0},{3,1},{4,6},{5,7},{6,4},{7,5},{8,10},{9,11},{10,... | collective-permute-start | bytes 1572872 | tf_op jit(solution)/shard_map/ppermute | solution.py:516
  245.2 51.6 %collective-permute-start.26 = (bf16[128,768]{1,0:T(8,128)(2,1)}, bf16[128,768]{1,0:T(8,128)(2,1)}, u32[]{:S(2)}, u32[]{:S(2)}) collective-permute-start(bf16[128,768]{1,0:T(8,128)(2,1)} %get-tuple-element.477), channel_id=1, source_target_pairs={{0,4},{1,5},{2,6},{3,7},{4,0},{5,1},{6,2},{7,3},{8,12},{9,13},{10,... | collective-permute-start | bytes 589832 | tf_op jit(solution)/shard_map/ppermute | solution.py:516
  248.2 48.6 %collective-permute-start.29 = (bf16[2,256,1024]{2,1,0:T(8,128)(2,1)}, bf16[2,256,1024]{2,1,0:T(8,128)(2,1)S(1)}, u32[]{:S(2)}, u32[]{:S(2)}) collective-permute-start(bf16[2,256,1024]{2,1,0:T(8,128)(2,1)} %get-tuple-element.361), channel_id=1, source_target_pairs={{0,1},{1,0},{2,3},{3,2},{4,5},{5,4},{6,7},{7,6},{8,9},{9,8},{10,11... | collective-permute-start | bytes 3145736 | tf_op jit(solution)/shard_map/ppermute | solution.py:516
  248.5 48.4 %collective-permute-start.30 = (bf16[2,256,1024]{2,1,0:T(8,128)(2,1)}, bf16[2,256,1024]{2,1,0:T(8,128)(2,1)}, u32[]{:S(2)}, u32[]{:S(2)}) collective-permute-start(bf16[2,256,1024]{2,1,0:T(8,128)(2,1)} %get-tuple-element.362), channel_id=1, source_target_pairs={{0,16},{1,17},{2,18},{3,19},{4,20},{5,21},{6,22},{7,23},{8,24},{9,... | collective-permute-start | bytes 3145736 | tf_op jit(solution)/shard_map/ppermute | solution.py:516
  298.2 8.6 %collective-permute-start.31 = (bf16[128,768]{1,0:T(8,128)(2,1)S(1)}, bf16[128,768]{1,0:T(8,128)(2,1)S(1)}, u32[]{:S(2)}, u32[]{:S(2)}) collective-permute-start(bf16[128,768]{1,0:T(8,128)(2,1)S(1)} %add_convert_fusion.13), channel_id=1, source_target_pairs={{0,16},{1,17},{2,18},{3,19},{4,20},{5,21},{6,22},{7,23},{8,24},{9,... | collective-permute-start | bytes 589832 | tf_op jit(solution)/shard_map/ppermute | solution.py:516
  301.2 43.5 %collective-permute-start.34 = (bf16[256,1024]{1,0:T(8,128)(2,1)}, bf16[256,1024]{1,0:T(8,128)(2,1)}, u32[]{:S(2)}, u32[]{:S(2)}) collective-permute-start(bf16[256,1024]{1,0:T(8,128)(2,1)} %get-tuple-element.469), channel_id=1, source_target_pairs={{0,1},{1,0},{2,3},{3,2},{4,5},{5,4},{6,7},{7,6},{8,9},{9,8},{10,11... | collective-permute-start | bytes 1572872 | tf_op jit(solution)/shard_map/ppermute | solution.py:516
  303.0 41.8 %collective-permute-start.35 = (bf16[256,1024]{1,0:T(8,128)(2,1)}, bf16[256,1024]{1,0:T(8,128)(2,1)}, u32[]{:S(2)}, u32[]{:S(2)}) collective-permute-start(bf16[256,1024]{1,0:T(8,128)(2,1)} %get-tuple-element.468), channel_id=1, source_target_pairs={{0,2},{1,3},{2,0},{3,1},{4,6},{5,7},{6,4},{7,5},{8,10},{9,11},{10,... | collective-permute-start | bytes 1572872 | tf_op jit(solution)/shard_map/ppermute | solution.py:516
  305.4 39.4 %collective-permute-start.33 = (bf16[256,1024]{1,0:T(8,128)(2,1)S(1)}, bf16[256,1024]{1,0:T(8,128)(2,1)S(1)}, u32[]{:S(2)}, u32[]{:S(2)}) collective-permute-start(bf16[256,1024]{1,0:T(8,128)(2,1)S(1)} %get-tuple-element.467), channel_id=1, source_target_pairs={{0,4},{1,5},{2,6},{3,7},{4,0},{5,1},{6,2},{7,3},{8,12},{9,13},{10,... | collective-permute-start | bytes 1572872 | tf_op jit(solution)/shard_map/ppermute | solution.py:516
  306.9 12.7 %collective-permute-start.32 = (bf16[128,768]{1,0:T(8,128)(2,1)S(1)}, bf16[128,768]{1,0:T(8,128)(2,1)S(1)}, u32[]{:S(2)}, u32[]{:S(2)}) collective-permute-start(bf16[128,768]{1,0:T(8,128)(2,1)S(1)} %add_convert_fusion.12.own_a), channel_id=1, source_target_pairs={{0,8},{1,9},{2,10},{3,11},{4,12},{5,13},{6,14},{7,15},{8,0},{9,1},... | collective-permute-start | bytes 589832 | tf_op jit(solution)/shard_map/ppermute | solution.py:516
  319.2 26.3 %collective-permute-start.36 = (bf16[2,128,1280]{2,1,0:T(8,128)(2,1)}, bf16[2,128,1280]{2,1,0:T(8,128)(2,1)}, u32[]{:S(2)}, u32[]{:S(2)}) collective-permute-start(bf16[2,128,1280]{2,1,0:T(8,128)(2,1)} %get-tuple-element.394), channel_id=1, source_target_pairs={{0,1},{1,0},{2,3},{3,2},{4,5},{5,4},{6,7},{7,6},{8,9},{9,8},{10,11... | collective-permute-start | bytes 1966088 | tf_op jit(solution)/shard_map/ppermute | solution.py:516
  319.6 26.0 %collective-permute-start.37 = (bf16[2,128,1280]{2,1,0:T(8,128)(2,1)}, bf16[2,128,1280]{2,1,0:T(8,128)(2,1)}, u32[]{:S(2)}, u32[]{:S(2)}) collective-permute-start(bf16[2,128,1280]{2,1,0:T(8,128)(2,1)} %get-tuple-element.395), channel_id=1, source_target_pairs={{0,16},{1,17},{2,18},{3,19},{4,20},{5,21},{6,22},{7,23},{8,24},{9,... | collective-permute-start | bytes 1966088 | tf_op jit(solution)/shard_map/ppermute | solution.py:516
  345.6 19.1 %collective-permute-start.39 = (bf16[1024,1024]{1,0:T(8,128)(2,1)}, bf16[1024,1024]{1,0:T(8,128)(2,1)}, u32[]{:S(2)}, u32[]{:S(2)}) collective-permute-start(bf16[1024,1024]{1,0:T(8,128)(2,1)} %get-tuple-element.406), channel_id=1, source_target_pairs={{0,8},{1,9},{2,10},{3,11},{4,12},{5,13},{6,14},{7,15},{8,0},{9,1},... | collective-permute-start | bytes 6291464 | tf_op jit(solution)/shard_map/ppermute | solution.py:516
  345.6 19.2 %collective-permute-start.40 = (bf16[1024,1024]{1,0:T(8,128)(2,1)}, bf16[1024,1024]{1,0:T(8,128)(2,1)}, u32[]{:S(2)}, u32[]{:S(2)}) collective-permute-start(bf16[1024,1024]{1,0:T(8,128)(2,1)} %get-tuple-element.407), channel_id=1, source_target_pairs={{0,8},{1,9},{2,10},{3,11},{4,12},{5,13},{6,14},{7,15},{8,0},{9,1},... | collective-permute-start | bytes 6291464 | tf_op jit(solution)/shard_map/ppermute | solution.py:516
  349.5 14.0 %collective-permute-start.38 = (bf16[256,1024]{1,0:T(8,128)(2,1)S(1)}, bf16[256,1024]{1,0:T(8,128)(2,1)S(1)}, u32[]{:S(2)}, u32[]{:S(2)}) collective-permute-start(bf16[256,1024]{1,0:T(8,128)(2,1)S(1)} %add_convert_fusion.3), channel_id=1, source_target_pairs={{0,16},{1,17},{2,18},{3,19},{4,20},{5,21},{6,22},{7,23},{8,24},{9,... | collective-permute-start | bytes 1572872 | tf_op jit(solution)/shard_map/ppermute | solution.py:516
  351.6 38.8 %collective-permute-start.43 = (bf16[128,1280]{1,0:T(8,128)(2,1)}, bf16[128,1280]{1,0:T(8,128)(2,1)S(1)}, u32[]{:S(2)}, u32[]{:S(2)}) collective-permute-start(bf16[128,1280]{1,0:T(8,128)(2,1)} %get-tuple-element.475), channel_id=1, source_target_pairs={{0,1},{1,0},{2,3},{3,2},{4,5},{5,4},{6,7},{7,6},{8,9},{9,8},{10,11... | collective-permute-start | bytes 983048 | tf_op jit(solution)/shard_map/ppermute | solution.py:516
  353.4 37.1 %collective-permute-start.44 = (bf16[128,1280]{1,0:T(8,128)(2,1)}, bf16[128,1280]{1,0:T(8,128)(2,1)S(1)}, u32[]{:S(2)}, u32[]{:S(2)}) collective-permute-start(bf16[128,1280]{1,0:T(8,128)(2,1)} %get-tuple-element.474), channel_id=1, source_target_pairs={{0,2},{1,3},{2,0},{3,1},{4,6},{5,7},{6,4},{7,5},{8,10},{9,11},{10,... | collective-permute-start | bytes 983048 | tf_op jit(solution)/shard_map/ppermute | solution.py:516
  363.5 27.0 %collective-permute-start.42 = (bf16[256,1024]{1,0:T(8,128)(2,1)S(1)}, bf16[256,1024]{1,0:T(8,128)(2,1)S(1)}, u32[]{:S(2)}, u32[]{:S(2)}) collective-permute-start(bf16[256,1024]{1,0:T(8,128)(2,1)S(1)} %get-tuple-element.465), channel_id=1, source_target_pairs={{0,4},{1,5},{2,6},{3,7},{4,0},{5,1},{6,2},{7,3},{8,12},{9,13},{10,... | collective-permute-start | bytes 1572872 | tf_op jit(solution)/shard_map/ppermute | solution.py:516
  364.7 25.8 %collective-permute-start.41 = (bf16[256,1024]{1,0:T(8,128)(2,1)S(1)}, bf16[256,1024]{1,0:T(8,128)(2,1)S(1)}, u32[]{:S(2)}, u32[]{:S(2)}) collective-permute-start(bf16[256,1024]{1,0:T(8,128)(2,1)S(1)} %add_convert_fusion.2.own), channel_id=1, source_target_pairs={{0,8},{1,9},{2,10},{3,11},{4,12},{5,13},{6,14},{7,15},{8,0},{9,1},... | collective-permute-start | bytes 1572872 | tf_op jit(solution)/shard_map/ppermute | solution.py:516
  390.7 14.4 %collective-permute-start.46 = (bf16[256,1024]{1,0:T(8,128)(2,1)S(1)}, bf16[256,1024]{1,0:T(8,128)(2,1)S(1)}, u32[]{:S(2)}, u32[]{:S(2)}) collective-permute-start(bf16[256,1024]{1,0:T(8,128)(2,1)S(1)} %add_convert_fusion.1), channel_id=1, source_target_pairs={{0,16},{1,17},{2,18},{3,19},{4,20},{5,21},{6,22},{7,23},{8,24},{9,... | collective-permute-start | bytes 1572872 | tf_op jit(solution)/shard_map/ppermute | solution.py:516
  405.2 20.5 %collective-permute-start.47 = (bf16[256,1024]{1,0:T(8,128)(2,1)S(1)}, bf16[256,1024]{1,0:T(8,128)(2,1)S(1)}, u32[]{:S(2)}, u32[]{:S(2)}) collective-permute-start(bf16[256,1024]{1,0:T(8,128)(2,1)S(1)} %add_convert_fusion.own), channel_id=1, source_target_pairs={{0,8},{1,9},{2,10},{3,11},{4,12},{5,13},{6,14},{7,15},{8,0},{9,1},... | collective-permute-start | bytes 1572872 | tf_op jit(solution)/shard_map/ppermute | solution.py:516
  407.7 18.1 %collective-permute-start.45 = (bf16[128,1280]{1,0:T(8,128)(2,1)}, bf16[128,1280]{1,0:T(8,128)(2,1)S(1)}, u32[]{:S(2)}, u32[]{:S(2)}) collective-permute-start(bf16[128,1280]{1,0:T(8,128)(2,1)} %get-tuple-element.472), channel_id=1, source_target_pairs={{0,4},{1,5},{2,6},{3,7},{4,0},{5,1},{6,2},{7,3},{8,12},{9,13},{10,... | collective-permute-start | bytes 983048 | tf_op jit(solution)/shard_map/ppermute | solution.py:516
  425.9 14.2 %collective-permute-start.48 = (bf16[128,1280]{1,0:T(8,128)(2,1)S(1)}, bf16[128,1280]{1,0:T(8,128)(2,1)S(1)}, u32[]{:S(2)}, u32[]{:S(2)}) collective-permute-start(bf16[128,1280]{1,0:T(8,128)(2,1)S(1)} %add_convert_fusion.9), channel_id=1, source_target_pairs={{0,16},{1,17},{2,18},{3,19},{4,20},{5,21},{6,22},{7,23},{8,24},{9,... | collective-permute-start | bytes 983048 | tf_op jit(solution)/shard_map/adam/ppermute | solution.py:516
  440.2 16.1 %collective-permute-start.49 = (bf16[128,1280]{1,0:T(8,128)(2,1)S(1)}, bf16[128,1280]{1,0:T(8,128)(2,1)S(1)}, u32[]{:S(2)}, u32[]{:S(2)}) collective-permute-start(bf16[128,1280]{1,0:T(8,128)(2,1)S(1)} %add_convert_fusion.8.own_b), channel_id=1, source_target_pairs={{0,8},{1,9},{2,10},{3,11},{4,12},{5,13},{6,14},{7,15},{8,0},{9,1},... | collective-permute-start | bytes 983048 | tf_op jit(solution)/shard_map/adam/ppermute | solution.py:516
  (58 other events, 783.4 us)
Sparse Core Ops, SparseCore 0:
  73.9 95.7 all-gather.4
  171.9 48.3 all-gather.6

commit v3 on v2

v3 whole, which is shorter than its diff:
```python
import functools

import jax
import jax.numpy as jnp
from jax import lax
from jax.experimental import pallas as pl
from jax.experimental.pallas import tpu as pltpu
from jax.sharding import PartitionSpec as P

HEAD_DIM = 64
ROT_DIM = 16
STEP = 10
EPS_NORM = 1e-05
BETA_ONE = 0.9
BETA_TWO = 0.999
ADAM_EPS = 1e-08
RATE_MATRIX = 0.05
RATE_VECTOR = 0.2
DECAY_MATRIX = 0.1
ROPE_BASE = 10000.0
INV_ROOT_TWO = 0.7071067811865476
INV_ROOT_TAU = 0.3989422804014327
MASKED = -1e30
LANES = 128
AXES = ("dp", "zero")
F32 = jnp.float32
BF16 = jnp.bfloat16
VMEM_LIMIT = 58 * 1024 * 1024


def spec(block, index, single=False):
    if single:
        return pl.BlockSpec(block, index, pipeline_mode=pl.Buffered(1))
    return pl.BlockSpec(block, index)


def whole(shape):
    return spec(shape, lambda *_: (0,) * len(shape), single=True)


def scalars():
    return pl.BlockSpec(memory_space=pltpu.SMEM)


def kernel_call(body, grid, in_specs, out_specs, out_shape, flops, moved, scratch=(), name=None):
    return pl.pallas_call(
        body,
        grid=grid,
        in_specs=in_specs,
        out_specs=out_specs,
        out_shape=out_shape,
        scratch_shapes=list(scratch),
        cost_estimate=pl.CostEstimate(flops=int(flops), bytes_accessed=int(moved), transcendentals=0),
        compiler_params=pltpu.CompilerParams(
            vmem_limit_bytes=VMEM_LIMIT, dimension_semantics=("arbitrary",) * len(grid)
        ),
        name=name,
    )


def nn(left, right):
    return lax.dot_general(left, right, (((1,), (0,)), ((), ())), preferred_element_type=F32)


def nt(left, right):
    return lax.dot_general(left, right, (((1,), (1,)), ((), ())), preferred_element_type=F32)


def tn(left, right):
    return lax.dot_general(left, right, (((0,), (0,)), ((), ())), preferred_element_type=F32)


def piece_owner(ids, place):
    step = place % 4
    if step > 1:
        step = 2 + ids[2] if step == 2 else 3 - ids[2]
    return jnp.bitwise_xor(ids[0], 2 * step + place // 4)


SLOTS = ((0, 0), (1, 0), (2, 0), (2, 1), (0, 1), (1, 1), (3, 0), (3, 1))


def slot_owner(ids, slot):
    step, side = SLOTS[slot]
    if step > 1:
        step = 2 + ids[2] if step == 2 else 3 - ids[2]
    return jnp.bitwise_xor(ids[0], 2 * step + side)


def slot_ref(outs, slot):
    return (outs[0], slot) if slot < 4 else (outs[1], slot - 4) if slot < 6 else (outs[2], slot - 6)


def low_lanes():
    return lax.broadcasted_iota(jnp.int32, (1, LANES), 1) < HEAD_DIM


def pick_parity(core, tile_a, tile_b):
    low = low_lanes()
    even = jnp.where(low, tile_a, pltpu.roll(tile_b, HEAD_DIM, 1))
    odd = jnp.where(low, pltpu.roll(tile_a, HEAD_DIM, 1), tile_b)
    return jnp.where(core == 0, even, odd)


def prep_attn_body(ids, w_qkv, w_out, out):
    core = ids[1]
    for part in range(3):
        for tile in range(2):
            base = part * 1024 + tile * 256
            at = part * 256 + tile * 128
            out[:, at : at + 128] = pick_parity(
                core, w_qkv[:, base : base + 128], w_qkv[:, base + 128 : base + 256]
            ).astype(BF16)
    rows = w_out[pl.ds(pl.multiple_of(core * 64, 64), 64), :].astype(BF16)
    for panel in range(4):
        at = 768 + 256 * (panel // 2)
        base = (panel % 2) * 64
        out[base : base + 64, at : at + 256] = rows[:, 256 * panel : 256 * panel + 256]


def prep_mlp_body(ids, w_up, w_down, w_qkv, out_a, out_b):
    core = ids[1]
    for part, out in enumerate((out_a, out_b)):
        for owner in range(8):
            start = pl.multiple_of(owner * 512 + part * 256 + core * 128, 128)
            out[0:128, owner * 128 : (owner + 1) * 128] = w_up[:, pl.ds(start, 128)].astype(BF16)
        out[128:256, :] = w_down[pl.ds(pl.multiple_of(part * 256 + core * 128, 128), 128), :].astype(BF16)
    for part in range(3):
        for tile in range(2):
            base = part * 1024 + 512 + tile * 256
            value = pick_parity(core, w_qkv[:, base : base + 128], w_qkv[:, base + 128 : base + 256]).astype(BF16)
            for panel in range(4):
                at = panel * 256 + tile * 128
                out_b[256 + 32 * part : 288 + 32 * part, at : at + 128] = value[32 * panel : 32 * panel + 32]


def join_vec_body(ids, pieces, vec, bias):
    for step in range(8):
        owner = jnp.bitwise_xor(ids[0], 2 * (step & 3) + step // 4)
        vec[:, pl.ds(pl.multiple_of(owner * 128, 128), 128)] = pieces[step].astype(F32)
    for part in range(3):
        for tile in range(4):
            base = tile * 256
            row = slice(4 + part, 5 + part)
            at = (tile // 2) * 768 + part * 256 + (tile % 2) * 128
            bias[:, at : at + 128] = pick_parity(
                ids[1], vec[row, base : base + 128], vec[row, base + 128 : base + 256]
            )


def normalize(inputs):
    centred = inputs - jnp.mean(inputs, axis=-1, keepdims=True)
    variance = jnp.mean(centred * centred, axis=-1, keepdims=True)
    inv_std = lax.rsqrt(variance + EPS_NORM)
    return centred * inv_std, inv_std


def turned(x, cos, sin_lo, sin_hi, sign):
    return x * cos[...] + sign * (pltpu.roll(x, 8, 1) * sin_hi[...] + pltpu.roll(x, 120, 1) * sin_lo[...])


def project(group, rows, w_qkv, bias, tables, outs):
    for part, out in enumerate(outs):
        cols = slice(part * 256, (part + 1) * 256)
        at = group * 768 + part * 256
        acc = nn(rows, w_qkv[:, cols]) + bias[:, at : at + 256]
        if part == 2:
            out[...] = acc.astype(BF16)
            continue
        for tile in range(2):
            x = turned(acc[:, tile * 128 : (tile + 1) * 128], *tables, 1.0)
            if part == 0:
                x = x * HEAD_DIM ** (-0.5)
            out[:, tile * 128 : (tile + 1) * 128] = x.astype(BF16)


def qkv_first_body(steps, ids, *refs):
    pieces, refs = refs[:8], refs[8:]
    tok_own, tok_other, dy_own, dy_other, vec, bias, cos, sin_lo, sin_hi = refs[:9]
    q, k, v, d_att, attn_in, attn_t, mlp_in, w_qkv, w_out = refs[9:]
    step = pl.program_id(0)

    @pl.when(step == 0)
    def _():
        for place, piece in enumerate(pieces):
            owner = piece_owner(ids, place)
            w_qkv[pl.ds(pl.multiple_of(owner * 128, 128), 128), :] = piece[:, 0:768]
            for panel in range(4):
                at = 768 + 256 * (panel // 2)
                base = (panel % 2) * 64
                w_out[pl.ds(pl.multiple_of(owner * 64, 64), 64), 256 * panel : 256 * panel + 256] = piece[
                    base : base + 64, at : at + 256
                ]

    first = step < steps // 2
    d_att[...] = nt(jnp.where(first, dy_own[...], dy_other[...]), w_out[...]).astype(BF16)
    normed, _ = normalize(jnp.where(first, tok_own[...], tok_other[...]).astype(F32))
    rows = (normed * vec[0:1, :] + vec[1:2, :]).astype(BF16)
    mlp_in[...] = (normed * vec[2:3, :] + vec[3:4, :]).astype(BF16)
    attn_in[...] = rows
    attn_t[...] = rows.T
    project(0, rows, w_qkv, bias, (cos, sin_lo, sin_hi), (q, k, v))


def qkv_second_body(ids, *refs):
    pieces, (attn_in, bias, cos, sin_lo, sin_hi, q, k, v, w_qkv) = refs[:8], refs[8:]

    @pl.when(pl.program_id(0) == 0)
    def _():
        for place, piece in enumerate(pieces):
            owner = piece_owner(ids, place)
            for part in range(3):
                for panel in range(4):
                    at = pl.ds(pl.multiple_of(owner * 128 + 32 * panel, 32), 32)
                    w_qkv[at, part * 256 : part * 256 + 256] = piece[
                        256 + 32 * part : 288 + 32 * part, panel * 256 : panel * 256 + 256
                    ]

    project(1, attn_in[...], w_qkv, bias, (cos, sin_lo, sin_hi), (q, k, v))


ATTN_ROWS = 256


def cat(parts, axis=0):
    return jnp.concatenate(parts, axis=axis) if len(parts) > 1 else parts[0]


def attn_body(q, k, v, d_att, seg_col, seg_row, cos, sin_lo, sin_hi, att, grad):
    count = q.shape[0]
    size = ATTN_ROWS
    blocks = count // size
    span = [slice(j * size, (j + 1) * size) for j in range(blocks)]
    low = low_lanes()
    zero = jnp.zeros((), BF16)
    causal = lax.broadcasted_iota(jnp.int32, (size, size), 0) >= lax.broadcasted_iota(
        jnp.int32, (size, size), 1
    )
    q_t, da_t = q[...].T, d_att[...].T

    def row_total(parts, reduce, join):
        cols = [reduce(part, axis=-1, keepdims=True) for part in parts]
        return [
            functools.reduce(join, [cols[j][(i - j) * size : (i - j + 1) * size] for j in range(i + 1)])
            for i in range(blocks)
        ]

    def row_sum(parts):
        return cat(
            [
                functools.reduce(jnp.add, [parts[j][(i - j) * size : (i - j + 1) * size] for j in range(i + 1)])
                for i in range(blocks)
            ]
        )

    def products(half):
        lanes = low if half == 0 else jnp.logical_not(low)
        q_h = jnp.where(lanes, q[...], zero)
        da_h = jnp.where(lanes, d_att[...], zero)
        scores = [nt(q_h[j * size :], k[span[j], :]) for j in range(blocks)]
        return scores, [nt(da_h[j * size :], v[span[j], :]) for j in range(blocks)]

    def softmax_both(scores, grad_probs):
        masked = []
        for j in range(blocks):
            allowed = seg_col[j * size :, :] == seg_row[0, :, span[j]]
            allowed = cat([allowed[:size] & causal] + ([allowed[size:]] if j < blocks - 1 else []))
            masked.append(jnp.where(allowed, scores[j], MASKED))
        top = row_total(masked, jnp.max, jnp.maximum)
        raised = [jnp.exp(masked[j] - cat(top[j:])) for j in range(blocks)]
        inv = [1.0 / total for total in row_total(raised, jnp.sum, jnp.add)]
        probs = [raised[j] * cat(inv[j:]) for j in range(blocks)]
        delta = row_total([g * p for g, p in zip(grad_probs, probs)], jnp.sum, jnp.add)
        grad_scores = [
            (probs[j] * (grad_probs[j] - cat(delta[j:]))).astype(BF16) for j in range(blocks)
        ]
        return [p.astype(BF16) for p in probs], grad_scores

    def results(half, probs, grad_scores):
        rows = slice(half * HEAD_DIM, (half + 1) * HEAD_DIM)
        return (
            row_sum([nn(probs[j], v[span[j], :]) for j in range(blocks)]),
            row_sum([nn(grad_scores[j], k[span[j], :]) for j in range(blocks)]),
            cat([nn(q_t[rows, j * size :], grad_scores[j]) for j in range(blocks)], 1),
            cat([nn(da_t[rows, j * size :], probs[j]) for j in range(blocks)], 1),
        )

    first = softmax_both(*products(0))
    second = products(1)
    out_a, dq_a, dk_a, dv_a = results(0, *first)
    out_b, dq_b, dk_b, dv_b = results(1, *softmax_both(*second))
    tables = (cos, sin_lo, sin_hi)
    att[...] = jnp.where(low, out_a, out_b).astype(BF16)
    grad[0] = turned(jnp.where(low, dq_a, dq_b) * HEAD_DIM ** (-0.5), *tables, -1.0).astype(BF16)
    grad[1] = turned(jnp.concatenate([dk_a, dk_b], axis=0).T, *tables, -1.0).astype(BF16)
    grad[2] = jnp.concatenate([dv_a, dv_b], axis=0).T.astype(BF16)


def attn_weights_body(ids, attn_t, grad_a, grad_b, att_a, att_b, dy_own, dy_other, keep, send_x, send_y, bias, result):
    step = pl.program_id(0)
    outs = (keep, send_x, send_y)

    @pl.when(step < 6)
    def _():
        rhs = jnp.where(step < 3, grad_a[0], grad_b[0])
        result[...] = nn(attn_t[...], rhs).astype(BF16)
        cols = pl.ds(pl.multiple_of(step * 256, 256), 256)
        bias[0:1, cols] = jnp.sum(rhs.astype(F32), axis=0, keepdims=True)
        for slot in range(8):
            out, at = slot_ref(outs, slot)
            base = pl.multiple_of(slot_owner(ids, slot) * 128, 128)
            out[at, :, cols] = result[pl.ds(base, 128), :]

    @pl.when(step == 6)
    def _():
        count = dy_own.shape[0]
        for group, att in enumerate((att_a, att_b)):
            flipped = att[...].T
            for panel in range(4):
                cols = slice(panel * 256, panel * 256 + 256)
                term = nn(flipped[:, :count], dy_own[:, cols]) + nn(flipped[:, count:], dy_other[:, cols])
                result[group * 256 : group * 256 + 256, :] = term.astype(BF16)
                for slot in range(8):
                    out, at = slot_ref(outs, slot)
                    owner = slot_owner(ids, slot)
                    col = 1536 + 256 * (panel // 2)
                    base = (panel % 2) * 64

                    @pl.when(owner // 4 == group)
                    def _():
                        out[at, base : base + 64, col : col + 256] = result[
                            pl.ds(pl.multiple_of(owner * 64, 64), 64), :
                        ]


def mlp_body(part, steps, ids, *refs):
    pieces = refs[:8]
    vec, mlp_in, dy_own, dy_other, keep, send_x, send_y, hidden_out, grad_out, sums, w_up, w_down = refs[8:-6]
    mlp_t, hidden_t, grad_pre, dy, bias, result = refs[-6:]
    outs = (keep, send_x, send_y)
    core = ids[1]
    step = pl.program_id(0)

    @pl.when(step == 0)
    def _():
        for owner in range(8):
            start = pl.multiple_of((owner % 2) * 512 + part * 256 + core * 128, 128)
            row = 8 + owner // 2
            bias[0:1, owner * 128 : (owner + 1) * 128] = vec[row : row + 1, pl.ds(start, 128)]
        sums[...] = jnp.zeros_like(sums)
        for place, piece in enumerate(pieces):
            at = pl.ds(pl.multiple_of(piece_owner(ids, place) * 128, 128), 128)
            w_up[at, :] = piece[0:128, :]
            w_down[at, :] = piece[128:256, :]

    rows = mlp_in[...]
    grads = jnp.where(step < steps // 2, dy_own[...], dy_other[...])
    count = rows.shape[0]
    at = pl.ds(pl.multiple_of(step * count, count), count)
    mlp_t[:, at] = rows.T
    dy[at, :] = grads
    sums[1:2, :] += jnp.sum(grads.astype(F32), axis=0, keepdims=True)
    for col in range(0, 1024, 256):
        cols = slice(col, col + 256)
        pre = nn(rows, w_up[:, cols]) + bias[0:1, cols]
        grad_hidden = nt(grads, w_down[cols, :])
        cdf = 0.5 + 0.5 * lax.erf(pre * INV_ROOT_TWO)
        pdf = jnp.exp(-0.5 * pre * pre) * INV_ROOT_TAU
        act = (pre * cdf).astype(BF16)
        hidden_t[cols, at] = act.T
        hidden_out[:, cols] = act
        gp = (grad_hidden * (cdf + pre * pdf)).astype(BF16)
        grad_pre[at, cols] = gp
        grad_out[:, cols] = gp
        sums[0:1, cols] += jnp.sum(gp.astype(F32), axis=0, keepdims=True)

    @pl.when(step == steps - 1)
    def _():
        for base_row, left, right in ((0, mlp_t, grad_pre), (128, hidden_t, dy)):
            for col in range(0, 1024, 512):
                cols = slice(col, col + 512)
                result[...] = nn(left[...], right[:, cols]).astype(BF16)
                for slot in range(8):
                    out, place = slot_ref(outs, slot)
                    base = pl.multiple_of(slot_owner(ids, slot) * 128, 128)
                    out[place, base_row : base_row + 128, cols] = result[pl.ds(base, 128), :]


def back_body(own, grad_a, grad_b, att_a, att_b, hid_a, hid_b, gp_a, gp_b, wq_a, wq_b, w_out, up_a, up_b, down_a, down_b, tok, vec, *refs):
    if own:
        dy, out_other, scaled_other, out, result, sums = refs
    else:
        out, result, sums = refs
    inputs = tok[...].astype(F32)
    normed, inv_std = normalize(inputs)
    branch = nn(att_a[...], w_out[0:256, :]) + nn(att_b[...], w_out[256:512, :])
    back_mlp = None
    for hid, gp, up, down in ((hid_a, gp_a, up_a, down_a), (hid_b, gp_b, up_b, down_b)):
        branch = branch + nn(hid[...], down[...])
        term = nt(gp[...], up[...])
        back_mlp = term if back_mlp is None else back_mlp + term
    back_attn = None
    for grad, w in ((grad_a, wq_a), (grad_b, wq_b)):
        for part in range(3):
            term = nt(grad[part], w[:, part * 256 : part * 256 + 256])
            back_attn = term if back_attn is None else back_attn + term
    scaled = back_attn * vec[0:1, :] + back_mlp * vec[2:3, :]

    @pl.when(pl.program_id(0) == 0)
    def _():
        sums[...] = jnp.zeros_like(sums)

    for row, value in enumerate((back_attn * normed, back_attn, back_mlp * normed, back_mlp)):
        sums[row : row + 1, :] += jnp.sum(value, axis=0, keepdims=True)
    if not own:
        out[...] = branch.astype(BF16)
        result[...] = scaled.astype(BF16)
        return
    branch = branch + out_other[...].astype(F32)
    out[...] = (inputs + branch + (vec[7:8, :] + vec[12:13, :])).astype(BF16)
    scaled = scaled + scaled_other[...].astype(F32)
    result[...] = dy[...].astype(F32) + inv_std * (
        scaled
        - jnp.mean(scaled, axis=-1, keepdims=True)
        - normed * jnp.mean(scaled * normed, axis=-1, keepdims=True)
    )


def adam_math(weight, first, second, gradient, rate, decay):
    first_new = BETA_ONE * first + (1.0 - BETA_ONE) * gradient
    second_new = BETA_TWO * second + (1.0 - BETA_TWO) * gradient * gradient
    first_hat = first_new / (1.0 - BETA_ONE**STEP)
    second_hat = second_new / (1.0 - BETA_TWO**STEP)
    weight_new = weight - rate * (first_hat / (jnp.sqrt(second_hat) + ADAM_EPS) + decay * weight)
    return (first_new, second_new, weight_new)


def adam_store(refs, at, gradient):
    w, m, v, m_out, v_out, w_out = refs
    first, second, weight = adam_math(w[at], m[at], v[at], gradient, RATE_MATRIX, DECAY_MATRIX)
    m_out[at] = first
    v_out[at] = second
    w_out[at] = weight


def parities(core, own, other):
    return jnp.where(core == 0, own, other), jnp.where(core == 0, other, own)


def adam_attn_body(ids, own, other, *refs):
    core = ids[1]
    low = low_lanes()
    qkv_refs = refs[0:3] + refs[6:9]
    for tile in range(4):
        start = (tile // 2) * 768 + (tile % 2) * 128
        cols = pl.ds(pl.multiple_of(pl.program_id(0) * 256 + start, 128), 128)
        even, odd = parities(core, own[:, cols].astype(F32), other[:, cols].astype(F32))
        first = jnp.where(low, even, pltpu.roll(odd, HEAD_DIM, 1))
        second = jnp.where(low, pltpu.roll(even, HEAD_DIM, 1), odd)
        adam_store(qkv_refs, (slice(None), slice(tile * 256, tile * 256 + 128)), first)
        adam_store(qkv_refs, (slice(None), slice(tile * 256 + 128, tile * 256 + 256)), second)

    @pl.when(pl.program_id(0) == 0)
    def _():
        out_refs = refs[3:6] + refs[9:12]
        for panel in range(4):
            rows = slice((panel % 2) * 64, (panel % 2) * 64 + 64)
            cols = slice(1536 + 256 * (panel // 2), 1792 + 256 * (panel // 2))
            span = slice(panel * 256, panel * 256 + 256)
            even, odd = parities(core, own[rows, cols].astype(F32), other[rows, cols].astype(F32))
            adam_store(out_refs, (slice(0, 64), span), even)
            adam_store(out_refs, (slice(64, 128), span), odd)


def adam_mlp_body(ids, own, other, *refs):
    core = ids[1]
    up_refs = refs[0:3] + refs[-6:-3]
    down_refs = refs[3:6] + refs[-3:]
    cols = pl.ds(pl.multiple_of(pl.program_id(0) * 128, 128), 128)
    for base, refs_of in ((0, up_refs), (128, down_refs)):
        rows = slice(base, base + 128)
        for parity, grad in enumerate(
            parities(core, own[rows, cols].astype(F32), other[rows, cols].astype(F32))
        ):
            span = slice(parity * 128, (parity + 1) * 128)
            adam_store(refs_of, (slice(None), span) if base == 0 else (span, slice(None)), grad)


def rotary_tables(segments):
    row_count = segments.shape[0]
    row_index = jnp.arange(row_count, dtype=jnp.int32)
    earlier = jnp.concatenate([jnp.full((1,), -1, jnp.int32), segments[:-1]])
    starts = jnp.where(segments != earlier, row_index, 0)
    position = (row_index - lax.cummax(starts, axis=0)).astype(F32)
    half_dim = ROT_DIM // 2
    dims = jnp.arange(LANES, dtype=jnp.int32) % HEAD_DIM
    frequency = ROPE_BASE ** (-2.0 * (dims % half_dim).astype(F32) / ROT_DIM)
    turned = dims < ROT_DIM
    angles = position[:, None] * jnp.where(turned, frequency, 0.0)[None, :]
    cosine, sine = jnp.cos(angles), jnp.sin(angles)
    front = (dims < half_dim)[None, :]
    return cosine, jnp.where(front, -sine, 0.0), jnp.where(front, 0.0, sine)


def on_device(
    sizes,
    tokens,
    segments,
    cotangent,
    w_qkv,
    w_out,
    w_up,
    w_down,
    vectors,
    m_qkv,
    m_out,
    m_up,
    m_down,
    m_vectors,
    v_qkv,
    v_out,
    v_up,
    v_down,
    v_vectors,
):
    copies, owners = sizes
    me = lax.axis_index("zero")
    plane = lax.axis_index("dp")
    core = plane % 2
    ids = jnp.stack([me, core, (plane // 2) % 2]).astype(jnp.int32)

    def move(value, target):
        pairs = []
        for d in range(copies):
            for z in range(owners):
                to_d, to_z = target(d, z)
                pairs.append((d * owners + z, to_d * owners + to_z))
        return lax.ppermute(value, AXES, pairs)

    def swap(value, dp_bits, zero_bits):
        return move(value, lambda d, z: (d ^ dp_bits, z ^ zero_bits))

    def swap_far(value):
        return move(value, lambda d, z: (d, z ^ (6 if d & 2 else 4)))

    def sync(*values):
        return lax.optimization_barrier(values)

    def add(*terms):
        return functools.reduce(jnp.add, [t.astype(F32) for t in terms])

    def reduce_first(keep, send_x, send_y):
        return keep, swap(send_x, 0, 1), swap(send_y, 2, 0)

    def reduce_second(state):
        keep, got_x, got_y = state
        far = add(keep[3], got_y[1]).astype(BF16)
        near = add(keep[1], got_x[1]).astype(BF16)
        return keep, got_x, got_y, far, near, swap(far, 0, 1), swap(near, 0, 2)

    def reduce_third(state):
        keep, got_x, got_y, _, _, got_far, got_near = state
        far = add(keep[2], got_y[0], got_far).astype(BF16)
        return add(keep[0], got_x[0], got_near), far, swap_far(far)

    def reduce_fourth(state):
        total = (state[0] + state[2].astype(F32)).astype(BF16)
        return total, swap(total, 2, 0)

    def reduce_fifth(state):
        total = add(*state).astype(BF16)
        bit = 4
        while bit < copies:
            total = add(total, swap(total, bit, 0)).astype(BF16)
            bit *= 2
        return total, swap(total, 1, 0)

    T, width = tokens.shape
    rows = 2 * T
    sds = jax.ShapeDtypeStruct
    row_block = lambda n, c=width: spec((n, c), lambda i: (i, 0))
    col_block = lambda n: spec((width, n), lambda i: (0, i))

    def block_call(body, grid, ins, outs, flops, moved, scratch=(), name=None):
        return kernel_call(
            body,
            grid,
            [place for _, place in ins],
            [place for _, place in outs],
            [shape for shape, _ in outs],
            flops,
            moved,
            scratch=scratch,
            name=name,
        )(*[value for value, _ in ins])

    def const(value):
        return value, whole(value.shape)

    def kept(shape, dtype):
        return sds(shape, dtype), whole(shape)

    steps = rows // 256
    with jax.named_scope("prep"):
        own_a = block_call(
            prep_attn_body,
            (1,),
            [(ids, scalars()), const(w_qkv), const(w_out)],
            [kept((128, 1280), BF16)],
            0,
            3e6,
            name="prep_attn",
        )[0]
        own_b, own_c = block_call(
            prep_mlp_body,
            (1,),
            [(ids, scalars()), const(w_up), const(w_down), const(w_qkv)],
            [kept((256, 1024), BF16), kept((352, 1024), BF16)],
            0,
            6e6,
            name="prep_mlp",
        )

    def z_moves(own):
        return swap(own, 0, 2), swap_far(own)

    with jax.named_scope("gather"):
        next_a, far_a = z_moves(own_a)
        across_a = swap(own_a, 0, 1)
        seg_other = swap(segments, 1, 0)
        vec_pieces = jnp.pad(vectors, ((0, 3), (0, 0))).astype(BF16)[None]
        next_a, far_a, across_a, own_b, own_c, seg_other, vec_pieces = sync(
            next_a, far_a, across_a, own_b, own_c, seg_other, vec_pieces
        )
        next_across_a, far_across_a, rest_a = swap(next_a, 0, 1), swap(far_a, 0, 1), swap(far_a, 2, 0)
        next_b, far_b = z_moves(own_b)
        tok_other = swap(tokens, 1, 0)
        dy_other = swap(cotangent, 1, 0)
        for bits in (2, 4):
            vec_pieces = jnp.concatenate([vec_pieces, swap(vec_pieces, 0, bits)], axis=0)

    with jax.named_scope("rows"):
        tables = [
            jnp.concatenate(pair, axis=0)
            for pair in zip(rotary_tables(segments), rotary_tables(seg_other))
        ]
        seg_row = jnp.stack([segments, seg_other])[:, None, :]
        seg_col = jnp.concatenate([segments, seg_other])[:, None]

    (next_across_a, far_across_a, rest_a, next_b, far_b, own_c, tables, seg_row, seg_col, tok_other, dy_other) = sync(
        next_across_a, far_across_a, rest_a, next_b, far_b, own_c, tables, seg_row, seg_col, tok_other, dy_other
    )
    with jax.named_scope("gather"):
        vec_pieces = jnp.concatenate([vec_pieces, swap(vec_pieces, 0, 1)], axis=0)
        rest_across_a = swap(far_across_a, 2, 0)
        far_across_b, next_across_b, rest_b = swap(far_b, 0, 1), swap(next_b, 0, 1), swap(far_b, 2, 0)
        next_c, far_c = z_moves(own_c)
        vec, bias_qkv = block_call(
            join_vec_body,
            (1,),
            [(ids, scalars()), const(vec_pieces)],
            [kept((16, 1024), F32), kept((1, 1536), F32)],
            0,
            1e5,
            name="join_vec",
        )
    attn_pieces = [own_a, next_a, far_a, rest_a, across_a, next_across_a, far_across_a, rest_across_a]

    def table_blocks(count):
        return [(t, row_block(count, 128)) for t in tables]

    def halves(own, other, count):
        last = T // count - 1
        return [
            (own, spec((count, width), lambda i: (jnp.minimum(i, last), 0))),
            (other, spec((count, width), lambda i: (jnp.maximum(i - last - 1, 0), 0))),
        ]

    def attention(group, projected, d_att):
        with jax.named_scope("attention"):
            head_block = spec((T, 128), lambda h, m: (h, m))
            return block_call(
                attn_body,
                (2, 2),
                [(value, head_block) for value in projected]
                + [(d_att, spec((T, 128), lambda h, m: (h, m + 2 * group)))]
                + [(seg_col, spec((T, 1), lambda h, m: (h, 0)))]
                + [(seg_row, spec((1, 1, T), lambda h, m: (h, 0, 0)))]
                + [(t, spec((T, 128), lambda h, m: (h, 0))) for t in tables],
                [
                    (sds((rows, 256), BF16), head_block),
                    (sds((3, rows, 256), BF16), spec((3, T, 128), lambda h, m: (0, h, m))),
                ],
                30e9,
                10e6,
                name="attention",
            )

    def blocks_of(shape):
        return [kept((n,) + shape, BF16) for n in (4, 2, 2)]

    with jax.named_scope("qkv"):
        *projected, d_att, attn_in, attn_t, mlp_in, wq_a, full_out = block_call(
            functools.partial(qkv_first_body, rows // 256),
            (rows // 256,),
            [(ids, scalars())]
            + [const(piece) for piece in attn_pieces]
            + halves(tokens, tok_other, 256)
            + halves(cotangent, dy_other, 256)
            + [const(vec), const(bias_qkv)]
            + table_blocks(256),
            [(sds((rows, 256), BF16), row_block(256, 256))] * 3
            + [(sds((rows, 512), BF16), row_block(256, 512)), (sds((rows, width), BF16), row_block(256))]
            + [(sds((width, rows), BF16), col_block(256)), (sds((rows, width), BF16), row_block(256))]
            + [kept((1024, 768), BF16), kept((512, 1024), BF16)],
            2 * rows * 1024 * 1280,
            30e6,
            name="qkv",
        )
    projected, far_across_b, next_across_b, rest_b, own_b, next_c, far_c = sync(
        projected, far_across_b, next_across_b, rest_b, own_b, next_c, far_c
    )
    with jax.named_scope("gather"):
        rest_across_b, across_b = swap(far_across_b, 2, 0), swap(own_b, 0, 1)
        far_across_c, rest_c = swap(far_c, 0, 1), swap(far_c, 2, 0)
    att_a, grad_a = attention(0, projected, d_att)
    att_a, grad_a, rest_across_b, across_b, far_across_c, rest_c, own_c, next_c, attn_t, mlp_in = sync(
        att_a, grad_a, rest_across_b, across_b, far_across_c, rest_c, own_c, next_c, attn_t, mlp_in
    )
    with jax.named_scope("gather"):
        across_c, next_across_c, rest_across_c = swap(own_c, 0, 1), swap(next_c, 0, 1), swap(far_across_c, 2, 0)
    pieces_b = [own_b, next_b, far_b, rest_b, across_b, next_across_b, far_across_b, rest_across_b]

    def mlp(part, weights, rows_in):
        with jax.named_scope("mlp"):
            *results, hid, gp, sums, w_up_full, w_down_full = block_call(
                functools.partial(mlp_body, part, steps),
                (steps,),
                [(ids, scalars())]
                + [const(w) for w in weights]
                + [const(vec), (rows_in, row_block(256))]
                + halves(cotangent, dy_other, 256),
                blocks_of((256, 1024))
                + [(sds((rows, width), BF16), row_block(256))] * 2
                + [kept((8, 1024), F32)]
                + [kept((1024, 1024), BF16)] * 2,
                2 * rows * 1024 * 1024 * 4,
                40e6,
                scratch=[
                    pltpu.VMEM((1024, rows), BF16),
                    pltpu.VMEM((1024, rows), BF16),
                    pltpu.VMEM((rows, 1024), BF16),
                    pltpu.VMEM((rows, 1024), BF16),
                    pltpu.VMEM((8, 1024), F32),
                    pltpu.VMEM((1024, 512), BF16),
                ],
                name="mlp",
            )
            return results, hid, gp, sums, w_up_full, w_down_full

    mlp_a = mlp(0, pieces_b, mlp_in)
    mlp_a, mlp_in, across_c, next_across_c, rest_across_c = sync(
        mlp_a, mlp_in, across_c, next_across_c, rest_across_c
    )
    pieces_c = [own_c, next_c, far_c, rest_c, across_c, next_across_c, far_across_c, rest_across_c]
    reduce_a = reduce_first(*mlp_a[0])
    mlp_b = mlp(1, pieces_c, mlp_in)
    mlp_b, reduce_a, attn_in = sync(mlp_b, reduce_a, attn_in)
    reduce_a = reduce_second(reduce_a)
    reduce_b = reduce_first(*mlp_b[0])
    attn_in, *ready = sync(attn_in, *reduce_a[3:5])

    with jax.named_scope("qkv"):
        *projected, wq_b = block_call(
            qkv_second_body,
            (rows // 512,),
            [(ids, scalars())]
            + [const(piece) for piece in pieces_c]
            + [(attn_in, row_block(512)), const(bias_qkv)]
            + table_blocks(512),
            [(sds((rows, 256), BF16), row_block(512, 256))] * 3 + [kept((1024, 768), BF16)],
            2 * rows * 1024 * 768,
            12e6,
            name="qkv",
        )
    att_b, grad_b = attention(1, projected, d_att)
    att_b, grad_b, reduce_a, reduce_b = sync(att_b, grad_b, reduce_a, reduce_b)
    reduce_a = reduce_third(reduce_a)
    reduce_b = reduce_second(reduce_b)
    grad_b, *ready = sync(grad_b, reduce_a[1], *reduce_b[3:5])
    with jax.named_scope("attn_weights"):
        *blocks, bias_sum = block_call(
            attn_weights_body,
            (7,),
            [(ids, scalars()), const(attn_t)]
            + [(grad_a, spec((1, rows, 256), lambda n: (jnp.minimum(n, 2), 0, 0)))]
            + [(grad_b, spec((1, rows, 256), lambda n: (jnp.clip(n - 3, 0, 2), 0, 0)))]
            + [const(value) for value in (att_a, att_b, cotangent, dy_other)],
            blocks_of((128, 2048)) + [kept((8, 1536), F32)],
            2 * rows * 1024 * 2048,
            24e6,
            scratch=[pltpu.VMEM((1024, 256), BF16)],
            name="attn_weights",
        )
    blocks, grad_b = sync(blocks, grad_b)
    reduce_o = reduce_first(*blocks)

    _, hid_a, gp_a, sums_a, up_a, down_a = mlp_a
    _, hid_b, gp_b, sums_b, up_b, down_b = mlp_b

    def adam_mlp(part, totals, previous):
        wide = [spec((128, 256), lambda n: (0, 2 * n + part))] * 3
        wide += [spec((256, 128), lambda n: (part, n))] * 3
        return pl.pallas_call(
            adam_mlp_body,
            grid=(8,),
            in_specs=[scalars()]
            + [whole((256, 1024))] * 2
            + wide
            + [pl.BlockSpec(memory_space=pl.ANY)] * len(previous),
            out_specs=wide,
            out_shape=[sds((128, 4096), F32)] * 3 + [sds((512, 1024), F32)] * 3,
            input_output_aliases={9 + n: n for n in range(len(previous))},
            cost_estimate=pl.CostEstimate(flops=0, bytes_accessed=14000000, transcendentals=0),
            compiler_params=pltpu.CompilerParams(
                vmem_limit_bytes=VMEM_LIMIT, dimension_semantics=("arbitrary",)
            ),
            name="adam_mlp",
        )(ids, *totals, w_up, m_up, v_up, w_down, m_down, v_down, *previous)

    def back(own, grad, rows_tok, extra, outs):
        first = 0 if own else T // 256
        block = lambda c=width: spec((256, c), lambda i: (i + first, 0))
        lead = spec((3, 256, 256), lambda i: (0, i + first, 0))
        with jax.named_scope("back"):
            return block_call(
                functools.partial(back_body, own),
                (T // 256,),
                [(grad_a, lead), (grad, lead), (att_a, block(256)), (att_b, block(256))]
                + [(value, block()) for value in (hid_a, hid_b, gp_a, gp_b)]
                + [const(w) for w in (wq_a, wq_b, full_out, up_a, up_b, down_a, down_b)]
                + [(rows_tok, row_block(256)), const(vec)]
                + [(value, row_block(256)) for value in extra],
                [(sds((T, width), t), row_block(256)) for t in outs] + [kept((8, width), F32)],
                2 * T * 1024 * 6144,
                40e6,
                name="back",
            )

    reduce_a = reduce_fourth(reduce_a)
    reduce_b = reduce_third(reduce_b)
    out_part, scaled_part, sums_other = back(False, grad_b, tok_other, [], (BF16, BF16))
    out_part, scaled_part, sums_other, grad_b, reduce_a, reduce_b, reduce_o = sync(
        out_part, scaled_part, sums_other, grad_b, reduce_a, reduce_b, reduce_o
    )
    reduce_a = reduce_fifth(reduce_a)
    reduce_o = reduce_second(reduce_o)
    reduce_b = reduce_fourth(reduce_b)
    out_got, scaled_got = swap(out_part, 1, 0), swap(scaled_part, 1, 0)
    updated_mlp = adam_mlp(0, reduce_a, [])
    updated_mlp, grad_b, reduce_b, reduce_o, out_got, scaled_got = sync(
        updated_mlp, grad_b, reduce_b, reduce_o, out_got, scaled_got
    )
    reduce_o = reduce_third(reduce_o)
    reduce_b = reduce_fifth(reduce_b)
    grad_b, *ready = sync(grad_b, reduce_o[1], reduce_b[0])
    layer_out, tokens_grad, sums_own = back(
        True, grad_b, tokens, [cotangent, out_got, scaled_got], (BF16, F32)
    )
    sums_own, updated_mlp, reduce_b, reduce_o = sync(sums_own, updated_mlp, reduce_b, reduce_o)
    reduce_o = reduce_fourth(reduce_o)

    with jax.named_scope("vectors"):
        is_core = jnp.arange(2) == core
        grad_bias = jnp.where(core == 0, sums_a[1:2], 0.0)
        bias_sum = jnp.swapaxes(bias_sum[0].reshape(2, 3, 256), 0, 1)
        grad_bias_qkv = jnp.where(
            is_core[None, None, :, None], bias_sum.reshape(3, 8, 1, 64), 0.0
        ).reshape(3, width)
        grad_bias_up = jnp.where(
            is_core[None, None, :, None],
            jnp.swapaxes(jnp.stack([sums_a[0], sums_b[0]]).reshape(2, 8, 128), 0, 1)[:, :, None],
            0.0,
        ).reshape(4, width)
        total = jnp.concatenate(
            [
                sums_own[0:4] + sums_other[0:4],
                grad_bias_qkv,
                grad_bias,
                grad_bias_up,
                grad_bias,
                jnp.zeros((3, width), F32),
            ],
            axis=0,
        )
        for step in (2, 4):
            total = total + swap(total, 0, step)
        across, beside, both = swap(total, 0, 1), swap(total, 2, 0), swap(total, 2, 1)
        total = (total + across) + (beside + both)
        bit = 4
        while bit < copies:
            total = total + swap(total, bit, 0)
            bit *= 2
        total = total + swap(total, 1, 0)
        share = lax.dynamic_slice_in_dim(total[0:13], me * 128, 128, 1)
        first_vectors, second_vectors, new_vectors = adam_math(
            vectors, m_vectors, v_vectors, share, RATE_VECTOR, 0.0
        )

    updated_mlp = adam_mlp(1, reduce_b, updated_mlp)
    updated_mlp, reduce_o = sync(updated_mlp, reduce_o)
    reduce_o = reduce_fifth(reduce_o)
    with jax.named_scope("adam"):
        wide = [spec((128, 1024), lambda n: (0, n))] * 3 + [whole((128, 1024))] * 3
        updated_attn = kernel_call(
            adam_attn_body,
            (3,),
            [scalars()] + [whole((128, 2048))] * 2 + wide,
            wide,
            [sds((128, 3072), F32)] * 3 + [sds((128, 1024), F32)] * 3,
            0,
            13e6,
            name="adam_attn",
        )(ids, *reduce_o, w_qkv, m_qkv, v_qkv, w_out, m_out, v_out)
    first_qkv, second_qkv, new_qkv, first_out, second_out, new_out = updated_attn
    first_up, second_up, new_up, first_down, second_down, new_down = updated_mlp
    return (
        layer_out,
        tokens_grad,
        first_qkv,
        first_out,
        first_up,
        first_down,
        first_vectors,
        second_qkv,
        second_out,
        second_up,
        second_down,
        second_vectors,
        new_qkv,
        new_out,
        new_up,
        new_down,
        new_vectors,
    )


def solution(mesh):
    rows, owned, spread = P(AXES, None), P("zero", None), P(None, "zero")
    state = (owned, owned, owned, owned, spread)
    return jax.shard_map(
        functools.partial(on_device, (mesh.shape["dp"], mesh.shape["zero"])),
        mesh=mesh,
        in_specs=(rows, P(AXES), rows) + state * 3,
        out_specs=(rows, rows) + state * 3,
        check_vma=False,
    )
```

time: 478 us -> 401 us (0.84)
  Pallas kernels: 273 us -> 247 us
  waiting for transfers between devices: 75.4 us -> 52.5 us
  between operations: 15.2 us -> 1.79 us
  starting transfers between devices: 61.7 us -> 54.2 us
  other arithmetic: 32.5 us -> 26.9 us
    pallas_call x14 -> x12, Pallas kernels: 247 us -> 221 us  [block_call(): kernel_call(body, grid, [place for _, place in ins], [place for _, place...]
    ppermute x55 -> x56, waiting for transfers between devices: 73.3 us -> 52.5 us  [move(): return lax.ppermute(value, AXES, pairs)]
    ppermute x55 -> x56, starting transfers between devices: 61.4 us -> 54.2 us  [move(): return lax.ppermute(value, AXES, pairs)]
  transfers between devices with their start and end apart: 57 -> 56, of which waited for: 16 -> 15; matrix products, arithmetic and copies ran while one was open for 9% -> 7% of each run, Pallas kernels for 56% -> 60%
where the time goes in v3:
time: 401 us; the launch traced here: 394 us
  Pallas kernels  247 us (62%)
  starting transfers between devices  54.2 us (14%)
  waiting for transfers between devices  52.5 us (13%)
  other arithmetic  26.9 us (7%)
  local copies, waits for them, and re-layouts  11.7 us (3%)
    pallas_call x12, Pallas kernels, block_call(): kernel_call(body, grid, [place for _, place in ins], [place for _, place...  221 us
    ppermute x56, starting transfers between devices, move(): return lax.ppermute(value, AXES, pairs)  54.2 us
    ppermute x56, waiting for transfers between devices, move(): return lax.ppermute(value, AXES, pairs)  52.5 us
    pallas_call x2, Pallas kernels, adam_mlp(): pl.pallas_call(adam_mlp_body, grid=(8,), in_specs=[scalars()] + [whole((2...  18.2 us
    pallas_call x1, Pallas kernels, on_device(): kernel_call(adam_attn_body, (3,), [scalars()] + [whole((128, 2048))] * 2...  8.1 us
  transfers between devices with their start and end apart: 56, of which 15 were waited for; matrix products, arithmetic and copies ran while one was open for 7% of the time, Pallas kernels for 60%

profile of v3, /device:TPU:0, one launch (start us, length us, event | category | flops | bytes accessed | tf_op | source)
XLA Modules:
  0.0 394.2 jit_solution(13941282529637823860)
XLA Ops:
  1.3 2.4 prep_attn.1.refs_0_
  3.7 2.9 collective-permute-start.2
  6.7 2.6 collective-permute-start.1
  10.4 4.0 %prep_mlp.1 = (bf16[256,1024]{1,0:T(8,128)(2,1)}, bf16[352,1024]{1,0:T(8,128)(2,1)}) custom-call(s32[3]{0:T(128)} %pad_add_fusion.4.ids, f32[128,4096]{1,0:T(8,128)} %refs_0_.6, f32[512,1024]{1,0:T(8,128)} %refs_3_.4, f32[128,3072]{1,0:T(8,128)} %refs_0_.7), custom_call_target="tpu_custom_call" | custom-call | bytes 6000000 | tf_op jit(solution)/shard_map/prep/prep_mlp/pallas_call | solution.py:585
  14.4 1.6 collective-permute-start
  16.2 7.9 %collective-permute-done.1.refs_2_ = bf16[128,1280]{1,0:T(8,128)(2,1)S(1)} collective-permute-done((bf16[128,1280]{1,0:T(8,128)(2,1)}, bf16[128,1280]{1,0:T(8,128)(2,1)S(1)}, u32[]{:S(2)}, u32[]{:S(2)}) %collective-permute-start.1) | collective-permute-done | bytes 327712 | tf_op jit(solution)/shard_map/gather/ppermute | solution.py:538
  24.1 6.4 %collective-permute-done.refs_1_ = bf16[128,1280]{1,0:T(8,128)(2,1)S(1)} collective-permute-done((bf16[128,1280]{1,0:T(8,128)(2,1)S(1)}, bf16[128,1280]{1,0:T(8,128)(2,1)S(1)}, u32[]{:S(2)}, u32[]{:S(2)}) %collective-permute-start) | collective-permute-done | bytes 327712 | tf_op jit(solution)/shard_map/gather/ppermute | solution.py:538
  31.0 2.5 collective-permute-start.7
  34.7 3.8 fusion.5
  38.5 4.3 %collective-permute-done.4.refs_5_ = bf16[128,1280]{1,0:T(8,128)(2,1)S(1)} collective-permute-done((bf16[128,1280]{1,0:T(8,128)(2,1)S(1)}, bf16[128,1280]{1,0:T(8,128)(2,1)S(1)}, u32[]{:S(2)}, u32[]{:S(2)}) %collective-permute-start.4) | collective-permute-done | bytes 327712 | tf_op jit(solution)/shard_map/gather/ppermute | solution.py:538
  44.6 6.2 %collective-permute-done.6.refs_3_ = bf16[128,1280]{1,0:T(8,128)(2,1)S(1)} collective-permute-done((bf16[128,1280]{1,0:T(8,128)(2,1)S(1)}, bf16[128,1280]{1,0:T(8,128)(2,1)S(1)}, u32[]{:S(2)}, u32[]{:S(2)}) %collective-permute-start.6) | collective-permute-done | bytes 327712 | tf_op jit(solution)/shard_map/gather/ppermute | solution.py:538
  51.9 1.5 pad_maximum_fusion
  53.4 4.5 %collective-permute-done.5.refs_6_ = bf16[128,1280]{1,0:T(8,128)(2,1)S(1)} collective-permute-done((bf16[128,1280]{1,0:T(8,128)(2,1)S(1)}, bf16[128,1280]{1,0:T(8,128)(2,1)S(1)}, u32[]{:S(2)}, u32[]{:S(2)}) %collective-permute-start.5) | collective-permute-done | bytes 327712 | tf_op jit(solution)/shard_map/gather/ppermute | solution.py:538
  59.4 2.8 collective-permute-done.12
  63.4 1.7 collective-permute-start.19
  66.0 9.3 %collective-permute-done.13 = bf16[2,16,128]{2,1,0:T(8,128)(2,1)S(1)} collective-permute-done((bf16[2,16,128]{2,1,0:T(8,128)(2,1)S(1)}, bf16[2,16,128]{2,1,0:T(8,128)(2,1)S(1)}, u32[]{:S(2)}, u32[]{:S(2)}) %collective-permute-start.13) | collective-permute-done | bytes 8224 | tf_op jit(solution)/shard_map/gather/ppermute | solution.py:538
  77.2 2.0 collective-permute-done.14
  80.7 1.4 collective-permute-start.16
  82.7 1.5 join_vec.1
  85.5 17.8 %qkv.2 = (bf16[2048,256]{1,0:T(8,128)(2,1)}, bf16[2048,256]{1,0:T(8,128)(2,1)}, bf16[2048,256]{1,0:T(8,128)(2,1)}, bf16[2048,512]{1,0:T(8,128)(2,1)}, bf16[2048,...) custom-call(s32[3]{0:T(128)} %pad_add_fusion.4.ids, ...), custom_call_target="tpu_custom_call" | custom-call | flops 5368709120 | bytes 30000000 | tf_op jit(solution)/shard_map/qkv/qkv/pallas_call | solution.py:585
  107.5 27.6 %attention.2 = (bf16[2048,256]{1,0:T(8,128)(2,1)}, bf16[3,2048,256]{2,1,0:T(8,128)(2,1)}) custom-call(bf16[2048,256]{1,0:T(8,128)(2,1)} %get-tuple-element.233.q, bf16[2048,256]{1,0:T(8,128)(2,1)} %get-tuple-element.234.k, bf16[2048,256]{1,0:T(8,128)(2,1)} %get-tuple-element.235.v, bf16[2048,512]{1,0:T(8,128)(2,1)} %get-tuple-element.236.d_att, ...), custom_call_target="tpu_custom_call" | custom-call | flops 30000001024 | bytes 10000000 | tf_op jit(solution)/shard_map/attention/attention/pallas_call | solution.py:585
  139.3 29.7 %mlp.2 = (bf16[4,256,1024]{2,1,0:T(8,128)(2,1)}, bf16[2,256,1024]{2,1,0:T(8,128)(2,1)}, bf16[2,256,1024]{2,1,0:T(8,128)(2,1)}, bf16[2048,1024]{1,0:T(8,128)(2,1)...) custom-call(s32[3]{0:T(128)} %pad_add_fusion.4.ids, ...), custom_call_target="tpu_custom_call" | custom-call | flops 17179869184 | bytes 40000000 | tf_op jit(solution)/shard_map/mlp/mlp/pallas_call | solution.py:585
  171.7 30.4 %mlp.3 = (bf16[4,256,1024]{2,1,0:T(8,128)(2,1)}, bf16[2,256,1024]{2,1,0:T(8,128)(2,1)}, bf16[2,256,1024]{2,1,0:T(8,128)(2,1)}, bf16[2048,1024]{1,0:T(8,128)(2,1)...) custom-call(s32[3]{0:T(128)} %pad_add_fusion.4.ids, ...), custom_call_target="tpu_custom_call" | custom-call | flops 17179869184 | bytes 40000000 | tf_op jit(solution)/shard_map/mlp/mlp/pallas_call | solution.py:585
  202.1 1.4 fusion.12
  204.9 9.6 %qkv.3 = (bf16[2048,256]{1,0:T(8,128)(2,1)}, bf16[2048,256]{1,0:T(8,128)(2,1)}, bf16[2048,256]{1,0:T(8,128)(2,1)}, bf16[1024,768]{1,0:T(8,128)(2,1)}) custom-call(s32[3]{0:T(128)} %pad_add_fusion.4.ids, bf16[352,1024]{1,0:T(8,128)(2,1)} %get-tuple-element.249.refs_0_, bf16[352,1024]{1,0:T(8,128)(2,1)} %copy-done.16, bf16[352,1024]{1,0:T(8,128)(2,1)} %copy-done.15, ...), custom_call_target="tpu_custom_call" | custom-call | flops 3221225472 | bytes 12000000 | tf_op jit(solution)/shard_map/qkv/qkv/pallas_call | solution.py:585
  216.5 27.8 %attention.3 = (bf16[2048,256]{1,0:T(8,128)(2,1)}, bf16[3,2048,256]{2,1,0:T(8,128)(2,1)}) custom-call(bf16[2048,256]{1,0:T(8,128)(2,1)} %get-tuple-element.287.q, bf16[2048,256]{1,0:T(8,128)(2,1)} %get-tuple-element.288.k, bf16[2048,256]{1,0:T(8,128)(2,1)} %get-tuple-element.289.v, bf16[2048,512]{1,0:T(8,128)(2,1)} %get-tuple-element.236.d_att, ...), custom_call_target="tpu_custom_call" | custom-call | flops 30000001024 | bytes 10000000 | tf_op jit(solution)/shard_map/attention/attention/pallas_call | solution.py:585
  244.3 3.1 fusion.4
  247.4 2.4 collective-permute-start.33
  249.8 1.4 fusion.14
  251.2 1.6 collective-permute-start.36
  252.8 21.6 %attn_weights.1 = (bf16[4,128,2048]{2,1,0:T(8,128)(2,1)}, bf16[2,128,2048]{2,1,0:T(8,128)(2,1)}, bf16[2,128,2048]{2,1,0:T(8,128)(2,1)}, f32[8,1536]{1,0:T(8,128)}) custom-call(s32[3]{0:T(128)} %pad_add_fusion.4.ids, bf16[1024,2048]{1,0:T(8,128)(2,1)} %get-tuple-element.248.attn_t, bf16[3,2048,256]{2,1,0:T(8,128)(2,1)} %get-tuple-element.247.grad_a, ...), custom_call_target="tpu_custom_call" | custom-call | flops 8589934592 | bytes 24000000 | tf_op jit(solution)/shard_map/attn_weights/attn_weights/pallas_call | solution.py:585
  275.0 1.6 collective-permute-start.39
  276.5 1.4 fusion.3
  279.3 2.1 fusion.1
  281.4 2.6 collective-permute-start.37
  283.9 22.9 %back.2 = (bf16[1024,1024]{1,0:T(8,128)(2,1)}, bf16[1024,1024]{1,0:T(8,128)(2,1)}, f32[8,1024]{1,0:T(8,128)}) custom-call(bf16[3,2048,256]{2,1,0:T(8,128)(2,1)} %get-tuple-element.247.grad_a, bf16[3,2048,256]{2,1,0:T(8,128)(2,1)} %get-tuple-element.350.grad_b, bf16[2048,256]{1,0:T(8,128)(2,1)} %get-tuple-element.303.att_a, ...), custom_call_target="tpu_custom_call" | custom-call | flops 12884901888 | bytes 40000000 | tf_op jit(solution)/shard_map/back/back/pallas_call | solution.py:585
  308.7 1.4 add_convert_fusion.6.own
  312.4 2.4 fusion.16
  314.8 1.4 collective-permute-start.42
  319.1 9.2 %adam_mlp.2 = (f32[128,4096]{1,0:T(8,128)}, f32[128,4096]{1,0:T(8,128)}, f32[128,4096]{1,0:T(8,128)}, f32[512,1024]{1,0:T(8,128)}, f32[512,1024]{1,0:T(8,128)}, /*index=5*/f32[512,1024]{1,0:T(8,128)}) custom-call(s32[3]{0:T(128)} %pad_add_fusion.4.ids, bf16[256,1024]{1,0:T(8,128)(2,1)} %copy-done.7, bf16[256,1024]{1,0:T(8,128)(2,1)} %copy-done.29, ...), custom_call_target="tpu_custom_call" | custom-call | bytes 14000000 | tf_op jit(solution)/shard_map/adam_mlp/pallas_call | solution.py:814
  330.2 1.9 bitcast_add_fusion
  332.2 2.3 collective-permute-start.47
  334.5 25.6 %back.3 = (bf16[1024,1024]{1,0:T(8,128)(2,1)}, f32[1024,1024]{1,0:T(8,128)}, f32[8,1024]{1,0:T(8,128)}) custom-call(bf16[3,2048,256]{2,1,0:T(8,128)(2,1)} %get-tuple-element.247.grad_a, bf16[3,2048,256]{2,1,0:T(8,128)(2,1)} %get-tuple-element.350.grad_b, bf16[2048,256]{1,0:T(8,128)(2,1)} %get-tuple-element.303.att_a, ...), custom_call_target="tpu_custom_call" | custom-call | flops 12884901888 | bytes 40000000 | tf_op jit(solution)/shard_map/back/back/pallas_call | solution.py:585
  362.0 3.6 collective-permute-done.50
  366.9 9.0 %adam_mlp.3 = (f32[128,4096]{1,0:T(8,128)}, f32[128,4096]{1,0:T(8,128)}, f32[128,4096]{1,0:T(8,128)}, f32[512,1024]{1,0:T(8,128)}, f32[512,1024]{1,0:T(8,128)}, /*index=5*/f32[512,1024]{1,0:T(8,128)}) custom-call(s32[3]{0:T(128)} %pad_add_fusion.4.ids, ...), custom_call_target="tpu_custom_call", output_to_operand_aliasing={{0}: (9, {}), {1}: (10, {}), {2}: (11, {}), {3}: (12, {}), ... | custom-call | bytes 14000000 | tf_op jit(solution)/shard_map/adam_mlp/pallas_call | solution.py:814
  376.0 1.5 collective-permute-start.54
  379.8 1.5 collective-permute-done.54
  385.9 8.1 %adam_attn.1 = (f32[128,3072]{1,0:T(8,128)}, f32[128,3072]{1,0:T(8,128)}, f32[128,3072]{1,0:T(8,128)}, f32[128,1024]{1,0:T(8,128)}, f32[128,1024]{1,0:T(8,128)}, /*index=5*/f32[128,1024]{1,0:T(8,128)}) custom-call(s32[3]{0:T(128)} %pad_add_fusion.4.ids, bf16[128,2048]{1,0:T(8,128)(2,1)} %copy-done.6, bf16[128,2048]{1,0:T(8,128)(2,1)} %copy-done.28, ...), custom_call_target="tpu_custom_call" | custom-call | bytes 13000000 | tf_op jit(solution)/shard_map/adam/adam_attn/pallas_call | solution.py:915
  (238 shorter events, 50.3 us)
Async XLA Ops:
  3.7 12.4 %collective-permute-start.2 = (bf16[128,1280]{1,0:T(8,128)(2,1)}, bf16[128,1280]{1,0:T(8,128)(2,1)S(1)}, u32[]{:S(2)}, u32[]{:S(2)}) collective-permute-start(bf16[128,1280]{1,0:T(8,128)(2,1)} %prep_attn.1.refs_0_), channel_id=1, source_target_pairs={{0,1},{1,0},{2,3},{3,2},{4,5},{5,4},{6,7},{7,6},{8,9},{9,8},{10,11... | collective-permute-start | bytes 983048 | tf_op jit(solution)/shard_map/gather/ppermute | solution.py:538
  6.7 17.4 %collective-permute-start.1 = (bf16[128,1280]{1,0:T(8,128)(2,1)}, bf16[128,1280]{1,0:T(8,128)(2,1)S(1)}, u32[]{:S(2)}, u32[]{:S(2)}) collective-permute-start(bf16[128,1280]{1,0:T(8,128)(2,1)} %prep_attn.1.refs_0_), channel_id=1, source_target_pairs={{0,4},{1,5},{2,6},{3,7},{4,0},{5,1},{6,2},{7,3},{8,12},{9,13},{10,... | collective-permute-start | bytes 983048 | tf_op jit(solution)/shard_map/gather/ppermute | solution.py:538
  9.3 48.7 %collective-permute-start.9 = (bf16[1024,1024]{1,0:T(8,128)(2,1)}, bf16[1024,1024]{1,0:T(8,128)(2,1)}, u32[]{:S(2)}, u32[]{:S(2)}) collective-permute-start(bf16[1024,1024]{1,0:T(8,128)(2,1)} %tok.1), channel_id=1, source_target_pairs={{0,8},{1,9},{2,10},{3,11},{4,12},{5,13},{6,14},{7,15},{8,0},{9,1},... | collective-permute-start | bytes 6291464 | tf_op jit(solution)/shard_map/gather/ppermute | solution.py:538
  9.8 48.2 %collective-permute-start.10 = (bf16[1024,1024]{1,0:T(8,128)(2,1)}, bf16[1024,1024]{1,0:T(8,128)(2,1)}, u32[]{:S(2)}, u32[]{:S(2)}) collective-permute-start(bf16[1024,1024]{1,0:T(8,128)(2,1)} %refs_0_.5), channel_id=1, source_target_pairs={{0,8},{1,9},{2,10},{3,11},{4,12},{5,13},{6,14},{7,15},{8,0},{9,1},... | collective-permute-start | bytes 6291464 | tf_op jit(solution)/shard_map/gather/ppermute | solution.py:538
  14.4 16.1 %collective-permute-start = (bf16[128,1280]{1,0:T(8,128)(2,1)S(1)}, bf16[128,1280]{1,0:T(8,128)(2,1)S(1)}, u32[]{:S(2)}, u32[]{:S(2)}) collective-permute-start(bf16[128,1280]{1,0:T(8,128)(2,1)S(1)} %copy-done.30), channel_id=1, source_target_pairs={{0,2},{1,3},{2,0},{3,1},{4,6},{5,7},{6,4},{7,5},{8,10},{9,11},{10,... | collective-permute-start | bytes 983048 | tf_op jit(solution)/shard_map/gather/ppermute | solution.py:538
  30.5 27.4 %collective-permute-start.8 = (bf16[256,1024]{1,0:T(8,128)(2,1)}, bf16[256,1024]{1,0:T(8,128)(2,1)}, u32[]{:S(2)}, u32[]{:S(2)}) collective-permute-start(bf16[256,1024]{1,0:T(8,128)(2,1)} %get-tuple-element.242.refs_0_), channel_id=1, source_target_pairs={{0,4},{1,5},{2,6},{3,7},{4,0},{5,1},{6,2},{7,3},{8,12},{9,13},{10,... | collective-permute-start | bytes 1572872 | tf_op jit(solution)/shard_map/gather/ppermute | solution.py:538
  31.0 27.0 %collective-permute-start.7 = (bf16[256,1024]{1,0:T(8,128)(2,1)}, bf16[256,1024]{1,0:T(8,128)(2,1)}, u32[]{:S(2)}, u32[]{:S(2)}) collective-permute-start(bf16[256,1024]{1,0:T(8,128)(2,1)} %get-tuple-element.242.refs_0_), channel_id=1, source_target_pairs={{0,2},{1,3},{2,0},{3,1},{4,6},{5,7},{6,4},{7,5},{8,10},{9,11},{10,... | collective-permute-start | bytes 1572872 | tf_op jit(solution)/shard_map/gather/ppermute | solution.py:538
  33.9 8.9 %collective-permute-start.4 = (bf16[128,1280]{1,0:T(8,128)(2,1)S(1)}, bf16[128,1280]{1,0:T(8,128)(2,1)S(1)}, u32[]{:S(2)}, u32[]{:S(2)}) collective-permute-start(bf16[128,1280]{1,0:T(8,128)(2,1)S(1)} %collective-permute-done.refs_1_), channel_id=1, source_target_pairs={{0,1},{1,0},{2,3},{3,2},{4,5},{5,4},{6,7},{7,6},{8,9},{9,8},{10,11... | collective-permute-start | bytes 983048 | tf_op jit(solution)/shard_map/gather/ppermute | solution.py:538
  42.8 8.0 %collective-permute-start.6 = (bf16[128,1280]{1,0:T(8,128)(2,1)S(1)}, bf16[128,1280]{1,0:T(8,128)(2,1)S(1)}, u32[]{:S(2)}, u32[]{:S(2)}) collective-permute-start(bf16[128,1280]{1,0:T(8,128)(2,1)S(1)} %collective-permute-done.1.refs_2_), channel_id=1, source_target_pairs={{0,16},{1,17},{2,18},{3,19},{4,20},{5,21},{6,22},{7,23},{8,24},{9,... | collective-permute-start | bytes 983048 | tf_op jit(solution)/shard_map/gather/ppermute | solution.py:538
  50.8 7.2 %collective-permute-start.5 = (bf16[128,1280]{1,0:T(8,128)(2,1)S(1)}, bf16[128,1280]{1,0:T(8,128)(2,1)S(1)}, u32[]{:S(2)}, u32[]{:S(2)}) collective-permute-start(bf16[128,1280]{1,0:T(8,128)(2,1)S(1)} %collective-permute-done.1.refs_2_), channel_id=1, source_target_pairs={{0,1},{1,0},{2,3},{3,2},{4,5},{5,4},{6,7},{7,6},{8,9},{9,8},{10,11... | collective-permute-start | bytes 983048 | tf_op jit(solution)/shard_map/gather/ppermute | solution.py:538
  58.0 22.0 %collective-permute-start.11 = (bf16[128,1280]{1,0:T(8,128)(2,1)S(1)}, bf16[128,1280]{1,0:T(8,128)(2,1)S(1)}, u32[]{:S(2)}, u32[]{:S(2)}) collective-permute-start(bf16[128,1280]{1,0:T(8,128)(2,1)S(1)} %collective-permute-done.5.refs_6_), channel_id=1, source_target_pairs={{0,16},{1,17},{2,18},{3,19},{4,20},{5,21},{6,22},{7,23},{8,24},{9,... | collective-permute-start | bytes 983048 | tf_op jit(solution)/shard_map/gather/ppermute | solution.py:538
  62.2 13.1 %collective-permute-start.13 = (bf16[2,16,128]{2,1,0:T(8,128)(2,1)S(1)}, bf16[2,16,128]{2,1,0:T(8,128)(2,1)S(1)}, u32[]{:S(2)}, u32[]{:S(2)}) collective-permute-start(bf16[2,16,128]{2,1,0:T(8,128)(2,1)S(1)} %pad_maximum_fusion.5), channel_id=1, source_target_pairs={{0,4},{1,5},{2,6},{3,7},{4,0},{5,1},{6,2},{7,3},{8,12},{9,13},{10,... | collective-permute-start | bytes 24584 | tf_op jit(solution)/shard_map/gather/ppermute | solution.py:538
  63.4 39.9 %collective-permute-start.19 = (bf16[352,1024]{1,0:T(8,128)(2,1)S(1)}, bf16[352,1024]{1,0:T(8,128)(2,1)S(1)}, u32[]{:S(2)}, u32[]{:S(2)}) collective-permute-start(bf16[352,1024]{1,0:T(8,128)(2,1)S(1)} %copy-done.14), channel_id=1, source_target_pairs={{0,4},{1,5},{2,6},{3,7},{4,0},{5,1},{6,2},{7,3},{8,12},{9,13},{10,... | collective-permute-start | bytes 2162696 | tf_op jit(solution)/shard_map/gather/ppermute | solution.py:538
  65.1 38.2 %collective-permute-start.18 = (bf16[352,1024]{1,0:T(8,128)(2,1)S(1)}, bf16[352,1024]{1,0:T(8,128)(2,1)S(1)}, u32[]{:S(2)}, u32[]{:S(2)}) collective-permute-start(bf16[352,1024]{1,0:T(8,128)(2,1)S(1)} %copy-done.14), channel_id=1, source_target_pairs={{0,2},{1,3},{2,0},{3,1},{4,6},{5,7},{6,4},{7,5},{8,10},{9,11},{10,... | collective-permute-start | bytes 2162696 | tf_op jit(solution)/shard_map/gather/ppermute | solution.py:538
  75.9 27.4 %collective-permute-start.17 = (bf16[256,1024]{1,0:T(8,128)(2,1)}, bf16[256,1024]{1,0:T(8,128)(2,1)}, u32[]{:S(2)}, u32[]{:S(2)}) collective-permute-start(bf16[256,1024]{1,0:T(8,128)(2,1)} %collective-permute-done.8.refs_2_), channel_id=1, source_target_pairs={{0,16},{1,17},{2,18},{3,19},{4,20},{5,21},{6,22},{7,23},{8,24},{9,... | collective-permute-start | bytes 1572872 | tf_op jit(solution)/shard_map/gather/ppermute | solution.py:538
  79.3 24.1 %collective-permute-start.15 = (bf16[256,1024]{1,0:T(8,128)(2,1)}, bf16[256,1024]{1,0:T(8,128)(2,1)}, u32[]{:S(2)}, u32[]{:S(2)}) collective-permute-start(bf16[256,1024]{1,0:T(8,128)(2,1)} %collective-permute-done.8.refs_2_), channel_id=1, source_target_pairs={{0,1},{1,0},{2,3},{3,2},{4,5},{5,4},{6,7},{7,6},{8,9},{9,8},{10,11... | collective-permute-start | bytes 1572872 | tf_op jit(solution)/shard_map/gather/ppermute | solution.py:538
  80.7 22.6 %collective-permute-start.16 = (bf16[256,1024]{1,0:T(8,128)(2,1)}, bf16[256,1024]{1,0:T(8,128)(2,1)}, u32[]{:S(2)}, u32[]{:S(2)}) collective-permute-start(bf16[256,1024]{1,0:T(8,128)(2,1)} %collective-permute-done.7.refs_1_), channel_id=1, source_target_pairs={{0,1},{1,0},{2,3},{3,2},{4,5},{5,4},{6,7},{7,6},{8,9},{9,8},{10,11... | collective-permute-start | bytes 1572872 | tf_op jit(solution)/shard_map/gather/ppermute | solution.py:538
  103.4 31.8 %collective-permute-start.23 = (bf16[352,1024]{1,0:T(8,128)(2,1)S(1)}, bf16[352,1024]{1,0:T(8,128)(2,1)S(1)}, u32[]{:S(2)}, u32[]{:S(2)}) collective-permute-start(bf16[352,1024]{1,0:T(8,128)(2,1)S(1)} %collective-permute-done.19.refs_2_), channel_id=1, source_target_pairs={{0,16},{1,17},{2,18},{3,19},{4,20},{5,21},{6,22},{7,23},{8,24},{9,... | collective-permute-start | bytes 2162696 | tf_op jit(solution)/shard_map/gather/ppermute | solution.py:538
  104.6 30.6 %collective-permute-start.22 = (bf16[352,1024]{1,0:T(8,128)(2,1)S(1)}, bf16[352,1024]{1,0:T(8,128)(2,1)S(1)}, u32[]{:S(2)}, u32[]{:S(2)}) collective-permute-start(bf16[352,1024]{1,0:T(8,128)(2,1)S(1)} %collective-permute-done.19.refs_2_), channel_id=1, source_target_pairs={{0,1},{1,0},{2,3},{3,2},{4,5},{5,4},{6,7},{7,6},{8,9},{9,8},{10,11... | collective-permute-start | bytes 2162696 | tf_op jit(solution)/shard_map/gather/ppermute | solution.py:538
  105.4 29.7 %collective-permute-start.20 = (bf16[256,1024]{1,0:T(8,128)(2,1)}, bf16[256,1024]{1,0:T(8,128)(2,1)S(1)}, u32[]{:S(2)}, u32[]{:S(2)}) collective-permute-start(bf16[256,1024]{1,0:T(8,128)(2,1)} %collective-permute-done.15.refs_6_), channel_id=1, source_target_pairs={{0,16},{1,17},{2,18},{3,19},{4,20},{5,21},{6,22},{7,23},{8,24},{9,... | collective-permute-start | bytes 1572872 | tf_op jit(solution)/shard_map/gather/ppermute | solution.py:538
  106.1 29.0 %collective-permute-start.21 = (bf16[256,1024]{1,0:T(8,128)(2,1)S(1)}, bf16[256,1024]{1,0:T(8,128)(2,1)S(1)}, u32[]{:S(2)}, u32[]{:S(2)}) collective-permute-start(bf16[256,1024]{1,0:T(8,128)(2,1)S(1)} %copy-done.38), channel_id=1, source_target_pairs={{0,1},{1,0},{2,3},{3,2},{4,5},{5,4},{6,7},{7,6},{8,9},{9,8},{10,11... | collective-permute-start | bytes 1572872 | tf_op jit(solution)/shard_map/gather/ppermute | solution.py:538
  136.1 32.9 %collective-permute-start.24 = (bf16[352,1024]{1,0:T(8,128)(2,1)S(1)}, bf16[352,1024]{1,0:T(8,128)(2,1)S(1)}, u32[]{:S(2)}, u32[]{:S(2)}) collective-permute-start(bf16[352,1024]{1,0:T(8,128)(2,1)S(1)} %copy-done.14), channel_id=1, source_target_pairs={{0,1},{1,0},{2,3},{3,2},{4,5},{5,4},{6,7},{7,6},{8,9},{9,8},{10,11... | collective-permute-start | bytes 2162696 | tf_op jit(solution)/shard_map/gather/ppermute | solution.py:538
  136.7 32.2 %collective-permute-start.25 = (bf16[352,1024]{1,0:T(8,128)(2,1)S(1)}, bf16[352,1024]{1,0:T(8,128)(2,1)S(1)}, u32[]{:S(2)}, u32[]{:S(2)}) collective-permute-start(bf16[352,1024]{1,0:T(8,128)(2,1)S(1)} %collective-permute-done.18.refs_1_), channel_id=1, source_target_pairs={{0,1},{1,0},{2,3},{3,2},{4,5},{5,4},{6,7},{7,6},{8,9},{9,8},{10,11... | collective-permute-start | bytes 2162696 | tf_op jit(solution)/shard_map/gather/ppermute | solution.py:538
  138.1 30.9 %collective-permute-start.26 = (bf16[352,1024]{1,0:T(8,128)(2,1)S(1)}, bf16[352,1024]{1,0:T(8,128)(2,1)S(1)}, u32[]{:S(2)}, u32[]{:S(2)}) collective-permute-start(bf16[352,1024]{1,0:T(8,128)(2,1)S(1)} %collective-permute-done.22.refs_6_), channel_id=1, source_target_pairs={{0,16},{1,17},{2,18},{3,19},{4,20},{5,21},{6,22},{7,23},{8,24},{9,... | collective-permute-start | bytes 2162696 | tf_op jit(solution)/shard_map/gather/ppermute | solution.py:538
  170.2 31.9 %collective-permute-start.27 = (bf16[2,256,1024]{2,1,0:T(8,128)(2,1)}, bf16[2,256,1024]{2,1,0:T(8,128)(2,1)S(1)}, u32[]{:S(2)}, u32[]{:S(2)}) collective-permute-start(bf16[2,256,1024]{2,1,0:T(8,128)(2,1)} %get-tuple-element.279), channel_id=1, source_target_pairs={{0,1},{1,0},{2,3},{3,2},{4,5},{5,4},{6,7},{7,6},{8,9},{9,8},{10,11... | collective-permute-start | bytes 3145736 | tf_op jit(solution)/shard_map/ppermute | solution.py:538
  170.9 31.1 %collective-permute-start.28 = (bf16[2,256,1024]{2,1,0:T(8,128)(2,1)}, bf16[2,256,1024]{2,1,0:T(8,128)(2,1)S(1)}, u32[]{:S(2)}, u32[]{:S(2)}) collective-permute-start(bf16[2,256,1024]{2,1,0:T(8,128)(2,1)} %get-tuple-element.280), channel_id=1, source_target_pairs={{0,16},{1,17},{2,18},{3,19},{4,20},{5,21},{6,22},{7,23},{8,24},{9,... | collective-permute-start | bytes 3145736 | tf_op jit(solution)/shard_map/ppermute | solution.py:538
  203.5 40.7 %collective-permute-start.30 = (bf16[256,1024]{1,0:T(8,128)(2,1)}, bf16[256,1024]{1,0:T(8,128)(2,1)S(1)}, u32[]{:S(2)}, u32[]{:S(2)}) collective-permute-start(bf16[256,1024]{1,0:T(8,128)(2,1)} %get-tuple-element.410), channel_id=1, source_target_pairs={{0,2},{1,3},{2,0},{3,1},{4,6},{5,7},{6,4},{7,5},{8,10},{9,11},{10,... | collective-permute-start | bytes 1572872 | tf_op jit(solution)/shard_map/ppermute | solution.py:538
  203.5 40.8 %collective-permute-start.29 = (bf16[256,1024]{1,0:T(8,128)(2,1)}, bf16[256,1024]{1,0:T(8,128)(2,1)}, u32[]{:S(2)}, u32[]{:S(2)}) collective-permute-start(bf16[256,1024]{1,0:T(8,128)(2,1)} %get-tuple-element.411), channel_id=1, source_target_pairs={{0,1},{1,0},{2,3},{3,2},{4,5},{5,4},{6,7},{7,6},{8,9},{9,8},{10,11... | collective-permute-start | bytes 1572872 | tf_op jit(solution)/shard_map/ppermute | solution.py:538
  214.5 29.8 %collective-permute-start.31 = (bf16[2,256,1024]{2,1,0:T(8,128)(2,1)}, bf16[2,256,1024]{2,1,0:T(8,128)(2,1)S(1)}, u32[]{:S(2)}, u32[]{:S(2)}) collective-permute-start(bf16[2,256,1024]{2,1,0:T(8,128)(2,1)} %get-tuple-element.293), channel_id=1, source_target_pairs={{0,1},{1,0},{2,3},{3,2},{4,5},{5,4},{6,7},{7,6},{8,9},{9,8},{10,11... | collective-permute-start | bytes 3145736 | tf_op jit(solution)/shard_map/ppermute | solution.py:538
  215.2 29.1 %collective-permute-start.32 = (bf16[2,256,1024]{2,1,0:T(8,128)(2,1)}, bf16[2,256,1024]{2,1,0:T(8,128)(2,1)S(1)}, u32[]{:S(2)}, u32[]{:S(2)}) collective-permute-start(bf16[2,256,1024]{2,1,0:T(8,128)(2,1)} %get-tuple-element.294), channel_id=1, source_target_pairs={{0,16},{1,17},{2,18},{3,19},{4,20},{5,21},{6,22},{7,23},{8,24},{9,... | collective-permute-start | bytes 3145736 | tf_op jit(solution)/shard_map/ppermute | solution.py:538
  247.4 29.1 %collective-permute-start.33 = (bf16[256,1024]{1,0:T(8,128)(2,1)}, bf16[256,1024]{1,0:T(8,128)(2,1)}, u32[]{:S(2)}, u32[]{:S(2)}) collective-permute-start(bf16[256,1024]{1,0:T(8,128)(2,1)} %fusion.4), channel_id=1, source_target_pairs={{0,4},{1,5},{2,6},{3,7},{4,0},{5,1},{6,2},{7,3},{8,12},{9,13},{10,... | collective-permute-start | bytes 1572872 | tf_op jit(solution)/shard_map/ppermute | solution.py:538
  251.2 27.3 %collective-permute-start.35 = (bf16[256,1024]{1,0:T(8,128)(2,1)}, bf16[256,1024]{1,0:T(8,128)(2,1)S(1)}, u32[]{:S(2)}, u32[]{:S(2)}) collective-permute-start(bf16[256,1024]{1,0:T(8,128)(2,1)} %get-tuple-element.408), channel_id=1, source_target_pairs={{0,2},{1,3},{2,0},{3,1},{4,6},{5,7},{6,4},{7,5},{8,10},{9,11},{10,... | collective-permute-start | bytes 1572872 | tf_op jit(solution)/shard_map/ppermute | solution.py:538
  251.2 28.1 %collective-permute-start.36 = (bf16[256,1024]{1,0:T(8,128)(2,1)}, bf16[256,1024]{1,0:T(8,128)(2,1)}, u32[]{:S(2)}, u32[]{:S(2)}) collective-permute-start(bf16[256,1024]{1,0:T(8,128)(2,1)} %get-tuple-element.409), channel_id=1, source_target_pairs={{0,1},{1,0},{2,3},{3,2},{4,5},{5,4},{6,7},{7,6},{8,9},{9,8},{10,11... | collective-permute-start | bytes 1572872 | tf_op jit(solution)/shard_map/ppermute | solution.py:538
  274.4 32.5 %collective-permute-start.38 = (bf16[2,128,2048]{2,1,0:T(8,128)(2,1)}, bf16[2,128,2048]{2,1,0:T(8,128)(2,1)S(1)}, u32[]{:S(2)}, u32[]{:S(2)}) collective-permute-start(bf16[2,128,2048]{2,1,0:T(8,128)(2,1)} %get-tuple-element.326), channel_id=1, source_target_pairs={{0,1},{1,0},{2,3},{3,2},{4,5},{5,4},{6,7},{7,6},{8,9},{9,8},{10,11... | collective-permute-start | bytes 3145736 | tf_op jit(solution)/shard_map/ppermute | solution.py:538
  275.0 32.7 %collective-permute-start.39 = (bf16[2,128,2048]{2,1,0:T(8,128)(2,1)}, bf16[2,128,2048]{2,1,0:T(8,128)(2,1)}, u32[]{:S(2)}, u32[]{:S(2)}) collective-permute-start(bf16[2,128,2048]{2,1,0:T(8,128)(2,1)} %get-tuple-element.327), channel_id=1, source_target_pairs={{0,16},{1,17},{2,18},{3,19},{4,20},{5,21},{6,22},{7,23},{8,24},{9,... | collective-permute-start | bytes 3145736 | tf_op jit(solution)/shard_map/ppermute | solution.py:538
  277.9 28.9 %collective-permute-start.34 = (bf16[256,1024]{1,0:T(8,128)(2,1)S(1)}, bf16[256,1024]{1,0:T(8,128)(2,1)S(1)}, u32[]{:S(2)}, u32[]{:S(2)}) collective-permute-start(bf16[256,1024]{1,0:T(8,128)(2,1)S(1)} %fusion.3), channel_id=1, source_target_pairs={{0,16},{1,17},{2,18},{3,19},{4,20},{5,21},{6,22},{7,23},{8,24},{9,... | collective-permute-start | bytes 1572872 | tf_op jit(solution)/shard_map/ppermute | solution.py:538
  281.4 25.5 %collective-permute-start.37 = (bf16[256,1024]{1,0:T(8,128)(2,1)S(1)}, bf16[256,1024]{1,0:T(8,128)(2,1)S(1)}, u32[]{:S(2)}, u32[]{:S(2)}) collective-permute-start(bf16[256,1024]{1,0:T(8,128)(2,1)S(1)} %get-tuple-element.406), channel_id=1, source_target_pairs={{0,4},{1,5},{2,6},{3,7},{4,0},{5,1},{6,2},{7,3},{8,12},{9,13},{10,... | collective-permute-start | bytes 1572872 | tf_op jit(solution)/shard_map/ppermute | solution.py:538
  307.8 21.2 %collective-permute-start.44 = (bf16[1024,1024]{1,0:T(8,128)(2,1)}, bf16[1024,1024]{1,0:T(8,128)(2,1)}, u32[]{:S(2)}, u32[]{:S(2)}) collective-permute-start(bf16[1024,1024]{1,0:T(8,128)(2,1)} %get-tuple-element.342), channel_id=1, source_target_pairs={{0,8},{1,9},{2,10},{3,11},{4,12},{5,13},{6,14},{7,15},{8,0},{9,1},... | collective-permute-start | bytes 6291464 | tf_op jit(solution)/shard_map/ppermute | solution.py:538
  307.8 21.2 %collective-permute-start.45 = (bf16[1024,1024]{1,0:T(8,128)(2,1)}, bf16[1024,1024]{1,0:T(8,128)(2,1)}, u32[]{:S(2)}, u32[]{:S(2)}) collective-permute-start(bf16[1024,1024]{1,0:T(8,128)(2,1)} %get-tuple-element.343), channel_id=1, source_target_pairs={{0,8},{1,9},{2,10},{3,11},{4,12},{5,13},{6,14},{7,15},{8,0},{9,1},... | collective-permute-start | bytes 6291464 | tf_op jit(solution)/shard_map/ppermute | solution.py:538
  311.5 16.7 %collective-permute-start.41 = (bf16[256,1024]{1,0:T(8,128)(2,1)S(1)}, bf16[256,1024]{1,0:T(8,128)(2,1)S(1)}, u32[]{:S(2)}, u32[]{:S(2)}) collective-permute-start(bf16[256,1024]{1,0:T(8,128)(2,1)S(1)} %add_convert_fusion.5), channel_id=1, source_target_pairs={{0,16},{1,17},{2,18},{3,19},{4,20},{5,21},{6,22},{7,23},{8,24},{9,... | collective-permute-start | bytes 1572872 | tf_op jit(solution)/shard_map/ppermute | solution.py:538
  314.8 14.1 %collective-permute-start.43 = (bf16[128,2048]{1,0:T(8,128)(2,1)}, bf16[128,2048]{1,0:T(8,128)(2,1)S(1)}, u32[]{:S(2)}, u32[]{:S(2)}) collective-permute-start(bf16[128,2048]{1,0:T(8,128)(2,1)} %get-tuple-element.404), channel_id=1, source_target_pairs={{0,2},{1,3},{2,0},{3,1},{4,6},{5,7},{6,4},{7,5},{8,10},{9,11},{10,... | collective-permute-start | bytes 1572872 | tf_op jit(solution)/shard_map/ppermute | solution.py:538
  314.8 14.2 %collective-permute-start.42 = (bf16[128,2048]{1,0:T(8,128)(2,1)}, bf16[128,2048]{1,0:T(8,128)(2,1)S(1)}, u32[]{:S(2)}, u32[]{:S(2)}) collective-permute-start(bf16[128,2048]{1,0:T(8,128)(2,1)} %get-tuple-element.405), channel_id=1, source_target_pairs={{0,1},{1,0},{2,3},{3,2},{4,5},{5,4},{6,7},{7,6},{8,9},{9,8},{10,11... | collective-permute-start | bytes 1572872 | tf_op jit(solution)/shard_map/ppermute | solution.py:538
  330.1 30.0 %collective-permute-start.46 = (bf16[256,1024]{1,0:T(8,128)(2,1)S(1)}, bf16[256,1024]{1,0:T(8,128)(2,1)S(1)}, u32[]{:S(2)}, u32[]{:S(2)}) collective-permute-start(bf16[256,1024]{1,0:T(8,128)(2,1)S(1)} %add_convert_fusion.2.own), channel_id=1, source_target_pairs={{0,8},{1,9},{2,10},{3,11},{4,12},{5,13},{6,14},{7,15},{8,0},{9,1},... | collective-permute-start | bytes 1572872 | tf_op jit(solution)/shard_map/ppermute | solution.py:538
  332.2 28.0 %collective-permute-start.47 = (bf16[128,2048]{1,0:T(8,128)(2,1)S(1)}, bf16[128,2048]{1,0:T(8,128)(2,1)S(1)}, u32[]{:S(2)}, u32[]{:S(2)}) collective-permute-start(bf16[128,2048]{1,0:T(8,128)(2,1)S(1)} %get-tuple-element.403), channel_id=1, source_target_pairs={{0,4},{1,5},{2,6},{3,7},{4,0},{5,1},{6,2},{7,3},{8,12},{9,13},{10,... | collective-permute-start | bytes 1572872 | tf_op jit(solution)/shard_map/ppermute | solution.py:538
  360.3 19.3 %collective-permute-start.48 = (bf16[128,2048]{1,0:T(8,128)(2,1)S(1)}, bf16[128,2048]{1,0:T(8,128)(2,1)S(1)}, u32[]{:S(2)}, u32[]{:S(2)}) collective-permute-start(bf16[128,2048]{1,0:T(8,128)(2,1)S(1)} %add_convert_fusion.1), channel_id=1, source_target_pairs={{0,16},{1,17},{2,18},{3,19},{4,20},{5,21},{6,22},{7,23},{8,24},{9,... | collective-permute-start | bytes 1572872 | tf_op jit(solution)/shard_map/ppermute | solution.py:538
  365.7 10.3 %collective-permute-start.51 = (f32[16,1024]{1,0:T(8,128)S(1)}, f32[16,1024]{1,0:T(8,128)S(1)}, u32[]{:S(2)}, u32[]{:S(2)}) collective-permute-start(f32[16,1024]{1,0:T(8,128)S(1)} %add.217), channel_id=1, source_target_pairs={{0,4},{1,5},{2,6},{3,7},{4,0},{5,1},{6,2},{7,3},{8,12},{9,13},{10,... | collective-permute-start | bytes 196616 | tf_op jit(solution)/shard_map/vectors/ppermute | solution.py:538
  376.0 5.2 %collective-permute-start.54 = (f32[16,1024]{1,0:T(8,128)S(1)}, f32[16,1024]{1,0:T(8,128)S(1)}, u32[]{:S(2)}, u32[]{:S(2)}) collective-permute-start(f32[16,1024]{1,0:T(8,128)S(1)} %add.218), channel_id=1, source_target_pairs={{0,17},{1,16},{2,19},{3,18},{4,21},{5,20},{6,23},{7,22},{8,25},{9,... | collective-permute-start | bytes 196616 | tf_op jit(solution)/shard_map/vectors/ppermute | solution.py:538
  379.7 5.3 %collective-permute-start.49 = (bf16[128,2048]{1,0:T(8,128)(2,1)S(1)}, bf16[128,2048]{1,0:T(8,128)(2,1)S(1)}, u32[]{:S(2)}, u32[]{:S(2)}) collective-permute-start(bf16[128,2048]{1,0:T(8,128)(2,1)S(1)} %add_convert_fusion.own), channel_id=1, source_target_pairs={{0,8},{1,9},{2,10},{3,11},{4,12},{5,13},{6,14},{7,15},{8,0},{9,1},... | collective-permute-start | bytes 1572872 | tf_op jit(solution)/shard_map/ppermute | solution.py:538
  (56 other events, 470.2 us)

commit v4 on v3

--- a/solution.py
+++ b/solution.py
@@ -25,7 +25,8 @@
 AXES = ("dp", "zero")
 F32 = jnp.float32
 BF16 = jnp.bfloat16
-VMEM_LIMIT = 58 * 1024 * 1024
+MIB = 1024 * 1024
+VMEM_NEED = 58
 
 
 def spec(block, index, single=False):
@@ -36,6 +37,10 @@
 
 def whole(shape):
     return spec(shape, lambda *_: (0,) * len(shape), single=True)
+
+
+def distant():
+    return pl.BlockSpec(memory_space=pl.ANY)
 
 
 def scalars():
@@ -52,7 +57,7 @@
         scratch_shapes=list(scratch),
         cost_estimate=pl.CostEstimate(flops=int(flops), bytes_accessed=int(moved), transcendentals=0),
         compiler_params=pltpu.CompilerParams(
-            vmem_limit_bytes=VMEM_LIMIT, dimension_semantics=("arbitrary",) * len(grid)
+            vmem_limit_bytes=VMEM_NEED * MIB, dimension_semantics=("arbitrary",) * len(grid)
         ),
         name=name,
     )
@@ -102,13 +107,13 @@
     return jnp.where(core == 0, even, odd)
 
 
-def prep_attn_body(ids, w_qkv, w_out, out):
+def prep_attn_body(ids, w_qkv, w_out, vec, out):
     core = ids[1]
     for part in range(3):
         for tile in range(2):
             base = part * 1024 + tile * 256
             at = part * 256 + tile * 128
-            out[:, at : at + 128] = pick_parity(
+            out[0:128, at : at + 128] = pick_parity(
                 core, w_qkv[:, base : base + 128], w_qkv[:, base + 128 : base + 256]
             ).astype(BF16)
     rows = w_out[pl.ds(pl.multiple_of(core * 64, 64), 64), :].astype(BF16)
@@ -116,6 +121,8 @@
         at = 768 + 256 * (panel // 2)
         base = (panel % 2) * 64
         out[base : base + 64, at : at + 256] = rows[:, 256 * panel : 256 * panel + 256]
+    out[128:144, 0:128] = jnp.where(lax.broadcasted_iota(jnp.int32, (16, 128), 0) < 13, vec[...], 0.0).astype(BF16)
+    out[128:144, 128:1280] = jnp.zeros((16, 1152), BF16)
 
 
 def prep_mlp_body(ids, w_up, w_down, w_qkv, out_a, out_b):
@@ -134,20 +141,6 @@
                 out_b[256 + 32 * part : 288 + 32 * part, at : at + 128] = value[32 * panel : 32 * panel + 32]
 
 
-def join_vec_body(ids, pieces, vec, bias):
-    for step in range(8):
-        owner = jnp.bitwise_xor(ids[0], 2 * (step & 3) + step // 4)
-        vec[:, pl.ds(pl.multiple_of(owner * 128, 128), 128)] = pieces[step].astype(F32)
-    for part in range(3):
-        for tile in range(4):
-            base = tile * 256
-            row = slice(4 + part, 5 + part)
-            at = (tile // 2) * 768 + part * 256 + (tile % 2) * 128
-            bias[:, at : at + 128] = pick_parity(
-                ids[1], vec[row, base : base + 128], vec[row, base + 128 : base + 256]
-            )
-
-
 def normalize(inputs):
     centred = inputs - jnp.mean(inputs, axis=-1, keepdims=True)
     variance = jnp.mean(centred * centred, axis=-1, keepdims=True)
@@ -176,21 +169,31 @@
 
 def qkv_first_body(steps, ids, *refs):
     pieces, refs = refs[:8], refs[8:]
-    tok_own, tok_other, dy_own, dy_other, vec, bias, cos, sin_lo, sin_hi = refs[:9]
-    q, k, v, d_att, attn_in, attn_t, mlp_in, w_qkv, w_out = refs[9:]
+    tok_own, tok_other, dy_own, dy_other, cos, sin_lo, sin_hi = refs[:7]
+    q, k, v, d_att, attn_in, attn_t, mlp_in, w_qkv, w_out, vec, bias = refs[7:]
     step = pl.program_id(0)
 
     @pl.when(step == 0)
     def _():
         for place, piece in enumerate(pieces):
             owner = piece_owner(ids, place)
-            w_qkv[pl.ds(pl.multiple_of(owner * 128, 128), 128), :] = piece[:, 0:768]
+            at_owner = pl.ds(pl.multiple_of(owner * 128, 128), 128)
+            w_qkv[at_owner, :] = piece[0:128, 0:768]
+            vec[:, at_owner] = piece[128:144, 0:128].astype(F32)
             for panel in range(4):
                 at = 768 + 256 * (panel // 2)
                 base = (panel % 2) * 64
                 w_out[pl.ds(pl.multiple_of(owner * 64, 64), 64), 256 * panel : 256 * panel + 256] = piece[
                     base : base + 64, at : at + 256
                 ]
+        for part in range(3):
+            for tile in range(4):
+                base = tile * 256
+                row = slice(4 + part, 5 + part)
+                at = (tile // 2) * 768 + part * 256 + (tile % 2) * 128
+                bias[:, at : at + 128] = pick_parity(
+                    ids[1], vec[row, base : base + 128], vec[row, base + 128 : base + 256]
+                )
 
     first = step < steps // 2
     d_att[...] = nt(jnp.where(first, dy_own[...], dy_other[...]), w_out[...]).astype(BF16)
@@ -296,7 +299,20 @@
     grad[2] = jnp.concatenate([dv_a, dv_b], axis=0).T.astype(BF16)
 
 
-def attn_weights_body(ids, attn_t, grad_a, grad_b, att_a, att_b, dy_own, dy_other, keep, send_x, send_y, bias, result):
+def attn_weights_body(ids, attn_t, grad_a, grad_b, far_att_a, far_att_b, far_own, far_other, *refs):
+    keep, send_x, send_y, bias, result, att_a, att_b, dy_own, dy_other, sems = refs
+    copies = [
+        pltpu.make_async_copy(source, target, sems.at[n])
+        for n, (source, target) in enumerate(
+            ((far_att_a, att_a), (far_att_b, att_b), (far_own, dy_own), (far_other, dy_other))
+        )
+    ]
+
+    @pl.when(pl.program_id(0) == 0)
+    def _():
+        for copy in copies:
+            copy.start()
+
     step = pl.program_id(0)
     outs = (keep, send_x, send_y)
 
@@ -313,6 +329,8 @@
 
     @pl.when(step == 6)
     def _():
+        for copy in copies:
+            copy.wait()
         count = dy_own.shape[0]
         for group, att in enumerate((att_a, att_b)):
             flipped = att[...].T
@@ -334,10 +352,14 @@
 
 
 def mlp_body(part, steps, ids, *refs):
-    pieces = refs[:8]
-    vec, mlp_in, dy_own, dy_other, keep, send_x, send_y, hidden_out, grad_out, sums, w_up, w_down = refs[8:-6]
-    mlp_t, hidden_t, grad_pre, dy, bias, result = refs[-6:]
+    pieces, (vec, mlp_in, dy_own, dy_other) = refs[:8], refs[8:12]
+    far_outs, (hidden_out, grad_out, sums, far_up, far_down) = refs[12:15], refs[15:20]
+    mlp_t, hidden_t, grad_pre, dy, bias, result, keep, send_x, send_y, w_up, w_down, sems = refs[20:]
     outs = (keep, send_x, send_y)
+    weight_copies = [
+        pltpu.make_async_copy(w_up, far_up, sems.at[0]),
+        pltpu.make_async_copy(w_down, far_down, sems.at[1]),
+    ]
     core = ids[1]
     step = pl.program_id(0)
 
@@ -352,6 +374,8 @@
             at = pl.ds(pl.multiple_of(piece_owner(ids, place) * 128, 128), 128)
             w_up[at, :] = piece[0:128, :]
             w_down[at, :] = piece[128:256, :]
+        for copy in weight_copies:
+            copy.start()
 
     rows = mlp_in[...]
     grads = jnp.where(step < steps // 2, dy_own[...], dy_other[...])
@@ -360,8 +384,8 @@
     mlp_t[:, at] = rows.T
     dy[at, :] = grads
     sums[1:2, :] += jnp.sum(grads.astype(F32), axis=0, keepdims=True)
-    for col in range(0, 1024, 256):
-        cols = slice(col, col + 256)
+    for col in range(0, 1024, 512):
+        cols = slice(col, col + 512)
         pre = nn(rows, w_up[:, cols]) + bias[0:1, cols]
         grad_hidden = nt(grads, w_down[cols, :])
         cdf = 0.5 + 0.5 * lax.erf(pre * INV_ROOT_TWO)
@@ -376,6 +400,7 @@
 
     @pl.when(step == steps - 1)
     def _():
+        copies = list(weight_copies)
         for base_row, left, right in ((0, mlp_t, grad_pre), (128, hidden_t, dy)):
             for col in range(0, 1024, 512):
                 cols = slice(col, col + 512)
@@ -384,21 +409,26 @@
                     out, place = slot_ref(outs, slot)
                     base = pl.multiple_of(slot_owner(ids, slot) * 128, 128)
                     out[place, base_row : base_row + 128, cols] = result[pl.ds(base, 128), :]
-
-
-def back_body(own, grad_a, grad_b, att_a, att_b, hid_a, hid_b, gp_a, gp_b, wq_a, wq_b, w_out, up_a, up_b, down_a, down_b, tok, vec, *refs):
+            span = pl.ds(base_row, 128)
+            for out, far_out in zip(outs, far_outs):
+                copy = pltpu.make_async_copy(out.at[:, span, :], far_out.at[:, span, :], sems.at[len(copies)])
+                copy.start()
+                copies.append(copy)
+        for copy in copies:
+            copy.wait()
+
+
+def back_body(own, grad_a, grad_b, att_a, att_b, hid_a, hid_b, gp_a, gp_b, *refs):
+    w_out, down_a, down_b, up_a, up_b, wq_a, wq_b, tok, vec = refs[:9]
     if own:
-        dy, out_other, scaled_other, out, result, sums = refs
+        dy, other, out, result, sums = refs[9:]
     else:
-        out, result, sums = refs
+        out, sums = refs[9:]
     inputs = tok[...].astype(F32)
     normed, inv_std = normalize(inputs)
     branch = nn(att_a[...], w_out[0:256, :]) + nn(att_b[...], w_out[256:512, :])
-    back_mlp = None
-    for hid, gp, up, down in ((hid_a, gp_a, up_a, down_a), (hid_b, gp_b, up_b, down_b)):
-        branch = branch + nn(hid[...], down[...])
-        term = nt(gp[...], up[...])
-        back_mlp = term if back_mlp is None else back_mlp + term
+    branch = branch + nn(hid_a[...], down_a[...]) + nn(hid_b[...], down_b[...])
+    back_mlp = nt(gp_a[...], up_a[...]) + nt(gp_b[...], up_b[...])
     back_attn = None
     for grad, w in ((grad_a, wq_a), (grad_b, wq_b)):
         for part in range(3):
@@ -413,12 +443,12 @@
     for row, value in enumerate((back_attn * normed, back_attn, back_mlp * normed, back_mlp)):
         sums[row : row + 1, :] += jnp.sum(value, axis=0, keepdims=True)
     if not own:
-        out[...] = branch.astype(BF16)
-        result[...] = scaled.astype(BF16)
+        out[0] = branch.astype(BF16)
+        out[1] = scaled.astype(BF16)
         return
-    branch = branch + out_other[...].astype(F32)
+    branch = branch + other[0].astype(F32)
     out[...] = (inputs + branch + (vec[7:8, :] + vec[12:13, :])).astype(BF16)
-    scaled = scaled + scaled_other[...].astype(F32)
+    scaled = scaled + other[1].astype(F32)
     result[...] = dy[...].astype(F32) + inv_std * (
         scaled
         - jnp.mean(scaled, axis=-1, keepdims=True)
@@ -605,8 +635,8 @@
         own_a = block_call(
             prep_attn_body,
             (1,),
-            [(ids, scalars()), const(w_qkv), const(w_out)],
-            [kept((128, 1280), BF16)],
+            [(ids, scalars()), const(w_qkv), const(w_out), (vectors, whole((16, 128)))],
+            [kept((144, 1280), BF16)],
             0,
             3e6,
             name="prep_attn",
@@ -628,42 +658,27 @@
         next_a, far_a = z_moves(own_a)
         across_a = swap(own_a, 0, 1)
         seg_other = swap(segments, 1, 0)
-        vec_pieces = jnp.pad(vectors, ((0, 3), (0, 0))).astype(BF16)[None]
-        next_a, far_a, across_a, own_b, own_c, seg_other, vec_pieces = sync(
-            next_a, far_a, across_a, own_b, own_c, seg_other, vec_pieces
-        )
-        next_across_a, far_across_a, rest_a = swap(next_a, 0, 1), swap(far_a, 0, 1), swap(far_a, 2, 0)
-        next_b, far_b = z_moves(own_b)
-        tok_other = swap(tokens, 1, 0)
-        dy_other = swap(cotangent, 1, 0)
-        for bits in (2, 4):
-            vec_pieces = jnp.concatenate([vec_pieces, swap(vec_pieces, 0, bits)], axis=0)
-
-    with jax.named_scope("rows"):
         tables = [
             jnp.concatenate(pair, axis=0)
             for pair in zip(rotary_tables(segments), rotary_tables(seg_other))
         ]
         seg_row = jnp.stack([segments, seg_other])[:, None, :]
         seg_col = jnp.concatenate([segments, seg_other])[:, None]
-
-    (next_across_a, far_across_a, rest_a, next_b, far_b, own_c, tables, seg_row, seg_col, tok_other, dy_other) = sync(
-        next_across_a, far_across_a, rest_a, next_b, far_b, own_c, tables, seg_row, seg_col, tok_other, dy_other
+        next_a, far_a, across_a, own_b, own_c, tables, seg_row, seg_col = sync(
+            next_a, far_a, across_a, own_b, own_c, tables, seg_row, seg_col
+        )
+        next_across_a, far_across_a, rest_a = swap(next_a, 0, 1), swap(far_a, 0, 1), swap(far_a, 2, 0)
+        rest_across_a = swap(far_a, 2, 1)
+        next_b, far_b = z_moves(own_b)
+        tok_other = swap(tokens, 1, 0)
+        dy_other = swap(cotangent, 1, 0)
+
+    (next_across_a, far_across_a, rest_a, rest_across_a, next_b, far_b, own_c, tok_other, dy_other) = sync(
+        next_across_a, far_across_a, rest_a, rest_across_a, next_b, far_b, own_c, tok_other, dy_other
     )
     with jax.named_scope("gather"):
-        vec_pieces = jnp.concatenate([vec_pieces, swap(vec_pieces, 0, 1)], axis=0)
-        rest_across_a = swap(far_across_a, 2, 0)
         far_across_b, next_across_b, rest_b = swap(far_b, 0, 1), swap(next_b, 0, 1), swap(far_b, 2, 0)
         next_c, far_c = z_moves(own_c)
-        vec, bias_qkv = block_call(
-            join_vec_body,
-            (1,),
-            [(ids, scalars()), const(vec_pieces)],
-            [kept((16, 1024), F32), kept((1, 1536), F32)],
-            0,
-            1e5,
-            name="join_vec",
-        )
     attn_pieces = [own_a, next_a, far_a, rest_a, across_a, next_across_a, far_across_a, rest_across_a]
 
     def table_blocks(count):
@@ -700,19 +715,18 @@
         return [kept((n,) + shape, BF16) for n in (4, 2, 2)]
 
     with jax.named_scope("qkv"):
-        *projected, d_att, attn_in, attn_t, mlp_in, wq_a, full_out = block_call(
+        *projected, d_att, attn_in, attn_t, mlp_in, wq_a, full_out, vec, bias_qkv = block_call(
             functools.partial(qkv_first_body, rows // 256),
             (rows // 256,),
             [(ids, scalars())]
             + [const(piece) for piece in attn_pieces]
             + halves(tokens, tok_other, 256)
             + halves(cotangent, dy_other, 256)
-            + [const(vec), const(bias_qkv)]
             + table_blocks(256),
             [(sds((rows, 256), BF16), row_block(256, 256))] * 3
             + [(sds((rows, 512), BF16), row_block(256, 512)), (sds((rows, width), BF16), row_block(256))]
             + [(sds((width, rows), BF16), col_block(256)), (sds((rows, width), BF16), row_block(256))]
-            + [kept((1024, 768), BF16), kept((512, 1024), BF16)],
+            + [kept((1024, 768), BF16), kept((512, 1024), BF16), kept((16, 1024), F32), kept((1, 1536), F32)],
             2 * rows * 1024 * 1280,
             30e6,
             name="qkv",
@@ -740,10 +754,10 @@
                 + [const(w) for w in weights]
                 + [const(vec), (rows_in, row_block(256))]
                 + halves(cotangent, dy_other, 256),
-                blocks_of((256, 1024))
+                [(sds((n, 256, 1024), BF16), distant()) for n in (4, 2, 2)]
                 + [(sds((rows, width), BF16), row_block(256))] * 2
                 + [kept((8, 1024), F32)]
-                + [kept((1024, 1024), BF16)] * 2,
+                + [(sds((1024, 1024), BF16), distant())] * 2,
                 2 * rows * 1024 * 1024 * 4,
                 40e6,
                 scratch=[
@@ -753,7 +767,10 @@
                     pltpu.VMEM((rows, 1024), BF16),
                     pltpu.VMEM((8, 1024), F32),
                     pltpu.VMEM((1024, 512), BF16),
-                ],
+                ]
+                + [pltpu.VMEM((n, 256, 1024), BF16) for n in (4, 2, 2)]
+                + [pltpu.VMEM((1024, 1024), BF16)] * 2
+                + [pltpu.SemaphoreType.DMA((8,))],
                 name="mlp",
             )
             return results, hid, gp, sums, w_up_full, w_down_full
@@ -795,11 +812,14 @@
             [(ids, scalars()), const(attn_t)]
             + [(grad_a, spec((1, rows, 256), lambda n: (jnp.minimum(n, 2), 0, 0)))]
             + [(grad_b, spec((1, rows, 256), lambda n: (jnp.clip(n - 3, 0, 2), 0, 0)))]
-            + [const(value) for value in (att_a, att_b, cotangent, dy_other)],
+            + [(value, distant()) for value in (att_a, att_b, cotangent, dy_other)],
             blocks_of((128, 2048)) + [kept((8, 1536), F32)],
             2 * rows * 1024 * 2048,
             24e6,
-            scratch=[pltpu.VMEM((1024, 256), BF16)],
+            scratch=[pltpu.VMEM((1024, 256), BF16)]
+            + [pltpu.VMEM((rows, 256), BF16)] * 2
+            + [pltpu.VMEM((T, width), BF16)] * 2
+            + [pltpu.SemaphoreType.DMA((4,))],
             name="attn_weights",
         )
     blocks, grad_b = sync(blocks, grad_b)
@@ -823,7 +843,7 @@
             input_output_aliases={9 + n: n for n in range(len(previous))},
             cost_estimate=pl.CostEstimate(flops=0, bytes_accessed=14000000, transcendentals=0),
             compiler_params=pltpu.CompilerParams(
-                vmem_limit_bytes=VMEM_LIMIT, dimension_semantics=("arbitrary",)
+                vmem_limit_bytes=VMEM_NEED * MIB, dimension_semantics=("arbitrary",)
             ),
             name="adam_mlp",
         )(ids, *totals, w_up, m_up, v_up, w_down, m_down, v_down, *previous)
@@ -838,10 +858,10 @@
                 (T // 256,),
                 [(grad_a, lead), (grad, lead), (att_a, block(256)), (att_b, block(256))]
                 + [(value, block()) for value in (hid_a, hid_b, gp_a, gp_b)]
-                + [const(w) for w in (wq_a, wq_b, full_out, up_a, up_b, down_a, down_b)]
+                + [const(w) for w in (full_out, down_a, down_b, up_a, up_b, wq_a, wq_b)]
                 + [(rows_tok, row_block(256)), const(vec)]
-                + [(value, row_block(256)) for value in extra],
-                [(sds((T, width), t), row_block(256)) for t in outs] + [kept((8, width), F32)],
+                + extra,
+                outs + [kept((8, width), F32)],
                 2 * T * 1024 * 6144,
                 40e6,
                 name="back",
@@ -849,23 +869,29 @@
 
     reduce_a = reduce_fourth(reduce_a)
     reduce_b = reduce_third(reduce_b)
-    out_part, scaled_part, sums_other = back(False, grad_b, tok_other, [], (BF16, BF16))
-    out_part, scaled_part, sums_other, grad_b, reduce_a, reduce_b, reduce_o = sync(
-        out_part, scaled_part, sums_other, grad_b, reduce_a, reduce_b, reduce_o
-    )
+    pair_block = spec((2, 256, width), lambda i: (0, i, 0))
+    part_other, sums_other = back(False, grad_b, tok_other, [], [(sds((2, T, width), BF16), pair_block)])
+    part_other, sums_other, grad_b, reduce_a, reduce_b, reduce_o = sync(
+        part_other, sums_other, grad_b, reduce_a, reduce_b, reduce_o
+    )
+    reduce_o = reduce_second(reduce_o)
+    part_other, reduce_a, reduce_b, *ready = sync(part_other, reduce_a, reduce_b, *reduce_o[3:5])
     reduce_a = reduce_fifth(reduce_a)
-    reduce_o = reduce_second(reduce_o)
     reduce_b = reduce_fourth(reduce_b)
-    out_got, scaled_got = swap(out_part, 1, 0), swap(scaled_part, 1, 0)
+    part_got = swap(part_other, 1, 0)
     updated_mlp = adam_mlp(0, reduce_a, [])
-    updated_mlp, grad_b, reduce_b, reduce_o, out_got, scaled_got = sync(
-        updated_mlp, grad_b, reduce_b, reduce_o, out_got, scaled_got
+    updated_mlp, grad_b, reduce_b, reduce_o, part_got = sync(
+        updated_mlp, grad_b, reduce_b, reduce_o, part_got
     )
     reduce_o = reduce_third(reduce_o)
     reduce_b = reduce_fifth(reduce_b)
     grad_b, *ready = sync(grad_b, reduce_o[1], reduce_b[0])
     layer_out, tokens_grad, sums_own = back(
-        True, grad_b, tokens, [cotangent, out_got, scaled_got], (BF16, F32)
+        True,
+        grad_b,
+        tokens,
+        [(cotangent, row_block(256)), (part_got, pair_block)],
+        [(sds((T, width), BF16), row_block(256)), (sds((T, width), F32), row_block(256))],
     )
     sums_own, updated_mlp, reduce_b, reduce_o = sync(sums_own, updated_mlp, reduce_b, reduce_o)
     reduce_o = reduce_fourth(reduce_o)
@@ -893,8 +919,11 @@
             ],
             axis=0,
         )
-        for step in (2, 4):
-            total = total + swap(total, 0, step)
+        moved = [swap(total, 0, step) for step in (2, 4, 6)]
+        updated_mlp = adam_mlp(1, reduce_b, updated_mlp)
+        updated_mlp, reduce_o, total, moved = sync(updated_mlp, reduce_o, total, moved)
+        reduce_o = reduce_fifth(reduce_o)
+        total = functools.reduce(jnp.add, moved, total)
         across, beside, both = swap(total, 0, 1), swap(total, 2, 0), swap(total, 2, 1)
         total = (total + across) + (beside + both)
         bit = 4
@@ -907,9 +936,6 @@
             vectors, m_vectors, v_vectors, share, RATE_VECTOR, 0.0
         )
 
-    updated_mlp = adam_mlp(1, reduce_b, updated_mlp)
-    updated_mlp, reduce_o = sync(updated_mlp, reduce_o)
-    reduce_o = reduce_fifth(reduce_o)
     with jax.named_scope("adam"):
         wide = [spec((128, 1024), lambda n: (0, n))] * 3 + [whole((128, 1024))] * 3
         updated_attn = kernel_call(
@@ -920,7 +946,7 @@
             [sds((128, 3072), F32)] * 3 + [sds((128, 1024), F32)] * 3,
             0,
             13e6,
-            name="adam_attn",
+            name="adam",
         )(ids, *reduce_o, w_qkv, m_qkv, v_qkv, w_out, m_out, v_out)
     first_qkv, second_qkv, new_qkv, first_out, second_out, new_out = updated_attn
     first_up, second_up, new_up, first_down, second_down, new_down = updated_mlp

time: 401 us -> 391 us (0.975)
  Pallas kernels: 247 us -> 240 us
  local copies, waits for them, and re-layouts: 11.7 us -> 7.19 us
    pallas_call x12 -> x11, Pallas kernels: 221 us -> 214 us  [block_call(): kernel_call(body, grid, [place for _, place in ins], [place for _, place...]
    unnamed x97 -> x83, local copies, waits for them, and re-layouts: 7.33 us -> 2.82 us
    ppermute x56 -> x53, waiting for transfers between devices: 52.5 us -> 56.5 us  [move(): return lax.ppermute(value, AXES, pairs)]
    ppermute x56 -> x53, starting transfers between devices: 54.2 us -> 53 us  [move(): return lax.ppermute(value, AXES, pairs)]
  transfers between devices with their start and end apart: 56 -> 53, of which waited for: 15 -> 19; matrix products, arithmetic and copies ran while one was open for 7% -> 6% of each run, Pallas kernels for 60% -> 60%
where the time goes in v4:
time: 391 us; the launch traced here: 385 us
  Pallas kernels  240 us (61%)
  waiting for transfers between devices  56.5 us (14%)
  starting transfers between devices  53 us (14%)
  other arithmetic  26.4 us (7%)
  local copies, waits for them, and re-layouts  7.19 us (2%)
    pallas_call x11, Pallas kernels, block_call(): kernel_call(body, grid, [place for _, place in ins], [place for _, place...  214 us
    ppermute x53, waiting for transfers between devices, move(): return lax.ppermute(value, AXES, pairs)  56.5 us
    ppermute x53, starting transfers between devices, move(): return lax.ppermute(value, AXES, pairs)  53 us
    pallas_call x2, Pallas kernels, adam_mlp(): pl.pallas_call(adam_mlp_body, grid=(8,), in_specs=[scalars()] + [whole((2...  18.2 us
    pallas_call x1, Pallas kernels, on_device(): kernel_call(adam_attn_body, (3,), [scalars()] + [whole((128, 2048))] * 2...  8.1 us
  transfers between devices with their start and end apart: 53, of which 19 were waited for; matrix products, arithmetic and copies ran while one was open for 6% of the time, Pallas kernels for 60%

profile of v4, /device:TPU:0, one launch (start us, length us, event | category | flops | bytes accessed | tf_op | source)
XLA Modules:
  0.0 384.8 jit_solution(12421829834904401157)
XLA Ops:
  1.3 2.5 prep_attn.1.refs_0_
  3.8 2.9 collective-permute-start.2
  6.8 2.6 collective-permute-start.1
  9.4 1.6 collective-permute-start
  12.1 3.9 %prep_mlp.1 = (bf16[256,1024]{1,0:T(8,128)(2,1)}, bf16[352,1024]{1,0:T(8,128)(2,1)}) custom-call(s32[3]{0:T(128)} %pad_add_fusion.4.ids, f32[128,4096]{1,0:T(8,128)} %refs_0_.4, f32[512,1024]{1,0:T(8,128)} %refs_3_.4, f32[128,3072]{1,0:T(8,128)} %refs_0_.5), custom_call_target="tpu_custom_call" | custom-call | bytes 6000000 | tf_op jit(solution)/shard_map/prep/prep_mlp/pallas_call | solution.py:615
  17.4 3.8 fusion.5
  22.3 1.4 pad_maximum_fusion
  23.7 2.3 collective-permute-done.1.refs_2_
  26.7 3.3 collective-permute-start.7
  30.0 8.0 %collective-permute-done.4.refs_5_ = bf16[144,1280]{1,0:T(8,128)(2,1)S(1)} collective-permute-done((bf16[144,1280]{1,0:T(8,128)(2,1)}, bf16[144,1280]{1,0:T(8,128)(2,1)S(1)}, u32[]{:S(2)}, u32[]{:S(2)}) %collective-permute-start.4) | collective-permute-done | bytes 368672 | tf_op jit(solution)/shard_map/gather/ppermute | solution.py:568
  39.3 7.4 %collective-permute-done.7.refs_7_ = bf16[144,1280]{1,0:T(8,128)(2,1)S(1)} collective-permute-done((bf16[144,1280]{1,0:T(8,128)(2,1)}, bf16[144,1280]{1,0:T(8,128)(2,1)S(1)}, u32[]{:S(2)}, u32[]{:S(2)}) %collective-permute-start.7) | collective-permute-done | bytes 368672 | tf_op jit(solution)/shard_map/gather/ppermute | solution.py:568
  48.6 8.0 %collective-permute-done.5.refs_6_ = bf16[144,1280]{1,0:T(8,128)(2,1)S(1)} collective-permute-done((bf16[144,1280]{1,0:T(8,128)(2,1)}, bf16[144,1280]{1,0:T(8,128)(2,1)S(1)}, u32[]{:S(2)}, u32[]{:S(2)}) %collective-permute-start.5) | collective-permute-done | bytes 368672 | tf_op jit(solution)/shard_map/gather/ppermute | solution.py:568
  56.6 3.0 collective-permute-done.9.refs_2_
  59.6 8.0 %collective-permute-done.8.refs_1_ = bf16[256,1024]{1,0:T(8,128)(2,1)} collective-permute-done((bf16[256,1024]{1,0:T(8,128)(2,1)S(1)}, bf16[256,1024]{1,0:T(8,128)(2,1)}, u32[]{:S(2)}, u32[]{:S(2)}) %collective-permute-start.8) | collective-permute-done | bytes 524320 | tf_op jit(solution)/shard_map/gather/ppermute | solution.py:568
  68.6 2.6 collective-permute-start.15
  71.1 1.5 collective-permute-start.13
  74.6 17.0 %qkv.2 = (bf16[2048,256]{1,0:T(8,128)(2,1)}, bf16[2048,256]{1,0:T(8,128)(2,1)}, bf16[2048,256]{1,0:T(8,128)(2,1)}, bf16[2048,512]{1,0:T(8,128)(2,1)}, bf16[2048,...) custom-call(s32[3]{0:T(128)} %pad_add_fusion.4.ids, ...), custom_call_target="tpu_custom_call" | custom-call | flops 5368709120 | bytes 30000000 | tf_op jit(solution)/shard_map/qkv/qkv/pallas_call | solution.py:615
  91.7 2.5 collective-permute-done.12.refs_6_
  94.1 6.1 %collective-permute-done.16.refs_2_ = bf16[352,1024]{1,0:T(8,128)(2,1)S(1)} collective-permute-done((bf16[352,1024]{1,0:T(8,128)(2,1)S(1)}, bf16[352,1024]{1,0:T(8,128)(2,1)S(1)}, u32[]{:S(2)}, u32[]{:S(2)}) %collective-permute-start.16) | collective-permute-done | bytes 720928 | tf_op jit(solution)/shard_map/gather/ppermute | solution.py:568
  100.4 1.6 collective-permute-start.19
  102.1 2.0 collective-permute-start.17
  104.5 27.7 %attention.2 = (bf16[2048,256]{1,0:T(8,128)(2,1)}, bf16[3,2048,256]{2,1,0:T(8,128)(2,1)}) custom-call(bf16[2048,256]{1,0:T(8,128)(2,1)} %get-tuple-element.235.q, bf16[2048,256]{1,0:T(8,128)(2,1)} %get-tuple-element.236.k, bf16[2048,256]{1,0:T(8,128)(2,1)} %get-tuple-element.237.v, bf16[2048,512]{1,0:T(8,128)(2,1)} %get-tuple-element.238.d_att, ...), custom_call_target="tpu_custom_call" | custom-call | flops 30000001024 | bytes 10000000 | tf_op jit(solution)/shard_map/attention/attention/pallas_call | solution.py:615
  133.0 1.5 collective-permute-start.21
  135.1 27.8 %mlp.2 = (bf16[4,256,1024]{2,1,0:T(8,128)(2,1)}, bf16[2,256,1024]{2,1,0:T(8,128)(2,1)}, bf16[2,256,1024]{2,1,0:T(8,128)(2,1)}, bf16[2048,1024]{1,0:T(8,128)(2,1)...) custom-call(s32[3]{0:T(128)} %pad_add_fusion.4.ids, ...), custom_call_target="tpu_custom_call" | custom-call | flops 17179869184 | bytes 40000000 | tf_op jit(solution)/shard_map/mlp/mlp/pallas_call | solution.py:615
  162.9 2.3 collective-permute-done.22.refs_5_
  167.8 28.4 %mlp.3 = (bf16[4,256,1024]{2,1,0:T(8,128)(2,1)}, bf16[2,256,1024]{2,1,0:T(8,128)(2,1)}, bf16[2,256,1024]{2,1,0:T(8,128)(2,1)}, bf16[2048,1024]{1,0:T(8,128)(2,1)...) custom-call(s32[3]{0:T(128)} %pad_add_fusion.4.ids, ...), custom_call_target="tpu_custom_call" | custom-call | flops 17179869184 | bytes 40000000 | tf_op jit(solution)/shard_map/mlp/mlp/pallas_call | solution.py:615
  196.2 1.4 fusion.12
  199.7 1.7 collective-permute-start.29
  201.4 9.6 %qkv.3 = (bf16[2048,256]{1,0:T(8,128)(2,1)}, bf16[2048,256]{1,0:T(8,128)(2,1)}, bf16[2048,256]{1,0:T(8,128)(2,1)}, bf16[1024,768]{1,0:T(8,128)(2,1)}) custom-call(s32[3]{0:T(128)} %pad_add_fusion.4.ids, bf16[352,1024]{1,0:T(8,128)(2,1)} %get-tuple-element.251.refs_0_, bf16[352,1024]{1,0:T(8,128)(2,1)} %copy-done.15, bf16[352,1024]{1,0:T(8,128)(2,1)} %copy-done.14, ...), custom_call_target="tpu_custom_call" | custom-call | flops 3221225472 | bytes 12000000 | tf_op jit(solution)/shard_map/qkv/qkv/pallas_call | solution.py:615
  211.0 27.8 %attention.3 = (bf16[2048,256]{1,0:T(8,128)(2,1)}, bf16[3,2048,256]{2,1,0:T(8,128)(2,1)}) custom-call(bf16[2048,256]{1,0:T(8,128)(2,1)} %get-tuple-element.291.q, bf16[2048,256]{1,0:T(8,128)(2,1)} %get-tuple-element.292.k, bf16[2048,256]{1,0:T(8,128)(2,1)} %get-tuple-element.293.v, bf16[2048,512]{1,0:T(8,128)(2,1)} %get-tuple-element.238.d_att, ...), custom_call_target="tpu_custom_call" | custom-call | flops 30000001024 | bytes 10000000 | tf_op jit(solution)/shard_map/attention/attention/pallas_call | solution.py:615
  238.8 3.1 fusion.4
  241.9 3.0 collective-permute-start.30
  247.0 20.3 %attn_weights.1 = (bf16[4,128,2048]{2,1,0:T(8,128)(2,1)}, bf16[2,128,2048]{2,1,0:T(8,128)(2,1)}, bf16[2,128,2048]{2,1,0:T(8,128)(2,1)}, f32[8,1536]{1,0:T(8,128)}) custom-call(s32[3]{0:T(128)} %pad_add_fusion.4.ids, bf16[1024,2048]{1,0:T(8,128)(2,1)} %get-tuple-element.250.attn_t, bf16[3,2048,256]{2,1,0:T(8,128)(2,1)} %get-tuple-element.249.grad_a, ...), custom_call_target="tpu_custom_call" | custom-call | flops 8589934592 | bytes 24000000 | tf_op jit(solution)/shard_map/attn_weights/attn_weights/pallas_call | solution.py:615
  272.2 2.1 fusion.1
  274.4 2.0 collective-permute-start.34
  276.3 23.1 %back.2 = (bf16[2,1024,1024]{2,1,0:T(8,128)(2,1)}, f32[8,1024]{1,0:T(8,128)}) custom-call(bf16[3,2048,256]{2,1,0:T(8,128)(2,1)} %get-tuple-element.249.grad_a, bf16[3,2048,256]{2,1,0:T(8,128)(2,1)} %get-tuple-element.357.grad_b, bf16[2048,256]{1,0:T(8,128)(2,1)} %get-tuple-element.307.far_att_a.att_a, bf16[2048,256]{1,0:T(8,128)(2,1)} %get-tuple-element.308.far_att_b.att_b, ...), custom_call_target="tpu_custom_call" | custom-call | flops 12884901888 | bytes 40000000 | tf_op jit(solution)/shard_map/back/back/pallas_call | solution.py:615
  300.5 2.8 fusion.16
  303.5 1.7 collective-permute-start.40
  309.7 1.7 collective-permute-done.37.other
  311.4 9.1 %adam_mlp.2 = (f32[128,4096]{1,0:T(8,128)}, f32[128,4096]{1,0:T(8,128)}, f32[128,4096]{1,0:T(8,128)}, f32[512,1024]{1,0:T(8,128)}, f32[512,1024]{1,0:T(8,128)}, /*index=5*/f32[512,1024]{1,0:T(8,128)}) custom-call(s32[3]{0:T(128)} %pad_add_fusion.4.ids, bf16[256,1024]{1,0:T(8,128)(2,1)} %copy-done.7, bf16[256,1024]{1,0:T(8,128)(2,1)} %collective-permute-done.37.other, ...), custom_call_target="tpu_custom_call" | custom-call | bytes 14000000 | tf_op jit(solution)/shard_map/adam_mlp/pallas_call | solution.py:834
  322.5 1.9 bitcast_add_fusion
  325.2 25.7 %back.3 = (bf16[1024,1024]{1,0:T(8,128)(2,1)}, f32[1024,1024]{1,0:T(8,128)}, f32[8,1024]{1,0:T(8,128)}) custom-call(bf16[3,2048,256]{2,1,0:T(8,128)(2,1)} %get-tuple-element.249.grad_a, bf16[3,2048,256]{2,1,0:T(8,128)(2,1)} %get-tuple-element.357.grad_b, bf16[2048,256]{1,0:T(8,128)(2,1)} %get-tuple-element.307.far_att_a.att_a, ...), custom_call_target="tpu_custom_call" | custom-call | flops 12884901888 | bytes 40000000 | tf_op jit(solution)/shard_map/back/back/pallas_call | solution.py:615
  353.5 2.4 collective-permute-start.47
  355.9 2.0 collective-permute-start.45
  357.9 9.0 %adam_mlp.3 = (f32[128,4096]{1,0:T(8,128)}, f32[128,4096]{1,0:T(8,128)}, f32[128,4096]{1,0:T(8,128)}, f32[512,1024]{1,0:T(8,128)}, f32[512,1024]{1,0:T(8,128)}, /*index=5*/f32[512,1024]{1,0:T(8,128)}) custom-call(s32[3]{0:T(128)} %pad_add_fusion.4.ids, ...), custom_call_target="tpu_custom_call", output_to_operand_aliasing={{0}: (9, {}), {1}: (10, {}), {2}: (11, {}), {3}: (12, {}), ... | custom-call | bytes 14000000 | tf_op jit(solution)/shard_map/vectors/adam_mlp/pallas_call | solution.py:834
  367.1 1.6 collective-permute-start.51
  370.8 1.8 collective-permute-done.51
  376.5 8.1 %adam.1 = (f32[128,3072]{1,0:T(8,128)}, f32[128,3072]{1,0:T(8,128)}, f32[128,3072]{1,0:T(8,128)}, f32[128,1024]{1,0:T(8,128)}, f32[128,1024]{1,0:T(8,128)}, /*index=5*/f32[128,1024]{1,0:T(8,128)}) custom-call(s32[3]{0:T(128)} %pad_add_fusion.4.ids, bf16[128,2048]{1,0:T(8,128)(2,1)} %copy-done.6, bf16[128,2048]{1,0:T(8,128)(2,1)} %copy-done.24, ...), custom_call_target="tpu_custom_call" | custom-call | bytes 13000000 | tf_op jit(solution)/shard_map/adam/adam/pallas_call | solution.py:941
  (211 shorter events, 41.4 us)
Async XLA Ops:
  3.8 19.9 %collective-permute-start.2 = (bf16[144,1280]{1,0:T(8,128)(2,1)}, bf16[144,1280]{1,0:T(8,128)(2,1)}, u32[]{:S(2)}, u32[]{:S(2)}) collective-permute-start(bf16[144,1280]{1,0:T(8,128)(2,1)} %prep_attn.1.refs_0_), channel_id=1, source_target_pairs={{0,1},{1,0},{2,3},{3,2},{4,5},{5,4},{6,7},{7,6},{8,9},{9,8},{10,11... | collective-permute-start | bytes 1105928 | tf_op jit(solution)/shard_map/gather/ppermute | solution.py:568
  6.8 19.3 %collective-permute-start.1 = (bf16[144,1280]{1,0:T(8,128)(2,1)}, bf16[144,1280]{1,0:T(8,128)(2,1)}, u32[]{:S(2)}, u32[]{:S(2)}) collective-permute-start(bf16[144,1280]{1,0:T(8,128)(2,1)} %prep_attn.1.refs_0_), channel_id=1, source_target_pairs={{0,4},{1,5},{2,6},{3,7},{4,0},{5,1},{6,2},{7,3},{8,12},{9,13},{10,... | collective-permute-start | bytes 1105928 | tf_op jit(solution)/shard_map/gather/ppermute | solution.py:568
  9.4 16.9 %collective-permute-start = (bf16[144,1280]{1,0:T(8,128)(2,1)}, bf16[144,1280]{1,0:T(8,128)(2,1)}, u32[]{:S(2)}, u32[]{:S(2)}) collective-permute-start(bf16[144,1280]{1,0:T(8,128)(2,1)} %prep_attn.1.refs_0_), channel_id=1, source_target_pairs={{0,2},{1,3},{2,0},{3,1},{4,6},{5,7},{6,4},{7,5},{8,10},{9,11},{10,... | collective-permute-start | bytes 1105928 | tf_op jit(solution)/shard_map/gather/ppermute | solution.py:568
  10.9 5.1 %collective-permute-start.3 = (s32[1024]{0:T(1024)S(1)}, s32[1024]{0:T(1024)S(1)}, u32[]{:S(2)}, u32[]{:S(2)}) collective-permute-start(s32[1024]{0:T(1024)S(1)} %copy-done.25), channel_id=1, source_target_pairs={{0,8},{1,9},{2,10},{3,11},{4,12},{5,13},{6,14},{7,15},{8,0},{9,1},... | collective-permute-start | bytes 12296 | tf_op jit(solution)/shard_map/gather/ppermute | solution.py:568
  10.9 56.7 %collective-permute-start.10 = (bf16[1024,1024]{1,0:T(8,128)(2,1)S(1)}, bf16[1024,1024]{1,0:T(8,128)(2,1)}, u32[]{:S(2)}, u32[]{:S(2)}) collective-permute-start(bf16[1024,1024]{1,0:T(8,128)(2,1)S(1)} %copy-done.31), channel_id=1, source_target_pairs={{0,8},{1,9},{2,10},{3,11},{4,12},{5,13},{6,14},{7,15},{8,0},{9,1},... | collective-permute-start | bytes 6291464 | tf_op jit(solution)/shard_map/gather/ppermute | solution.py:568
  16.1 51.6 %collective-permute-start.11 = (bf16[1024,1024]{1,0:T(8,128)(2,1)}, bf16[1024,1024]{1,0:T(8,128)(2,1)}, u32[]{:S(2)}, u32[]{:S(2)}) collective-permute-start(bf16[1024,1024]{1,0:T(8,128)(2,1)} %refs_9_.1), channel_id=1, source_target_pairs={{0,8},{1,9},{2,10},{3,11},{4,12},{5,13},{6,14},{7,15},{8,0},{9,1},... | collective-permute-start | bytes 6291464 | tf_op jit(solution)/shard_map/gather/ppermute | solution.py:568
  26.2 11.7 %collective-permute-start.4 = (bf16[144,1280]{1,0:T(8,128)(2,1)}, bf16[144,1280]{1,0:T(8,128)(2,1)S(1)}, u32[]{:S(2)}, u32[]{:S(2)}) collective-permute-start(bf16[144,1280]{1,0:T(8,128)(2,1)} %collective-permute-done.refs_1_), channel_id=1, source_target_pairs={{0,1},{1,0},{2,3},{3,2},{4,5},{5,4},{6,7},{7,6},{8,9},{9,8},{10,11... | collective-permute-start | bytes 1105928 | tf_op jit(solution)/shard_map/gather/ppermute | solution.py:568
  26.7 20.0 %collective-permute-start.7 = (bf16[144,1280]{1,0:T(8,128)(2,1)}, bf16[144,1280]{1,0:T(8,128)(2,1)S(1)}, u32[]{:S(2)}, u32[]{:S(2)}) collective-permute-start(bf16[144,1280]{1,0:T(8,128)(2,1)} %collective-permute-done.1.refs_2_), channel_id=1, source_target_pairs={{0,17},{1,16},{2,19},{3,18},{4,21},{5,20},{6,23},{7,22},{8,25},{9,... | collective-permute-start | bytes 1105928 | tf_op jit(solution)/shard_map/gather/ppermute | solution.py:568
  30.0 18.1 %collective-permute-start.6 = (bf16[144,1280]{1,0:T(8,128)(2,1)}, bf16[144,1280]{1,0:T(8,128)(2,1)S(1)}, u32[]{:S(2)}, u32[]{:S(2)}) collective-permute-start(bf16[144,1280]{1,0:T(8,128)(2,1)} %collective-permute-done.1.refs_2_), channel_id=1, source_target_pairs={{0,16},{1,17},{2,18},{3,19},{4,20},{5,21},{6,22},{7,23},{8,24},{9,... | collective-permute-start | bytes 1105928 | tf_op jit(solution)/shard_map/gather/ppermute | solution.py:568
  38.0 21.7 %collective-permute-start.9 = (bf16[256,1024]{1,0:T(8,128)(2,1)S(1)}, bf16[256,1024]{1,0:T(8,128)(2,1)}, u32[]{:S(2)}, u32[]{:S(2)}) collective-permute-start(bf16[256,1024]{1,0:T(8,128)(2,1)S(1)} %copy-done.32), channel_id=1, source_target_pairs={{0,4},{1,5},{2,6},{3,7},{4,0},{5,1},{6,2},{7,3},{8,12},{9,13},{10,... | collective-permute-start | bytes 1572872 | tf_op jit(solution)/shard_map/gather/ppermute | solution.py:568
  46.7 20.9 %collective-permute-start.8 = (bf16[256,1024]{1,0:T(8,128)(2,1)S(1)}, bf16[256,1024]{1,0:T(8,128)(2,1)}, u32[]{:S(2)}, u32[]{:S(2)}) collective-permute-start(bf16[256,1024]{1,0:T(8,128)(2,1)S(1)} %copy-done.32), channel_id=1, source_target_pairs={{0,2},{1,3},{2,0},{3,1},{4,6},{5,7},{6,4},{7,5},{8,10},{9,11},{10,... | collective-permute-start | bytes 1572872 | tf_op jit(solution)/shard_map/gather/ppermute | solution.py:568
  48.1 8.5 %collective-permute-start.5 = (bf16[144,1280]{1,0:T(8,128)(2,1)}, bf16[144,1280]{1,0:T(8,128)(2,1)S(1)}, u32[]{:S(2)}, u32[]{:S(2)}) collective-permute-start(bf16[144,1280]{1,0:T(8,128)(2,1)} %collective-permute-done.1.refs_2_), channel_id=1, source_target_pairs={{0,1},{1,0},{2,3},{3,2},{4,5},{5,4},{6,7},{7,6},{8,9},{9,8},{10,11... | collective-permute-start | bytes 1105928 | tf_op jit(solution)/shard_map/gather/ppermute | solution.py:568
  67.7 32.6 %collective-permute-start.16 = (bf16[352,1024]{1,0:T(8,128)(2,1)S(1)}, bf16[352,1024]{1,0:T(8,128)(2,1)S(1)}, u32[]{:S(2)}, u32[]{:S(2)}) collective-permute-start(bf16[352,1024]{1,0:T(8,128)(2,1)S(1)} %copy-done.13), channel_id=1, source_target_pairs={{0,4},{1,5},{2,6},{3,7},{4,0},{5,1},{6,2},{7,3},{8,12},{9,13},{10,... | collective-permute-start | bytes 2162696 | tf_op jit(solution)/shard_map/gather/ppermute | solution.py:568
  68.6 31.9 %collective-permute-start.15 = (bf16[352,1024]{1,0:T(8,128)(2,1)S(1)}, bf16[352,1024]{1,0:T(8,128)(2,1)S(1)}, u32[]{:S(2)}, u32[]{:S(2)}) collective-permute-start(bf16[352,1024]{1,0:T(8,128)(2,1)S(1)} %copy-done.13), channel_id=1, source_target_pairs={{0,2},{1,3},{2,0},{3,1},{4,6},{5,7},{6,4},{7,5},{8,10},{9,11},{10,... | collective-permute-start | bytes 2162696 | tf_op jit(solution)/shard_map/gather/ppermute | solution.py:568
  71.1 20.5 %collective-permute-start.13 = (bf16[256,1024]{1,0:T(8,128)(2,1)}, bf16[256,1024]{1,0:T(8,128)(2,1)S(1)}, u32[]{:S(2)}, u32[]{:S(2)}) collective-permute-start(bf16[256,1024]{1,0:T(8,128)(2,1)} %collective-permute-done.8.refs_1_), channel_id=1, source_target_pairs={{0,1},{1,0},{2,3},{3,2},{4,5},{5,4},{6,7},{7,6},{8,9},{9,8},{10,11... | collective-permute-start | bytes 1572872 | tf_op jit(solution)/shard_map/gather/ppermute | solution.py:568
  72.6 19.0 %collective-permute-start.14 = (bf16[256,1024]{1,0:T(8,128)(2,1)}, bf16[256,1024]{1,0:T(8,128)(2,1)}, u32[]{:S(2)}, u32[]{:S(2)}) collective-permute-start(bf16[256,1024]{1,0:T(8,128)(2,1)} %collective-permute-done.9.refs_2_), channel_id=1, source_target_pairs={{0,16},{1,17},{2,18},{3,19},{4,20},{5,21},{6,22},{7,23},{8,24},{9,... | collective-permute-start | bytes 1572872 | tf_op jit(solution)/shard_map/gather/ppermute | solution.py:568
  72.6 21.5 %collective-permute-start.12 = (bf16[256,1024]{1,0:T(8,128)(2,1)}, bf16[256,1024]{1,0:T(8,128)(2,1)}, u32[]{:S(2)}, u32[]{:S(2)}) collective-permute-start(bf16[256,1024]{1,0:T(8,128)(2,1)} %collective-permute-done.9.refs_2_), channel_id=1, source_target_pairs={{0,1},{1,0},{2,3},{3,2},{4,5},{5,4},{6,7},{7,6},{8,9},{9,8},{10,11... | collective-permute-start | bytes 1572872 | tf_op jit(solution)/shard_map/gather/ppermute | solution.py:568
  100.4 31.8 %collective-permute-start.20 = (bf16[352,1024]{1,0:T(8,128)(2,1)S(1)}, bf16[352,1024]{1,0:T(8,128)(2,1)S(1)}, u32[]{:S(2)}, u32[]{:S(2)}) collective-permute-start(bf16[352,1024]{1,0:T(8,128)(2,1)S(1)} %collective-permute-done.16.refs_2_), channel_id=1, source_target_pairs={{0,16},{1,17},{2,18},{3,19},{4,20},{5,21},{6,22},{7,23},{8,24},{9,... | collective-permute-start | bytes 2162696 | tf_op jit(solution)/shard_map/gather/ppermute | solution.py:568
  100.4 31.8 %collective-permute-start.19 = (bf16[352,1024]{1,0:T(8,128)(2,1)S(1)}, bf16[352,1024]{1,0:T(8,128)(2,1)S(1)}, u32[]{:S(2)}, u32[]{:S(2)}) collective-permute-start(bf16[352,1024]{1,0:T(8,128)(2,1)S(1)} %collective-permute-done.16.refs_2_), channel_id=1, source_target_pairs={{0,1},{1,0},{2,3},{3,2},{4,5},{5,4},{6,7},{7,6},{8,9},{9,8},{10,11... | collective-permute-start | bytes 2162696 | tf_op jit(solution)/shard_map/gather/ppermute | solution.py:568
  102.1 30.1 %collective-permute-start.17 = (bf16[256,1024]{1,0:T(8,128)(2,1)}, bf16[256,1024]{1,0:T(8,128)(2,1)S(1)}, u32[]{:S(2)}, u32[]{:S(2)}) collective-permute-start(bf16[256,1024]{1,0:T(8,128)(2,1)} %collective-permute-done.12.refs_6_), channel_id=1, source_target_pairs={{0,16},{1,17},{2,18},{3,19},{4,20},{5,21},{6,22},{7,23},{8,24},{9,... | collective-permute-start | bytes 1572872 | tf_op jit(solution)/shard_map/gather/ppermute | solution.py:568
  104.0 28.2 %collective-permute-start.18 = (bf16[256,1024]{1,0:T(8,128)(2,1)S(1)}, bf16[256,1024]{1,0:T(8,128)(2,1)S(1)}, u32[]{:S(2)}, u32[]{:S(2)}) collective-permute-start(bf16[256,1024]{1,0:T(8,128)(2,1)S(1)} %copy-done.33), channel_id=1, source_target_pairs={{0,1},{1,0},{2,3},{3,2},{4,5},{5,4},{6,7},{7,6},{8,9},{9,8},{10,11... | collective-permute-start | bytes 1572872 | tf_op jit(solution)/shard_map/gather/ppermute | solution.py:568
  133.0 29.9 %collective-permute-start.21 = (bf16[352,1024]{1,0:T(8,128)(2,1)S(1)}, bf16[352,1024]{1,0:T(8,128)(2,1)S(1)}, u32[]{:S(2)}, u32[]{:S(2)}) collective-permute-start(bf16[352,1024]{1,0:T(8,128)(2,1)S(1)} %copy-done.13), channel_id=1, source_target_pairs={{0,1},{1,0},{2,3},{3,2},{4,5},{5,4},{6,7},{7,6},{8,9},{9,8},{10,11... | collective-permute-start | bytes 2162696 | tf_op jit(solution)/shard_map/gather/ppermute | solution.py:568
  134.5 30.6 %collective-permute-start.22 = (bf16[352,1024]{1,0:T(8,128)(2,1)S(1)}, bf16[352,1024]{1,0:T(8,128)(2,1)S(1)}, u32[]{:S(2)}, u32[]{:S(2)}) collective-permute-start(bf16[352,1024]{1,0:T(8,128)(2,1)S(1)} %collective-permute-done.15.refs_1_), channel_id=1, source_target_pairs={{0,1},{1,0},{2,3},{3,2},{4,5},{5,4},{6,7},{7,6},{8,9},{9,8},{10,11... | collective-permute-start | bytes 2162696 | tf_op jit(solution)/shard_map/gather/ppermute | solution.py:568
  135.0 30.2 %collective-permute-start.23 = (bf16[352,1024]{1,0:T(8,128)(2,1)S(1)}, bf16[352,1024]{1,0:T(8,128)(2,1)S(1)}, u32[]{:S(2)}, u32[]{:S(2)}) collective-permute-start(bf16[352,1024]{1,0:T(8,128)(2,1)S(1)} %collective-permute-done.19.refs_6_), channel_id=1, source_target_pairs={{0,16},{1,17},{2,18},{3,19},{4,20},{5,21},{6,22},{7,23},{8,24},{9,... | collective-permute-start | bytes 2162696 | tf_op jit(solution)/shard_map/gather/ppermute | solution.py:568
  166.3 29.9 %collective-permute-start.24 = (bf16[2,256,1024]{2,1,0:T(8,128)(2,1)}, bf16[2,256,1024]{2,1,0:T(8,128)(2,1)S(1)}, u32[]{:S(2)}, u32[]{:S(2)}) collective-permute-start(bf16[2,256,1024]{2,1,0:T(8,128)(2,1)} %get-tuple-element.282), channel_id=1, source_target_pairs={{0,1},{1,0},{2,3},{3,2},{4,5},{5,4},{6,7},{7,6},{8,9},{9,8},{10,11... | collective-permute-start | bytes 3145736 | tf_op jit(solution)/shard_map/ppermute | solution.py:568
  167.4 28.8 %collective-permute-start.25 = (bf16[2,256,1024]{2,1,0:T(8,128)(2,1)}, bf16[2,256,1024]{2,1,0:T(8,128)(2,1)S(1)}, u32[]{:S(2)}, u32[]{:S(2)}) collective-permute-start(bf16[2,256,1024]{2,1,0:T(8,128)(2,1)} %get-tuple-element.283), channel_id=1, source_target_pairs={{0,16},{1,17},{2,18},{3,19},{4,20},{5,21},{6,22},{7,23},{8,24},{9,... | collective-permute-start | bytes 3145736 | tf_op jit(solution)/shard_map/ppermute | solution.py:568
  197.7 41.1 %collective-permute-start.27 = (bf16[256,1024]{1,0:T(8,128)(2,1)}, bf16[256,1024]{1,0:T(8,128)(2,1)S(1)}, u32[]{:S(2)}, u32[]{:S(2)}) collective-permute-start(bf16[256,1024]{1,0:T(8,128)(2,1)} %get-tuple-element.420), channel_id=1, source_target_pairs={{0,2},{1,3},{2,0},{3,1},{4,6},{5,7},{6,4},{7,5},{8,10},{9,11},{10,... | collective-permute-start | bytes 1572872 | tf_op jit(solution)/shard_map/ppermute | solution.py:568
  197.7 41.1 %collective-permute-start.26 = (bf16[256,1024]{1,0:T(8,128)(2,1)}, bf16[256,1024]{1,0:T(8,128)(2,1)}, u32[]{:S(2)}, u32[]{:S(2)}) collective-permute-start(bf16[256,1024]{1,0:T(8,128)(2,1)} %get-tuple-element.421), channel_id=1, source_target_pairs={{0,1},{1,0},{2,3},{3,2},{4,5},{5,4},{6,7},{7,6},{8,9},{9,8},{10,11... | collective-permute-start | bytes 1572872 | tf_op jit(solution)/shard_map/ppermute | solution.py:568
  198.5 40.3 %collective-permute-start.28 = (bf16[2,256,1024]{2,1,0:T(8,128)(2,1)}, bf16[2,256,1024]{2,1,0:T(8,128)(2,1)S(1)}, u32[]{:S(2)}, u32[]{:S(2)}) collective-permute-start(bf16[2,256,1024]{2,1,0:T(8,128)(2,1)} %get-tuple-element.297), channel_id=1, source_target_pairs={{0,1},{1,0},{2,3},{3,2},{4,5},{5,4},{6,7},{7,6},{8,9},{9,8},{10,11... | collective-permute-start | bytes 3145736 | tf_op jit(solution)/shard_map/ppermute | solution.py:568
  199.7 39.1 %collective-permute-start.29 = (bf16[2,256,1024]{2,1,0:T(8,128)(2,1)}, bf16[2,256,1024]{2,1,0:T(8,128)(2,1)S(1)}, u32[]{:S(2)}, u32[]{:S(2)}) collective-permute-start(bf16[2,256,1024]{2,1,0:T(8,128)(2,1)} %get-tuple-element.298), channel_id=1, source_target_pairs={{0,16},{1,17},{2,18},{3,19},{4,20},{5,21},{6,22},{7,23},{8,24},{9,... | collective-permute-start | bytes 3145736 | tf_op jit(solution)/shard_map/ppermute | solution.py:568
  241.9 27.8 %collective-permute-start.30 = (bf16[256,1024]{1,0:T(8,128)(2,1)}, bf16[256,1024]{1,0:T(8,128)(2,1)}, u32[]{:S(2)}, u32[]{:S(2)}) collective-permute-start(bf16[256,1024]{1,0:T(8,128)(2,1)} %fusion.4), channel_id=1, source_target_pairs={{0,4},{1,5},{2,6},{3,7},{4,0},{5,1},{6,2},{7,3},{8,12},{9,13},{10,... | collective-permute-start | bytes 1572872 | tf_op jit(solution)/shard_map/ppermute | solution.py:568
  246.3 25.9 %collective-permute-start.32 = (bf16[256,1024]{1,0:T(8,128)(2,1)}, bf16[256,1024]{1,0:T(8,128)(2,1)}, u32[]{:S(2)}, u32[]{:S(2)}) collective-permute-start(bf16[256,1024]{1,0:T(8,128)(2,1)} %get-tuple-element.418), channel_id=1, source_target_pairs={{0,2},{1,3},{2,0},{3,1},{4,6},{5,7},{6,4},{7,5},{8,10},{9,11},{10,... | collective-permute-start | bytes 1572872 | tf_op jit(solution)/shard_map/ppermute | solution.py:568
  246.3 25.9 %collective-permute-start.33 = (bf16[256,1024]{1,0:T(8,128)(2,1)}, bf16[256,1024]{1,0:T(8,128)(2,1)}, u32[]{:S(2)}, u32[]{:S(2)}) collective-permute-start(bf16[256,1024]{1,0:T(8,128)(2,1)} %get-tuple-element.419), channel_id=1, source_target_pairs={{0,1},{1,0},{2,3},{3,2},{4,5},{5,4},{6,7},{7,6},{8,9},{9,8},{10,11... | collective-permute-start | bytes 1572872 | tf_op jit(solution)/shard_map/ppermute | solution.py:568
  267.3 33.2 %collective-permute-start.35 = (bf16[2,128,2048]{2,1,0:T(8,128)(2,1)}, bf16[2,128,2048]{2,1,0:T(8,128)(2,1)S(1)}, u32[]{:S(2)}, u32[]{:S(2)}) collective-permute-start(bf16[2,128,2048]{2,1,0:T(8,128)(2,1)} %get-tuple-element.329), channel_id=1, source_target_pairs={{0,1},{1,0},{2,3},{3,2},{4,5},{5,4},{6,7},{7,6},{8,9},{9,8},{10,11... | collective-permute-start | bytes 3145736 | tf_op jit(solution)/shard_map/ppermute | solution.py:568
  268.7 31.8 %collective-permute-start.36 = (bf16[2,128,2048]{2,1,0:T(8,128)(2,1)}, bf16[2,128,2048]{2,1,0:T(8,128)(2,1)}, u32[]{:S(2)}, u32[]{:S(2)}) collective-permute-start(bf16[2,128,2048]{2,1,0:T(8,128)(2,1)} %get-tuple-element.330), channel_id=1, source_target_pairs={{0,16},{1,17},{2,18},{3,19},{4,20},{5,21},{6,22},{7,23},{8,24},{9,... | collective-permute-start | bytes 3145736 | tf_op jit(solution)/shard_map/ppermute | solution.py:568
  271.1 29.4 %collective-permute-start.31 = (bf16[256,1024]{1,0:T(8,128)(2,1)S(1)}, bf16[256,1024]{1,0:T(8,128)(2,1)S(1)}, u32[]{:S(2)}, u32[]{:S(2)}) collective-permute-start(bf16[256,1024]{1,0:T(8,128)(2,1)S(1)} %fusion.3), channel_id=1, source_target_pairs={{0,16},{1,17},{2,18},{3,19},{4,20},{5,21},{6,22},{7,23},{8,24},{9,... | collective-permute-start | bytes 1572872 | tf_op jit(solution)/shard_map/ppermute | solution.py:568
  274.4 26.1 %collective-permute-start.34 = (bf16[256,1024]{1,0:T(8,128)(2,1)S(1)}, bf16[256,1024]{1,0:T(8,128)(2,1)}, u32[]{:S(2)}, u32[]{:S(2)}) collective-permute-start(bf16[256,1024]{1,0:T(8,128)(2,1)S(1)} %get-tuple-element.416), channel_id=1, source_target_pairs={{0,4},{1,5},{2,6},{3,7},{4,0},{5,1},{6,2},{7,3},{8,12},{9,13},{10,... | collective-permute-start | bytes 1572872 | tf_op jit(solution)/shard_map/ppermute | solution.py:568
  303.3 17.8 %collective-permute-start.41 = (bf16[2,1024,1024]{2,1,0:T(8,128)(2,1)}, bf16[2,1024,1024]{2,1,0:T(8,128)(2,1)}, u32[]{:S(2)}, u32[]{:S(2)}) collective-permute-start(bf16[2,1024,1024]{2,1,0:T(8,128)(2,1)} %get-tuple-element.350), channel_id=1, source_target_pairs={{0,8},{1,9},{2,10},{3,11},{4,12},{5,13},{6,14},{7,15},{8,0},{9,1},... | collective-permute-start | bytes 12582920 | tf_op jit(solution)/shard_map/ppermute | solution.py:568
  303.5 17.6 %collective-permute-start.40 = (bf16[128,2048]{1,0:T(8,128)(2,1)}, bf16[128,2048]{1,0:T(8,128)(2,1)}, u32[]{:S(2)}, u32[]{:S(2)}) collective-permute-start(bf16[128,2048]{1,0:T(8,128)(2,1)} %get-tuple-element.414), channel_id=1, source_target_pairs={{0,2},{1,3},{2,0},{3,1},{4,6},{5,7},{6,4},{7,5},{8,10},{9,11},{10,... | collective-permute-start | bytes 1572872 | tf_op jit(solution)/shard_map/ppermute | solution.py:568
  305.3 15.9 %collective-permute-start.39 = (bf16[128,2048]{1,0:T(8,128)(2,1)}, bf16[128,2048]{1,0:T(8,128)(2,1)}, u32[]{:S(2)}, u32[]{:S(2)}) collective-permute-start(bf16[128,2048]{1,0:T(8,128)(2,1)} %get-tuple-element.415), channel_id=1, source_target_pairs={{0,1},{1,0},{2,3},{3,2},{4,5},{5,4},{6,7},{7,6},{8,9},{9,8},{10,11... | collective-permute-start | bytes 1572872 | tf_op jit(solution)/shard_map/ppermute | solution.py:568
  307.2 13.9 %collective-permute-start.38 = (bf16[256,1024]{1,0:T(8,128)(2,1)S(1)}, bf16[256,1024]{1,0:T(8,128)(2,1)}, u32[]{:S(2)}, u32[]{:S(2)}) collective-permute-start(bf16[256,1024]{1,0:T(8,128)(2,1)S(1)} %add_convert_fusion.3), channel_id=1, source_target_pairs={{0,16},{1,17},{2,18},{3,19},{4,20},{5,21},{6,22},{7,23},{8,24},{9,... | collective-permute-start | bytes 1572872 | tf_op jit(solution)/shard_map/ppermute | solution.py:568
  322.4 28.5 %collective-permute-start.42 = (bf16[256,1024]{1,0:T(8,128)(2,1)S(1)}, bf16[256,1024]{1,0:T(8,128)(2,1)S(1)}, u32[]{:S(2)}, u32[]{:S(2)}) collective-permute-start(bf16[256,1024]{1,0:T(8,128)(2,1)S(1)} %add_convert_fusion.2.own), channel_id=1, source_target_pairs={{0,8},{1,9},{2,10},{3,11},{4,12},{5,13},{6,14},{7,15},{8,0},{9,1},... | collective-permute-start | bytes 1572872 | tf_op jit(solution)/shard_map/ppermute | solution.py:568
  324.5 26.5 %collective-permute-start.43 = (bf16[128,2048]{1,0:T(8,128)(2,1)S(1)}, bf16[128,2048]{1,0:T(8,128)(2,1)S(1)}, u32[]{:S(2)}, u32[]{:S(2)}) collective-permute-start(bf16[128,2048]{1,0:T(8,128)(2,1)S(1)} %get-tuple-element.413), channel_id=1, source_target_pairs={{0,4},{1,5},{2,6},{3,7},{4,0},{5,1},{6,2},{7,3},{8,12},{9,13},{10,... | collective-permute-start | bytes 1572872 | tf_op jit(solution)/shard_map/ppermute | solution.py:568
  351.1 15.9 %collective-permute-start.44 = (bf16[128,2048]{1,0:T(8,128)(2,1)S(1)}, bf16[128,2048]{1,0:T(8,128)(2,1)S(1)}, u32[]{:S(2)}, u32[]{:S(2)}) collective-permute-start(bf16[128,2048]{1,0:T(8,128)(2,1)S(1)} %add_convert_fusion.1), channel_id=1, source_target_pairs={{0,16},{1,17},{2,18},{3,19},{4,20},{5,21},{6,22},{7,23},{8,24},{9,... | collective-permute-start | bytes 1572872 | tf_op jit(solution)/shard_map/ppermute | solution.py:568
  353.5 13.5 %collective-permute-start.47 = (f32[16,1024]{1,0:T(8,128)S(1)}, f32[16,1024]{1,0:T(8,128)S(1)}, u32[]{:S(2)}, u32[]{:S(2)}) collective-permute-start(f32[16,1024]{1,0:T(8,128)S(1)} %concatenate.27), channel_id=1, source_target_pairs={{0,6},{1,7},{2,4},{3,5},{4,2},{5,3},{6,0},{7,1},{8,14},{9,15},{10,... | collective-permute-start | bytes 196616 | tf_op jit(solution)/shard_map/vectors/ppermute | solution.py:568
  355.9 11.1 %collective-permute-start.46 = (f32[16,1024]{1,0:T(8,128)S(1)}, f32[16,1024]{1,0:T(8,128)S(1)}, u32[]{:S(2)}, u32[]{:S(2)}) collective-permute-start(f32[16,1024]{1,0:T(8,128)S(1)} %concatenate.27), channel_id=1, source_target_pairs={{0,4},{1,5},{2,6},{3,7},{4,0},{5,1},{6,2},{7,3},{8,12},{9,13},{10,... | collective-permute-start | bytes 196616 | tf_op jit(solution)/shard_map/vectors/ppermute | solution.py:568
  355.9 11.1 %collective-permute-start.45 = (f32[16,1024]{1,0:T(8,128)S(1)}, f32[16,1024]{1,0:T(8,128)S(1)}, u32[]{:S(2)}, u32[]{:S(2)}) collective-permute-start(f32[16,1024]{1,0:T(8,128)S(1)} %concatenate.27), channel_id=1, source_target_pairs={{0,2},{1,3},{2,0},{3,1},{4,6},{5,7},{6,4},{7,5},{8,10},{9,11},{10,... | collective-permute-start | bytes 196616 | tf_op jit(solution)/shard_map/vectors/ppermute | solution.py:568
  367.1 5.5 %collective-permute-start.51 = (f32[16,1024]{1,0:T(8,128)S(1)}, f32[16,1024]{1,0:T(8,128)S(1)}, u32[]{:S(2)}, u32[]{:S(2)}) collective-permute-start(f32[16,1024]{1,0:T(8,128)S(1)} %add_add_fusion.1), channel_id=1, source_target_pairs={{0,17},{1,16},{2,19},{3,18},{4,21},{5,20},{6,23},{7,22},{8,25},{9,... | collective-permute-start | bytes 196616 | tf_op jit(solution)/shard_map/vectors/ppermute | solution.py:568
  (46 other events, 579.9 us)

commit v5 on v4

--- a/solution.py
+++ b/solution.py
@@ -125,20 +125,24 @@
     out[128:144, 128:1280] = jnp.zeros((16, 1152), BF16)
 
 
-def prep_mlp_body(ids, w_up, w_down, w_qkv, out_a, out_b):
+def prep_mlp_body(part, ids, w_up, w_down, *refs):
+    out = refs[-1]
     core = ids[1]
-    for part, out in enumerate((out_a, out_b)):
-        for owner in range(8):
-            start = pl.multiple_of(owner * 512 + part * 256 + core * 128, 128)
-            out[0:128, owner * 128 : (owner + 1) * 128] = w_up[:, pl.ds(start, 128)].astype(BF16)
-        out[128:256, :] = w_down[pl.ds(pl.multiple_of(part * 256 + core * 128, 128), 128), :].astype(BF16)
-    for part in range(3):
+    top = 96 * part
+    for owner in range(8):
+        start = pl.multiple_of(owner * 512 + part * 256 + core * 128, 128)
+        out[top : top + 128, owner * 128 : (owner + 1) * 128] = w_up[:, pl.ds(start, 128)].astype(BF16)
+    out[top + 128 : top + 256, :] = w_down[pl.ds(pl.multiple_of(core * 128, 128), 128), :].astype(BF16)
+    if not part:
+        return
+    w_qkv = refs[0]
+    for third in range(3):
         for tile in range(2):
-            base = part * 1024 + 512 + tile * 256
+            base = third * 1024 + 512 + tile * 256
             value = pick_parity(core, w_qkv[:, base : base + 128], w_qkv[:, base + 128 : base + 256]).astype(BF16)
             for panel in range(4):
                 at = panel * 256 + tile * 128
-                out_b[256 + 32 * part : 288 + 32 * part, at : at + 128] = value[32 * panel : 32 * panel + 32]
+                out[32 * third : 32 * third + 32, at : at + 128] = value[32 * panel : 32 * panel + 32]
 
 
 def normalize(inputs):
@@ -216,7 +220,7 @@
                 for panel in range(4):
                     at = pl.ds(pl.multiple_of(owner * 128 + 32 * panel, 32), 32)
                     w_qkv[at, part * 256 : part * 256 + 256] = piece[
-                        256 + 32 * part : 288 + 32 * part, panel * 256 : panel * 256 + 256
+                        32 * part : 32 * part + 32, panel * 256 : panel * 256 + 256
                     ]
 
     project(1, attn_in[...], w_qkv, bias, (cos, sin_lo, sin_hi), (q, k, v))
@@ -229,7 +233,8 @@
     return jnp.concatenate(parts, axis=axis) if len(parts) > 1 else parts[0]
 
 
-def attn_body(q, k, v, d_att, seg_col, seg_row, cos, sin_lo, sin_hi, att, grad):
+def attn_body(q, k, v, d_att, seg_col, seg_row, cos, sin_lo, sin_hi, *refs):
+    att, grad = refs[-2:]
     count = q.shape[0]
     size = ATTN_ROWS
     blocks = count // size
@@ -266,7 +271,7 @@
     def softmax_both(scores, grad_probs):
         masked = []
         for j in range(blocks):
-            allowed = seg_col[j * size :, :] == seg_row[0, :, span[j]]
+            allowed = seg_col[j * size :, 0:1] == seg_row[0, :, span[j]]
             allowed = cat([allowed[:size] & causal] + ([allowed[size:]] if j < blocks - 1 else []))
             masked.append(jnp.where(allowed, scores[j], MASKED))
         top = row_total(masked, jnp.max, jnp.maximum)
@@ -372,8 +377,9 @@
         sums[...] = jnp.zeros_like(sums)
         for place, piece in enumerate(pieces):
             at = pl.ds(pl.multiple_of(piece_owner(ids, place) * 128, 128), 128)
-            w_up[at, :] = piece[0:128, :]
-            w_down[at, :] = piece[128:256, :]
+            top = 96 * part
+            w_up[at, :] = piece[top : top + 128, :]
+            w_down[at, :] = piece[top + 128 : top + 256, :]
         for copy in weight_copies:
             copy.start()
 
@@ -641,44 +647,51 @@
             3e6,
             name="prep_attn",
         )[0]
-        own_b, own_c = block_call(
-            prep_mlp_body,
-            (1,),
-            [(ids, scalars()), const(w_up), const(w_down), const(w_qkv)],
-            [kept((256, 1024), BF16), kept((352, 1024), BF16)],
-            0,
-            6e6,
-            name="prep_mlp",
-        )
+
+    def prep_mlp(part, shape, ins, beside):
+        with jax.named_scope("prep"):
+            return block_call(
+                functools.partial(prep_mlp_body, part),
+                (1,),
+                [(ids, scalars()), const(ins[0]), (ins[1], spec((256, width), lambda i: (part, 0), single=True))]
+                + [const(value) for value in ins[2:]],
+                [kept(shape, BF16)],
+                0,
+                beside * 3e6,
+                name="prep_mlp",
+            )[0]
 
     def z_moves(own):
         return swap(own, 0, 2), swap_far(own)
 
     with jax.named_scope("gather"):
+        seg_other = swap(segments, 1, 0)
+        tok_other = swap(tokens, 1, 0)
+        dy_other = swap(cotangent, 1, 0)
+        own_a, w_up_in = sync(own_a, w_up)
         next_a, far_a = z_moves(own_a)
         across_a = swap(own_a, 0, 1)
-        seg_other = swap(segments, 1, 0)
+        own_b = prep_mlp(0, (256, 1024), (w_up_in, w_down), 20)
         tables = [
             jnp.concatenate(pair, axis=0)
             for pair in zip(rotary_tables(segments), rotary_tables(seg_other))
         ]
-        seg_row = jnp.stack([segments, seg_other])[:, None, :]
-        seg_col = jnp.concatenate([segments, seg_other])[:, None]
-        next_a, far_a, across_a, own_b, own_c, tables, seg_row, seg_col = sync(
-            next_a, far_a, across_a, own_b, own_c, tables, seg_row, seg_col
+        seg_row = jnp.stack([segments, seg_other]).astype(F32)[:, None, :]
+        seg_ids = jnp.concatenate([segments, seg_other]).astype(F32)
+        next_a, far_a, across_a, own_b, w_up_in, tables, seg_row, seg_ids, tok_other, dy_other = sync(
+            next_a, far_a, across_a, own_b, w_up_in, tables, seg_row, seg_ids, tok_other, dy_other
         )
-        next_across_a, far_across_a, rest_a = swap(next_a, 0, 1), swap(far_a, 0, 1), swap(far_a, 2, 0)
-        rest_across_a = swap(far_a, 2, 1)
-        next_b, far_b = z_moves(own_b)
-        tok_other = swap(tokens, 1, 0)
-        dy_other = swap(cotangent, 1, 0)
-
-    (next_across_a, far_across_a, rest_a, rest_across_a, next_b, far_b, own_c, tok_other, dy_other) = sync(
-        next_across_a, far_across_a, rest_a, rest_across_a, next_b, far_b, own_c, tok_other, dy_other
-    )
-    with jax.named_scope("gather"):
-        far_across_b, next_across_b, rest_b = swap(far_b, 0, 1), swap(next_b, 0, 1), swap(far_b, 2, 0)
-        next_c, far_c = z_moves(own_c)
+        next_across_a, far_across_a, rest_across_a = swap(next_a, 0, 1), swap(far_a, 0, 1), swap(far_a, 2, 1)
+        rest_a = swap(far_a, 2, 0)
+        far_b = swap_far(own_b)
+        seg_col = jnp.broadcast_to(seg_ids[:, None], (rows, LANES))
+        own_c = prep_mlp(1, (352, 1024), (w_up_in, w_down, w_qkv), 25)
+        next_across_a, far_across_a, rest_a, rest_across_a, far_b, own_b, own_c, seg_col = sync(
+            next_across_a, far_across_a, rest_a, rest_across_a, far_b, own_b, own_c, seg_col
+        )
+        far_across_b, across_b, rest_b = swap(far_b, 0, 1), swap(own_b, 0, 1), swap(far_b, 2, 0)
+        next_b = swap(own_b, 0, 2)
+        far_c = swap_far(own_c)
     attn_pieces = [own_a, next_a, far_a, rest_a, across_a, next_across_a, far_across_a, rest_across_a]
 
     def table_blocks(count):
@@ -691,25 +704,37 @@
             (other, spec((count, width), lambda i: (jnp.maximum(i - last - 1, 0), 0))),
         ]
 
-    def attention(group, projected, d_att):
+    def attention(group, pairs, projected, d_att, previous):
         with jax.named_scope("attention"):
-            head_block = spec((T, 128), lambda h, m: (h, m))
-            return block_call(
+            first = pairs[0]
+            head_block = spec((T, 128), lambda h, m: (h, m + first))
+            outs = [
+                (sds((rows, 256), BF16), head_block),
+                (sds((3, rows, 256), BF16), spec((3, T, 128), lambda h, m: (0, h, m + first))),
+            ]
+            ins = (
+                [(value, head_block) for value in projected]
+                + [(d_att, spec((T, 128), lambda h, m: (h, m + first + 2 * group)))]
+                + [(seg_col, spec((T, LANES), lambda h, m: (h, 0)))]
+                + [(seg_row, spec((1, 1, T), lambda h, m: (h, 0, 0)))]
+                + [(t, spec((T, 128), lambda h, m: (h, 0))) for t in tables]
+            )
+            aliases = {len(ins) + n: n for n in range(len(previous))}
+            return pl.pallas_call(
                 attn_body,
-                (2, 2),
-                [(value, head_block) for value in projected]
-                + [(d_att, spec((T, 128), lambda h, m: (h, m + 2 * group)))]
-                + [(seg_col, spec((T, 1), lambda h, m: (h, 0)))]
-                + [(seg_row, spec((1, 1, T), lambda h, m: (h, 0, 0)))]
-                + [(t, spec((T, 128), lambda h, m: (h, 0))) for t in tables],
-                [
-                    (sds((rows, 256), BF16), head_block),
-                    (sds((3, rows, 256), BF16), spec((3, T, 128), lambda h, m: (0, h, m))),
-                ],
-                30e9,
-                10e6,
+                grid=(2, len(pairs)),
+                in_specs=[place for _, place in ins] + [distant()] * len(previous),
+                out_specs=[place for _, place in outs],
+                out_shape=[shape for shape, _ in outs],
+                input_output_aliases=aliases,
+                cost_estimate=pl.CostEstimate(
+                    flops=len(pairs) * 15000000000, bytes_accessed=len(pairs) * 5000000, transcendentals=0
+                ),
+                compiler_params=pltpu.CompilerParams(
+                    vmem_limit_bytes=VMEM_NEED * MIB, dimension_semantics=("arbitrary",) * 2
+                ),
                 name="attention",
-            )
+            )(*[value for value, _ in ins], *previous)
 
     def blocks_of(shape):
         return [kept((n,) + shape, BF16) for n in (4, 2, 2)]
@@ -731,15 +756,18 @@
             30e6,
             name="qkv",
         )
-    projected, far_across_b, next_across_b, rest_b, own_b, next_c, far_c = sync(
-        projected, far_across_b, next_across_b, rest_b, own_b, next_c, far_c
+    projected, far_across_b, across_b, rest_b, next_b = sync(
+        projected, far_across_b, across_b, rest_b, next_b
     )
     with jax.named_scope("gather"):
-        rest_across_b, across_b = swap(far_across_b, 2, 0), swap(own_b, 0, 1)
-        far_across_c, rest_c = swap(far_c, 0, 1), swap(far_c, 2, 0)
-    att_a, grad_a = attention(0, projected, d_att)
-    att_a, grad_a, rest_across_b, across_b, far_across_c, rest_c, own_c, next_c, attn_t, mlp_in = sync(
-        att_a, grad_a, rest_across_b, across_b, far_across_c, rest_c, own_c, next_c, attn_t, mlp_in
+        rest_across_b, next_across_b = swap(far_across_b, 2, 0), swap(next_b, 0, 1)
+    half_a = attention(0, (0,), projected, d_att, [])
+    half_a, projected, far_c, own_c = sync(half_a, projected, far_c, own_c)
+    with jax.named_scope("gather"):
+        far_across_c, rest_c, next_c = swap(far_c, 0, 1), swap(far_c, 2, 0), swap(own_c, 0, 2)
+    att_a, grad_a = attention(0, (1,), projected, d_att, half_a)
+    att_a, grad_a, rest_across_b, next_across_b, far_across_c, rest_c, own_c, next_c, attn_t, mlp_in = sync(
+        att_a, grad_a, rest_across_b, next_across_b, far_across_c, rest_c, own_c, next_c, attn_t, mlp_in
     )
     with jax.named_scope("gather"):
         across_c, next_across_c, rest_across_c = swap(own_c, 0, 1), swap(next_c, 0, 1), swap(far_across_c, 2, 0)
@@ -792,7 +820,7 @@
             qkv_second_body,
             (rows // 512,),
             [(ids, scalars())]
-            + [const(piece) for piece in pieces_c]
+            + [(piece, whole((96, width))) for piece in pieces_c]
             + [(attn_in, row_block(512)), const(bias_qkv)]
             + table_blocks(512),
             [(sds((rows, 256), BF16), row_block(512, 256))] * 3 + [kept((1024, 768), BF16)],
@@ -800,7 +828,7 @@
             12e6,
             name="qkv",
         )
-    att_b, grad_b = attention(1, projected, d_att)
+    att_b, grad_b = attention(1, (0, 1), projected, d_att, [])
     att_b, grad_b, reduce_a, reduce_b = sync(att_b, grad_b, reduce_a, reduce_b)
     reduce_a = reduce_third(reduce_a)
     reduce_b = reduce_second(reduce_b)

time: 391 us -> 376 us (0.962)
  waiting for transfers between devices: 56.5 us -> 36.4 us
  Pallas kernels: 240 us -> 244 us
    pallas_call x0 -> x3, Pallas kernels: none -> 58.5 us  [attention(): pl.pallas_call(attn_body, grid=(2, len(pairs)), in_specs=[place for _, pl...]
    pallas_call x11 -> x10, Pallas kernels: 214 us -> 160 us  [block_call(): kernel_call(body, grid, [place for _, place in ins], [place for _, place...]
    ppermute x53, waiting for transfers between devices: 56.5 us -> 36.4 us  [move(): return lax.ppermute(value, AXES, pairs)]
  transfers between devices with their start and end apart: 53 -> 53, of which waited for: 19 -> 13; matrix products, arithmetic and copies ran while one was open for 6% -> 5% of each run, Pallas kernels for 60% -> 63%
where the time goes in v5:
time: 376 us; the launch traced here: 369 us
  Pallas kernels  244 us (65%)
  starting transfers between devices  53.2 us (14%)
  waiting for transfers between devices  36.4 us (10%)
  other arithmetic  26.9 us (7%)
  local copies, waits for them, and re-layouts  6.58 us (2%)
    pallas_call x10, Pallas kernels, block_call(): kernel_call(body, grid, [place for _, place in ins], [place for _, place...  160 us
    pallas_call x3, Pallas kernels, attention(): pl.pallas_call(attn_body, grid=(2, len(pairs)), in_specs=[place for _, pl...  58.5 us
    ppermute x53, starting transfers between devices, move(): return lax.ppermute(value, AXES, pairs)  53.2 us
    ppermute x53, waiting for transfers between devices, move(): return lax.ppermute(value, AXES, pairs)  36.4 us
    pallas_call x2, Pallas kernels, adam_mlp(): pl.pallas_call(adam_mlp_body, grid=(8,), in_specs=[scalars()] + [whole((2...  18.2 us
    pallas_call x1, Pallas kernels, on_device(): kernel_call(adam_attn_body, (3,), [scalars()] + [whole((128, 2048))] * 2...  8.1 us
  transfers between devices with their start and end apart: 53, of which 13 were waited for; matrix products, arithmetic and copies ran while one was open for 5% of the time, Pallas kernels for 63%

profile of v5, /device:TPU:0, one launch (start us, length us, event | category | flops | bytes accessed | tf_op | source)
XLA Modules:
  0.0 369.5 jit_solution(1762405272822500170)
XLA Ops:
  1.3 2.5 prep_attn.1.refs_0_
  3.8 2.9 collective-permute-start.2
  6.7 2.6 collective-permute-start.1
  10.6 2.8 prep_mlp.2.refs_0_
  13.4 1.6 collective-permute-start
  16.2 3.8 %fusion.5 = (f32[1024,128]{1,0:T(8,128)S(1)}, f32[1024,128]{1,0:T(8,128)S(1)}, f32[1024,128]{1,0:T(8,128)S(1)}, f32[1024,128]{1,0:T(8,128)S(1)}, f32[1024,128]{1,0:T(8,128)S(1)}, /*index=5*/f32[1024,128]{1,0:T(8,128)S(1)}) fusion(f32[128]{0:T(128)S(1)} %compare_select_fusion.2, f32[1024]{0:T(1024)S(1)} %fusion.21, ...), kind=kLoop, calls=%fused_computation.29 | loop fusion | flops 1048576 | bytes 3154560 | tf_op jit(solution)/shard_map/gather/jit(_where)/select_n | solution.py:538
  22.5 3.5 collective-permute-done.1.refs_2_
  26.0 5.2 %collective-permute-done.refs_1_ = bf16[144,1280]{1,0:T(8,128)(2,1)} collective-permute-done((bf16[144,1280]{1,0:T(8,128)(2,1)S(1)}, bf16[144,1280]{1,0:T(8,128)(2,1)}, u32[]{:S(2)}, u32[]{:S(2)}) %collective-permute-start) | collective-permute-done | bytes 368672 | tf_op jit(solution)/shard_map/gather/ppermute | solution.py:574
  33.6 1.6 collective-permute-start.8
  35.7 3.5 prep_mlp.3.refs_0_
  39.1 4.3 %collective-permute-done.6.refs_5_ = bf16[144,1280]{1,0:T(8,128)(2,1)S(1)} collective-permute-done((bf16[144,1280]{1,0:T(8,128)(2,1)}, bf16[144,1280]{1,0:T(8,128)(2,1)S(1)}, u32[]{:S(2)}, u32[]{:S(2)}) %collective-permute-start.6) | collective-permute-done | bytes 368672 | tf_op jit(solution)/shard_map/gather/ppermute | solution.py:574
  43.4 7.8 %collective-permute-done.9.refs_7_ = bf16[144,1280]{1,0:T(8,128)(2,1)S(1)} collective-permute-done((bf16[144,1280]{1,0:T(8,128)(2,1)}, bf16[144,1280]{1,0:T(8,128)(2,1)S(1)}, u32[]{:S(2)}, u32[]{:S(2)}) %collective-permute-start.9) | collective-permute-done | bytes 368672 | tf_op jit(solution)/shard_map/gather/ppermute | solution.py:574
  51.4 6.2 %collective-permute-done.7.refs_6_ = bf16[144,1280]{1,0:T(8,128)(2,1)S(1)} collective-permute-done((bf16[144,1280]{1,0:T(8,128)(2,1)}, bf16[144,1280]{1,0:T(8,128)(2,1)S(1)}, u32[]{:S(2)}, u32[]{:S(2)}) %collective-permute-start.7) | collective-permute-done | bytes 368672 | tf_op jit(solution)/shard_map/gather/ppermute | solution.py:574
  60.3 1.7 collective-permute-start.14
  62.0 1.5 collective-permute-start.12
  63.9 17.1 %qkv.2 = (bf16[2048,256]{1,0:T(8,128)(2,1)}, bf16[2048,256]{1,0:T(8,128)(2,1)}, bf16[2048,256]{1,0:T(8,128)(2,1)}, bf16[2048,512]{1,0:T(8,128)(2,1)}, bf16[2048,...) custom-call(s32[3]{0:T(128)} %pad_add_fusion.2.ids, ...), custom_call_target="tpu_custom_call" | custom-call | flops 5368709120 | bytes 30000000 | tf_op jit(solution)/shard_map/qkv/qkv/pallas_call | solution.py:621
  81.2 2.2 collective-permute-done.12.refs_4_
  85.4 15.2 %attention.3 = (bf16[2048,256]{1,0:T(8,128)(2,1)}, bf16[3,2048,256]{2,1,0:T(8,128)(2,1)}) custom-call(bf16[2048,256]{1,0:T(8,128)(2,1)} %get-tuple-element.252.q, bf16[2048,256]{1,0:T(8,128)(2,1)} %get-tuple-element.253.k, bf16[2048,256]{1,0:T(8,128)(2,1)} %get-tuple-element.254.v, bf16[2048,512]{1,0:T(8,128)(2,1)} %get-tuple-element.246.d_att, ...), custom_call_target="tpu_custom_call" | custom-call | flops 15000000512 | bytes 5000000 | tf_op jit(solution)/shard_map/attention/attention/pallas_call | solution.py:723
  101.3 1.5 collective-permute-start.18
  102.8 1.6 collective-permute-start.20
  104.4 15.4 %attention.4 = (bf16[2048,256]{1,0:T(8,128)(2,1)}, bf16[3,2048,256]{2,1,0:T(8,128)(2,1)}) custom-call(bf16[2048,256]{1,0:T(8,128)(2,1)} %get-tuple-element.252.q, bf16[2048,256]{1,0:T(8,128)(2,1)} %get-tuple-element.253.k, bf16[2048,256]{1,0:T(8,128)(2,1)} %get-tuple-element.254.v, ...), custom_call_target="tpu_custom_call", output_to_operand_aliasing={{0}: (9, {}), {1}: (10, {})} | custom-call | flops 15000000512 | bytes 5000000 | tf_op jit(solution)/shard_map/attention/attention/pallas_call | solution.py:723
  121.2 1.5 collective-permute-start.22
  122.7 1.8 collective-permute-start.23
  124.5 28.0 %mlp.2 = (bf16[4,256,1024]{2,1,0:T(8,128)(2,1)}, bf16[2,256,1024]{2,1,0:T(8,128)(2,1)}, bf16[2,256,1024]{2,1,0:T(8,128)(2,1)}, bf16[2048,1024]{1,0:T(8,128)(2,1)...) custom-call(s32[3]{0:T(128)} %pad_add_fusion.2.ids, ...), custom_call_target="tpu_custom_call" | custom-call | flops 17179869184 | bytes 40000000 | tf_op jit(solution)/shard_map/mlp/mlp/pallas_call | solution.py:621
  154.5 28.1 %mlp.3 = (bf16[4,256,1024]{2,1,0:T(8,128)(2,1)}, bf16[2,256,1024]{2,1,0:T(8,128)(2,1)}, bf16[2,256,1024]{2,1,0:T(8,128)(2,1)}, bf16[2048,1024]{1,0:T(8,128)(2,1)...) custom-call(s32[3]{0:T(128)} %pad_add_fusion.2.ids, ...), custom_call_target="tpu_custom_call" | custom-call | flops 17179869184 | bytes 40000000 | tf_op jit(solution)/shard_map/mlp/mlp/pallas_call | solution.py:621
  187.9 8.4 %qkv.3 = (bf16[2048,256]{1,0:T(8,128)(2,1)}, bf16[2048,256]{1,0:T(8,128)(2,1)}, bf16[2048,256]{1,0:T(8,128)(2,1)}, bf16[1024,768]{1,0:T(8,128)(2,1)}) custom-call(s32[3]{0:T(128)} %pad_add_fusion.2.ids, bf16[352,1024]{1,0:T(8,128)(2,1)} %prep_mlp.3.refs_0_, bf16[352,1024]{1,0:T(8,128)(2,1)} %copy-done.17, bf16[352,1024]{1,0:T(8,128)(2,1)} %copy-done.14, ...), custom_call_target="tpu_custom_call" | custom-call | flops 3221225472 | bytes 12000000 | tf_op jit(solution)/shard_map/qkv/qkv/pallas_call | solution.py:621
  196.3 27.9 %attention.5 = (bf16[2048,256]{1,0:T(8,128)(2,1)}, bf16[3,2048,256]{2,1,0:T(8,128)(2,1)}) custom-call(bf16[2048,256]{1,0:T(8,128)(2,1)} %get-tuple-element.307.q, bf16[2048,256]{1,0:T(8,128)(2,1)} %get-tuple-element.308.k, bf16[2048,256]{1,0:T(8,128)(2,1)} %get-tuple-element.309.v, bf16[2048,512]{1,0:T(8,128)(2,1)} %get-tuple-element.246.d_att, ...), custom_call_target="tpu_custom_call" | custom-call | flops 30000001024 | bytes 10000000 | tf_op jit(solution)/shard_map/attention/attention/pallas_call | solution.py:723
  224.2 3.1 fusion.4
  227.3 2.0 collective-permute-start.30
  231.3 1.5 collective-permute-start.33
  232.8 20.3 %attn_weights.1 = (bf16[4,128,2048]{2,1,0:T(8,128)(2,1)}, bf16[2,128,2048]{2,1,0:T(8,128)(2,1)}, bf16[2,128,2048]{2,1,0:T(8,128)(2,1)}, f32[8,1536]{1,0:T(8,128)}) custom-call(s32[3]{0:T(128)} %pad_add_fusion.2.ids, bf16[1024,2048]{1,0:T(8,128)(2,1)} %get-tuple-element.266.attn_t, bf16[3,2048,256]{2,1,0:T(8,128)(2,1)} %get-tuple-element.265.grad_a, ...), custom_call_target="tpu_custom_call" | custom-call | flops 8589934592 | bytes 24000000 | tf_op jit(solution)/shard_map/attn_weights/attn_weights/pallas_call | solution.py:621
  255.6 1.7 collective-permute-start.31
  257.3 2.1 fusion.1
  259.4 2.3 collective-permute-start.34
  261.7 23.1 %back.2 = (bf16[2,1024,1024]{2,1,0:T(8,128)(2,1)}, f32[8,1024]{1,0:T(8,128)}) custom-call(bf16[3,2048,256]{2,1,0:T(8,128)(2,1)} %get-tuple-element.265.grad_a, bf16[3,2048,256]{2,1,0:T(8,128)(2,1)} %get-tuple-element.373.grad_b, bf16[2048,256]{1,0:T(8,128)(2,1)} %get-tuple-element.323.far_att_a.att_a, bf16[2048,256]{1,0:T(8,128)(2,1)} %get-tuple-element.324.far_att_b.att_b, ...), custom_call_target="tpu_custom_call" | custom-call | flops 12884901888 | bytes 40000000 | tf_op jit(solution)/shard_map/back/back/pallas_call | solution.py:621
  284.9 2.8 fusion.16
  288.0 1.5 collective-permute-start.39
  293.5 2.3 collective-permute-done.37.other
  295.8 9.1 %adam_mlp.2 = (f32[128,4096]{1,0:T(8,128)}, f32[128,4096]{1,0:T(8,128)}, f32[128,4096]{1,0:T(8,128)}, f32[512,1024]{1,0:T(8,128)}, f32[512,1024]{1,0:T(8,128)}, /*index=5*/f32[512,1024]{1,0:T(8,128)}) custom-call(s32[3]{0:T(128)} %pad_add_fusion.2.ids, bf16[256,1024]{1,0:T(8,128)(2,1)} %copy-done.8, bf16[256,1024]{1,0:T(8,128)(2,1)} %collective-permute-done.37.other, ...), custom_call_target="tpu_custom_call" | custom-call | bytes 14000000 | tf_op jit(solution)/shard_map/adam_mlp/pallas_call | solution.py:862
  306.4 1.9 bitcast_add_fusion
  308.3 1.7 collective-permute-start.43
  310.0 25.7 %back.3 = (bf16[1024,1024]{1,0:T(8,128)(2,1)}, f32[1024,1024]{1,0:T(8,128)}, f32[8,1024]{1,0:T(8,128)}) custom-call(bf16[3,2048,256]{2,1,0:T(8,128)(2,1)} %get-tuple-element.265.grad_a, bf16[3,2048,256]{2,1,0:T(8,128)(2,1)} %get-tuple-element.373.grad_b, bf16[2048,256]{1,0:T(8,128)(2,1)} %get-tuple-element.323.far_att_a.att_a, ...), custom_call_target="tpu_custom_call" | custom-call | flops 12884901888 | bytes 40000000 | tf_op jit(solution)/shard_map/back/back/pallas_call | solution.py:621
  337.5 2.2 collective-permute-start.47
  339.7 2.3 collective-permute-start.45
  342.0 9.0 %adam_mlp.3 = (f32[128,4096]{1,0:T(8,128)}, f32[128,4096]{1,0:T(8,128)}, f32[128,4096]{1,0:T(8,128)}, f32[512,1024]{1,0:T(8,128)}, f32[512,1024]{1,0:T(8,128)}, /*index=5*/f32[512,1024]{1,0:T(8,128)}) custom-call(s32[3]{0:T(128)} %pad_add_fusion.2.ids, ...), custom_call_target="tpu_custom_call", output_to_operand_aliasing={{0}: (9, {}), {1}: (10, {}), {2}: (11, {}), {3}: (12, {}), ... | custom-call | bytes 14000000 | tf_op jit(solution)/shard_map/vectors/adam_mlp/pallas_call | solution.py:862
  351.1 1.6 collective-permute-start.51
  354.9 1.8 collective-permute-done.51
  360.9 8.1 %adam.1 = (f32[128,3072]{1,0:T(8,128)}, f32[128,3072]{1,0:T(8,128)}, f32[128,3072]{1,0:T(8,128)}, f32[128,1024]{1,0:T(8,128)}, f32[128,1024]{1,0:T(8,128)}, /*index=5*/f32[128,1024]{1,0:T(8,128)}) custom-call(s32[3]{0:T(128)} %pad_add_fusion.2.ids, bf16[128,2048]{1,0:T(8,128)(2,1)} %copy-done.7, bf16[128,2048]{1,0:T(8,128)(2,1)} %copy-done.25, ...), custom_call_target="tpu_custom_call" | custom-call | bytes 13000000 | tf_op jit(solution)/shard_map/adam/adam/pallas_call | solution.py:969
  (220 shorter events, 41.2 us)
Async XLA Ops:
  3.8 18.7 %collective-permute-start.2 = (bf16[144,1280]{1,0:T(8,128)(2,1)}, bf16[144,1280]{1,0:T(8,128)(2,1)S(1)}, u32[]{:S(2)}, u32[]{:S(2)}) collective-permute-start(bf16[144,1280]{1,0:T(8,128)(2,1)} %prep_attn.1.refs_0_), channel_id=1, source_target_pairs={{0,1},{1,0},{2,3},{3,2},{4,5},{5,4},{6,7},{7,6},{8,9},{9,8},{10,11... | collective-permute-start | bytes 1105928 | tf_op jit(solution)/shard_map/gather/ppermute | solution.py:574
  6.7 19.3 %collective-permute-start.1 = (bf16[144,1280]{1,0:T(8,128)(2,1)}, bf16[144,1280]{1,0:T(8,128)(2,1)}, u32[]{:S(2)}, u32[]{:S(2)}) collective-permute-start(bf16[144,1280]{1,0:T(8,128)(2,1)} %prep_attn.1.refs_0_), channel_id=1, source_target_pairs={{0,4},{1,5},{2,6},{3,7},{4,0},{5,1},{6,2},{7,3},{8,12},{9,13},{10,... | collective-permute-start | bytes 1105928 | tf_op jit(solution)/shard_map/gather/ppermute | solution.py:574
  9.3 21.9 %collective-permute-start.4 = (bf16[1024,1024]{1,0:T(8,128)(2,1)S(1)}, bf16[1024,1024]{1,0:T(8,128)(2,1)}, u32[]{:S(2)}, u32[]{:S(2)}) collective-permute-start(bf16[1024,1024]{1,0:T(8,128)(2,1)S(1)} %copy-done.33), channel_id=1, source_target_pairs={{0,8},{1,9},{2,10},{3,11},{4,12},{5,13},{6,14},{7,15},{8,0},{9,1},... | collective-permute-start | bytes 6291464 | tf_op jit(solution)/shard_map/gather/ppermute | solution.py:574
  9.8 21.4 %collective-permute-start.5 = (bf16[1024,1024]{1,0:T(8,128)(2,1)}, bf16[1024,1024]{1,0:T(8,128)(2,1)}, u32[]{:S(2)}, u32[]{:S(2)}) collective-permute-start(bf16[1024,1024]{1,0:T(8,128)(2,1)} %refs_9_.1), channel_id=1, source_target_pairs={{0,8},{1,9},{2,10},{3,11},{4,12},{5,13},{6,14},{7,15},{8,0},{9,1},... | collective-permute-start | bytes 6291464 | tf_op jit(solution)/shard_map/gather/ppermute | solution.py:574
  13.4 17.8 %collective-permute-start = (bf16[144,1280]{1,0:T(8,128)(2,1)S(1)}, bf16[144,1280]{1,0:T(8,128)(2,1)}, u32[]{:S(2)}, u32[]{:S(2)}) collective-permute-start(bf16[144,1280]{1,0:T(8,128)(2,1)S(1)} %copy-done.26), channel_id=1, source_target_pairs={{0,2},{1,3},{2,0},{3,1},{4,6},{5,7},{6,4},{7,5},{8,10},{9,11},{10,... | collective-permute-start | bytes 1105928 | tf_op jit(solution)/shard_map/gather/ppermute | solution.py:574
  31.3 26.4 %collective-permute-start.10 = (bf16[256,1024]{1,0:T(8,128)(2,1)S(1)}, bf16[256,1024]{1,0:T(8,128)(2,1)S(1)}, u32[]{:S(2)}, u32[]{:S(2)}) collective-permute-start(bf16[256,1024]{1,0:T(8,128)(2,1)S(1)} %copy-done.21), channel_id=1, source_target_pairs={{0,4},{1,5},{2,6},{3,7},{4,0},{5,1},{6,2},{7,3},{8,12},{9,13},{10,... | collective-permute-start | bytes 1572872 | tf_op jit(solution)/shard_map/gather/ppermute | solution.py:574
  31.7 11.7 %collective-permute-start.6 = (bf16[144,1280]{1,0:T(8,128)(2,1)}, bf16[144,1280]{1,0:T(8,128)(2,1)S(1)}, u32[]{:S(2)}, u32[]{:S(2)}) collective-permute-start(bf16[144,1280]{1,0:T(8,128)(2,1)} %collective-permute-done.refs_1_), channel_id=1, source_target_pairs={{0,1},{1,0},{2,3},{3,2},{4,5},{5,4},{6,7},{7,6},{8,9},{9,8},{10,11... | collective-permute-start | bytes 1105928 | tf_op jit(solution)/shard_map/gather/ppermute | solution.py:574
  32.2 19.0 %collective-permute-start.9 = (bf16[144,1280]{1,0:T(8,128)(2,1)}, bf16[144,1280]{1,0:T(8,128)(2,1)S(1)}, u32[]{:S(2)}, u32[]{:S(2)}) collective-permute-start(bf16[144,1280]{1,0:T(8,128)(2,1)} %collective-permute-done.1.refs_2_), channel_id=1, source_target_pairs={{0,17},{1,16},{2,19},{3,18},{4,21},{5,20},{6,23},{7,22},{8,25},{9,... | collective-permute-start | bytes 1105928 | tf_op jit(solution)/shard_map/gather/ppermute | solution.py:574
  33.6 17.8 %collective-permute-start.8 = (bf16[144,1280]{1,0:T(8,128)(2,1)}, bf16[144,1280]{1,0:T(8,128)(2,1)S(1)}, u32[]{:S(2)}, u32[]{:S(2)}) collective-permute-start(bf16[144,1280]{1,0:T(8,128)(2,1)} %collective-permute-done.1.refs_2_), channel_id=1, source_target_pairs={{0,16},{1,17},{2,18},{3,19},{4,20},{5,21},{6,22},{7,23},{8,24},{9,... | collective-permute-start | bytes 1105928 | tf_op jit(solution)/shard_map/gather/ppermute | solution.py:574
  35.2 22.5 %collective-permute-start.7 = (bf16[144,1280]{1,0:T(8,128)(2,1)}, bf16[144,1280]{1,0:T(8,128)(2,1)S(1)}, u32[]{:S(2)}, u32[]{:S(2)}) collective-permute-start(bf16[144,1280]{1,0:T(8,128)(2,1)} %collective-permute-done.1.refs_2_), channel_id=1, source_target_pairs={{0,1},{1,0},{2,3},{3,2},{4,5},{5,4},{6,7},{7,6},{8,9},{9,8},{10,11... | collective-permute-start | bytes 1105928 | tf_op jit(solution)/shard_map/gather/ppermute | solution.py:574
  58.9 22.1 %collective-permute-start.13 = (bf16[256,1024]{1,0:T(8,128)(2,1)S(1)}, bf16[256,1024]{1,0:T(8,128)(2,1)S(1)}, u32[]{:S(2)}, u32[]{:S(2)}) collective-permute-start(bf16[256,1024]{1,0:T(8,128)(2,1)S(1)} %collective-permute-done.10.refs_2_), channel_id=1, source_target_pairs={{0,16},{1,17},{2,18},{3,19},{4,20},{5,21},{6,22},{7,23},{8,24},{9,... | collective-permute-start | bytes 1572872 | tf_op jit(solution)/shard_map/gather/ppermute | solution.py:574
  59.8 21.3 %collective-permute-start.11 = (bf16[256,1024]{1,0:T(8,128)(2,1)S(1)}, bf16[256,1024]{1,0:T(8,128)(2,1)S(1)}, u32[]{:S(2)}, u32[]{:S(2)}) collective-permute-start(bf16[256,1024]{1,0:T(8,128)(2,1)S(1)} %collective-permute-done.10.refs_2_), channel_id=1, source_target_pairs={{0,1},{1,0},{2,3},{3,2},{4,5},{5,4},{6,7},{7,6},{8,9},{9,8},{10,11... | collective-permute-start | bytes 1572872 | tf_op jit(solution)/shard_map/gather/ppermute | solution.py:574
  60.3 20.9 %collective-permute-start.14 = (bf16[256,1024]{1,0:T(8,128)(2,1)S(1)}, bf16[256,1024]{1,0:T(8,128)(2,1)}, u32[]{:S(2)}, u32[]{:S(2)}) collective-permute-start(bf16[256,1024]{1,0:T(8,128)(2,1)S(1)} %copy-done.21), channel_id=1, source_target_pairs={{0,2},{1,3},{2,0},{3,1},{4,6},{5,7},{6,4},{7,5},{8,10},{9,11},{10,... | collective-permute-start | bytes 1572872 | tf_op jit(solution)/shard_map/gather/ppermute | solution.py:574
  62.0 21.4 %collective-permute-start.12 = (bf16[256,1024]{1,0:T(8,128)(2,1)S(1)}, bf16[256,1024]{1,0:T(8,128)(2,1)S(1)}, u32[]{:S(2)}, u32[]{:S(2)}) collective-permute-start(bf16[256,1024]{1,0:T(8,128)(2,1)S(1)} %copy-done.21), channel_id=1, source_target_pairs={{0,1},{1,0},{2,3},{3,2},{4,5},{5,4},{6,7},{7,6},{8,9},{9,8},{10,11... | collective-permute-start | bytes 1572872 | tf_op jit(solution)/shard_map/gather/ppermute | solution.py:574
  63.5 37.1 %collective-permute-start.15 = (bf16[352,1024]{1,0:T(8,128)(2,1)}, bf16[352,1024]{1,0:T(8,128)(2,1)S(1)}, u32[]{:S(2)}, u32[]{:S(2)}) collective-permute-start(bf16[352,1024]{1,0:T(8,128)(2,1)} %prep_mlp.3.refs_0_), channel_id=1, source_target_pairs={{0,4},{1,5},{2,6},{3,7},{4,0},{5,1},{6,2},{7,3},{8,12},{9,13},{10,... | collective-permute-start | bytes 2162696 | tf_op jit(solution)/shard_map/gather/ppermute | solution.py:574
  83.5 36.3 %collective-permute-start.16 = (bf16[256,1024]{1,0:T(8,128)(2,1)S(1)}, bf16[256,1024]{1,0:T(8,128)(2,1)S(1)}, u32[]{:S(2)}, u32[]{:S(2)}) collective-permute-start(bf16[256,1024]{1,0:T(8,128)(2,1)S(1)} %collective-permute-done.11.refs_6_), channel_id=1, source_target_pairs={{0,16},{1,17},{2,18},{3,19},{4,20},{5,21},{6,22},{7,23},{8,24},{9,... | collective-permute-start | bytes 1572872 | tf_op jit(solution)/shard_map/gather/ppermute | solution.py:574
  84.8 35.0 %collective-permute-start.17 = (bf16[256,1024]{1,0:T(8,128)(2,1)}, bf16[256,1024]{1,0:T(8,128)(2,1)S(1)}, u32[]{:S(2)}, u32[]{:S(2)}) collective-permute-start(bf16[256,1024]{1,0:T(8,128)(2,1)} %collective-permute-done.14.refs_1_), channel_id=1, source_target_pairs={{0,1},{1,0},{2,3},{3,2},{4,5},{5,4},{6,7},{7,6},{8,9},{9,8},{10,11... | collective-permute-start | bytes 1572872 | tf_op jit(solution)/shard_map/gather/ppermute | solution.py:574
  100.6 19.3 %collective-permute-start.19 = (bf16[352,1024]{1,0:T(8,128)(2,1)S(1)}, bf16[352,1024]{1,0:T(8,128)(2,1)S(1)}, u32[]{:S(2)}, u32[]{:S(2)}) collective-permute-start(bf16[352,1024]{1,0:T(8,128)(2,1)S(1)} %collective-permute-done.15.refs_2_), channel_id=1, source_target_pairs={{0,16},{1,17},{2,18},{3,19},{4,20},{5,21},{6,22},{7,23},{8,24},{9,... | collective-permute-start | bytes 2162696 | tf_op jit(solution)/shard_map/gather/ppermute | solution.py:574
  101.3 18.6 %collective-permute-start.18 = (bf16[352,1024]{1,0:T(8,128)(2,1)S(1)}, bf16[352,1024]{1,0:T(8,128)(2,1)S(1)}, u32[]{:S(2)}, u32[]{:S(2)}) collective-permute-start(bf16[352,1024]{1,0:T(8,128)(2,1)S(1)} %collective-permute-done.15.refs_2_), channel_id=1, source_target_pairs={{0,1},{1,0},{2,3},{3,2},{4,5},{5,4},{6,7},{7,6},{8,9},{9,8},{10,11... | collective-permute-start | bytes 2162696 | tf_op jit(solution)/shard_map/gather/ppermute | solution.py:574
  102.8 17.0 %collective-permute-start.20 = (bf16[352,1024]{1,0:T(8,128)(2,1)S(1)}, bf16[352,1024]{1,0:T(8,128)(2,1)S(1)}, u32[]{:S(2)}, u32[]{:S(2)}) collective-permute-start(bf16[352,1024]{1,0:T(8,128)(2,1)S(1)} %copy-done), channel_id=1, source_target_pairs={{0,2},{1,3},{2,0},{3,1},{4,6},{5,7},{6,4},{7,5},{8,10},{9,11},{10,... | collective-permute-start | bytes 2162696 | tf_op jit(solution)/shard_map/gather/ppermute | solution.py:574
  120.7 31.9 %collective-permute-start.21 = (bf16[352,1024]{1,0:T(8,128)(2,1)S(1)}, bf16[352,1024]{1,0:T(8,128)(2,1)S(1)}, u32[]{:S(2)}, u32[]{:S(2)}) collective-permute-start(bf16[352,1024]{1,0:T(8,128)(2,1)S(1)} %copy-done), channel_id=1, source_target_pairs={{0,1},{1,0},{2,3},{3,2},{4,5},{5,4},{6,7},{7,6},{8,9},{9,8},{10,11... | collective-permute-start | bytes 2162696 | tf_op jit(solution)/shard_map/gather/ppermute | solution.py:574
  121.2 31.3 %collective-permute-start.22 = (bf16[352,1024]{1,0:T(8,128)(2,1)S(1)}, bf16[352,1024]{1,0:T(8,128)(2,1)S(1)}, u32[]{:S(2)}, u32[]{:S(2)}) collective-permute-start(bf16[352,1024]{1,0:T(8,128)(2,1)S(1)} %collective-permute-done.20.refs_1_), channel_id=1, source_target_pairs={{0,1},{1,0},{2,3},{3,2},{4,5},{5,4},{6,7},{7,6},{8,9},{9,8},{10,11... | collective-permute-start | bytes 2162696 | tf_op jit(solution)/shard_map/gather/ppermute | solution.py:574
  122.7 29.9 %collective-permute-start.23 = (bf16[352,1024]{1,0:T(8,128)(2,1)S(1)}, bf16[352,1024]{1,0:T(8,128)(2,1)S(1)}, u32[]{:S(2)}, u32[]{:S(2)}) collective-permute-start(bf16[352,1024]{1,0:T(8,128)(2,1)S(1)} %collective-permute-done.18.refs_6_), channel_id=1, source_target_pairs={{0,16},{1,17},{2,18},{3,19},{4,20},{5,21},{6,22},{7,23},{8,24},{9,... | collective-permute-start | bytes 2162696 | tf_op jit(solution)/shard_map/gather/ppermute | solution.py:574
  153.7 28.9 %collective-permute-start.24 = (bf16[2,256,1024]{2,1,0:T(8,128)(2,1)}, bf16[2,256,1024]{2,1,0:T(8,128)(2,1)S(1)}, u32[]{:S(2)}, u32[]{:S(2)}) collective-permute-start(bf16[2,256,1024]{2,1,0:T(8,128)(2,1)} %get-tuple-element.298), channel_id=1, source_target_pairs={{0,1},{1,0},{2,3},{3,2},{4,5},{5,4},{6,7},{7,6},{8,9},{9,8},{10,11... | collective-permute-start | bytes 3145736 | tf_op jit(solution)/shard_map/ppermute | solution.py:574
  154.2 28.4 %collective-permute-start.25 = (bf16[2,256,1024]{2,1,0:T(8,128)(2,1)}, bf16[2,256,1024]{2,1,0:T(8,128)(2,1)S(1)}, u32[]{:S(2)}, u32[]{:S(2)}) collective-permute-start(bf16[2,256,1024]{2,1,0:T(8,128)(2,1)} %get-tuple-element.299), channel_id=1, source_target_pairs={{0,16},{1,17},{2,18},{3,19},{4,20},{5,21},{6,22},{7,23},{8,24},{9,... | collective-permute-start | bytes 3145736 | tf_op jit(solution)/shard_map/ppermute | solution.py:574
  184.1 40.1 %collective-permute-start.27 = (bf16[256,1024]{1,0:T(8,128)(2,1)}, bf16[256,1024]{1,0:T(8,128)(2,1)S(1)}, u32[]{:S(2)}, u32[]{:S(2)}) collective-permute-start(bf16[256,1024]{1,0:T(8,128)(2,1)} %get-tuple-element.436), channel_id=1, source_target_pairs={{0,2},{1,3},{2,0},{3,1},{4,6},{5,7},{6,4},{7,5},{8,10},{9,11},{10,... | collective-permute-start | bytes 1572872 | tf_op jit(solution)/shard_map/ppermute | solution.py:574
  184.6 39.6 %collective-permute-start.26 = (bf16[256,1024]{1,0:T(8,128)(2,1)}, bf16[256,1024]{1,0:T(8,128)(2,1)}, u32[]{:S(2)}, u32[]{:S(2)}) collective-permute-start(bf16[256,1024]{1,0:T(8,128)(2,1)} %get-tuple-element.437), channel_id=1, source_target_pairs={{0,1},{1,0},{2,3},{3,2},{4,5},{5,4},{6,7},{7,6},{8,9},{9,8},{10,11... | collective-permute-start | bytes 1572872 | tf_op jit(solution)/shard_map/ppermute | solution.py:574
  186.0 38.2 %collective-permute-start.28 = (bf16[2,256,1024]{2,1,0:T(8,128)(2,1)}, bf16[2,256,1024]{2,1,0:T(8,128)(2,1)S(1)}, u32[]{:S(2)}, u32[]{:S(2)}) collective-permute-start(bf16[2,256,1024]{2,1,0:T(8,128)(2,1)} %get-tuple-element.313), channel_id=1, source_target_pairs={{0,1},{1,0},{2,3},{3,2},{4,5},{5,4},{6,7},{7,6},{8,9},{9,8},{10,11... | collective-permute-start | bytes 3145736 | tf_op jit(solution)/shard_map/ppermute | solution.py:574
  186.6 37.6 %collective-permute-start.29 = (bf16[2,256,1024]{2,1,0:T(8,128)(2,1)}, bf16[2,256,1024]{2,1,0:T(8,128)(2,1)S(1)}, u32[]{:S(2)}, u32[]{:S(2)}) collective-permute-start(bf16[2,256,1024]{2,1,0:T(8,128)(2,1)} %get-tuple-element.314), channel_id=1, source_target_pairs={{0,16},{1,17},{2,18},{3,19},{4,20},{5,21},{6,22},{7,23},{8,24},{9,... | collective-permute-start | bytes 3145736 | tf_op jit(solution)/shard_map/ppermute | solution.py:574
  227.3 26.9 %collective-permute-start.30 = (bf16[256,1024]{1,0:T(8,128)(2,1)}, bf16[256,1024]{1,0:T(8,128)(2,1)}, u32[]{:S(2)}, u32[]{:S(2)}) collective-permute-start(bf16[256,1024]{1,0:T(8,128)(2,1)} %fusion.4), channel_id=1, source_target_pairs={{0,4},{1,5},{2,6},{3,7},{4,0},{5,1},{6,2},{7,3},{8,12},{9,13},{10,... | collective-permute-start | bytes 1572872 | tf_op jit(solution)/shard_map/ppermute | solution.py:574
  230.6 26.6 %collective-permute-start.32 = (bf16[256,1024]{1,0:T(8,128)(2,1)}, bf16[256,1024]{1,0:T(8,128)(2,1)}, u32[]{:S(2)}, u32[]{:S(2)}) collective-permute-start(bf16[256,1024]{1,0:T(8,128)(2,1)} %get-tuple-element.434), channel_id=1, source_target_pairs={{0,2},{1,3},{2,0},{3,1},{4,6},{5,7},{6,4},{7,5},{8,10},{9,11},{10,... | collective-permute-start | bytes 1572872 | tf_op jit(solution)/shard_map/ppermute | solution.py:574
  231.3 26.0 %collective-permute-start.33 = (bf16[256,1024]{1,0:T(8,128)(2,1)}, bf16[256,1024]{1,0:T(8,128)(2,1)}, u32[]{:S(2)}, u32[]{:S(2)}) collective-permute-start(bf16[256,1024]{1,0:T(8,128)(2,1)} %get-tuple-element.435), channel_id=1, source_target_pairs={{0,1},{1,0},{2,3},{3,2},{4,5},{5,4},{6,7},{7,6},{8,9},{9,8},{10,11... | collective-permute-start | bytes 1572872 | tf_op jit(solution)/shard_map/ppermute | solution.py:574
  253.2 31.7 %collective-permute-start.35 = (bf16[2,128,2048]{2,1,0:T(8,128)(2,1)}, bf16[2,128,2048]{2,1,0:T(8,128)(2,1)S(1)}, u32[]{:S(2)}, u32[]{:S(2)}) collective-permute-start(bf16[2,128,2048]{2,1,0:T(8,128)(2,1)} %get-tuple-element.345), channel_id=1, source_target_pairs={{0,1},{1,0},{2,3},{3,2},{4,5},{5,4},{6,7},{7,6},{8,9},{9,8},{10,11... | collective-permute-start | bytes 3145736 | tf_op jit(solution)/shard_map/ppermute | solution.py:574
  253.8 31.1 %collective-permute-start.36 = (bf16[2,128,2048]{2,1,0:T(8,128)(2,1)}, bf16[2,128,2048]{2,1,0:T(8,128)(2,1)}, u32[]{:S(2)}, u32[]{:S(2)}) collective-permute-start(bf16[2,128,2048]{2,1,0:T(8,128)(2,1)} %get-tuple-element.346), channel_id=1, source_target_pairs={{0,16},{1,17},{2,18},{3,19},{4,20},{5,21},{6,22},{7,23},{8,24},{9,... | collective-permute-start | bytes 3145736 | tf_op jit(solution)/shard_map/ppermute | solution.py:574
  255.6 29.3 %collective-permute-start.31 = (bf16[256,1024]{1,0:T(8,128)(2,1)S(1)}, bf16[256,1024]{1,0:T(8,128)(2,1)S(1)}, u32[]{:S(2)}, u32[]{:S(2)}) collective-permute-start(bf16[256,1024]{1,0:T(8,128)(2,1)S(1)} %fusion.3), channel_id=1, source_target_pairs={{0,16},{1,17},{2,18},{3,19},{4,20},{5,21},{6,22},{7,23},{8,24},{9,... | collective-permute-start | bytes 1572872 | tf_op jit(solution)/shard_map/ppermute | solution.py:574
  259.4 25.5 %collective-permute-start.34 = (bf16[256,1024]{1,0:T(8,128)(2,1)S(1)}, bf16[256,1024]{1,0:T(8,128)(2,1)}, u32[]{:S(2)}, u32[]{:S(2)}) collective-permute-start(bf16[256,1024]{1,0:T(8,128)(2,1)S(1)} %get-tuple-element.432), channel_id=1, source_target_pairs={{0,4},{1,5},{2,6},{3,7},{4,0},{5,1},{6,2},{7,3},{8,12},{9,13},{10,... | collective-permute-start | bytes 1572872 | tf_op jit(solution)/shard_map/ppermute | solution.py:574
  287.7 17.2 %collective-permute-start.41 = (bf16[2,1024,1024]{2,1,0:T(8,128)(2,1)}, bf16[2,1024,1024]{2,1,0:T(8,128)(2,1)}, u32[]{:S(2)}, u32[]{:S(2)}) collective-permute-start(bf16[2,1024,1024]{2,1,0:T(8,128)(2,1)} %get-tuple-element.366), channel_id=1, source_target_pairs={{0,8},{1,9},{2,10},{3,11},{4,12},{5,13},{6,14},{7,15},{8,0},{9,1},... | collective-permute-start | bytes 12582920 | tf_op jit(solution)/shard_map/ppermute | solution.py:574
  287.9 17.0 %collective-permute-start.40 = (bf16[128,2048]{1,0:T(8,128)(2,1)}, bf16[128,2048]{1,0:T(8,128)(2,1)}, u32[]{:S(2)}, u32[]{:S(2)}) collective-permute-start(bf16[128,2048]{1,0:T(8,128)(2,1)} %get-tuple-element.430), channel_id=1, source_target_pairs={{0,2},{1,3},{2,0},{3,1},{4,6},{5,7},{6,4},{7,5},{8,10},{9,11},{10,... | collective-permute-start | bytes 1572872 | tf_op jit(solution)/shard_map/ppermute | solution.py:574
  288.0 17.0 %collective-permute-start.39 = (bf16[128,2048]{1,0:T(8,128)(2,1)}, bf16[128,2048]{1,0:T(8,128)(2,1)}, u32[]{:S(2)}, u32[]{:S(2)}) collective-permute-start(bf16[128,2048]{1,0:T(8,128)(2,1)} %get-tuple-element.431), channel_id=1, source_target_pairs={{0,1},{1,0},{2,3},{3,2},{4,5},{5,4},{6,7},{7,6},{8,9},{9,8},{10,11... | collective-permute-start | bytes 1572872 | tf_op jit(solution)/shard_map/ppermute | solution.py:574
  290.7 14.2 %collective-permute-start.38 = (bf16[256,1024]{1,0:T(8,128)(2,1)S(1)}, bf16[256,1024]{1,0:T(8,128)(2,1)}, u32[]{:S(2)}, u32[]{:S(2)}) collective-permute-start(bf16[256,1024]{1,0:T(8,128)(2,1)S(1)} %add_convert_fusion.3), channel_id=1, source_target_pairs={{0,16},{1,17},{2,18},{3,19},{4,20},{5,21},{6,22},{7,23},{8,24},{9,... | collective-permute-start | bytes 1572872 | tf_op jit(solution)/shard_map/ppermute | solution.py:574
  306.2 29.5 %collective-permute-start.42 = (bf16[256,1024]{1,0:T(8,128)(2,1)S(1)}, bf16[256,1024]{1,0:T(8,128)(2,1)S(1)}, u32[]{:S(2)}, u32[]{:S(2)}) collective-permute-start(bf16[256,1024]{1,0:T(8,128)(2,1)S(1)} %add_convert_fusion.2.own), channel_id=1, source_target_pairs={{0,8},{1,9},{2,10},{3,11},{4,12},{5,13},{6,14},{7,15},{8,0},{9,1},... | collective-permute-start | bytes 1572872 | tf_op jit(solution)/shard_map/ppermute | solution.py:574
  308.3 27.5 %collective-permute-start.43 = (bf16[128,2048]{1,0:T(8,128)(2,1)S(1)}, bf16[128,2048]{1,0:T(8,128)(2,1)S(1)}, u32[]{:S(2)}, u32[]{:S(2)}) collective-permute-start(bf16[128,2048]{1,0:T(8,128)(2,1)S(1)} %get-tuple-element.429), channel_id=1, source_target_pairs={{0,4},{1,5},{2,6},{3,7},{4,0},{5,1},{6,2},{7,3},{8,12},{9,13},{10,... | collective-permute-start | bytes 1572872 | tf_op jit(solution)/shard_map/ppermute | solution.py:574
  335.9 15.2 %collective-permute-start.44 = (bf16[128,2048]{1,0:T(8,128)(2,1)S(1)}, bf16[128,2048]{1,0:T(8,128)(2,1)S(1)}, u32[]{:S(2)}, u32[]{:S(2)}) collective-permute-start(bf16[128,2048]{1,0:T(8,128)(2,1)S(1)} %add_convert_fusion.1), channel_id=1, source_target_pairs={{0,16},{1,17},{2,18},{3,19},{4,20},{5,21},{6,22},{7,23},{8,24},{9,... | collective-permute-start | bytes 1572872 | tf_op jit(solution)/shard_map/ppermute | solution.py:574
  337.5 13.5 %collective-permute-start.47 = (f32[16,1024]{1,0:T(8,128)S(1)}, f32[16,1024]{1,0:T(8,128)S(1)}, u32[]{:S(2)}, u32[]{:S(2)}) collective-permute-start(f32[16,1024]{1,0:T(8,128)S(1)} %concatenate.34), channel_id=1, source_target_pairs={{0,6},{1,7},{2,4},{3,5},{4,2},{5,3},{6,0},{7,1},{8,14},{9,15},{10,... | collective-permute-start | bytes 196616 | tf_op jit(solution)/shard_map/vectors/ppermute | solution.py:574
  339.7 11.4 %collective-permute-start.46 = (f32[16,1024]{1,0:T(8,128)S(1)}, f32[16,1024]{1,0:T(8,128)S(1)}, u32[]{:S(2)}, u32[]{:S(2)}) collective-permute-start(f32[16,1024]{1,0:T(8,128)S(1)} %concatenate.34), channel_id=1, source_target_pairs={{0,4},{1,5},{2,6},{3,7},{4,0},{5,1},{6,2},{7,3},{8,12},{9,13},{10,... | collective-permute-start | bytes 196616 | tf_op jit(solution)/shard_map/vectors/ppermute | solution.py:574
  339.7 11.4 %collective-permute-start.45 = (f32[16,1024]{1,0:T(8,128)S(1)}, f32[16,1024]{1,0:T(8,128)S(1)}, u32[]{:S(2)}, u32[]{:S(2)}) collective-permute-start(f32[16,1024]{1,0:T(8,128)S(1)} %concatenate.34), channel_id=1, source_target_pairs={{0,2},{1,3},{2,0},{3,1},{4,6},{5,7},{6,4},{7,5},{8,10},{9,11},{10,... | collective-permute-start | bytes 196616 | tf_op jit(solution)/shard_map/vectors/ppermute | solution.py:574
  351.1 5.5 %collective-permute-start.51 = (f32[16,1024]{1,0:T(8,128)S(1)}, f32[16,1024]{1,0:T(8,128)S(1)}, u32[]{:S(2)}, u32[]{:S(2)}) collective-permute-start(f32[16,1024]{1,0:T(8,128)S(1)} %add_add_fusion.1), channel_id=1, source_target_pairs={{0,17},{1,16},{2,19},{3,18},{4,21},{5,20},{6,23},{7,22},{8,25},{9,... | collective-permute-start | bytes 196616 | tf_op jit(solution)/shard_map/vectors/ppermute | solution.py:574
  354.8 5.3 %collective-permute-start.48 = (bf16[128,2048]{1,0:T(8,128)(2,1)S(1)}, bf16[128,2048]{1,0:T(8,128)(2,1)S(1)}, u32[]{:S(2)}, u32[]{:S(2)}) collective-permute-start(bf16[128,2048]{1,0:T(8,128)(2,1)S(1)} %add_convert_fusion.own), channel_id=1, source_target_pairs={{0,8},{1,9},{2,10},{3,11},{4,12},{5,13},{6,14},{7,15},{8,0},{9,1},... | collective-permute-start | bytes 1572872 | tf_op jit(solution)/shard_map/vectors/ppermute | solution.py:574
  (50 other events, 537.2 us)

commit v6 on v5

--- a/solution.py
+++ b/solution.py
@@ -209,23 +209,6 @@
     project(0, rows, w_qkv, bias, (cos, sin_lo, sin_hi), (q, k, v))
 
 
-def qkv_second_body(ids, *refs):
-    pieces, (attn_in, bias, cos, sin_lo, sin_hi, q, k, v, w_qkv) = refs[:8], refs[8:]
-
-    @pl.when(pl.program_id(0) == 0)
-    def _():
-        for place, piece in enumerate(pieces):
-            owner = piece_owner(ids, place)
-            for part in range(3):
-                for panel in range(4):
-                    at = pl.ds(pl.multiple_of(owner * 128 + 32 * panel, 32), 32)
-                    w_qkv[at, part * 256 : part * 256 + 256] = piece[
-                        32 * part : 32 * part + 32, panel * 256 : panel * 256 + 256
-                    ]
-
-    project(1, attn_in[...], w_qkv, bias, (cos, sin_lo, sin_hi), (q, k, v))
-
-
 ATTN_ROWS = 256
 
 
@@ -302,6 +285,30 @@
     grad[0] = turned(jnp.where(low, dq_a, dq_b) * HEAD_DIM ** (-0.5), *tables, -1.0).astype(BF16)
     grad[1] = turned(jnp.concatenate([dk_a, dk_b], axis=0).T, *tables, -1.0).astype(BF16)
     grad[2] = jnp.concatenate([dv_a, dv_b], axis=0).T.astype(BF16)
+
+
+def project_attn_body(ids, *refs):
+    pieces, (attn_in, bias, d_att, seg_col, seg_row, *tables) = refs[:8], refs[8:16]
+    att, grad, w_qkv, *projected = refs[16:]
+    half, pair = pl.program_id(0), pl.program_id(1)
+
+    @pl.when((half == 0) & (pair == 0))
+    def _():
+        for place, piece in enumerate(pieces):
+            owner = piece_owner(ids, place)
+            for part in range(3):
+                for panel in range(4):
+                    at = pl.ds(pl.multiple_of(owner * 128 + 32 * panel, 32), 32)
+                    w_qkv[at, part * 256 : part * 256 + 256] = piece[
+                        32 * part : 32 * part + 32, panel * 256 : panel * 256 + 256
+                    ]
+
+    @pl.when(pair == 0)
+    def _():
+        project(1, attn_in[...], w_qkv, bias, tables, projected)
+
+    lanes = pl.ds(pl.multiple_of(pair * LANES, LANES), LANES)
+    attn_body(*[value.at[:, lanes] for value in projected], d_att, seg_col, seg_row, *tables, att, grad)
 
 
 def attn_weights_body(ids, attn_t, grad_a, grad_b, far_att_a, far_att_b, far_own, far_other, *refs):
@@ -508,18 +515,26 @@
             adam_store(out_refs, (slice(64, 128), span), odd)
 
 
-def adam_mlp_body(ids, own, other, *refs):
-    core = ids[1]
+def adam_down_body(ids, own, other, *refs):
+    core, parity = ids[1], pl.program_id(0)
+    grad = jnp.where(core == parity, own[128:256, :], other[128:256, :]).astype(F32)
+    adam_store(refs, (slice(None), slice(None)), grad)
+
+
+def adam_mlp_body(ids, own_a, other_a, own_b, other_b, *refs):
+    core, step = ids[1], pl.program_id(0)
     up_refs = refs[0:3] + refs[-6:-3]
     down_refs = refs[3:6] + refs[-3:]
-    cols = pl.ds(pl.multiple_of(pl.program_id(0) * 128, 128), 128)
-    for base, refs_of in ((0, up_refs), (128, down_refs)):
-        rows = slice(base, base + 128)
-        for parity, grad in enumerate(
-            parities(core, own[rows, cols].astype(F32), other[rows, cols].astype(F32))
-        ):
-            span = slice(parity * 128, (parity + 1) * 128)
-            adam_store(refs_of, (slice(None), span) if base == 0 else (span, slice(None)), grad)
+    for owner in range(2):
+        cols = pl.ds(pl.multiple_of(step * 256 + owner * 128, 128), 128)
+        for part, (own, other) in enumerate(((own_a, other_a), (own_b, other_b))):
+            halves = parities(core, own[0:128, cols].astype(F32), other[0:128, cols].astype(F32))
+            for parity, grad in enumerate(halves):
+                base = owner * 512 + part * 256 + parity * 128
+                adam_store(up_refs, (slice(None), slice(base, base + 128)), grad)
+    rows = pl.ds(pl.multiple_of(128 + (step % 2) * 64, 64), 64)
+    grad = jnp.where(core == step // 2, own_b[rows, :], other_b[rows, :]).astype(F32)
+    adam_store(down_refs, (slice(None), slice(None)), grad)
 
 
 def rotary_tables(segments):
@@ -588,6 +603,9 @@
     def reduce_first(keep, send_x, send_y):
         return keep, swap(send_x, 0, 1), swap(send_y, 2, 0)
 
+    def reduce_first_part(keep, send_x, send_y):
+        return keep, [send_x[0], swap(send_x[1], 0, 1)], swap(send_y, 2, 0)
+
     def reduce_second(state):
         keep, got_x, got_y = state
         far = add(keep[3], got_y[1]).astype(BF16)
@@ -597,10 +615,11 @@
     def reduce_third(state):
         keep, got_x, got_y, _, _, got_far, got_near = state
         far = add(keep[2], got_y[0], got_far).astype(BF16)
-        return add(keep[0], got_x[0], got_near), far, swap_far(far)
+        return (keep, got_x, got_near), far, swap_far(far)
 
     def reduce_fourth(state):
-        total = (state[0] + state[2].astype(F32)).astype(BF16)
+        (keep, got_x, got_near), _, got = state
+        total = add(keep[0], got_x[0], got_near, got).astype(BF16)
         return total, swap(total, 2, 0)
 
     def reduce_fifth(state):
@@ -756,13 +775,13 @@
             30e6,
             name="qkv",
         )
-    projected, far_across_b, across_b, rest_b, next_b = sync(
-        projected, far_across_b, across_b, rest_b, next_b
+    projected, far_across_b, across_b, rest_b, own_b = sync(
+        projected, far_across_b, across_b, rest_b, own_b
     )
     with jax.named_scope("gather"):
-        rest_across_b, next_across_b = swap(far_across_b, 2, 0), swap(next_b, 0, 1)
+        rest_across_b, next_across_b = swap(far_across_b, 2, 0), swap(own_b, 0, 3)
     half_a = attention(0, (0,), projected, d_att, [])
-    half_a, projected, far_c, own_c = sync(half_a, projected, far_c, own_c)
+    half_a, projected, far_c, own_c, next_b = sync(half_a, projected, far_c, own_c, next_b)
     with jax.named_scope("gather"):
         far_across_c, rest_c, next_c = swap(far_c, 0, 1), swap(far_c, 2, 0), swap(own_c, 0, 2)
     att_a, grad_a = attention(0, (1,), projected, d_att, half_a)
@@ -812,25 +831,34 @@
     mlp_b = mlp(1, pieces_c, mlp_in)
     mlp_b, reduce_a, attn_in = sync(mlp_b, reduce_a, attn_in)
     reduce_a = reduce_second(reduce_a)
-    reduce_b = reduce_first(*mlp_b[0])
+    reduce_b = reduce_first_part(*mlp_b[0])
     attn_in, *ready = sync(attn_in, *reduce_a[3:5])
 
-    with jax.named_scope("qkv"):
-        *projected, wq_b = block_call(
-            qkv_second_body,
-            (rows // 512,),
+    with jax.named_scope("attention"):
+        head_block = spec((T, 128), lambda h, m: (h, m))
+        att_b, grad_b, wq_b = block_call(
+            project_attn_body,
+            (2, 2),
             [(ids, scalars())]
             + [(piece, whole((96, width))) for piece in pieces_c]
-            + [(attn_in, row_block(512)), const(bias_qkv)]
-            + table_blocks(512),
-            [(sds((rows, 256), BF16), row_block(512, 256))] * 3 + [kept((1024, 768), BF16)],
-            2 * rows * 1024 * 768,
-            12e6,
-            name="qkv",
+            + [(attn_in, spec((T, width), lambda h, m: (h, 0))), const(bias_qkv)]
+            + [(d_att, spec((T, 128), lambda h, m: (h, m + 2)))]
+            + [(seg_col, spec((T, LANES), lambda h, m: (h, 0)))]
+            + [(seg_row, spec((1, 1, T), lambda h, m: (h, 0, 0)))]
+            + [(t, spec((T, 128), lambda h, m: (h, 0))) for t in tables],
+            [
+                (sds((rows, 256), BF16), head_block),
+                (sds((3, rows, 256), BF16), spec((3, T, 128), lambda h, m: (0, h, m))),
+                kept((1024, 768), BF16),
+            ],
+            38e9,
+            20e6,
+            scratch=[pltpu.VMEM((T, 256), BF16)] * 3,
+            name="attention",
         )
-    att_b, grad_b = attention(1, (0, 1), projected, d_att, [])
     att_b, grad_b, reduce_a, reduce_b = sync(att_b, grad_b, reduce_a, reduce_b)
     reduce_a = reduce_third(reduce_a)
+    reduce_b[1][0] = swap(reduce_b[1][0], 0, 1)
     reduce_b = reduce_second(reduce_b)
     grad_b, *ready = sync(grad_b, reduce_a[1], *reduce_b[3:5])
     with jax.named_scope("attn_weights"):
@@ -850,31 +878,40 @@
             + [pltpu.SemaphoreType.DMA((4,))],
             name="attn_weights",
         )
-    blocks, grad_b = sync(blocks, grad_b)
+    blocks, grad_b, reduce_a, reduce_b = sync(blocks, grad_b, reduce_a, reduce_b)
     reduce_o = reduce_first(*blocks)
 
     _, hid_a, gp_a, sums_a, up_a, down_a = mlp_a
     _, hid_b, gp_b, sums_b, up_b, down_b = mlp_b
 
-    def adam_mlp(part, totals, previous):
-        wide = [spec((128, 256), lambda n: (0, 2 * n + part))] * 3
-        wide += [spec((256, 128), lambda n: (part, n))] * 3
+    def adam_down(totals):
+        wide = [spec((128, width), lambda n: (n, 0))] * 3
+        return kernel_call(
+            adam_down_body,
+            (2,),
+            [scalars()] + [whole((256, 1024))] * 2 + wide,
+            wide,
+            [sds((512, 1024), F32)] * 3,
+            0,
+            7e6,
+            name="adam_down",
+        )(ids, *totals, w_down, m_down, v_down)
+
+    def adam_mlp(totals_a, totals_b, previous):
+        wide = [spec((128, 1024), lambda n: (0, n))] * 3 + [spec((64, width), lambda n: (4 + n, 0))] * 3
         return pl.pallas_call(
             adam_mlp_body,
-            grid=(8,),
-            in_specs=[scalars()]
-            + [whole((256, 1024))] * 2
-            + wide
-            + [pl.BlockSpec(memory_space=pl.ANY)] * len(previous),
+            grid=(4,),
+            in_specs=[scalars()] + [whole((256, 1024))] * 4 + wide + [distant()] * 3,
             out_specs=wide,
             out_shape=[sds((128, 4096), F32)] * 3 + [sds((512, 1024), F32)] * 3,
-            input_output_aliases={9 + n: n for n in range(len(previous))},
-            cost_estimate=pl.CostEstimate(flops=0, bytes_accessed=14000000, transcendentals=0),
+            input_output_aliases={11 + n: 3 + n for n in range(3)},
+            cost_estimate=pl.CostEstimate(flops=0, bytes_accessed=21000000, transcendentals=0),
             compiler_params=pltpu.CompilerParams(
                 vmem_limit_bytes=VMEM_NEED * MIB, dimension_semantics=("arbitrary",)
             ),
             name="adam_mlp",
-        )(ids, *totals, w_up, m_up, v_up, w_down, m_down, v_down, *previous)
+        )(ids, *totals_a, *totals_b, w_up, m_up, v_up, w_down, m_down, v_down, *previous)
 
     def back(own, grad, rows_tok, extra, outs):
         first = 0 if own else T // 256
@@ -907,7 +944,7 @@
     reduce_a = reduce_fifth(reduce_a)
     reduce_b = reduce_fourth(reduce_b)
     part_got = swap(part_other, 1, 0)
-    updated_mlp = adam_mlp(0, reduce_a, [])
+    updated_mlp = adam_down(reduce_a)
     updated_mlp, grad_b, reduce_b, reduce_o, part_got = sync(
         updated_mlp, grad_b, reduce_b, reduce_o, part_got
     )
@@ -948,21 +985,11 @@
             axis=0,
         )
         moved = [swap(total, 0, step) for step in (2, 4, 6)]
-        updated_mlp = adam_mlp(1, reduce_b, updated_mlp)
+        updated_mlp = adam_mlp(reduce_a, reduce_b, updated_mlp)
         updated_mlp, reduce_o, total, moved = sync(updated_mlp, reduce_o, total, moved)
         reduce_o = reduce_fifth(reduce_o)
         total = functools.reduce(jnp.add, moved, total)
-        across, beside, both = swap(total, 0, 1), swap(total, 2, 0), swap(total, 2, 1)
-        total = (total + across) + (beside + both)
-        bit = 4
-        while bit < copies:
-            total = total + swap(total, bit, 0)
-            bit *= 2
-        total = total + swap(total, 1, 0)
-        share = lax.dynamic_slice_in_dim(total[0:13], me * 128, 128, 1)
-        first_vectors, second_vectors, new_vectors = adam_math(
-            vectors, m_vectors, v_vectors, share, RATE_VECTOR, 0.0
-        )
+        others = swap(total, 0, 1), swap(total, 2, 0), swap(total, 2, 1)
 
     with jax.named_scope("adam"):
         wide = [spec((128, 1024), lambda n: (0, n))] * 3 + [whole((128, 1024))] * 3
@@ -976,6 +1003,19 @@
             13e6,
             name="adam",
         )(ids, *reduce_o, w_qkv, m_qkv, v_qkv, w_out, m_out, v_out)
+
+    with jax.named_scope("vectors"):
+        updated_attn, total, (across, beside, both) = sync(updated_attn, total, others)
+        total = (total + across) + (beside + both)
+        bit = 4
+        while bit < copies:
+            total = total + swap(total, bit, 0)
+            bit *= 2
+        total = total + swap(total, 1, 0)
+        share = lax.dynamic_slice_in_dim(total[0:13], me * 128, 128, 1)
+        first_vectors, second_vectors, new_vectors = adam_math(
+            vectors, m_vectors, v_vectors, share, RATE_VECTOR, 0.0
+        )
     first_qkv, second_qkv, new_qkv, first_out, second_out, new_out = updated_attn
     first_up, second_up, new_up, first_down, second_down, new_down = updated_mlp
     return (

time: 376 us -> 371 us (0.987)
  Pallas kernels: 244 us -> 238 us
  waiting for transfers between devices: 36.4 us -> 31.3 us
    pallas_call x3 -> x2, Pallas kernels: 58.5 us -> 30.9 us  [attention(): pl.pallas_call(attn_body, grid=(2, len(pairs)), in_specs=[place for _, pl...]
    pallas_call x10, Pallas kernels: 160 us -> 185 us  [block_call(): kernel_call(body, grid, [place for _, place in ins], [place for _, place...]
    ppermute x53 -> x54, waiting for transfers between devices: 36.4 us -> 31.3 us  [move(): return lax.ppermute(value, AXES, pairs)]
    pallas_call x2, Pallas kernels: 18.2 us -> 13.7 us  [the longest x1 9.6 us: adam_mlp(): pl.pallas_call(adam_mlp_body, grid=(4,), in_specs=[scalars()] + [whole((2...]
    ppermute x53 -> x54, starting transfers between devices: 53.2 us -> 56.7 us  [move(): return lax.ppermute(value, AXES, pairs)]
  transfers between devices with their start and end apart: 53 -> 54, of which waited for: 13 -> 10; matrix products, arithmetic and copies ran while one was open for 5% -> 5% of each run, Pallas kernels for 63% -> 65%
where the time goes in v6:
time: 371 us; the launch traced here: 365 us
  Pallas kernels  238 us (64%)
  starting transfers between devices  56.7 us (15%)
  waiting for transfers between devices  31.3 us (8%)
  other arithmetic  27.5 us (7%)
  local copies, waits for them, and re-layouts  9.2 us (2%)
    pallas_call x10, Pallas kernels, block_call(): kernel_call(body, grid, [place for _, place in ins], [place for _, place...  185 us
    ppermute x54, starting transfers between devices, move(): return lax.ppermute(value, AXES, pairs)  56.7 us
    ppermute x54, waiting for transfers between devices, move(): return lax.ppermute(value, AXES, pairs)  31.3 us
    pallas_call x2, Pallas kernels, attention(): pl.pallas_call(attn_body, grid=(2, len(pairs)), in_specs=[place for _, pl...  30.9 us
    pallas_call x1, Pallas kernels, adam_mlp(): pl.pallas_call(adam_mlp_body, grid=(4,), in_specs=[scalars()] + [whole((2...  9.6 us
    pallas_call x1, Pallas kernels, on_device(): kernel_call(adam_attn_body, (3,), [scalars()] + [whole((128, 2048))] * 2...  8.1 us
  transfers between devices with their start and end apart: 54, of which 10 were waited for; matrix products, arithmetic and copies ran while one was open for 5% of the time, Pallas kernels for 65%

profile of v6, /device:TPU:0, one launch (start us, length us, event | category | flops | bytes accessed | tf_op | source)
XLA Modules:
  0.0 364.7 jit_solution(12944095062248282880)
XLA Ops:
  1.4 2.5 prep_attn.1.refs_0_
  3.9 3.0 collective-permute-start
  6.9 2.6 collective-permute-start.1
  10.7 2.8 prep_mlp.2.refs_0_
  13.6 1.5 collective-permute-start.2
  16.3 3.8 %fusion.11 = (f32[1024,128]{1,0:T(8,128)S(1)}, f32[1024,128]{1,0:T(8,128)S(1)}, f32[1024,128]{1,0:T(8,128)S(1)}, f32[1024,128]{1,0:T(8,128)S(1)}, f32[1024,128]{1,0:T(8,128)S(1)}, /*index=5*/f32[1024,128]{1,0:T(8,128)S(1)}) fusion(f32[128]{0:T(128)S(1)} %compare_select_fusion.2, f32[1024]{0:T(1024)S(1)} %fusion.26, ...), kind=kLoop, calls=%fused_computation.33 | loop fusion | flops 1048576 | bytes 3154560 | tf_op jit(solution)/shard_map/gather/jit(_where)/select_n | solution.py:553
  23.5 2.6 collective-permute-done.1.refs_2_
  29.1 2.6 collective-permute-start.8
  32.6 3.5 prep_mlp.3.refs_0_
  36.1 2.5 collective-permute-done.6.refs_5_
  38.6 7.9 %collective-permute-done.7.refs_6_ = bf16[144,1280]{1,0:T(8,128)(2,1)S(1)} collective-permute-done((bf16[144,1280]{1,0:T(8,128)(2,1)}, bf16[144,1280]{1,0:T(8,128)(2,1)S(1)}, u32[]{:S(2)}, u32[]{:S(2)}) %collective-permute-start.7) | collective-permute-done | bytes 368672 | tf_op jit(solution)/shard_map/gather/ppermute | solution.py:589
  46.5 7.3 %collective-permute-done.9.refs_7_ = bf16[144,1280]{1,0:T(8,128)(2,1)S(1)} collective-permute-done((bf16[144,1280]{1,0:T(8,128)(2,1)}, bf16[144,1280]{1,0:T(8,128)(2,1)S(1)}, u32[]{:S(2)}, u32[]{:S(2)}) %collective-permute-start.9) | collective-permute-done | bytes 368672 | tf_op jit(solution)/shard_map/gather/ppermute | solution.py:589
  55.2 1.5 collective-permute-start.11
  57.8 2.5 collective-permute-start.14
  60.2 17.2 %qkv.1 = (bf16[2048,256]{1,0:T(8,128)(2,1)}, bf16[2048,256]{1,0:T(8,128)(2,1)}, bf16[2048,256]{1,0:T(8,128)(2,1)}, bf16[2048,512]{1,0:T(8,128)(2,1)}, bf16[2048,...) custom-call(s32[3]{0:T(128)} %pad_add_fusion.2.ids, ...), custom_call_target="tpu_custom_call" | custom-call | flops 5368709120 | bytes 30000000 | tf_op jit(solution)/shard_map/qkv/qkv/pallas_call | solution.py:640
  79.0 2.1 collective-permute-start.17
  81.1 15.2 %attention.3 = (bf16[2048,256]{1,0:T(8,128)(2,1)}, bf16[3,2048,256]{2,1,0:T(8,128)(2,1)}) custom-call(bf16[2048,256]{1,0:T(8,128)(2,1)} %get-tuple-element.267.q, bf16[2048,256]{1,0:T(8,128)(2,1)} %get-tuple-element.268.k, bf16[2048,256]{1,0:T(8,128)(2,1)} %get-tuple-element.269.v, bf16[2048,512]{1,0:T(8,128)(2,1)} %get-tuple-element.261.d_att.refs_10_, ...), custom_call_target="tpu_custom_call" | custom-call | flops 15000000512 | bytes 5000000 | tf_op jit(solution)/shard_map/attention/attention/pallas_call | solution.py:742
  97.7 1.7 collective-permute-start.20
  99.4 15.7 %attention.4 = (bf16[2048,256]{1,0:T(8,128)(2,1)}, bf16[3,2048,256]{2,1,0:T(8,128)(2,1)}) custom-call(bf16[2048,256]{1,0:T(8,128)(2,1)} %get-tuple-element.267.q, bf16[2048,256]{1,0:T(8,128)(2,1)} %get-tuple-element.268.k, bf16[2048,256]{1,0:T(8,128)(2,1)} %get-tuple-element.269.v, ...), custom_call_target="tpu_custom_call", output_to_operand_aliasing={{0}: (9, {}), {1}: (10, {})} | custom-call | flops 15000000512 | bytes 5000000 | tf_op jit(solution)/shard_map/attention/attention/pallas_call | solution.py:742
  115.2 1.6 collective-permute-start.21
  118.5 27.7 %mlp.2 = (bf16[4,256,1024]{2,1,0:T(8,128)(2,1)}, bf16[2,256,1024]{2,1,0:T(8,128)(2,1)}, bf16[2,256,1024]{2,1,0:T(8,128)(2,1)}, bf16[2048,1024]{1,0:T(8,128)(2,1)...) custom-call(s32[3]{0:T(128)} %pad_add_fusion.2.ids, ...), custom_call_target="tpu_custom_call" | custom-call | flops 17179869184 | bytes 40000000 | tf_op jit(solution)/shard_map/mlp/mlp/pallas_call | solution.py:640
  149.7 28.2 %mlp.3 = (bf16[4,256,1024]{2,1,0:T(8,128)(2,1)}, bf16[2,256,1024]{2,1,0:T(8,128)(2,1)}, bf16[2,256,1024]{2,1,0:T(8,128)(2,1)}, bf16[2048,1024]{1,0:T(8,128)(2,1)...) custom-call(s32[3]{0:T(128)} %pad_add_fusion.2.ids, ...), custom_call_target="tpu_custom_call" | custom-call | flops 17179869184 | bytes 40000000 | tf_op jit(solution)/shard_map/mlp/mlp/pallas_call | solution.py:640
  181.3 1.5 collective-permute-start.28
  182.8 1.9 collective-permute-start.29
  184.7 34.1 %attention.5 = (bf16[2048,256]{1,0:T(8,128)(2,1)}, bf16[3,2048,256]{2,1,0:T(8,128)(2,1)}, bf16[1024,768]{1,0:T(8,128)(2,1)}) custom-call(s32[3]{0:T(128)} %pad_add_fusion.2.ids, bf16[352,1024]{1,0:T(8,128)(2,1)} %prep_mlp.3.refs_0_, bf16[352,1024]{1,0:T(8,128)(2,1)} %copy-done.32, bf16[352,1024]{1,0:T(8,128)(2,1)} %copy-done.29, ...), custom_call_target="tpu_custom_call" | custom-call | flops 38000001024 | bytes 20000000 | tf_op jit(solution)/shard_map/attention/attention/pallas_call | solution.py:640
  222.3 2.1 fusion.10
  225.4 1.5 collective-permute-start.31
  226.9 20.6 %attn_weights.1 = (bf16[4,128,2048]{2,1,0:T(8,128)(2,1)}, bf16[2,128,2048]{2,1,0:T(8,128)(2,1)}, bf16[2,128,2048]{2,1,0:T(8,128)(2,1)}, f32[8,1536]{1,0:T(8,128)}) custom-call(s32[3]{0:T(128)} %pad_add_fusion.2.ids, bf16[1024,2048]{1,0:T(8,128)(2,1)} %get-tuple-element.281.attn_t, bf16[3,2048,256]{2,1,0:T(8,128)(2,1)} %get-tuple-element.280.grad_a, ...), custom_call_target="tpu_custom_call" | custom-call | flops 8589934592 | bytes 24000000 | tf_op jit(solution)/shard_map/attn_weights/attn_weights/pallas_call | solution.py:640
  247.6 2.3 fusion.7
  249.9 1.9 collective-permute-start.35
  251.8 1.6 fusion.9
  253.4 1.8 collective-permute-start.34
  256.0 23.1 %back.2 = (bf16[2,1024,1024]{2,1,0:T(8,128)(2,1)}, f32[8,1024]{1,0:T(8,128)}) custom-call(bf16[3,2048,256]{2,1,0:T(8,128)(2,1)} %get-tuple-element.280.grad_a, bf16[3,2048,256]{2,1,0:T(8,128)(2,1)} %get-tuple-element.397.grad_b, bf16[2048,256]{1,0:T(8,128)(2,1)} %get-tuple-element.336.far_att_a.att_a, bf16[2048,256]{1,0:T(8,128)(2,1)} %get-tuple-element.337.far_att_b.att_b, ...), custom_call_target="tpu_custom_call" | custom-call | flops 12884901888 | bytes 40000000 | tf_op jit(solution)/shard_map/back/back/pallas_call | solution.py:640
  279.2 1.9 collective-permute-done.37
  281.1 2.6 fusion.21
  284.4 1.6 collective-permute-start.41
  286.1 1.7 fusion.2
  292.4 4.1 %adam_down.1 = (f32[512,1024]{1,0:T(8,128)}, f32[512,1024]{1,0:T(8,128)}, f32[512,1024]{1,0:T(8,128)}) custom-call(s32[3]{0:T(128)} %pad_add_fusion.2.ids, bf16[256,1024]{1,0:T(8,128)(2,1)} %copy-done, bf16[256,1024]{1,0:T(8,128)(2,1)} %copy-done.6, f32[512,1024]{1,0:T(8,128)} %refs_3_.2, f32[512,1024]{1,0:T(8,128)} %refs_4_.2, f32[512,1024]{1,0:T(8,128)} %refs_5_.2), custom_call_target="tpu_custom_call" | custom-call | bytes 7000000 | tf_op jit(solution)/shard_map/adam_down/pallas_call | solution.py:889
  296.5 5.2 %collective-permute-done.39 = bf16[256,1024]{1,0:T(8,128)(2,1)S(1)} collective-permute-done((bf16[256,1024]{1,0:T(8,128)(2,1)S(1)}, bf16[256,1024]{1,0:T(8,128)(2,1)S(1)}, u32[]{:S(2)}, u32[]{:S(2)}) %collective-permute-start.39) | collective-permute-done | bytes 524320 | tf_op jit(solution)/shard_map/ppermute | solution.py:589
  302.0 1.5 fusion.6
  303.5 1.8 collective-permute-start.44
  305.3 25.9 %back.3 = (bf16[1024,1024]{1,0:T(8,128)(2,1)}, f32[1024,1024]{1,0:T(8,128)}, f32[8,1024]{1,0:T(8,128)}) custom-call(bf16[3,2048,256]{2,1,0:T(8,128)(2,1)} %get-tuple-element.280.grad_a, bf16[3,2048,256]{2,1,0:T(8,128)(2,1)} %get-tuple-element.397.grad_b, bf16[2048,256]{1,0:T(8,128)(2,1)} %get-tuple-element.336.far_att_a.att_a, ...), custom_call_target="tpu_custom_call" | custom-call | flops 12884901888 | bytes 40000000 | tf_op jit(solution)/shard_map/back/back/pallas_call | solution.py:640
  331.2 1.7 fusion.5
  332.9 1.5 collective-permute-start.45
  337.3 2.8 collective-permute-start.48
  340.1 9.6 %adam_mlp.1 = (f32[128,4096]{1,0:T(8,128)}, f32[128,4096]{1,0:T(8,128)}, f32[128,4096]{1,0:T(8,128)}, f32[512,1024]{1,0:T(8,128)}, f32[512,1024]{1,0:T(8,128)}, /*index=5*/f32[512,1024]{1,0:T(8,128)}) custom-call(s32[3]{0:T(128)} %pad_add_fusion.2.ids, bf16[256,1024]{1,0:T(8,128)(2,1)} %copy-done, ...), custom_call_target="tpu_custom_call", output_to_operand_aliasing={{3}: (11, {}), {4}: (12, {}), {5}: (13, {})} | custom-call | bytes 21000000 | tf_op jit(solution)/shard_map/vectors/adam_mlp/pallas_call | solution.py:902
  350.0 1.6 collective-permute-start.50
  354.4 8.1 %adam.1 = (f32[128,3072]{1,0:T(8,128)}, f32[128,3072]{1,0:T(8,128)}, f32[128,3072]{1,0:T(8,128)}, f32[128,1024]{1,0:T(8,128)}, f32[128,1024]{1,0:T(8,128)}, /*index=5*/f32[128,1024]{1,0:T(8,128)}) custom-call(s32[3]{0:T(128)} %pad_add_fusion.2.ids, bf16[128,2048]{1,0:T(8,128)(2,1)} %copy-done.7, bf16[128,2048]{1,0:T(8,128)(2,1)} %copy-done.20, ...), custom_call_target="tpu_custom_call" | custom-call | bytes 13000000 | tf_op jit(solution)/shard_map/adam/adam/pallas_call | solution.py:996
  (229 shorter events, 43.2 us)
Async XLA Ops:
  3.9 19.6 %collective-permute-start = (bf16[144,1280]{1,0:T(8,128)(2,1)}, bf16[144,1280]{1,0:T(8,128)(2,1)S(1)}, u32[]{:S(2)}, u32[]{:S(2)}) collective-permute-start(bf16[144,1280]{1,0:T(8,128)(2,1)} %prep_attn.1.refs_0_), channel_id=1, source_target_pairs={{0,2},{1,3},{2,0},{3,1},{4,6},{5,7},{6,4},{7,5},{8,10},{9,11},{10,... | collective-permute-start | bytes 1105928 | tf_op jit(solution)/shard_map/gather/ppermute | solution.py:589
  6.9 19.1 %collective-permute-start.1 = (bf16[144,1280]{1,0:T(8,128)(2,1)}, bf16[144,1280]{1,0:T(8,128)(2,1)S(1)}, u32[]{:S(2)}, u32[]{:S(2)}) collective-permute-start(bf16[144,1280]{1,0:T(8,128)(2,1)} %prep_attn.1.refs_0_), channel_id=1, source_target_pairs={{0,4},{1,5},{2,6},{3,7},{4,0},{5,1},{6,2},{7,3},{8,12},{9,13},{10,... | collective-permute-start | bytes 1105928 | tf_op jit(solution)/shard_map/gather/ppermute | solution.py:589
  9.5 16.5 %collective-permute-start.4 = (bf16[1024,1024]{1,0:T(8,128)(2,1)S(1)}, bf16[1024,1024]{1,0:T(8,128)(2,1)}, u32[]{:S(2)}, u32[]{:S(2)}) collective-permute-start(bf16[1024,1024]{1,0:T(8,128)(2,1)S(1)} %copy-done.28), channel_id=1, source_target_pairs={{0,8},{1,9},{2,10},{3,11},{4,12},{5,13},{6,14},{7,15},{8,0},{9,1},... | collective-permute-start | bytes 6291464 | tf_op jit(solution)/shard_map/gather/ppermute | solution.py:589
  10.0 16.0 %collective-permute-start.5 = (bf16[1024,1024]{1,0:T(8,128)(2,1)}, bf16[1024,1024]{1,0:T(8,128)(2,1)}, u32[]{:S(2)}, u32[]{:S(2)}) collective-permute-start(bf16[1024,1024]{1,0:T(8,128)(2,1)} %refs_9_.1), channel_id=1, source_target_pairs={{0,8},{1,9},{2,10},{3,11},{4,12},{5,13},{6,14},{7,15},{8,0},{9,1},... | collective-permute-start | bytes 6291464 | tf_op jit(solution)/shard_map/gather/ppermute | solution.py:589
  13.6 12.5 %collective-permute-start.2 = (bf16[144,1280]{1,0:T(8,128)(2,1)S(1)}, bf16[144,1280]{1,0:T(8,128)(2,1)}, u32[]{:S(2)}, u32[]{:S(2)}) collective-permute-start(bf16[144,1280]{1,0:T(8,128)(2,1)S(1)} %copy-done.21), channel_id=1, source_target_pairs={{0,1},{1,0},{2,3},{3,2},{4,5},{5,4},{6,7},{7,6},{8,9},{9,8},{10,11... | collective-permute-start | bytes 1105928 | tf_op jit(solution)/shard_map/gather/ppermute | solution.py:589
  26.8 27.1 %collective-permute-start.10 = (bf16[256,1024]{1,0:T(8,128)(2,1)S(1)}, bf16[256,1024]{1,0:T(8,128)(2,1)S(1)}, u32[]{:S(2)}, u32[]{:S(2)}) collective-permute-start(bf16[256,1024]{1,0:T(8,128)(2,1)S(1)} %copy-done.14), channel_id=1, source_target_pairs={{0,4},{1,5},{2,6},{3,7},{4,0},{5,1},{6,2},{7,3},{8,12},{9,13},{10,... | collective-permute-start | bytes 1572872 | tf_op jit(solution)/shard_map/gather/ppermute | solution.py:589
  27.1 11.5 %collective-permute-start.6 = (bf16[144,1280]{1,0:T(8,128)(2,1)S(1)}, bf16[144,1280]{1,0:T(8,128)(2,1)S(1)}, u32[]{:S(2)}, u32[]{:S(2)}) collective-permute-start(bf16[144,1280]{1,0:T(8,128)(2,1)S(1)} %collective-permute-done.refs_1_), channel_id=1, source_target_pairs={{0,1},{1,0},{2,3},{3,2},{4,5},{5,4},{6,7},{7,6},{8,9},{9,8},{10,11... | collective-permute-start | bytes 1105928 | tf_op jit(solution)/shard_map/gather/ppermute | solution.py:589
  28.6 17.9 %collective-permute-start.7 = (bf16[144,1280]{1,0:T(8,128)(2,1)}, bf16[144,1280]{1,0:T(8,128)(2,1)S(1)}, u32[]{:S(2)}, u32[]{:S(2)}) collective-permute-start(bf16[144,1280]{1,0:T(8,128)(2,1)} %copy-done.43), channel_id=1, source_target_pairs={{0,1},{1,0},{2,3},{3,2},{4,5},{5,4},{6,7},{7,6},{8,9},{9,8},{10,11... | collective-permute-start | bytes 1105928 | tf_op jit(solution)/shard_map/gather/ppermute | solution.py:589
  29.1 17.4 %collective-permute-start.8 = (bf16[144,1280]{1,0:T(8,128)(2,1)}, bf16[144,1280]{1,0:T(8,128)(2,1)S(1)}, u32[]{:S(2)}, u32[]{:S(2)}) collective-permute-start(bf16[144,1280]{1,0:T(8,128)(2,1)} %copy-done.43), channel_id=1, source_target_pairs={{0,16},{1,17},{2,18},{3,19},{4,20},{5,21},{6,22},{7,23},{8,24},{9,... | collective-permute-start | bytes 1105928 | tf_op jit(solution)/shard_map/gather/ppermute | solution.py:589
  31.7 22.2 %collective-permute-start.9 = (bf16[144,1280]{1,0:T(8,128)(2,1)}, bf16[144,1280]{1,0:T(8,128)(2,1)S(1)}, u32[]{:S(2)}, u32[]{:S(2)}) collective-permute-start(bf16[144,1280]{1,0:T(8,128)(2,1)} %copy-done.43), channel_id=1, source_target_pairs={{0,17},{1,16},{2,19},{3,18},{4,21},{5,20},{6,23},{7,22},{8,25},{9,... | collective-permute-start | bytes 1105928 | tf_op jit(solution)/shard_map/gather/ppermute | solution.py:589
  55.2 22.3 %collective-permute-start.11 = (bf16[256,1024]{1,0:T(8,128)(2,1)S(1)}, bf16[256,1024]{1,0:T(8,128)(2,1)S(1)}, u32[]{:S(2)}, u32[]{:S(2)}) collective-permute-start(bf16[256,1024]{1,0:T(8,128)(2,1)S(1)} %collective-permute-done.10.refs_2_), channel_id=1, source_target_pairs={{0,1},{1,0},{2,3},{3,2},{4,5},{5,4},{6,7},{7,6},{8,9},{9,8},{10,11... | collective-permute-start | bytes 1572872 | tf_op jit(solution)/shard_map/gather/ppermute | solution.py:589
  56.7 21.1 %collective-permute-start.12 = (bf16[256,1024]{1,0:T(8,128)(2,1)S(1)}, bf16[256,1024]{1,0:T(8,128)(2,1)S(1)}, u32[]{:S(2)}, u32[]{:S(2)}) collective-permute-start(bf16[256,1024]{1,0:T(8,128)(2,1)S(1)} %copy-done.14), channel_id=1, source_target_pairs={{0,1},{1,0},{2,3},{3,2},{4,5},{5,4},{6,7},{7,6},{8,9},{9,8},{10,11... | collective-permute-start | bytes 1572872 | tf_op jit(solution)/shard_map/gather/ppermute | solution.py:589
  57.2 20.6 %collective-permute-start.13 = (bf16[256,1024]{1,0:T(8,128)(2,1)S(1)}, bf16[256,1024]{1,0:T(8,128)(2,1)S(1)}, u32[]{:S(2)}, u32[]{:S(2)}) collective-permute-start(bf16[256,1024]{1,0:T(8,128)(2,1)S(1)} %collective-permute-done.10.refs_2_), channel_id=1, source_target_pairs={{0,16},{1,17},{2,18},{3,19},{4,20},{5,21},{6,22},{7,23},{8,24},{9,... | collective-permute-start | bytes 1572872 | tf_op jit(solution)/shard_map/gather/ppermute | solution.py:589
  57.2 39.1 %collective-permute-start.15 = (bf16[256,1024]{1,0:T(8,128)(2,1)S(1)}, bf16[256,1024]{1,0:T(8,128)(2,1)S(1)}, u32[]{:S(2)}, u32[]{:S(2)}) collective-permute-start(bf16[256,1024]{1,0:T(8,128)(2,1)S(1)} %copy-done.14), channel_id=1, source_target_pairs={{0,2},{1,3},{2,0},{3,1},{4,6},{5,7},{6,4},{7,5},{8,10},{9,11},{10,... | collective-permute-start | bytes 1572872 | tf_op jit(solution)/shard_map/gather/ppermute | solution.py:589
  57.8 38.6 %collective-permute-start.14 = (bf16[352,1024]{1,0:T(8,128)(2,1)}, bf16[352,1024]{1,0:T(8,128)(2,1)S(1)}, u32[]{:S(2)}, u32[]{:S(2)}) collective-permute-start(bf16[352,1024]{1,0:T(8,128)(2,1)} %prep_mlp.3.refs_0_), channel_id=1, source_target_pairs={{0,4},{1,5},{2,6},{3,7},{4,0},{5,1},{6,2},{7,3},{8,12},{9,13},{10,... | collective-permute-start | bytes 2162696 | tf_op jit(solution)/shard_map/gather/ppermute | solution.py:589
  77.8 37.3 %collective-permute-start.16 = (bf16[256,1024]{1,0:T(8,128)(2,1)S(1)}, bf16[256,1024]{1,0:T(8,128)(2,1)S(1)}, u32[]{:S(2)}, u32[]{:S(2)}) collective-permute-start(bf16[256,1024]{1,0:T(8,128)(2,1)S(1)} %collective-permute-done.11.refs_6_), channel_id=1, source_target_pairs={{0,16},{1,17},{2,18},{3,19},{4,20},{5,21},{6,22},{7,23},{8,24},{9,... | collective-permute-start | bytes 1572872 | tf_op jit(solution)/shard_map/gather/ppermute | solution.py:589
  79.0 36.1 %collective-permute-start.17 = (bf16[256,1024]{1,0:T(8,128)(2,1)S(1)}, bf16[256,1024]{1,0:T(8,128)(2,1)}, u32[]{:S(2)}, u32[]{:S(2)}) collective-permute-start(bf16[256,1024]{1,0:T(8,128)(2,1)S(1)} %copy-done.14), channel_id=1, source_target_pairs={{0,3},{1,2},{2,1},{3,0},{4,7},{5,6},{6,5},{7,4},{8,11},{9,10},{10,... | collective-permute-start | bytes 1572872 | tf_op jit(solution)/shard_map/gather/ppermute | solution.py:589
  97.1 18.0 %collective-permute-start.18 = (bf16[352,1024]{1,0:T(8,128)(2,1)S(1)}, bf16[352,1024]{1,0:T(8,128)(2,1)S(1)}, u32[]{:S(2)}, u32[]{:S(2)}) collective-permute-start(bf16[352,1024]{1,0:T(8,128)(2,1)S(1)} %collective-permute-done.14.refs_2_), channel_id=1, source_target_pairs={{0,1},{1,0},{2,3},{3,2},{4,5},{5,4},{6,7},{7,6},{8,9},{9,8},{10,11... | collective-permute-start | bytes 2162696 | tf_op jit(solution)/shard_map/gather/ppermute | solution.py:589
  97.7 17.5 %collective-permute-start.19 = (bf16[352,1024]{1,0:T(8,128)(2,1)S(1)}, bf16[352,1024]{1,0:T(8,128)(2,1)S(1)}, u32[]{:S(2)}, u32[]{:S(2)}) collective-permute-start(bf16[352,1024]{1,0:T(8,128)(2,1)S(1)} %collective-permute-done.14.refs_2_), channel_id=1, source_target_pairs={{0,16},{1,17},{2,18},{3,19},{4,20},{5,21},{6,22},{7,23},{8,24},{9,... | collective-permute-start | bytes 2162696 | tf_op jit(solution)/shard_map/gather/ppermute | solution.py:589
  97.7 17.4 %collective-permute-start.20 = (bf16[352,1024]{1,0:T(8,128)(2,1)S(1)}, bf16[352,1024]{1,0:T(8,128)(2,1)S(1)}, u32[]{:S(2)}, u32[]{:S(2)}) collective-permute-start(bf16[352,1024]{1,0:T(8,128)(2,1)S(1)} %copy-done.13), channel_id=1, source_target_pairs={{0,2},{1,3},{2,0},{3,1},{4,6},{5,7},{6,4},{7,5},{8,10},{9,11},{10,... | collective-permute-start | bytes 2162696 | tf_op jit(solution)/shard_map/gather/ppermute | solution.py:589
  115.2 31.0 %collective-permute-start.21 = (bf16[352,1024]{1,0:T(8,128)(2,1)S(1)}, bf16[352,1024]{1,0:T(8,128)(2,1)S(1)}, u32[]{:S(2)}, u32[]{:S(2)}) collective-permute-start(bf16[352,1024]{1,0:T(8,128)(2,1)S(1)} %copy-done.13), channel_id=1, source_target_pairs={{0,1},{1,0},{2,3},{3,2},{4,5},{5,4},{6,7},{7,6},{8,9},{9,8},{10,11... | collective-permute-start | bytes 2162696 | tf_op jit(solution)/shard_map/gather/ppermute | solution.py:589
  116.7 29.5 %collective-permute-start.22 = (bf16[352,1024]{1,0:T(8,128)(2,1)S(1)}, bf16[352,1024]{1,0:T(8,128)(2,1)S(1)}, u32[]{:S(2)}, u32[]{:S(2)}) collective-permute-start(bf16[352,1024]{1,0:T(8,128)(2,1)S(1)} %collective-permute-done.20.refs_1_), channel_id=1, source_target_pairs={{0,1},{1,0},{2,3},{3,2},{4,5},{5,4},{6,7},{7,6},{8,9},{9,8},{10,11... | collective-permute-start | bytes 2162696 | tf_op jit(solution)/shard_map/gather/ppermute | solution.py:589
  117.3 28.9 %collective-permute-start.23 = (bf16[352,1024]{1,0:T(8,128)(2,1)S(1)}, bf16[352,1024]{1,0:T(8,128)(2,1)S(1)}, u32[]{:S(2)}, u32[]{:S(2)}) collective-permute-start(bf16[352,1024]{1,0:T(8,128)(2,1)S(1)} %collective-permute-done.18.refs_6_), channel_id=1, source_target_pairs={{0,16},{1,17},{2,18},{3,19},{4,20},{5,21},{6,22},{7,23},{8,24},{9,... | collective-permute-start | bytes 2162696 | tf_op jit(solution)/shard_map/gather/ppermute | solution.py:589
  147.4 30.5 %collective-permute-start.24 = (bf16[2,256,1024]{2,1,0:T(8,128)(2,1)}, bf16[2,256,1024]{2,1,0:T(8,128)(2,1)S(1)}, u32[]{:S(2)}, u32[]{:S(2)}) collective-permute-start(bf16[2,256,1024]{2,1,0:T(8,128)(2,1)} %get-tuple-element.314), channel_id=1, source_target_pairs={{0,1},{1,0},{2,3},{3,2},{4,5},{5,4},{6,7},{7,6},{8,9},{9,8},{10,11... | collective-permute-start | bytes 3145736 | tf_op jit(solution)/shard_map/ppermute | solution.py:589
  148.8 29.1 %collective-permute-start.25 = (bf16[2,256,1024]{2,1,0:T(8,128)(2,1)}, bf16[2,256,1024]{2,1,0:T(8,128)(2,1)S(1)}, u32[]{:S(2)}, u32[]{:S(2)}) collective-permute-start(bf16[2,256,1024]{2,1,0:T(8,128)(2,1)} %get-tuple-element.315), channel_id=1, source_target_pairs={{0,16},{1,17},{2,18},{3,19},{4,20},{5,21},{6,22},{7,23},{8,24},{9,... | collective-permute-start | bytes 3145736 | tf_op jit(solution)/shard_map/ppermute | solution.py:589
  179.3 39.6 %collective-permute-start.26 = (bf16[256,1024]{1,0:T(8,128)(2,1)}, bf16[256,1024]{1,0:T(8,128)(2,1)}, u32[]{:S(2)}, u32[]{:S(2)}) collective-permute-start(bf16[256,1024]{1,0:T(8,128)(2,1)} %get-tuple-element.461), channel_id=1, source_target_pairs={{0,1},{1,0},{2,3},{3,2},{4,5},{5,4},{6,7},{7,6},{8,9},{9,8},{10,11... | collective-permute-start | bytes 1572872 | tf_op jit(solution)/shard_map/ppermute | solution.py:589
  179.8 39.0 %collective-permute-start.27 = (bf16[256,1024]{1,0:T(8,128)(2,1)}, bf16[256,1024]{1,0:T(8,128)(2,1)}, u32[]{:S(2)}, u32[]{:S(2)}) collective-permute-start(bf16[256,1024]{1,0:T(8,128)(2,1)} %get-tuple-element.460), channel_id=1, source_target_pairs={{0,2},{1,3},{2,0},{3,1},{4,6},{5,7},{6,4},{7,5},{8,10},{9,11},{10,... | collective-permute-start | bytes 1572872 | tf_op jit(solution)/shard_map/ppermute | solution.py:589
  181.3 37.6 %collective-permute-start.28 = (bf16[256,1024]{1,0:T(8,128)(2,1)}, bf16[256,1024]{1,0:T(8,128)(2,1)S(1)}, u32[]{:S(2)}, u32[]{:S(2)}) collective-permute-start(bf16[256,1024]{1,0:T(8,128)(2,1)} %get-tuple-element.462), channel_id=1, source_target_pairs={{0,1},{1,0},{2,3},{3,2},{4,5},{5,4},{6,7},{7,6},{8,9},{9,8},{10,11... | collective-permute-start | bytes 1572872 | tf_op jit(solution)/shard_map/ppermute | solution.py:589
  182.8 36.1 %collective-permute-start.29 = (bf16[2,256,1024]{2,1,0:T(8,128)(2,1)}, bf16[2,256,1024]{2,1,0:T(8,128)(2,1)S(1)}, u32[]{:S(2)}, u32[]{:S(2)}) collective-permute-start(bf16[2,256,1024]{2,1,0:T(8,128)(2,1)} %get-tuple-element.327), channel_id=1, source_target_pairs={{0,16},{1,17},{2,18},{3,19},{4,20},{5,21},{6,22},{7,23},{8,24},{9,... | collective-permute-start | bytes 3145736 | tf_op jit(solution)/shard_map/ppermute | solution.py:589
  220.9 26.6 %collective-permute-start.33 = (bf16[256,1024]{1,0:T(8,128)(2,1)}, bf16[256,1024]{1,0:T(8,128)(2,1)S(1)}, u32[]{:S(2)}, u32[]{:S(2)}) collective-permute-start(bf16[256,1024]{1,0:T(8,128)(2,1)} %fusion.3), channel_id=1, source_target_pairs={{0,2},{1,3},{2,0},{3,1},{4,6},{5,7},{6,4},{7,5},{8,10},{9,11},{10,... | collective-permute-start | bytes 1572872 | tf_op jit(solution)/shard_map/ppermute | solution.py:589
  221.8 25.8 %collective-permute-start.32 = (bf16[256,1024]{1,0:T(8,128)(2,1)}, bf16[256,1024]{1,0:T(8,128)(2,1)}, u32[]{:S(2)}, u32[]{:S(2)}) collective-permute-start(bf16[256,1024]{1,0:T(8,128)(2,1)} %fusion.19), channel_id=1, source_target_pairs={{0,1},{1,0},{2,3},{3,2},{4,5},{5,4},{6,7},{7,6},{8,9},{9,8},{10,11... | collective-permute-start | bytes 1572872 | tf_op jit(solution)/shard_map/ppermute | solution.py:589
  224.4 23.1 %collective-permute-start.30 = (bf16[256,1024]{1,0:T(8,128)(2,1)}, bf16[256,1024]{1,0:T(8,128)(2,1)}, u32[]{:S(2)}, u32[]{:S(2)}) collective-permute-start(bf16[256,1024]{1,0:T(8,128)(2,1)} %fusion.10), channel_id=1, source_target_pairs={{0,4},{1,5},{2,6},{3,7},{4,0},{5,1},{6,2},{7,3},{8,12},{9,13},{10,... | collective-permute-start | bytes 1572872 | tf_op jit(solution)/shard_map/ppermute | solution.py:589
  225.4 22.1 %collective-permute-start.31 = (bf16[256,1024]{1,0:T(8,128)(2,1)}, bf16[256,1024]{1,0:T(8,128)(2,1)}, u32[]{:S(2)}, u32[]{:S(2)}) collective-permute-start(bf16[256,1024]{1,0:T(8,128)(2,1)} %get-tuple-element.343), channel_id=1, source_target_pairs={{0,1},{1,0},{2,3},{3,2},{4,5},{5,4},{6,7},{7,6},{8,9},{9,8},{10,11... | collective-permute-start | bytes 1572872 | tf_op jit(solution)/shard_map/ppermute | solution.py:589
  249.9 29.2 %collective-permute-start.35 = (bf16[256,1024]{1,0:T(8,128)(2,1)}, bf16[256,1024]{1,0:T(8,128)(2,1)S(1)}, u32[]{:S(2)}, u32[]{:S(2)}) collective-permute-start(bf16[256,1024]{1,0:T(8,128)(2,1)} %fusion.7), channel_id=1, source_target_pairs={{0,4},{1,5},{2,6},{3,7},{4,0},{5,1},{6,2},{7,3},{8,12},{9,13},{10,... | collective-permute-start | bytes 1572872 | tf_op jit(solution)/shard_map/ppermute | solution.py:589
  253.4 25.8 %collective-permute-start.34 = (bf16[256,1024]{1,0:T(8,128)(2,1)S(1)}, bf16[256,1024]{1,0:T(8,128)(2,1)S(1)}, u32[]{:S(2)}, u32[]{:S(2)}) collective-permute-start(bf16[256,1024]{1,0:T(8,128)(2,1)S(1)} %fusion.9), channel_id=1, source_target_pairs={{0,16},{1,17},{2,18},{3,19},{4,20},{5,21},{6,22},{7,23},{8,24},{9,... | collective-permute-start | bytes 1572872 | tf_op jit(solution)/shard_map/ppermute | solution.py:589
  255.2 24.0 %collective-permute-start.36 = (bf16[2,128,2048]{2,1,0:T(8,128)(2,1)}, bf16[2,128,2048]{2,1,0:T(8,128)(2,1)}, u32[]{:S(2)}, u32[]{:S(2)}) collective-permute-start(bf16[2,128,2048]{2,1,0:T(8,128)(2,1)} %get-tuple-element.368), channel_id=1, source_target_pairs={{0,1},{1,0},{2,3},{3,2},{4,5},{5,4},{6,7},{7,6},{8,9},{9,8},{10,11... | collective-permute-start | bytes 3145736 | tf_op jit(solution)/shard_map/ppermute | solution.py:589
  255.7 25.4 %collective-permute-start.37 = (bf16[2,128,2048]{2,1,0:T(8,128)(2,1)}, bf16[2,128,2048]{2,1,0:T(8,128)(2,1)}, u32[]{:S(2)}, u32[]{:S(2)}) collective-permute-start(bf16[2,128,2048]{2,1,0:T(8,128)(2,1)} %get-tuple-element.369), channel_id=1, source_target_pairs={{0,16},{1,17},{2,18},{3,19},{4,20},{5,21},{6,22},{7,23},{8,24},{9,... | collective-permute-start | bytes 3145736 | tf_op jit(solution)/shard_map/ppermute | solution.py:589
  283.7 18.0 %collective-permute-start.42 = (bf16[2,1024,1024]{2,1,0:T(8,128)(2,1)}, bf16[2,1024,1024]{2,1,0:T(8,128)(2,1)}, u32[]{:S(2)}, u32[]{:S(2)}) collective-permute-start(bf16[2,1024,1024]{2,1,0:T(8,128)(2,1)} %get-tuple-element.390), channel_id=1, source_target_pairs={{0,8},{1,9},{2,10},{3,11},{4,12},{5,13},{6,14},{7,15},{8,0},{9,1},... | collective-permute-start | bytes 12582920 | tf_op jit(solution)/shard_map/ppermute | solution.py:589
  283.9 17.8 %collective-permute-start.40 = (bf16[128,2048]{1,0:T(8,128)(2,1)}, bf16[128,2048]{1,0:T(8,128)(2,1)}, u32[]{:S(2)}, u32[]{:S(2)}) collective-permute-start(bf16[128,2048]{1,0:T(8,128)(2,1)} %get-tuple-element.459), channel_id=1, source_target_pairs={{0,1},{1,0},{2,3},{3,2},{4,5},{5,4},{6,7},{7,6},{8,9},{9,8},{10,11... | collective-permute-start | bytes 1572872 | tf_op jit(solution)/shard_map/ppermute | solution.py:589
  284.4 17.2 %collective-permute-start.41 = (bf16[128,2048]{1,0:T(8,128)(2,1)}, bf16[128,2048]{1,0:T(8,128)(2,1)}, u32[]{:S(2)}, u32[]{:S(2)}) collective-permute-start(bf16[128,2048]{1,0:T(8,128)(2,1)} %get-tuple-element.458), channel_id=1, source_target_pairs={{0,2},{1,3},{2,0},{3,1},{4,6},{5,7},{6,4},{7,5},{8,10},{9,11},{10,... | collective-permute-start | bytes 1572872 | tf_op jit(solution)/shard_map/ppermute | solution.py:589
  287.8 13.8 %collective-permute-start.39 = (bf16[256,1024]{1,0:T(8,128)(2,1)S(1)}, bf16[256,1024]{1,0:T(8,128)(2,1)S(1)}, u32[]{:S(2)}, u32[]{:S(2)}) collective-permute-start(bf16[256,1024]{1,0:T(8,128)(2,1)S(1)} %fusion.2), channel_id=1, source_target_pairs={{0,16},{1,17},{2,18},{3,19},{4,20},{5,21},{6,22},{7,23},{8,24},{9,... | collective-permute-start | bytes 1572872 | tf_op jit(solution)/shard_map/ppermute | solution.py:589
  301.9 29.3 %collective-permute-start.43 = (bf16[256,1024]{1,0:T(8,128)(2,1)S(1)}, bf16[256,1024]{1,0:T(8,128)(2,1)S(1)}, u32[]{:S(2)}, u32[]{:S(2)}) collective-permute-start(bf16[256,1024]{1,0:T(8,128)(2,1)S(1)} %add_convert_fusion.1.own_b), channel_id=1, source_target_pairs={{0,8},{1,9},{2,10},{3,11},{4,12},{5,13},{6,14},{7,15},{8,0},{9,1},... | collective-permute-start | bytes 1572872 | tf_op jit(solution)/shard_map/ppermute | solution.py:589
  303.5 27.7 %collective-permute-start.44 = (bf16[128,2048]{1,0:T(8,128)(2,1)S(1)}, bf16[128,2048]{1,0:T(8,128)(2,1)S(1)}, u32[]{:S(2)}, u32[]{:S(2)}) collective-permute-start(bf16[128,2048]{1,0:T(8,128)(2,1)S(1)} %fusion.6), channel_id=1, source_target_pairs={{0,4},{1,5},{2,6},{3,7},{4,0},{5,1},{6,2},{7,3},{8,12},{9,13},{10,... | collective-permute-start | bytes 1572872 | tf_op jit(solution)/shard_map/ppermute | solution.py:589
  332.9 16.8 %collective-permute-start.45 = (bf16[128,2048]{1,0:T(8,128)(2,1)S(1)}, bf16[128,2048]{1,0:T(8,128)(2,1)S(1)}, u32[]{:S(2)}, u32[]{:S(2)}) collective-permute-start(bf16[128,2048]{1,0:T(8,128)(2,1)S(1)} %fusion.5), channel_id=1, source_target_pairs={{0,16},{1,17},{2,18},{3,19},{4,20},{5,21},{6,22},{7,23},{8,24},{9,... | collective-permute-start | bytes 1572872 | tf_op jit(solution)/shard_map/ppermute | solution.py:589
  335.6 14.1 %collective-permute-start.46 = (f32[16,1024]{1,0:T(8,128)S(1)}, f32[16,1024]{1,0:T(8,128)S(1)}, u32[]{:S(2)}, u32[]{:S(2)}) collective-permute-start(f32[16,1024]{1,0:T(8,128)S(1)} %concatenate.34), channel_id=1, source_target_pairs={{0,2},{1,3},{2,0},{3,1},{4,6},{5,7},{6,4},{7,5},{8,10},{9,11},{10,... | collective-permute-start | bytes 196616 | tf_op jit(solution)/shard_map/vectors/ppermute | solution.py:589
  336.5 13.2 %collective-permute-start.47 = (f32[16,1024]{1,0:T(8,128)S(1)}, f32[16,1024]{1,0:T(8,128)S(1)}, u32[]{:S(2)}, u32[]{:S(2)}) collective-permute-start(f32[16,1024]{1,0:T(8,128)S(1)} %concatenate.34), channel_id=1, source_target_pairs={{0,4},{1,5},{2,6},{3,7},{4,0},{5,1},{6,2},{7,3},{8,12},{9,13},{10,... | collective-permute-start | bytes 196616 | tf_op jit(solution)/shard_map/vectors/ppermute | solution.py:589
  337.3 12.4 %collective-permute-start.48 = (f32[16,1024]{1,0:T(8,128)S(1)}, f32[16,1024]{1,0:T(8,128)S(1)}, u32[]{:S(2)}, u32[]{:S(2)}) collective-permute-start(f32[16,1024]{1,0:T(8,128)S(1)} %concatenate.34), channel_id=1, source_target_pairs={{0,6},{1,7},{2,4},{3,5},{4,2},{5,3},{6,0},{7,1},{8,14},{9,15},{10,... | collective-permute-start | bytes 196616 | tf_op jit(solution)/shard_map/vectors/ppermute | solution.py:589
  350.0 12.5 %collective-permute-start.50 = (f32[16,1024]{1,0:T(8,128)S(1)}, f32[16,1024]{1,0:T(8,128)S(1)}, u32[]{:S(2)}, u32[]{:S(2)}) collective-permute-start(f32[16,1024]{1,0:T(8,128)S(1)} %add_add_fusion.1), channel_id=1, source_target_pairs={{0,1},{1,0},{2,3},{3,2},{4,5},{5,4},{6,7},{7,6},{8,9},{9,8},{10,11... | collective-permute-start | bytes 196616 | tf_op jit(solution)/shard_map/vectors/ppermute | solution.py:589
  (54 other events, 578.1 us)

commit v7 on v6

--- a/solution.py
+++ b/solution.py
@@ -107,14 +107,14 @@
     return jnp.where(core == 0, even, odd)
 
 
-def prep_attn_body(ids, w_qkv, w_out, vec, out):
+def prep_attn_body(ids, w_q, w_k, w_v, w_out, vec, out):
     core = ids[1]
-    for part in range(3):
+    for part, w in enumerate((w_q, w_k, w_v)):
         for tile in range(2):
-            base = part * 1024 + tile * 256
+            base = tile * 256
             at = part * 256 + tile * 128
             out[0:128, at : at + 128] = pick_parity(
-                core, w_qkv[:, base : base + 128], w_qkv[:, base + 128 : base + 256]
+                core, w[:, base : base + 128], w[:, base + 128 : base + 256]
             ).astype(BF16)
     rows = w_out[pl.ds(pl.multiple_of(core * 64, 64), 64), :].astype(BF16)
     for panel in range(4):
@@ -494,9 +494,11 @@
     core = ids[1]
     low = low_lanes()
     qkv_refs = refs[0:3] + refs[6:9]
-    for tile in range(4):
-        start = (tile // 2) * 768 + (tile % 2) * 128
-        cols = pl.ds(pl.multiple_of(pl.program_id(0) * 256 + start, 128), 128)
+    for tile in range(6):
+        count = pl.program_id(0) * 6 + tile
+        part, place = count // 4, count % 4
+        start = (place // 2) * 768 + part * 256 + (place % 2) * 128
+        cols = pl.ds(pl.multiple_of(start, 128), 128)
         even, odd = parities(core, own[:, cols].astype(F32), other[:, cols].astype(F32))
         first = jnp.where(low, even, pltpu.roll(odd, HEAD_DIM, 1))
         second = jnp.where(low, pltpu.roll(even, HEAD_DIM, 1), odd)
@@ -660,7 +662,9 @@
         own_a = block_call(
             prep_attn_body,
             (1,),
-            [(ids, scalars()), const(w_qkv), const(w_out), (vectors, whole((16, 128)))],
+            [(ids, scalars())]
+            + [(w_qkv, spec((128, 512), lambda i, n=part: (0, 2 * n), single=True)) for part in range(3)]
+            + [const(w_out), (vectors, whole((16, 128)))],
             [kept((144, 1280), BF16)],
             0,
             3e6,
@@ -704,9 +708,10 @@
         rest_a = swap(far_a, 2, 0)
         far_b = swap_far(own_b)
         seg_col = jnp.broadcast_to(seg_ids[:, None], (rows, LANES))
+        w_up_in, seg_col = sync(w_up_in, seg_col)
         own_c = prep_mlp(1, (352, 1024), (w_up_in, w_down, w_qkv), 25)
-        next_across_a, far_across_a, rest_a, rest_across_a, far_b, own_b, own_c, seg_col = sync(
-            next_across_a, far_across_a, rest_a, rest_across_a, far_b, own_b, own_c, seg_col
+        next_across_a, far_across_a, rest_a, rest_across_a, far_b, own_b, own_c = sync(
+            next_across_a, far_across_a, rest_a, rest_across_a, far_b, own_b, own_c
         )
         far_across_b, across_b, rest_b = swap(far_b, 0, 1), swap(own_b, 0, 1), swap(far_b, 2, 0)
         next_b = swap(own_b, 0, 2)
@@ -992,10 +997,10 @@
         others = swap(total, 0, 1), swap(total, 2, 0), swap(total, 2, 1)
 
     with jax.named_scope("adam"):
-        wide = [spec((128, 1024), lambda n: (0, n))] * 3 + [whole((128, 1024))] * 3
+        wide = [spec((128, 1536), lambda n: (0, n))] * 3 + [whole((128, 1024))] * 3
         updated_attn = kernel_call(
             adam_attn_body,
-            (3,),
+            (2,),
             [scalars()] + [whole((128, 2048))] * 2 + wide,
             wide,
             [sds((128, 3072), F32)] * 3 + [sds((128, 1024), F32)] * 3,

time: 371 us -> 367 us (0.989)
  transfers between devices with their start and end apart: 54 -> 54, of which waited for: 10 -> 9; matrix products, arithmetic and copies ran while one was open for 5% -> 6% of each run, Pallas kernels for 65% -> 65%
where the time goes in v7:
time: 367 us; the launch traced here: 361 us
  Pallas kernels  237 us (65%)
  starting transfers between devices  56.6 us (15%)
  waiting for transfers between devices  29.7 us (8%)
  other arithmetic  27.5 us (7%)
  local copies, waits for them, and re-layouts  9.2 us (3%)
    pallas_call x10, Pallas kernels, block_call(): kernel_call(body, grid, [place for _, place in ins], [place for _, place...  185 us
    ppermute x54, starting transfers between devices, move(): return lax.ppermute(value, AXES, pairs)  56.6 us
    pallas_call x2, Pallas kernels, attention(): pl.pallas_call(attn_body, grid=(2, len(pairs)), in_specs=[place for _, pl...  30.9 us
    ppermute x54, waiting for transfers between devices, move(): return lax.ppermute(value, AXES, pairs)  29.7 us
    pallas_call x1, Pallas kernels, adam_mlp(): pl.pallas_call(adam_mlp_body, grid=(4,), in_specs=[scalars()] + [whole((2...  9.6 us
  transfers between devices with their start and end apart: 54, of which 9 were waited for; matrix products, arithmetic and copies ran while one was open for 6% of the time, Pallas kernels for 65%

profile of v7, /device:TPU:0, one launch (start us, length us, event | category | flops | bytes accessed | tf_op | source)
XLA Modules:
  0.0 361.4 jit_solution(13253970066429128402)
XLA Ops:
  1.3 2.3 prep_attn.1.refs_0_
  3.7 3.0 collective-permute-start
  6.7 2.6 collective-permute-start.1
  10.6 2.8 prep_mlp.2.refs_0_
  13.4 1.5 collective-permute-start.2
  16.1 3.8 %fusion.11 = (f32[1024,128]{1,0:T(8,128)S(1)}, f32[1024,128]{1,0:T(8,128)S(1)}, f32[1024,128]{1,0:T(8,128)S(1)}, f32[1024,128]{1,0:T(8,128)S(1)}, f32[1024,128]{1,0:T(8,128)S(1)}, /*index=5*/f32[1024,128]{1,0:T(8,128)S(1)}) fusion(f32[128]{0:T(128)S(1)} %compare_select_fusion.2, f32[1024]{0:T(1024)S(1)} %fusion.26, ...), kind=kLoop, calls=%fused_computation.33 | loop fusion | flops 1048576 | bytes 3154560 | tf_op jit(solution)/shard_map/gather/jit(_where)/select_n | solution.py:555
  23.3 2.6 collective-permute-done.1.refs_2_
  26.9 1.5 collective-permute-start.6
  28.9 2.6 collective-permute-start.8
  33.7 3.5 prep_mlp.3.refs_0_
  38.4 7.9 %collective-permute-done.7.refs_6_ = bf16[144,1280]{1,0:T(8,128)(2,1)S(1)} collective-permute-done((bf16[144,1280]{1,0:T(8,128)(2,1)}, bf16[144,1280]{1,0:T(8,128)(2,1)S(1)}, u32[]{:S(2)}, u32[]{:S(2)}) %collective-permute-start.7) | collective-permute-done | bytes 368672 | tf_op jit(solution)/shard_map/gather/ppermute | solution.py:591
  46.3 7.9 %collective-permute-done.9.refs_7_ = bf16[144,1280]{1,0:T(8,128)(2,1)S(1)} collective-permute-done((bf16[144,1280]{1,0:T(8,128)(2,1)}, bf16[144,1280]{1,0:T(8,128)(2,1)S(1)}, u32[]{:S(2)}, u32[]{:S(2)}) %collective-permute-start.9) | collective-permute-done | bytes 368672 | tf_op jit(solution)/shard_map/gather/ppermute | solution.py:591
  54.2 1.6 collective-permute-start.11
  57.7 1.6 collective-permute-start.14
  59.3 17.2 %qkv.1 = (bf16[2048,256]{1,0:T(8,128)(2,1)}, bf16[2048,256]{1,0:T(8,128)(2,1)}, bf16[2048,256]{1,0:T(8,128)(2,1)}, bf16[2048,512]{1,0:T(8,128)(2,1)}, bf16[2048,...) custom-call(s32[3]{0:T(128)} %pad_add_fusion.2.ids, ...), custom_call_target="tpu_custom_call" | custom-call | flops 5368709120 | bytes 30000000 | tf_op jit(solution)/shard_map/qkv/qkv/pallas_call | solution.py:642
  76.6 1.5 collective-permute-start.16
  78.1 2.1 collective-permute-start.17
  80.2 15.2 %attention.3 = (bf16[2048,256]{1,0:T(8,128)(2,1)}, bf16[3,2048,256]{2,1,0:T(8,128)(2,1)}) custom-call(bf16[2048,256]{1,0:T(8,128)(2,1)} %get-tuple-element.269.q, bf16[2048,256]{1,0:T(8,128)(2,1)} %get-tuple-element.270.k, bf16[2048,256]{1,0:T(8,128)(2,1)} %get-tuple-element.271.v, bf16[2048,512]{1,0:T(8,128)(2,1)} %get-tuple-element.263.d_att.refs_10_, ...), custom_call_target="tpu_custom_call" | custom-call | flops 15000000512 | bytes 5000000 | tf_op jit(solution)/shard_map/attention/attention/pallas_call | solution.py:747
  98.2 15.7 %attention.4 = (bf16[2048,256]{1,0:T(8,128)(2,1)}, bf16[3,2048,256]{2,1,0:T(8,128)(2,1)}) custom-call(bf16[2048,256]{1,0:T(8,128)(2,1)} %get-tuple-element.269.q, bf16[2048,256]{1,0:T(8,128)(2,1)} %get-tuple-element.270.k, bf16[2048,256]{1,0:T(8,128)(2,1)} %get-tuple-element.271.v, ...), custom_call_target="tpu_custom_call", output_to_operand_aliasing={{0}: (9, {}), {1}: (10, {})} | custom-call | flops 15000000512 | bytes 5000000 | tf_op jit(solution)/shard_map/attention/attention/pallas_call | solution.py:747
  114.0 1.6 collective-permute-start.21
  117.5 27.7 %mlp.2 = (bf16[4,256,1024]{2,1,0:T(8,128)(2,1)}, bf16[2,256,1024]{2,1,0:T(8,128)(2,1)}, bf16[2,256,1024]{2,1,0:T(8,128)(2,1)}, bf16[2048,1024]{1,0:T(8,128)(2,1)...) custom-call(s32[3]{0:T(128)} %pad_add_fusion.2.ids, ...), custom_call_target="tpu_custom_call" | custom-call | flops 17179869184 | bytes 40000000 | tf_op jit(solution)/shard_map/mlp/mlp/pallas_call | solution.py:642
  146.4 1.5 collective-permute-start.24
  148.5 28.2 %mlp.3 = (bf16[4,256,1024]{2,1,0:T(8,128)(2,1)}, bf16[2,256,1024]{2,1,0:T(8,128)(2,1)}, bf16[2,256,1024]{2,1,0:T(8,128)(2,1)}, bf16[2048,1024]{1,0:T(8,128)(2,1)...) custom-call(s32[3]{0:T(128)} %pad_add_fusion.2.ids, ...), custom_call_target="tpu_custom_call" | custom-call | flops 17179869184 | bytes 40000000 | tf_op jit(solution)/shard_map/mlp/mlp/pallas_call | solution.py:642
  180.3 1.5 collective-permute-start.28
  181.8 2.0 collective-permute-start.29
  183.8 34.1 %attention.5 = (bf16[2048,256]{1,0:T(8,128)(2,1)}, bf16[3,2048,256]{2,1,0:T(8,128)(2,1)}, bf16[1024,768]{1,0:T(8,128)(2,1)}) custom-call(s32[3]{0:T(128)} %pad_add_fusion.2.ids, bf16[352,1024]{1,0:T(8,128)(2,1)} %prep_mlp.3.refs_0_, bf16[352,1024]{1,0:T(8,128)(2,1)} %copy-done.32, bf16[352,1024]{1,0:T(8,128)(2,1)} %copy-done.29, ...), custom_call_target="tpu_custom_call" | custom-call | flops 38000001024 | bytes 20000000 | tf_op jit(solution)/shard_map/attention/attention/pallas_call | solution.py:642
  221.4 2.1 fusion.10
  224.5 1.5 collective-permute-start.31
  226.0 20.6 %attn_weights.1 = (bf16[4,128,2048]{2,1,0:T(8,128)(2,1)}, bf16[2,128,2048]{2,1,0:T(8,128)(2,1)}, bf16[2,128,2048]{2,1,0:T(8,128)(2,1)}, f32[8,1536]{1,0:T(8,128)}) custom-call(s32[3]{0:T(128)} %pad_add_fusion.2.ids, bf16[1024,2048]{1,0:T(8,128)(2,1)} %get-tuple-element.283.attn_t, bf16[3,2048,256]{2,1,0:T(8,128)(2,1)} %get-tuple-element.282.grad_a, ...), custom_call_target="tpu_custom_call" | custom-call | flops 8589934592 | bytes 24000000 | tf_op jit(solution)/shard_map/attn_weights/attn_weights/pallas_call | solution.py:642
  246.7 2.3 fusion.7
  249.0 1.9 collective-permute-start.35
  250.9 1.6 fusion.9
  252.5 1.5 collective-permute-start.34
  255.1 23.1 %back.2 = (bf16[2,1024,1024]{2,1,0:T(8,128)(2,1)}, f32[8,1024]{1,0:T(8,128)}) custom-call(bf16[3,2048,256]{2,1,0:T(8,128)(2,1)} %get-tuple-element.282.grad_a, bf16[3,2048,256]{2,1,0:T(8,128)(2,1)} %get-tuple-element.399.grad_b, bf16[2048,256]{1,0:T(8,128)(2,1)} %get-tuple-element.338.far_att_a.att_a, bf16[2048,256]{1,0:T(8,128)(2,1)} %get-tuple-element.339.far_att_b.att_b, ...), custom_call_target="tpu_custom_call" | custom-call | flops 12884901888 | bytes 40000000 | tf_op jit(solution)/shard_map/back/back/pallas_call | solution.py:642
  278.2 1.5 collective-permute-done.37
  279.7 2.6 fusion.21
  283.0 2.6 collective-permute-start.41
  285.6 1.7 fusion.2
  291.0 4.1 %adam_down.1 = (f32[512,1024]{1,0:T(8,128)}, f32[512,1024]{1,0:T(8,128)}, f32[512,1024]{1,0:T(8,128)}) custom-call(s32[3]{0:T(128)} %pad_add_fusion.2.ids, bf16[256,1024]{1,0:T(8,128)(2,1)} %copy-done, bf16[256,1024]{1,0:T(8,128)(2,1)} %copy-done.6, f32[512,1024]{1,0:T(8,128)} %refs_3_.2, f32[512,1024]{1,0:T(8,128)} %refs_4_.2, f32[512,1024]{1,0:T(8,128)} %refs_5_.2), custom_call_target="tpu_custom_call" | custom-call | bytes 7000000 | tf_op jit(solution)/shard_map/adam_down/pallas_call | solution.py:894
  295.0 6.1 %collective-permute-done.39 = bf16[256,1024]{1,0:T(8,128)(2,1)S(1)} collective-permute-done((bf16[256,1024]{1,0:T(8,128)(2,1)S(1)}, bf16[256,1024]{1,0:T(8,128)(2,1)S(1)}, u32[]{:S(2)}, u32[]{:S(2)}) %collective-permute-start.39) | collective-permute-done | bytes 524320 | tf_op jit(solution)/shard_map/ppermute | solution.py:591
  301.5 1.5 fusion.6
  303.4 25.9 %back.3 = (bf16[1024,1024]{1,0:T(8,128)(2,1)}, f32[1024,1024]{1,0:T(8,128)}, f32[8,1024]{1,0:T(8,128)}) custom-call(bf16[3,2048,256]{2,1,0:T(8,128)(2,1)} %get-tuple-element.282.grad_a, bf16[3,2048,256]{2,1,0:T(8,128)(2,1)} %get-tuple-element.399.grad_b, bf16[2048,256]{1,0:T(8,128)(2,1)} %get-tuple-element.338.far_att_a.att_a, ...), custom_call_target="tpu_custom_call" | custom-call | flops 12884901888 | bytes 40000000 | tf_op jit(solution)/shard_map/back/back/pallas_call | solution.py:642
  329.3 1.7 fusion.5
  331.1 1.5 collective-permute-start.45
  334.6 2.1 collective-permute-start.47
  338.2 9.6 %adam_mlp.1 = (f32[128,4096]{1,0:T(8,128)}, f32[128,4096]{1,0:T(8,128)}, f32[128,4096]{1,0:T(8,128)}, f32[512,1024]{1,0:T(8,128)}, f32[512,1024]{1,0:T(8,128)}, /*index=5*/f32[512,1024]{1,0:T(8,128)}) custom-call(s32[3]{0:T(128)} %pad_add_fusion.2.ids, bf16[256,1024]{1,0:T(8,128)(2,1)} %copy-done, ...), custom_call_target="tpu_custom_call", output_to_operand_aliasing={{3}: (11, {}), {4}: (12, {}), {5}: (13, {})} | custom-call | bytes 21000000 | tf_op jit(solution)/shard_map/vectors/adam_mlp/pallas_call | solution.py:907
  348.1 1.5 collective-permute-start.50
  352.5 6.7 %adam.1 = (f32[128,3072]{1,0:T(8,128)}, f32[128,3072]{1,0:T(8,128)}, f32[128,3072]{1,0:T(8,128)}, f32[128,1024]{1,0:T(8,128)}, f32[128,1024]{1,0:T(8,128)}, /*index=5*/f32[128,1024]{1,0:T(8,128)}) custom-call(s32[3]{0:T(128)} %pad_add_fusion.2.ids, bf16[128,2048]{1,0:T(8,128)(2,1)} %copy-done.7, bf16[128,2048]{1,0:T(8,128)(2,1)} %copy-done.20, ...), custom_call_target="tpu_custom_call" | custom-call | bytes 13000000 | tf_op jit(solution)/shard_map/adam/adam/pallas_call | solution.py:1001
  (229 shorter events, 42.6 us)
Async XLA Ops:
  3.7 19.6 %collective-permute-start = (bf16[144,1280]{1,0:T(8,128)(2,1)}, bf16[144,1280]{1,0:T(8,128)(2,1)S(1)}, u32[]{:S(2)}, u32[]{:S(2)}) collective-permute-start(bf16[144,1280]{1,0:T(8,128)(2,1)} %prep_attn.1.refs_0_), channel_id=1, source_target_pairs={{0,2},{1,3},{2,0},{3,1},{4,6},{5,7},{6,4},{7,5},{8,10},{9,11},{10,... | collective-permute-start | bytes 1105928 | tf_op jit(solution)/shard_map/gather/ppermute | solution.py:591
  6.7 19.1 %collective-permute-start.1 = (bf16[144,1280]{1,0:T(8,128)(2,1)}, bf16[144,1280]{1,0:T(8,128)(2,1)S(1)}, u32[]{:S(2)}, u32[]{:S(2)}) collective-permute-start(bf16[144,1280]{1,0:T(8,128)(2,1)} %prep_attn.1.refs_0_), channel_id=1, source_target_pairs={{0,4},{1,5},{2,6},{3,7},{4,0},{5,1},{6,2},{7,3},{8,12},{9,13},{10,... | collective-permute-start | bytes 1105928 | tf_op jit(solution)/shard_map/gather/ppermute | solution.py:591
  9.3 16.5 %collective-permute-start.4 = (bf16[1024,1024]{1,0:T(8,128)(2,1)S(1)}, bf16[1024,1024]{1,0:T(8,128)(2,1)}, u32[]{:S(2)}, u32[]{:S(2)}) collective-permute-start(bf16[1024,1024]{1,0:T(8,128)(2,1)S(1)} %copy-done.28), channel_id=1, source_target_pairs={{0,8},{1,9},{2,10},{3,11},{4,12},{5,13},{6,14},{7,15},{8,0},{9,1},... | collective-permute-start | bytes 6291464 | tf_op jit(solution)/shard_map/gather/ppermute | solution.py:591
  9.8 16.0 %collective-permute-start.5 = (bf16[1024,1024]{1,0:T(8,128)(2,1)}, bf16[1024,1024]{1,0:T(8,128)(2,1)}, u32[]{:S(2)}, u32[]{:S(2)}) collective-permute-start(bf16[1024,1024]{1,0:T(8,128)(2,1)} %refs_9_.1), channel_id=1, source_target_pairs={{0,8},{1,9},{2,10},{3,11},{4,12},{5,13},{6,14},{7,15},{8,0},{9,1},... | collective-permute-start | bytes 6291464 | tf_op jit(solution)/shard_map/gather/ppermute | solution.py:591
  13.4 12.5 %collective-permute-start.2 = (bf16[144,1280]{1,0:T(8,128)(2,1)S(1)}, bf16[144,1280]{1,0:T(8,128)(2,1)}, u32[]{:S(2)}, u32[]{:S(2)}) collective-permute-start(bf16[144,1280]{1,0:T(8,128)(2,1)S(1)} %copy-done.21), channel_id=1, source_target_pairs={{0,1},{1,0},{2,3},{3,2},{4,5},{5,4},{6,7},{7,6},{8,9},{9,8},{10,11... | collective-permute-start | bytes 1105928 | tf_op jit(solution)/shard_map/gather/ppermute | solution.py:591
  26.6 27.6 %collective-permute-start.10 = (bf16[256,1024]{1,0:T(8,128)(2,1)S(1)}, bf16[256,1024]{1,0:T(8,128)(2,1)S(1)}, u32[]{:S(2)}, u32[]{:S(2)}) collective-permute-start(bf16[256,1024]{1,0:T(8,128)(2,1)S(1)} %copy-done.14), channel_id=1, source_target_pairs={{0,4},{1,5},{2,6},{3,7},{4,0},{5,1},{6,2},{7,3},{8,12},{9,13},{10,... | collective-permute-start | bytes 1572872 | tf_op jit(solution)/shard_map/gather/ppermute | solution.py:591
  26.9 11.5 %collective-permute-start.6 = (bf16[144,1280]{1,0:T(8,128)(2,1)S(1)}, bf16[144,1280]{1,0:T(8,128)(2,1)S(1)}, u32[]{:S(2)}, u32[]{:S(2)}) collective-permute-start(bf16[144,1280]{1,0:T(8,128)(2,1)S(1)} %collective-permute-done.refs_1_), channel_id=1, source_target_pairs={{0,1},{1,0},{2,3},{3,2},{4,5},{5,4},{6,7},{7,6},{8,9},{9,8},{10,11... | collective-permute-start | bytes 1105928 | tf_op jit(solution)/shard_map/gather/ppermute | solution.py:591
  28.4 17.9 %collective-permute-start.7 = (bf16[144,1280]{1,0:T(8,128)(2,1)}, bf16[144,1280]{1,0:T(8,128)(2,1)S(1)}, u32[]{:S(2)}, u32[]{:S(2)}) collective-permute-start(bf16[144,1280]{1,0:T(8,128)(2,1)} %copy-done.43), channel_id=1, source_target_pairs={{0,1},{1,0},{2,3},{3,2},{4,5},{5,4},{6,7},{7,6},{8,9},{9,8},{10,11... | collective-permute-start | bytes 1105928 | tf_op jit(solution)/shard_map/gather/ppermute | solution.py:591
  28.9 17.4 %collective-permute-start.8 = (bf16[144,1280]{1,0:T(8,128)(2,1)}, bf16[144,1280]{1,0:T(8,128)(2,1)S(1)}, u32[]{:S(2)}, u32[]{:S(2)}) collective-permute-start(bf16[144,1280]{1,0:T(8,128)(2,1)} %copy-done.43), channel_id=1, source_target_pairs={{0,16},{1,17},{2,18},{3,19},{4,20},{5,21},{6,22},{7,23},{8,24},{9,... | collective-permute-start | bytes 1105928 | tf_op jit(solution)/shard_map/gather/ppermute | solution.py:591
  31.5 22.7 %collective-permute-start.9 = (bf16[144,1280]{1,0:T(8,128)(2,1)}, bf16[144,1280]{1,0:T(8,128)(2,1)S(1)}, u32[]{:S(2)}, u32[]{:S(2)}) collective-permute-start(bf16[144,1280]{1,0:T(8,128)(2,1)} %copy-done.43), channel_id=1, source_target_pairs={{0,17},{1,16},{2,19},{3,18},{4,21},{5,20},{6,23},{7,22},{8,25},{9,... | collective-permute-start | bytes 1105928 | tf_op jit(solution)/shard_map/gather/ppermute | solution.py:591
  54.2 22.3 %collective-permute-start.11 = (bf16[256,1024]{1,0:T(8,128)(2,1)S(1)}, bf16[256,1024]{1,0:T(8,128)(2,1)S(1)}, u32[]{:S(2)}, u32[]{:S(2)}) collective-permute-start(bf16[256,1024]{1,0:T(8,128)(2,1)S(1)} %collective-permute-done.10.refs_2_), channel_id=1, source_target_pairs={{0,1},{1,0},{2,3},{3,2},{4,5},{5,4},{6,7},{7,6},{8,9},{9,8},{10,11... | collective-permute-start | bytes 1572872 | tf_op jit(solution)/shard_map/gather/ppermute | solution.py:591
  55.8 20.8 %collective-permute-start.12 = (bf16[256,1024]{1,0:T(8,128)(2,1)S(1)}, bf16[256,1024]{1,0:T(8,128)(2,1)S(1)}, u32[]{:S(2)}, u32[]{:S(2)}) collective-permute-start(bf16[256,1024]{1,0:T(8,128)(2,1)S(1)} %copy-done.14), channel_id=1, source_target_pairs={{0,1},{1,0},{2,3},{3,2},{4,5},{5,4},{6,7},{7,6},{8,9},{9,8},{10,11... | collective-permute-start | bytes 1572872 | tf_op jit(solution)/shard_map/gather/ppermute | solution.py:591
  56.3 20.3 %collective-permute-start.13 = (bf16[256,1024]{1,0:T(8,128)(2,1)S(1)}, bf16[256,1024]{1,0:T(8,128)(2,1)S(1)}, u32[]{:S(2)}, u32[]{:S(2)}) collective-permute-start(bf16[256,1024]{1,0:T(8,128)(2,1)S(1)} %collective-permute-done.10.refs_2_), channel_id=1, source_target_pairs={{0,16},{1,17},{2,18},{3,19},{4,20},{5,21},{6,22},{7,23},{8,24},{9,... | collective-permute-start | bytes 1572872 | tf_op jit(solution)/shard_map/gather/ppermute | solution.py:591
  56.3 39.1 %collective-permute-start.15 = (bf16[256,1024]{1,0:T(8,128)(2,1)S(1)}, bf16[256,1024]{1,0:T(8,128)(2,1)S(1)}, u32[]{:S(2)}, u32[]{:S(2)}) collective-permute-start(bf16[256,1024]{1,0:T(8,128)(2,1)S(1)} %copy-done.14), channel_id=1, source_target_pairs={{0,2},{1,3},{2,0},{3,1},{4,6},{5,7},{6,4},{7,5},{8,10},{9,11},{10,... | collective-permute-start | bytes 1572872 | tf_op jit(solution)/shard_map/gather/ppermute | solution.py:591
  57.7 37.8 %collective-permute-start.14 = (bf16[352,1024]{1,0:T(8,128)(2,1)}, bf16[352,1024]{1,0:T(8,128)(2,1)S(1)}, u32[]{:S(2)}, u32[]{:S(2)}) collective-permute-start(bf16[352,1024]{1,0:T(8,128)(2,1)} %prep_mlp.3.refs_0_), channel_id=1, source_target_pairs={{0,4},{1,5},{2,6},{3,7},{4,0},{5,1},{6,2},{7,3},{8,12},{9,13},{10,... | collective-permute-start | bytes 2162696 | tf_op jit(solution)/shard_map/gather/ppermute | solution.py:591
  76.6 37.3 %collective-permute-start.16 = (bf16[256,1024]{1,0:T(8,128)(2,1)S(1)}, bf16[256,1024]{1,0:T(8,128)(2,1)S(1)}, u32[]{:S(2)}, u32[]{:S(2)}) collective-permute-start(bf16[256,1024]{1,0:T(8,128)(2,1)S(1)} %collective-permute-done.11.refs_6_), channel_id=1, source_target_pairs={{0,16},{1,17},{2,18},{3,19},{4,20},{5,21},{6,22},{7,23},{8,24},{9,... | collective-permute-start | bytes 1572872 | tf_op jit(solution)/shard_map/gather/ppermute | solution.py:591
  78.1 35.8 %collective-permute-start.17 = (bf16[256,1024]{1,0:T(8,128)(2,1)S(1)}, bf16[256,1024]{1,0:T(8,128)(2,1)}, u32[]{:S(2)}, u32[]{:S(2)}) collective-permute-start(bf16[256,1024]{1,0:T(8,128)(2,1)S(1)} %copy-done.14), channel_id=1, source_target_pairs={{0,3},{1,2},{2,1},{3,0},{4,7},{5,6},{6,5},{7,4},{8,11},{9,10},{10,... | collective-permute-start | bytes 1572872 | tf_op jit(solution)/shard_map/gather/ppermute | solution.py:591
  96.2 17.7 %collective-permute-start.18 = (bf16[352,1024]{1,0:T(8,128)(2,1)S(1)}, bf16[352,1024]{1,0:T(8,128)(2,1)S(1)}, u32[]{:S(2)}, u32[]{:S(2)}) collective-permute-start(bf16[352,1024]{1,0:T(8,128)(2,1)S(1)} %collective-permute-done.14.refs_2_), channel_id=1, source_target_pairs={{0,1},{1,0},{2,3},{3,2},{4,5},{5,4},{6,7},{7,6},{8,9},{9,8},{10,11... | collective-permute-start | bytes 2162696 | tf_op jit(solution)/shard_map/gather/ppermute | solution.py:591
  96.7 17.2 %collective-permute-start.19 = (bf16[352,1024]{1,0:T(8,128)(2,1)S(1)}, bf16[352,1024]{1,0:T(8,128)(2,1)S(1)}, u32[]{:S(2)}, u32[]{:S(2)}) collective-permute-start(bf16[352,1024]{1,0:T(8,128)(2,1)S(1)} %collective-permute-done.14.refs_2_), channel_id=1, source_target_pairs={{0,16},{1,17},{2,18},{3,19},{4,20},{5,21},{6,22},{7,23},{8,24},{9,... | collective-permute-start | bytes 2162696 | tf_op jit(solution)/shard_map/gather/ppermute | solution.py:591
  96.8 17.2 %collective-permute-start.20 = (bf16[352,1024]{1,0:T(8,128)(2,1)S(1)}, bf16[352,1024]{1,0:T(8,128)(2,1)S(1)}, u32[]{:S(2)}, u32[]{:S(2)}) collective-permute-start(bf16[352,1024]{1,0:T(8,128)(2,1)S(1)} %copy-done.13), channel_id=1, source_target_pairs={{0,2},{1,3},{2,0},{3,1},{4,6},{5,7},{6,4},{7,5},{8,10},{9,11},{10,... | collective-permute-start | bytes 2162696 | tf_op jit(solution)/shard_map/gather/ppermute | solution.py:591
  114.0 31.2 %collective-permute-start.21 = (bf16[352,1024]{1,0:T(8,128)(2,1)S(1)}, bf16[352,1024]{1,0:T(8,128)(2,1)S(1)}, u32[]{:S(2)}, u32[]{:S(2)}) collective-permute-start(bf16[352,1024]{1,0:T(8,128)(2,1)S(1)} %copy-done.13), channel_id=1, source_target_pairs={{0,1},{1,0},{2,3},{3,2},{4,5},{5,4},{6,7},{7,6},{8,9},{9,8},{10,11... | collective-permute-start | bytes 2162696 | tf_op jit(solution)/shard_map/gather/ppermute | solution.py:591
  115.6 29.7 %collective-permute-start.22 = (bf16[352,1024]{1,0:T(8,128)(2,1)S(1)}, bf16[352,1024]{1,0:T(8,128)(2,1)S(1)}, u32[]{:S(2)}, u32[]{:S(2)}) collective-permute-start(bf16[352,1024]{1,0:T(8,128)(2,1)S(1)} %collective-permute-done.20.refs_1_), channel_id=1, source_target_pairs={{0,1},{1,0},{2,3},{3,2},{4,5},{5,4},{6,7},{7,6},{8,9},{9,8},{10,11... | collective-permute-start | bytes 2162696 | tf_op jit(solution)/shard_map/gather/ppermute | solution.py:591
  116.1 29.2 %collective-permute-start.23 = (bf16[352,1024]{1,0:T(8,128)(2,1)S(1)}, bf16[352,1024]{1,0:T(8,128)(2,1)S(1)}, u32[]{:S(2)}, u32[]{:S(2)}) collective-permute-start(bf16[352,1024]{1,0:T(8,128)(2,1)S(1)} %collective-permute-done.18.refs_6_), channel_id=1, source_target_pairs={{0,16},{1,17},{2,18},{3,19},{4,20},{5,21},{6,22},{7,23},{8,24},{9,... | collective-permute-start | bytes 2162696 | tf_op jit(solution)/shard_map/gather/ppermute | solution.py:591
  146.4 30.3 %collective-permute-start.24 = (bf16[2,256,1024]{2,1,0:T(8,128)(2,1)}, bf16[2,256,1024]{2,1,0:T(8,128)(2,1)S(1)}, u32[]{:S(2)}, u32[]{:S(2)}) collective-permute-start(bf16[2,256,1024]{2,1,0:T(8,128)(2,1)} %get-tuple-element.316), channel_id=1, source_target_pairs={{0,1},{1,0},{2,3},{3,2},{4,5},{5,4},{6,7},{7,6},{8,9},{9,8},{10,11... | collective-permute-start | bytes 3145736 | tf_op jit(solution)/shard_map/ppermute | solution.py:591
  148.0 28.8 %collective-permute-start.25 = (bf16[2,256,1024]{2,1,0:T(8,128)(2,1)}, bf16[2,256,1024]{2,1,0:T(8,128)(2,1)S(1)}, u32[]{:S(2)}, u32[]{:S(2)}) collective-permute-start(bf16[2,256,1024]{2,1,0:T(8,128)(2,1)} %get-tuple-element.317), channel_id=1, source_target_pairs={{0,16},{1,17},{2,18},{3,19},{4,20},{5,21},{6,22},{7,23},{8,24},{9,... | collective-permute-start | bytes 3145736 | tf_op jit(solution)/shard_map/ppermute | solution.py:591
  178.1 39.8 %collective-permute-start.26 = (bf16[256,1024]{1,0:T(8,128)(2,1)}, bf16[256,1024]{1,0:T(8,128)(2,1)}, u32[]{:S(2)}, u32[]{:S(2)}) collective-permute-start(bf16[256,1024]{1,0:T(8,128)(2,1)} %get-tuple-element.463), channel_id=1, source_target_pairs={{0,1},{1,0},{2,3},{3,2},{4,5},{5,4},{6,7},{7,6},{8,9},{9,8},{10,11... | collective-permute-start | bytes 1572872 | tf_op jit(solution)/shard_map/ppermute | solution.py:591
  178.6 39.3 %collective-permute-start.27 = (bf16[256,1024]{1,0:T(8,128)(2,1)}, bf16[256,1024]{1,0:T(8,128)(2,1)}, u32[]{:S(2)}, u32[]{:S(2)}) collective-permute-start(bf16[256,1024]{1,0:T(8,128)(2,1)} %get-tuple-element.462), channel_id=1, source_target_pairs={{0,2},{1,3},{2,0},{3,1},{4,6},{5,7},{6,4},{7,5},{8,10},{9,11},{10,... | collective-permute-start | bytes 1572872 | tf_op jit(solution)/shard_map/ppermute | solution.py:591
  180.3 37.7 %collective-permute-start.28 = (bf16[256,1024]{1,0:T(8,128)(2,1)}, bf16[256,1024]{1,0:T(8,128)(2,1)S(1)}, u32[]{:S(2)}, u32[]{:S(2)}) collective-permute-start(bf16[256,1024]{1,0:T(8,128)(2,1)} %get-tuple-element.464), channel_id=1, source_target_pairs={{0,1},{1,0},{2,3},{3,2},{4,5},{5,4},{6,7},{7,6},{8,9},{9,8},{10,11... | collective-permute-start | bytes 1572872 | tf_op jit(solution)/shard_map/ppermute | solution.py:591
  181.8 36.1 %collective-permute-start.29 = (bf16[2,256,1024]{2,1,0:T(8,128)(2,1)}, bf16[2,256,1024]{2,1,0:T(8,128)(2,1)S(1)}, u32[]{:S(2)}, u32[]{:S(2)}) collective-permute-start(bf16[2,256,1024]{2,1,0:T(8,128)(2,1)} %get-tuple-element.329), channel_id=1, source_target_pairs={{0,16},{1,17},{2,18},{3,19},{4,20},{5,21},{6,22},{7,23},{8,24},{9,... | collective-permute-start | bytes 3145736 | tf_op jit(solution)/shard_map/ppermute | solution.py:591
  220.0 26.6 %collective-permute-start.33 = (bf16[256,1024]{1,0:T(8,128)(2,1)}, bf16[256,1024]{1,0:T(8,128)(2,1)S(1)}, u32[]{:S(2)}, u32[]{:S(2)}) collective-permute-start(bf16[256,1024]{1,0:T(8,128)(2,1)} %fusion.3), channel_id=1, source_target_pairs={{0,2},{1,3},{2,0},{3,1},{4,6},{5,7},{6,4},{7,5},{8,10},{9,11},{10,... | collective-permute-start | bytes 1572872 | tf_op jit(solution)/shard_map/ppermute | solution.py:591
  220.9 25.7 %collective-permute-start.32 = (bf16[256,1024]{1,0:T(8,128)(2,1)}, bf16[256,1024]{1,0:T(8,128)(2,1)}, u32[]{:S(2)}, u32[]{:S(2)}) collective-permute-start(bf16[256,1024]{1,0:T(8,128)(2,1)} %fusion.19), channel_id=1, source_target_pairs={{0,1},{1,0},{2,3},{3,2},{4,5},{5,4},{6,7},{7,6},{8,9},{9,8},{10,11... | collective-permute-start | bytes 1572872 | tf_op jit(solution)/shard_map/ppermute | solution.py:591
  223.5 23.1 %collective-permute-start.30 = (bf16[256,1024]{1,0:T(8,128)(2,1)}, bf16[256,1024]{1,0:T(8,128)(2,1)}, u32[]{:S(2)}, u32[]{:S(2)}) collective-permute-start(bf16[256,1024]{1,0:T(8,128)(2,1)} %fusion.10), channel_id=1, source_target_pairs={{0,4},{1,5},{2,6},{3,7},{4,0},{5,1},{6,2},{7,3},{8,12},{9,13},{10,... | collective-permute-start | bytes 1572872 | tf_op jit(solution)/shard_map/ppermute | solution.py:591
  224.5 22.1 %collective-permute-start.31 = (bf16[256,1024]{1,0:T(8,128)(2,1)}, bf16[256,1024]{1,0:T(8,128)(2,1)}, u32[]{:S(2)}, u32[]{:S(2)}) collective-permute-start(bf16[256,1024]{1,0:T(8,128)(2,1)} %get-tuple-element.345), channel_id=1, source_target_pairs={{0,1},{1,0},{2,3},{3,2},{4,5},{5,4},{6,7},{7,6},{8,9},{9,8},{10,11... | collective-permute-start | bytes 1572872 | tf_op jit(solution)/shard_map/ppermute | solution.py:591
  249.0 29.2 %collective-permute-start.35 = (bf16[256,1024]{1,0:T(8,128)(2,1)}, bf16[256,1024]{1,0:T(8,128)(2,1)S(1)}, u32[]{:S(2)}, u32[]{:S(2)}) collective-permute-start(bf16[256,1024]{1,0:T(8,128)(2,1)} %fusion.7), channel_id=1, source_target_pairs={{0,4},{1,5},{2,6},{3,7},{4,0},{5,1},{6,2},{7,3},{8,12},{9,13},{10,... | collective-permute-start | bytes 1572872 | tf_op jit(solution)/shard_map/ppermute | solution.py:591
  252.5 25.7 %collective-permute-start.34 = (bf16[256,1024]{1,0:T(8,128)(2,1)S(1)}, bf16[256,1024]{1,0:T(8,128)(2,1)S(1)}, u32[]{:S(2)}, u32[]{:S(2)}) collective-permute-start(bf16[256,1024]{1,0:T(8,128)(2,1)S(1)} %fusion.9), channel_id=1, source_target_pairs={{0,16},{1,17},{2,18},{3,19},{4,20},{5,21},{6,22},{7,23},{8,24},{9,... | collective-permute-start | bytes 1572872 | tf_op jit(solution)/shard_map/ppermute | solution.py:591
  254.0 24.2 %collective-permute-start.36 = (bf16[2,128,2048]{2,1,0:T(8,128)(2,1)}, bf16[2,128,2048]{2,1,0:T(8,128)(2,1)}, u32[]{:S(2)}, u32[]{:S(2)}) collective-permute-start(bf16[2,128,2048]{2,1,0:T(8,128)(2,1)} %get-tuple-element.370), channel_id=1, source_target_pairs={{0,1},{1,0},{2,3},{3,2},{4,5},{5,4},{6,7},{7,6},{8,9},{9,8},{10,11... | collective-permute-start | bytes 3145736 | tf_op jit(solution)/shard_map/ppermute | solution.py:591
  254.5 25.2 %collective-permute-start.37 = (bf16[2,128,2048]{2,1,0:T(8,128)(2,1)}, bf16[2,128,2048]{2,1,0:T(8,128)(2,1)}, u32[]{:S(2)}, u32[]{:S(2)}) collective-permute-start(bf16[2,128,2048]{2,1,0:T(8,128)(2,1)} %get-tuple-element.371), channel_id=1, source_target_pairs={{0,16},{1,17},{2,18},{3,19},{4,20},{5,21},{6,22},{7,23},{8,24},{9,... | collective-permute-start | bytes 3145736 | tf_op jit(solution)/shard_map/ppermute | solution.py:591
  282.3 18.9 %collective-permute-start.42 = (bf16[2,1024,1024]{2,1,0:T(8,128)(2,1)}, bf16[2,1024,1024]{2,1,0:T(8,128)(2,1)}, u32[]{:S(2)}, u32[]{:S(2)}) collective-permute-start(bf16[2,1024,1024]{2,1,0:T(8,128)(2,1)} %get-tuple-element.392), channel_id=1, source_target_pairs={{0,8},{1,9},{2,10},{3,11},{4,12},{5,13},{6,14},{7,15},{8,0},{9,1},... | collective-permute-start | bytes 12582920 | tf_op jit(solution)/shard_map/ppermute | solution.py:591
  282.4 18.7 %collective-permute-start.40 = (bf16[128,2048]{1,0:T(8,128)(2,1)}, bf16[128,2048]{1,0:T(8,128)(2,1)}, u32[]{:S(2)}, u32[]{:S(2)}) collective-permute-start(bf16[128,2048]{1,0:T(8,128)(2,1)} %get-tuple-element.461), channel_id=1, source_target_pairs={{0,1},{1,0},{2,3},{3,2},{4,5},{5,4},{6,7},{7,6},{8,9},{9,8},{10,11... | collective-permute-start | bytes 1572872 | tf_op jit(solution)/shard_map/ppermute | solution.py:591
  283.0 18.2 %collective-permute-start.41 = (bf16[128,2048]{1,0:T(8,128)(2,1)}, bf16[128,2048]{1,0:T(8,128)(2,1)}, u32[]{:S(2)}, u32[]{:S(2)}) collective-permute-start(bf16[128,2048]{1,0:T(8,128)(2,1)} %get-tuple-element.460), channel_id=1, source_target_pairs={{0,2},{1,3},{2,0},{3,1},{4,6},{5,7},{6,4},{7,5},{8,10},{9,11},{10,... | collective-permute-start | bytes 1572872 | tf_op jit(solution)/shard_map/ppermute | solution.py:591
  287.3 13.8 %collective-permute-start.39 = (bf16[256,1024]{1,0:T(8,128)(2,1)S(1)}, bf16[256,1024]{1,0:T(8,128)(2,1)S(1)}, u32[]{:S(2)}, u32[]{:S(2)}) collective-permute-start(bf16[256,1024]{1,0:T(8,128)(2,1)S(1)} %fusion.2), channel_id=1, source_target_pairs={{0,16},{1,17},{2,18},{3,19},{4,20},{5,21},{6,22},{7,23},{8,24},{9,... | collective-permute-start | bytes 1572872 | tf_op jit(solution)/shard_map/ppermute | solution.py:591
  301.4 27.9 %collective-permute-start.43 = (bf16[256,1024]{1,0:T(8,128)(2,1)S(1)}, bf16[256,1024]{1,0:T(8,128)(2,1)S(1)}, u32[]{:S(2)}, u32[]{:S(2)}) collective-permute-start(bf16[256,1024]{1,0:T(8,128)(2,1)S(1)} %add_convert_fusion.1.own_b), channel_id=1, source_target_pairs={{0,8},{1,9},{2,10},{3,11},{4,12},{5,13},{6,14},{7,15},{8,0},{9,1},... | collective-permute-start | bytes 1572872 | tf_op jit(solution)/shard_map/ppermute | solution.py:591
  303.0 26.3 %collective-permute-start.44 = (bf16[128,2048]{1,0:T(8,128)(2,1)S(1)}, bf16[128,2048]{1,0:T(8,128)(2,1)S(1)}, u32[]{:S(2)}, u32[]{:S(2)}) collective-permute-start(bf16[128,2048]{1,0:T(8,128)(2,1)S(1)} %fusion.6), channel_id=1, source_target_pairs={{0,4},{1,5},{2,6},{3,7},{4,0},{5,1},{6,2},{7,3},{8,12},{9,13},{10,... | collective-permute-start | bytes 1572872 | tf_op jit(solution)/shard_map/ppermute | solution.py:591
  331.1 16.8 %collective-permute-start.45 = (bf16[128,2048]{1,0:T(8,128)(2,1)S(1)}, bf16[128,2048]{1,0:T(8,128)(2,1)S(1)}, u32[]{:S(2)}, u32[]{:S(2)}) collective-permute-start(bf16[128,2048]{1,0:T(8,128)(2,1)S(1)} %fusion.5), channel_id=1, source_target_pairs={{0,16},{1,17},{2,18},{3,19},{4,20},{5,21},{6,22},{7,23},{8,24},{9,... | collective-permute-start | bytes 1572872 | tf_op jit(solution)/shard_map/ppermute | solution.py:591
  333.7 14.1 %collective-permute-start.46 = (f32[16,1024]{1,0:T(8,128)S(1)}, f32[16,1024]{1,0:T(8,128)S(1)}, u32[]{:S(2)}, u32[]{:S(2)}) collective-permute-start(f32[16,1024]{1,0:T(8,128)S(1)} %concatenate.34), channel_id=1, source_target_pairs={{0,2},{1,3},{2,0},{3,1},{4,6},{5,7},{6,4},{7,5},{8,10},{9,11},{10,... | collective-permute-start | bytes 196616 | tf_op jit(solution)/shard_map/vectors/ppermute | solution.py:591
  334.6 13.2 %collective-permute-start.47 = (f32[16,1024]{1,0:T(8,128)S(1)}, f32[16,1024]{1,0:T(8,128)S(1)}, u32[]{:S(2)}, u32[]{:S(2)}) collective-permute-start(f32[16,1024]{1,0:T(8,128)S(1)} %concatenate.34), channel_id=1, source_target_pairs={{0,4},{1,5},{2,6},{3,7},{4,0},{5,1},{6,2},{7,3},{8,12},{9,13},{10,... | collective-permute-start | bytes 196616 | tf_op jit(solution)/shard_map/vectors/ppermute | solution.py:591
  336.7 11.1 %collective-permute-start.48 = (f32[16,1024]{1,0:T(8,128)S(1)}, f32[16,1024]{1,0:T(8,128)S(1)}, u32[]{:S(2)}, u32[]{:S(2)}) collective-permute-start(f32[16,1024]{1,0:T(8,128)S(1)} %concatenate.34), channel_id=1, source_target_pairs={{0,6},{1,7},{2,4},{3,5},{4,2},{5,3},{6,0},{7,1},{8,14},{9,15},{10,... | collective-permute-start | bytes 196616 | tf_op jit(solution)/shard_map/vectors/ppermute | solution.py:591
  348.1 11.1 %collective-permute-start.50 = (f32[16,1024]{1,0:T(8,128)S(1)}, f32[16,1024]{1,0:T(8,128)S(1)}, u32[]{:S(2)}, u32[]{:S(2)}) collective-permute-start(f32[16,1024]{1,0:T(8,128)S(1)} %add_add_fusion.1), channel_id=1, source_target_pairs={{0,1},{1,0},{2,3},{3,2},{4,5},{5,4},{6,7},{7,6},{8,9},{9,8},{10,11... | collective-permute-start | bytes 196616 | tf_op jit(solution)/shard_map/vectors/ppermute | solution.py:591
  (54 other events, 563.7 us)

commit v8 on v7

--- a/solution.py
+++ b/solution.py
@@ -107,7 +107,7 @@
     return jnp.where(core == 0, even, odd)
 
 
-def prep_attn_body(ids, w_q, w_k, w_v, w_out, vec, out):
+def prep_attn_body(ids, w_q, w_k, w_v, w_out, vec, out, padded):
     core = ids[1]
     for part, w in enumerate((w_q, w_k, w_v)):
         for tile in range(2):
@@ -121,7 +121,9 @@
         at = 768 + 256 * (panel // 2)
         base = (panel % 2) * 64
         out[base : base + 64, at : at + 256] = rows[:, 256 * panel : 256 * panel + 256]
-    out[128:144, 0:128] = jnp.where(lax.broadcasted_iota(jnp.int32, (16, 128), 0) < 13, vec[...], 0.0).astype(BF16)
+    padded[...] = jnp.zeros_like(padded)
+    padded[0:13, :] = vec[...]
+    out[128:144, 0:128] = padded[...].astype(BF16)
     out[128:144, 128:1280] = jnp.zeros((16, 1152), BF16)
 
 
@@ -664,10 +666,11 @@
             (1,),
             [(ids, scalars())]
             + [(w_qkv, spec((128, 512), lambda i, n=part: (0, 2 * n), single=True)) for part in range(3)]
-            + [const(w_out), (vectors, whole((16, 128)))],
+            + [const(w_out), (vectors, whole((13, 128)))],
             [kept((144, 1280), BF16)],
             0,
             3e6,
+            scratch=[pltpu.VMEM((16, 128), F32)],
             name="prep_attn",
         )[0]
 
@@ -765,16 +768,16 @@
 
     with jax.named_scope("qkv"):
         *projected, d_att, attn_in, attn_t, mlp_in, wq_a, full_out, vec, bias_qkv = block_call(
-            functools.partial(qkv_first_body, rows // 256),
-            (rows // 256,),
+            functools.partial(qkv_first_body, rows // 512),
+            (rows // 512,),
             [(ids, scalars())]
             + [const(piece) for piece in attn_pieces]
-            + halves(tokens, tok_other, 256)
-            + halves(cotangent, dy_other, 256)
-            + table_blocks(256),
-            [(sds((rows, 256), BF16), row_block(256, 256))] * 3
-            + [(sds((rows, 512), BF16), row_block(256, 512)), (sds((rows, width), BF16), row_block(256))]
-            + [(sds((width, rows), BF16), col_block(256)), (sds((rows, width), BF16), row_block(256))]
+            + halves(tokens, tok_other, 512)
+            + halves(cotangent, dy_other, 512)
+            + table_blocks(512),
+            [(sds((rows, 256), BF16), row_block(512, 256))] * 3
+            + [(sds((rows, 512), BF16), row_block(512, 512)), (sds((rows, width), BF16), row_block(512))]
+            + [(sds((width, rows), BF16), col_block(512)), (sds((rows, width), BF16), row_block(512))]
             + [kept((1024, 768), BF16), kept((512, 1024), BF16), kept((16, 1024), F32), kept((1, 1536), F32)],
             2 * rows * 1024 * 1280,
             30e6,

time: 367 us -> 367 us (level)
  no operation moved by 1% of the time
where the time goes in v8:
time: 367 us; the launch traced here: 361 us
  Pallas kernels  237 us (65%)
  starting transfers between devices  56.4 us (15%)
  waiting for transfers between devices  29.7 us (8%)
  other arithmetic  27.5 us (7%)
  local copies, waits for them, and re-layouts  9.2 us (3%)
    pallas_call x10, Pallas kernels, block_call(): kernel_call(body, grid, [place for _, place in ins], [place for _, place...  185 us
    ppermute x54, starting transfers between devices, move(): return lax.ppermute(value, AXES, pairs)  56.4 us
    pallas_call x2, Pallas kernels, attention(): pl.pallas_call(attn_body, grid=(2, len(pairs)), in_specs=[place for _, pl...  30.9 us
    ppermute x54, waiting for transfers between devices, move(): return lax.ppermute(value, AXES, pairs)  29.7 us
    pallas_call x1, Pallas kernels, adam_mlp(): pl.pallas_call(adam_mlp_body, grid=(4,), in_specs=[scalars()] + [whole((2...  9.6 us
  transfers between devices with their start and end apart: 54, of which 9 were waited for; matrix products, arithmetic and copies ran while one was open for 6% of the time, Pallas kernels for 65%

profile of v8, /device:TPU:0, one launch (start us, length us, event | category | flops | bytes accessed | tf_op | source)
XLA Modules:
  0.0 361.4 jit_solution(3026977263702946217)
XLA Ops:
  1.3 2.3 prep_attn.1.refs_0_
  3.7 3.0 collective-permute-start
  6.7 2.6 collective-permute-start.1
  10.6 2.8 prep_mlp.2.refs_0_
  13.4 1.5 collective-permute-start.2
  16.1 3.8 %fusion.11 = (f32[1024,128]{1,0:T(8,128)S(1)}, f32[1024,128]{1,0:T(8,128)S(1)}, f32[1024,128]{1,0:T(8,128)S(1)}, f32[1024,128]{1,0:T(8,128)S(1)}, f32[1024,128]{1,0:T(8,128)S(1)}, /*index=5*/f32[1024,128]{1,0:T(8,128)S(1)}) fusion(f32[128]{0:T(128)S(1)} %compare_select_fusion.2, f32[1024]{0:T(1024)S(1)} %fusion.26, ...), kind=kLoop, calls=%fused_computation.33 | loop fusion | flops 1048576 | bytes 3154560 | tf_op jit(solution)/shard_map/gather/jit(_where)/select_n | solution.py:557
  23.3 2.6 collective-permute-done.1.refs_2_
  26.9 1.5 collective-permute-start.6
  28.9 2.6 collective-permute-start.8
  33.7 3.5 prep_mlp.3.refs_0_
  38.4 7.9 %collective-permute-done.7.refs_6_ = bf16[144,1280]{1,0:T(8,128)(2,1)S(1)} collective-permute-done((bf16[144,1280]{1,0:T(8,128)(2,1)}, bf16[144,1280]{1,0:T(8,128)(2,1)S(1)}, u32[]{:S(2)}, u32[]{:S(2)}) %collective-permute-start.7) | collective-permute-done | bytes 368672 | tf_op jit(solution)/shard_map/gather/ppermute | solution.py:593
  46.3 7.9 %collective-permute-done.9.refs_7_ = bf16[144,1280]{1,0:T(8,128)(2,1)S(1)} collective-permute-done((bf16[144,1280]{1,0:T(8,128)(2,1)}, bf16[144,1280]{1,0:T(8,128)(2,1)S(1)}, u32[]{:S(2)}, u32[]{:S(2)}) %collective-permute-start.9) | collective-permute-done | bytes 368672 | tf_op jit(solution)/shard_map/gather/ppermute | solution.py:593
  54.2 1.6 collective-permute-start.11
  57.7 1.6 collective-permute-start.14
  59.3 17.3 %qkv.1 = (bf16[2048,256]{1,0:T(8,128)(2,1)}, bf16[2048,256]{1,0:T(8,128)(2,1)}, bf16[2048,256]{1,0:T(8,128)(2,1)}, bf16[2048,512]{1,0:T(8,128)(2,1)}, bf16[2048,...) custom-call(s32[3]{0:T(128)} %pad_add_fusion.2.ids, ...), custom_call_target="tpu_custom_call" | custom-call | flops 5368709120 | bytes 30000000 | tf_op jit(solution)/shard_map/qkv/qkv/pallas_call | solution.py:644
  76.7 1.5 collective-permute-start.16
  78.2 2.1 collective-permute-start.17
  80.3 15.2 %attention.3 = (bf16[2048,256]{1,0:T(8,128)(2,1)}, bf16[3,2048,256]{2,1,0:T(8,128)(2,1)}) custom-call(bf16[2048,256]{1,0:T(8,128)(2,1)} %get-tuple-element.269.q, bf16[2048,256]{1,0:T(8,128)(2,1)} %get-tuple-element.270.k, bf16[2048,256]{1,0:T(8,128)(2,1)} %get-tuple-element.271.v, bf16[2048,512]{1,0:T(8,128)(2,1)} %get-tuple-element.263.d_att.refs_10_, ...), custom_call_target="tpu_custom_call" | custom-call | flops 15000000512 | bytes 5000000 | tf_op jit(solution)/shard_map/attention/attention/pallas_call | solution.py:750
  98.3 15.7 %attention.4 = (bf16[2048,256]{1,0:T(8,128)(2,1)}, bf16[3,2048,256]{2,1,0:T(8,128)(2,1)}) custom-call(bf16[2048,256]{1,0:T(8,128)(2,1)} %get-tuple-element.269.q, bf16[2048,256]{1,0:T(8,128)(2,1)} %get-tuple-element.270.k, bf16[2048,256]{1,0:T(8,128)(2,1)} %get-tuple-element.271.v, ...), custom_call_target="tpu_custom_call", output_to_operand_aliasing={{0}: (9, {}), {1}: (10, {})} | custom-call | flops 15000000512 | bytes 5000000 | tf_op jit(solution)/shard_map/attention/attention/pallas_call | solution.py:750
  114.1 1.6 collective-permute-start.21
  117.7 27.6 %mlp.2 = (bf16[4,256,1024]{2,1,0:T(8,128)(2,1)}, bf16[2,256,1024]{2,1,0:T(8,128)(2,1)}, bf16[2,256,1024]{2,1,0:T(8,128)(2,1)}, bf16[2048,1024]{1,0:T(8,128)(2,1)...) custom-call(s32[3]{0:T(128)} %pad_add_fusion.2.ids, ...), custom_call_target="tpu_custom_call" | custom-call | flops 17179869184 | bytes 40000000 | tf_op jit(solution)/shard_map/mlp/mlp/pallas_call | solution.py:644
  146.6 1.5 collective-permute-start.24
  148.6 28.2 %mlp.3 = (bf16[4,256,1024]{2,1,0:T(8,128)(2,1)}, bf16[2,256,1024]{2,1,0:T(8,128)(2,1)}, bf16[2,256,1024]{2,1,0:T(8,128)(2,1)}, bf16[2048,1024]{1,0:T(8,128)(2,1)...) custom-call(s32[3]{0:T(128)} %pad_add_fusion.2.ids, ...), custom_call_target="tpu_custom_call" | custom-call | flops 17179869184 | bytes 40000000 | tf_op jit(solution)/shard_map/mlp/mlp/pallas_call | solution.py:644
  180.5 1.6 collective-permute-start.28
  182.0 1.9 collective-permute-start.29
  183.9 34.1 %attention.5 = (bf16[2048,256]{1,0:T(8,128)(2,1)}, bf16[3,2048,256]{2,1,0:T(8,128)(2,1)}, bf16[1024,768]{1,0:T(8,128)(2,1)}) custom-call(s32[3]{0:T(128)} %pad_add_fusion.2.ids, bf16[352,1024]{1,0:T(8,128)(2,1)} %prep_mlp.3.refs_0_, bf16[352,1024]{1,0:T(8,128)(2,1)} %copy-done.32, bf16[352,1024]{1,0:T(8,128)(2,1)} %copy-done.29, ...), custom_call_target="tpu_custom_call" | custom-call | flops 38000001024 | bytes 20000000 | tf_op jit(solution)/shard_map/attention/attention/pallas_call | solution.py:644
  221.5 2.1 fusion.10
  224.7 1.5 collective-permute-start.31
  226.2 20.6 %attn_weights.1 = (bf16[4,128,2048]{2,1,0:T(8,128)(2,1)}, bf16[2,128,2048]{2,1,0:T(8,128)(2,1)}, bf16[2,128,2048]{2,1,0:T(8,128)(2,1)}, f32[8,1536]{1,0:T(8,128)}) custom-call(s32[3]{0:T(128)} %pad_add_fusion.2.ids, bf16[1024,2048]{1,0:T(8,128)(2,1)} %get-tuple-element.283.attn_t, bf16[3,2048,256]{2,1,0:T(8,128)(2,1)} %get-tuple-element.282.grad_a, ...), custom_call_target="tpu_custom_call" | custom-call | flops 8589934592 | bytes 24000000 | tf_op jit(solution)/shard_map/attn_weights/attn_weights/pallas_call | solution.py:644
  246.8 2.3 fusion.7
  249.2 1.9 collective-permute-start.35
  251.1 1.6 fusion.9
  252.6 1.5 collective-permute-start.34
  255.2 23.1 %back.2 = (bf16[2,1024,1024]{2,1,0:T(8,128)(2,1)}, f32[8,1024]{1,0:T(8,128)}) custom-call(bf16[3,2048,256]{2,1,0:T(8,128)(2,1)} %get-tuple-element.282.grad_a, bf16[3,2048,256]{2,1,0:T(8,128)(2,1)} %get-tuple-element.399.grad_b, bf16[2048,256]{1,0:T(8,128)(2,1)} %get-tuple-element.338.far_att_a.att_a, bf16[2048,256]{1,0:T(8,128)(2,1)} %get-tuple-element.339.far_att_b.att_b, ...), custom_call_target="tpu_custom_call" | custom-call | flops 12884901888 | bytes 40000000 | tf_op jit(solution)/shard_map/back/back/pallas_call | solution.py:644
  279.9 2.6 fusion.21
  283.1 2.3 collective-permute-start.41
  285.4 1.7 fusion.2
  291.1 4.1 %adam_down.1 = (f32[512,1024]{1,0:T(8,128)}, f32[512,1024]{1,0:T(8,128)}, f32[512,1024]{1,0:T(8,128)}) custom-call(s32[3]{0:T(128)} %pad_add_fusion.2.ids, bf16[256,1024]{1,0:T(8,128)(2,1)} %copy-done, bf16[256,1024]{1,0:T(8,128)(2,1)} %copy-done.6, f32[512,1024]{1,0:T(8,128)} %refs_3_.2, f32[512,1024]{1,0:T(8,128)} %refs_4_.2, f32[512,1024]{1,0:T(8,128)} %refs_5_.2), custom_call_target="tpu_custom_call" | custom-call | bytes 7000000 | tf_op jit(solution)/shard_map/adam_down/pallas_call | solution.py:897
  295.2 5.8 %collective-permute-done.39 = bf16[256,1024]{1,0:T(8,128)(2,1)S(1)} collective-permute-done((bf16[256,1024]{1,0:T(8,128)(2,1)S(1)}, bf16[256,1024]{1,0:T(8,128)(2,1)S(1)}, u32[]{:S(2)}, u32[]{:S(2)}) %collective-permute-start.39) | collective-permute-done | bytes 524320 | tf_op jit(solution)/shard_map/ppermute | solution.py:593
  301.3 1.5 fusion.6
  303.4 25.9 %back.3 = (bf16[1024,1024]{1,0:T(8,128)(2,1)}, f32[1024,1024]{1,0:T(8,128)}, f32[8,1024]{1,0:T(8,128)}) custom-call(bf16[3,2048,256]{2,1,0:T(8,128)(2,1)} %get-tuple-element.282.grad_a, bf16[3,2048,256]{2,1,0:T(8,128)(2,1)} %get-tuple-element.399.grad_b, bf16[2048,256]{1,0:T(8,128)(2,1)} %get-tuple-element.338.far_att_a.att_a, ...), custom_call_target="tpu_custom_call" | custom-call | flops 12884901888 | bytes 40000000 | tf_op jit(solution)/shard_map/back/back/pallas_call | solution.py:644
  329.3 1.7 fusion.5
  331.1 1.5 collective-permute-start.45
  334.7 1.9 collective-permute-start.47
  336.6 1.6 collective-permute-start.48
  338.2 9.6 %adam_mlp.1 = (f32[128,4096]{1,0:T(8,128)}, f32[128,4096]{1,0:T(8,128)}, f32[128,4096]{1,0:T(8,128)}, f32[512,1024]{1,0:T(8,128)}, f32[512,1024]{1,0:T(8,128)}, /*index=5*/f32[512,1024]{1,0:T(8,128)}) custom-call(s32[3]{0:T(128)} %pad_add_fusion.2.ids, bf16[256,1024]{1,0:T(8,128)(2,1)} %copy-done, ...), custom_call_target="tpu_custom_call", output_to_operand_aliasing={{3}: (11, {}), {4}: (12, {}), {5}: (13, {})} | custom-call | bytes 21000000 | tf_op jit(solution)/shard_map/vectors/adam_mlp/pallas_call | solution.py:910
  348.1 1.5 collective-permute-start.50
  352.5 6.7 %adam.1 = (f32[128,3072]{1,0:T(8,128)}, f32[128,3072]{1,0:T(8,128)}, f32[128,3072]{1,0:T(8,128)}, f32[128,1024]{1,0:T(8,128)}, f32[128,1024]{1,0:T(8,128)}, /*index=5*/f32[128,1024]{1,0:T(8,128)}) custom-call(s32[3]{0:T(128)} %pad_add_fusion.2.ids, bf16[128,2048]{1,0:T(8,128)(2,1)} %copy-done.7, bf16[128,2048]{1,0:T(8,128)(2,1)} %copy-done.20, ...), custom_call_target="tpu_custom_call" | custom-call | bytes 13000000 | tf_op jit(solution)/shard_map/adam/adam/pallas_call | solution.py:1004
  (229 shorter events, 43.1 us)
Async XLA Ops:
  3.7 19.6 %collective-permute-start = (bf16[144,1280]{1,0:T(8,128)(2,1)}, bf16[144,1280]{1,0:T(8,128)(2,1)S(1)}, u32[]{:S(2)}, u32[]{:S(2)}) collective-permute-start(bf16[144,1280]{1,0:T(8,128)(2,1)} %prep_attn.1.refs_0_), channel_id=1, source_target_pairs={{0,2},{1,3},{2,0},{3,1},{4,6},{5,7},{6,4},{7,5},{8,10},{9,11},{10,... | collective-permute-start | bytes 1105928 | tf_op jit(solution)/shard_map/gather/ppermute | solution.py:593
  6.7 19.1 %collective-permute-start.1 = (bf16[144,1280]{1,0:T(8,128)(2,1)}, bf16[144,1280]{1,0:T(8,128)(2,1)S(1)}, u32[]{:S(2)}, u32[]{:S(2)}) collective-permute-start(bf16[144,1280]{1,0:T(8,128)(2,1)} %prep_attn.1.refs_0_), channel_id=1, source_target_pairs={{0,4},{1,5},{2,6},{3,7},{4,0},{5,1},{6,2},{7,3},{8,12},{9,13},{10,... | collective-permute-start | bytes 1105928 | tf_op jit(solution)/shard_map/gather/ppermute | solution.py:593
  9.3 16.5 %collective-permute-start.4 = (bf16[1024,1024]{1,0:T(8,128)(2,1)S(1)}, bf16[1024,1024]{1,0:T(8,128)(2,1)}, u32[]{:S(2)}, u32[]{:S(2)}) collective-permute-start(bf16[1024,1024]{1,0:T(8,128)(2,1)S(1)} %copy-done.28), channel_id=1, source_target_pairs={{0,8},{1,9},{2,10},{3,11},{4,12},{5,13},{6,14},{7,15},{8,0},{9,1},... | collective-permute-start | bytes 6291464 | tf_op jit(solution)/shard_map/gather/ppermute | solution.py:593
  9.8 16.0 %collective-permute-start.5 = (bf16[1024,1024]{1,0:T(8,128)(2,1)}, bf16[1024,1024]{1,0:T(8,128)(2,1)}, u32[]{:S(2)}, u32[]{:S(2)}) collective-permute-start(bf16[1024,1024]{1,0:T(8,128)(2,1)} %refs_9_.1), channel_id=1, source_target_pairs={{0,8},{1,9},{2,10},{3,11},{4,12},{5,13},{6,14},{7,15},{8,0},{9,1},... | collective-permute-start | bytes 6291464 | tf_op jit(solution)/shard_map/gather/ppermute | solution.py:593
  13.4 12.5 %collective-permute-start.2 = (bf16[144,1280]{1,0:T(8,128)(2,1)S(1)}, bf16[144,1280]{1,0:T(8,128)(2,1)}, u32[]{:S(2)}, u32[]{:S(2)}) collective-permute-start(bf16[144,1280]{1,0:T(8,128)(2,1)S(1)} %copy-done.21), channel_id=1, source_target_pairs={{0,1},{1,0},{2,3},{3,2},{4,5},{5,4},{6,7},{7,6},{8,9},{9,8},{10,11... | collective-permute-start | bytes 1105928 | tf_op jit(solution)/shard_map/gather/ppermute | solution.py:593
  26.6 27.6 %collective-permute-start.10 = (bf16[256,1024]{1,0:T(8,128)(2,1)S(1)}, bf16[256,1024]{1,0:T(8,128)(2,1)S(1)}, u32[]{:S(2)}, u32[]{:S(2)}) collective-permute-start(bf16[256,1024]{1,0:T(8,128)(2,1)S(1)} %copy-done.14), channel_id=1, source_target_pairs={{0,4},{1,5},{2,6},{3,7},{4,0},{5,1},{6,2},{7,3},{8,12},{9,13},{10,... | collective-permute-start | bytes 1572872 | tf_op jit(solution)/shard_map/gather/ppermute | solution.py:593
  26.9 11.5 %collective-permute-start.6 = (bf16[144,1280]{1,0:T(8,128)(2,1)S(1)}, bf16[144,1280]{1,0:T(8,128)(2,1)S(1)}, u32[]{:S(2)}, u32[]{:S(2)}) collective-permute-start(bf16[144,1280]{1,0:T(8,128)(2,1)S(1)} %collective-permute-done.refs_1_), channel_id=1, source_target_pairs={{0,1},{1,0},{2,3},{3,2},{4,5},{5,4},{6,7},{7,6},{8,9},{9,8},{10,11... | collective-permute-start | bytes 1105928 | tf_op jit(solution)/shard_map/gather/ppermute | solution.py:593
  28.4 17.9 %collective-permute-start.7 = (bf16[144,1280]{1,0:T(8,128)(2,1)}, bf16[144,1280]{1,0:T(8,128)(2,1)S(1)}, u32[]{:S(2)}, u32[]{:S(2)}) collective-permute-start(bf16[144,1280]{1,0:T(8,128)(2,1)} %copy-done.43), channel_id=1, source_target_pairs={{0,1},{1,0},{2,3},{3,2},{4,5},{5,4},{6,7},{7,6},{8,9},{9,8},{10,11... | collective-permute-start | bytes 1105928 | tf_op jit(solution)/shard_map/gather/ppermute | solution.py:593
  28.9 17.4 %collective-permute-start.8 = (bf16[144,1280]{1,0:T(8,128)(2,1)}, bf16[144,1280]{1,0:T(8,128)(2,1)S(1)}, u32[]{:S(2)}, u32[]{:S(2)}) collective-permute-start(bf16[144,1280]{1,0:T(8,128)(2,1)} %copy-done.43), channel_id=1, source_target_pairs={{0,16},{1,17},{2,18},{3,19},{4,20},{5,21},{6,22},{7,23},{8,24},{9,... | collective-permute-start | bytes 1105928 | tf_op jit(solution)/shard_map/gather/ppermute | solution.py:593
  31.5 22.7 %collective-permute-start.9 = (bf16[144,1280]{1,0:T(8,128)(2,1)}, bf16[144,1280]{1,0:T(8,128)(2,1)S(1)}, u32[]{:S(2)}, u32[]{:S(2)}) collective-permute-start(bf16[144,1280]{1,0:T(8,128)(2,1)} %copy-done.43), channel_id=1, source_target_pairs={{0,17},{1,16},{2,19},{3,18},{4,21},{5,20},{6,23},{7,22},{8,25},{9,... | collective-permute-start | bytes 1105928 | tf_op jit(solution)/shard_map/gather/ppermute | solution.py:593
  54.2 22.5 %collective-permute-start.11 = (bf16[256,1024]{1,0:T(8,128)(2,1)S(1)}, bf16[256,1024]{1,0:T(8,128)(2,1)S(1)}, u32[]{:S(2)}, u32[]{:S(2)}) collective-permute-start(bf16[256,1024]{1,0:T(8,128)(2,1)S(1)} %collective-permute-done.10.refs_2_), channel_id=1, source_target_pairs={{0,1},{1,0},{2,3},{3,2},{4,5},{5,4},{6,7},{7,6},{8,9},{9,8},{10,11... | collective-permute-start | bytes 1572872 | tf_op jit(solution)/shard_map/gather/ppermute | solution.py:593
  55.8 20.9 %collective-permute-start.12 = (bf16[256,1024]{1,0:T(8,128)(2,1)S(1)}, bf16[256,1024]{1,0:T(8,128)(2,1)S(1)}, u32[]{:S(2)}, u32[]{:S(2)}) collective-permute-start(bf16[256,1024]{1,0:T(8,128)(2,1)S(1)} %copy-done.14), channel_id=1, source_target_pairs={{0,1},{1,0},{2,3},{3,2},{4,5},{5,4},{6,7},{7,6},{8,9},{9,8},{10,11... | collective-permute-start | bytes 1572872 | tf_op jit(solution)/shard_map/gather/ppermute | solution.py:593
  56.3 20.4 %collective-permute-start.13 = (bf16[256,1024]{1,0:T(8,128)(2,1)S(1)}, bf16[256,1024]{1,0:T(8,128)(2,1)S(1)}, u32[]{:S(2)}, u32[]{:S(2)}) collective-permute-start(bf16[256,1024]{1,0:T(8,128)(2,1)S(1)} %collective-permute-done.10.refs_2_), channel_id=1, source_target_pairs={{0,16},{1,17},{2,18},{3,19},{4,20},{5,21},{6,22},{7,23},{8,24},{9,... | collective-permute-start | bytes 1572872 | tf_op jit(solution)/shard_map/gather/ppermute | solution.py:593
  56.3 39.3 %collective-permute-start.15 = (bf16[256,1024]{1,0:T(8,128)(2,1)S(1)}, bf16[256,1024]{1,0:T(8,128)(2,1)S(1)}, u32[]{:S(2)}, u32[]{:S(2)}) collective-permute-start(bf16[256,1024]{1,0:T(8,128)(2,1)S(1)} %copy-done.14), channel_id=1, source_target_pairs={{0,2},{1,3},{2,0},{3,1},{4,6},{5,7},{6,4},{7,5},{8,10},{9,11},{10,... | collective-permute-start | bytes 1572872 | tf_op jit(solution)/shard_map/gather/ppermute | solution.py:593
  57.7 37.9 %collective-permute-start.14 = (bf16[352,1024]{1,0:T(8,128)(2,1)}, bf16[352,1024]{1,0:T(8,128)(2,1)S(1)}, u32[]{:S(2)}, u32[]{:S(2)}) collective-permute-start(bf16[352,1024]{1,0:T(8,128)(2,1)} %prep_mlp.3.refs_0_), channel_id=1, source_target_pairs={{0,4},{1,5},{2,6},{3,7},{4,0},{5,1},{6,2},{7,3},{8,12},{9,13},{10,... | collective-permute-start | bytes 2162696 | tf_op jit(solution)/shard_map/gather/ppermute | solution.py:593
  76.7 37.3 %collective-permute-start.16 = (bf16[256,1024]{1,0:T(8,128)(2,1)S(1)}, bf16[256,1024]{1,0:T(8,128)(2,1)S(1)}, u32[]{:S(2)}, u32[]{:S(2)}) collective-permute-start(bf16[256,1024]{1,0:T(8,128)(2,1)S(1)} %collective-permute-done.11.refs_6_), channel_id=1, source_target_pairs={{0,16},{1,17},{2,18},{3,19},{4,20},{5,21},{6,22},{7,23},{8,24},{9,... | collective-permute-start | bytes 1572872 | tf_op jit(solution)/shard_map/gather/ppermute | solution.py:593
  78.2 35.8 %collective-permute-start.17 = (bf16[256,1024]{1,0:T(8,128)(2,1)S(1)}, bf16[256,1024]{1,0:T(8,128)(2,1)}, u32[]{:S(2)}, u32[]{:S(2)}) collective-permute-start(bf16[256,1024]{1,0:T(8,128)(2,1)S(1)} %copy-done.14), channel_id=1, source_target_pairs={{0,3},{1,2},{2,1},{3,0},{4,7},{5,6},{6,5},{7,4},{8,11},{9,10},{10,... | collective-permute-start | bytes 1572872 | tf_op jit(solution)/shard_map/gather/ppermute | solution.py:593
  96.4 17.7 %collective-permute-start.18 = (bf16[352,1024]{1,0:T(8,128)(2,1)S(1)}, bf16[352,1024]{1,0:T(8,128)(2,1)S(1)}, u32[]{:S(2)}, u32[]{:S(2)}) collective-permute-start(bf16[352,1024]{1,0:T(8,128)(2,1)S(1)} %collective-permute-done.14.refs_2_), channel_id=1, source_target_pairs={{0,1},{1,0},{2,3},{3,2},{4,5},{5,4},{6,7},{7,6},{8,9},{9,8},{10,11... | collective-permute-start | bytes 2162696 | tf_op jit(solution)/shard_map/gather/ppermute | solution.py:593
  96.9 17.2 %collective-permute-start.19 = (bf16[352,1024]{1,0:T(8,128)(2,1)S(1)}, bf16[352,1024]{1,0:T(8,128)(2,1)S(1)}, u32[]{:S(2)}, u32[]{:S(2)}) collective-permute-start(bf16[352,1024]{1,0:T(8,128)(2,1)S(1)} %collective-permute-done.14.refs_2_), channel_id=1, source_target_pairs={{0,16},{1,17},{2,18},{3,19},{4,20},{5,21},{6,22},{7,23},{8,24},{9,... | collective-permute-start | bytes 2162696 | tf_op jit(solution)/shard_map/gather/ppermute | solution.py:593
  96.9 17.2 %collective-permute-start.20 = (bf16[352,1024]{1,0:T(8,128)(2,1)S(1)}, bf16[352,1024]{1,0:T(8,128)(2,1)S(1)}, u32[]{:S(2)}, u32[]{:S(2)}) collective-permute-start(bf16[352,1024]{1,0:T(8,128)(2,1)S(1)} %copy-done.13), channel_id=1, source_target_pairs={{0,2},{1,3},{2,0},{3,1},{4,6},{5,7},{6,4},{7,5},{8,10},{9,11},{10,... | collective-permute-start | bytes 2162696 | tf_op jit(solution)/shard_map/gather/ppermute | solution.py:593
  114.1 31.3 %collective-permute-start.21 = (bf16[352,1024]{1,0:T(8,128)(2,1)S(1)}, bf16[352,1024]{1,0:T(8,128)(2,1)S(1)}, u32[]{:S(2)}, u32[]{:S(2)}) collective-permute-start(bf16[352,1024]{1,0:T(8,128)(2,1)S(1)} %copy-done.13), channel_id=1, source_target_pairs={{0,1},{1,0},{2,3},{3,2},{4,5},{5,4},{6,7},{7,6},{8,9},{9,8},{10,11... | collective-permute-start | bytes 2162696 | tf_op jit(solution)/shard_map/gather/ppermute | solution.py:593
  115.7 29.7 %collective-permute-start.22 = (bf16[352,1024]{1,0:T(8,128)(2,1)S(1)}, bf16[352,1024]{1,0:T(8,128)(2,1)S(1)}, u32[]{:S(2)}, u32[]{:S(2)}) collective-permute-start(bf16[352,1024]{1,0:T(8,128)(2,1)S(1)} %collective-permute-done.20.refs_1_), channel_id=1, source_target_pairs={{0,1},{1,0},{2,3},{3,2},{4,5},{5,4},{6,7},{7,6},{8,9},{9,8},{10,11... | collective-permute-start | bytes 2162696 | tf_op jit(solution)/shard_map/gather/ppermute | solution.py:593
  116.2 29.2 %collective-permute-start.23 = (bf16[352,1024]{1,0:T(8,128)(2,1)S(1)}, bf16[352,1024]{1,0:T(8,128)(2,1)S(1)}, u32[]{:S(2)}, u32[]{:S(2)}) collective-permute-start(bf16[352,1024]{1,0:T(8,128)(2,1)S(1)} %collective-permute-done.18.refs_6_), channel_id=1, source_target_pairs={{0,16},{1,17},{2,18},{3,19},{4,20},{5,21},{6,22},{7,23},{8,24},{9,... | collective-permute-start | bytes 2162696 | tf_op jit(solution)/shard_map/gather/ppermute | solution.py:593
  146.6 30.3 %collective-permute-start.24 = (bf16[2,256,1024]{2,1,0:T(8,128)(2,1)}, bf16[2,256,1024]{2,1,0:T(8,128)(2,1)S(1)}, u32[]{:S(2)}, u32[]{:S(2)}) collective-permute-start(bf16[2,256,1024]{2,1,0:T(8,128)(2,1)} %get-tuple-element.316), channel_id=1, source_target_pairs={{0,1},{1,0},{2,3},{3,2},{4,5},{5,4},{6,7},{7,6},{8,9},{9,8},{10,11... | collective-permute-start | bytes 3145736 | tf_op jit(solution)/shard_map/ppermute | solution.py:593
  148.1 28.8 %collective-permute-start.25 = (bf16[2,256,1024]{2,1,0:T(8,128)(2,1)}, bf16[2,256,1024]{2,1,0:T(8,128)(2,1)S(1)}, u32[]{:S(2)}, u32[]{:S(2)}) collective-permute-start(bf16[2,256,1024]{2,1,0:T(8,128)(2,1)} %get-tuple-element.317), channel_id=1, source_target_pairs={{0,16},{1,17},{2,18},{3,19},{4,20},{5,21},{6,22},{7,23},{8,24},{9,... | collective-permute-start | bytes 3145736 | tf_op jit(solution)/shard_map/ppermute | solution.py:593
  178.3 39.8 %collective-permute-start.26 = (bf16[256,1024]{1,0:T(8,128)(2,1)}, bf16[256,1024]{1,0:T(8,128)(2,1)}, u32[]{:S(2)}, u32[]{:S(2)}) collective-permute-start(bf16[256,1024]{1,0:T(8,128)(2,1)} %get-tuple-element.463), channel_id=1, source_target_pairs={{0,1},{1,0},{2,3},{3,2},{4,5},{5,4},{6,7},{7,6},{8,9},{9,8},{10,11... | collective-permute-start | bytes 1572872 | tf_op jit(solution)/shard_map/ppermute | solution.py:593
  178.8 39.3 %collective-permute-start.27 = (bf16[256,1024]{1,0:T(8,128)(2,1)}, bf16[256,1024]{1,0:T(8,128)(2,1)}, u32[]{:S(2)}, u32[]{:S(2)}) collective-permute-start(bf16[256,1024]{1,0:T(8,128)(2,1)} %get-tuple-element.462), channel_id=1, source_target_pairs={{0,2},{1,3},{2,0},{3,1},{4,6},{5,7},{6,4},{7,5},{8,10},{9,11},{10,... | collective-permute-start | bytes 1572872 | tf_op jit(solution)/shard_map/ppermute | solution.py:593
  180.5 37.6 %collective-permute-start.28 = (bf16[256,1024]{1,0:T(8,128)(2,1)}, bf16[256,1024]{1,0:T(8,128)(2,1)S(1)}, u32[]{:S(2)}, u32[]{:S(2)}) collective-permute-start(bf16[256,1024]{1,0:T(8,128)(2,1)} %get-tuple-element.464), channel_id=1, source_target_pairs={{0,1},{1,0},{2,3},{3,2},{4,5},{5,4},{6,7},{7,6},{8,9},{9,8},{10,11... | collective-permute-start | bytes 1572872 | tf_op jit(solution)/shard_map/ppermute | solution.py:593
  182.0 36.1 %collective-permute-start.29 = (bf16[2,256,1024]{2,1,0:T(8,128)(2,1)}, bf16[2,256,1024]{2,1,0:T(8,128)(2,1)S(1)}, u32[]{:S(2)}, u32[]{:S(2)}) collective-permute-start(bf16[2,256,1024]{2,1,0:T(8,128)(2,1)} %get-tuple-element.329), channel_id=1, source_target_pairs={{0,16},{1,17},{2,18},{3,19},{4,20},{5,21},{6,22},{7,23},{8,24},{9,... | collective-permute-start | bytes 3145736 | tf_op jit(solution)/shard_map/ppermute | solution.py:593
  220.1 26.7 %collective-permute-start.33 = (bf16[256,1024]{1,0:T(8,128)(2,1)}, bf16[256,1024]{1,0:T(8,128)(2,1)S(1)}, u32[]{:S(2)}, u32[]{:S(2)}) collective-permute-start(bf16[256,1024]{1,0:T(8,128)(2,1)} %fusion.3), channel_id=1, source_target_pairs={{0,2},{1,3},{2,0},{3,1},{4,6},{5,7},{6,4},{7,5},{8,10},{9,11},{10,... | collective-permute-start | bytes 1572872 | tf_op jit(solution)/shard_map/ppermute | solution.py:593
  221.0 25.8 %collective-permute-start.32 = (bf16[256,1024]{1,0:T(8,128)(2,1)}, bf16[256,1024]{1,0:T(8,128)(2,1)}, u32[]{:S(2)}, u32[]{:S(2)}) collective-permute-start(bf16[256,1024]{1,0:T(8,128)(2,1)} %fusion.19), channel_id=1, source_target_pairs={{0,1},{1,0},{2,3},{3,2},{4,5},{5,4},{6,7},{7,6},{8,9},{9,8},{10,11... | collective-permute-start | bytes 1572872 | tf_op jit(solution)/shard_map/ppermute | solution.py:593
  223.6 23.2 %collective-permute-start.30 = (bf16[256,1024]{1,0:T(8,128)(2,1)}, bf16[256,1024]{1,0:T(8,128)(2,1)}, u32[]{:S(2)}, u32[]{:S(2)}) collective-permute-start(bf16[256,1024]{1,0:T(8,128)(2,1)} %fusion.10), channel_id=1, source_target_pairs={{0,4},{1,5},{2,6},{3,7},{4,0},{5,1},{6,2},{7,3},{8,12},{9,13},{10,... | collective-permute-start | bytes 1572872 | tf_op jit(solution)/shard_map/ppermute | solution.py:593
  224.7 22.1 %collective-permute-start.31 = (bf16[256,1024]{1,0:T(8,128)(2,1)}, bf16[256,1024]{1,0:T(8,128)(2,1)}, u32[]{:S(2)}, u32[]{:S(2)}) collective-permute-start(bf16[256,1024]{1,0:T(8,128)(2,1)} %get-tuple-element.345), channel_id=1, source_target_pairs={{0,1},{1,0},{2,3},{3,2},{4,5},{5,4},{6,7},{7,6},{8,9},{9,8},{10,11... | collective-permute-start | bytes 1572872 | tf_op jit(solution)/shard_map/ppermute | solution.py:593
  249.2 29.2 %collective-permute-start.35 = (bf16[256,1024]{1,0:T(8,128)(2,1)}, bf16[256,1024]{1,0:T(8,128)(2,1)S(1)}, u32[]{:S(2)}, u32[]{:S(2)}) collective-permute-start(bf16[256,1024]{1,0:T(8,128)(2,1)} %fusion.7), channel_id=1, source_target_pairs={{0,4},{1,5},{2,6},{3,7},{4,0},{5,1},{6,2},{7,3},{8,12},{9,13},{10,... | collective-permute-start | bytes 1572872 | tf_op jit(solution)/shard_map/ppermute | solution.py:593
  252.6 25.8 %collective-permute-start.34 = (bf16[256,1024]{1,0:T(8,128)(2,1)S(1)}, bf16[256,1024]{1,0:T(8,128)(2,1)S(1)}, u32[]{:S(2)}, u32[]{:S(2)}) collective-permute-start(bf16[256,1024]{1,0:T(8,128)(2,1)S(1)} %fusion.9), channel_id=1, source_target_pairs={{0,16},{1,17},{2,18},{3,19},{4,20},{5,21},{6,22},{7,23},{8,24},{9,... | collective-permute-start | bytes 1572872 | tf_op jit(solution)/shard_map/ppermute | solution.py:593
  254.1 24.3 %collective-permute-start.36 = (bf16[2,128,2048]{2,1,0:T(8,128)(2,1)}, bf16[2,128,2048]{2,1,0:T(8,128)(2,1)}, u32[]{:S(2)}, u32[]{:S(2)}) collective-permute-start(bf16[2,128,2048]{2,1,0:T(8,128)(2,1)} %get-tuple-element.370), channel_id=1, source_target_pairs={{0,1},{1,0},{2,3},{3,2},{4,5},{5,4},{6,7},{7,6},{8,9},{9,8},{10,11... | collective-permute-start | bytes 3145736 | tf_op jit(solution)/shard_map/ppermute | solution.py:593
  254.7 25.2 %collective-permute-start.37 = (bf16[2,128,2048]{2,1,0:T(8,128)(2,1)}, bf16[2,128,2048]{2,1,0:T(8,128)(2,1)}, u32[]{:S(2)}, u32[]{:S(2)}) collective-permute-start(bf16[2,128,2048]{2,1,0:T(8,128)(2,1)} %get-tuple-element.371), channel_id=1, source_target_pairs={{0,16},{1,17},{2,18},{3,19},{4,20},{5,21},{6,22},{7,23},{8,24},{9,... | collective-permute-start | bytes 3145736 | tf_op jit(solution)/shard_map/ppermute | solution.py:593
  282.4 18.6 %collective-permute-start.42 = (bf16[2,1024,1024]{2,1,0:T(8,128)(2,1)}, bf16[2,1024,1024]{2,1,0:T(8,128)(2,1)}, u32[]{:S(2)}, u32[]{:S(2)}) collective-permute-start(bf16[2,1024,1024]{2,1,0:T(8,128)(2,1)} %get-tuple-element.392), channel_id=1, source_target_pairs={{0,8},{1,9},{2,10},{3,11},{4,12},{5,13},{6,14},{7,15},{8,0},{9,1},... | collective-permute-start | bytes 12582920 | tf_op jit(solution)/shard_map/ppermute | solution.py:593
  282.6 18.4 %collective-permute-start.40 = (bf16[128,2048]{1,0:T(8,128)(2,1)}, bf16[128,2048]{1,0:T(8,128)(2,1)}, u32[]{:S(2)}, u32[]{:S(2)}) collective-permute-start(bf16[128,2048]{1,0:T(8,128)(2,1)} %get-tuple-element.461), channel_id=1, source_target_pairs={{0,1},{1,0},{2,3},{3,2},{4,5},{5,4},{6,7},{7,6},{8,9},{9,8},{10,11... | collective-permute-start | bytes 1572872 | tf_op jit(solution)/shard_map/ppermute | solution.py:593
  283.1 17.9 %collective-permute-start.41 = (bf16[128,2048]{1,0:T(8,128)(2,1)}, bf16[128,2048]{1,0:T(8,128)(2,1)}, u32[]{:S(2)}, u32[]{:S(2)}) collective-permute-start(bf16[128,2048]{1,0:T(8,128)(2,1)} %get-tuple-element.460), channel_id=1, source_target_pairs={{0,2},{1,3},{2,0},{3,1},{4,6},{5,7},{6,4},{7,5},{8,10},{9,11},{10,... | collective-permute-start | bytes 1572872 | tf_op jit(solution)/shard_map/ppermute | solution.py:593
  287.2 13.8 %collective-permute-start.39 = (bf16[256,1024]{1,0:T(8,128)(2,1)S(1)}, bf16[256,1024]{1,0:T(8,128)(2,1)S(1)}, u32[]{:S(2)}, u32[]{:S(2)}) collective-permute-start(bf16[256,1024]{1,0:T(8,128)(2,1)S(1)} %fusion.2), channel_id=1, source_target_pairs={{0,16},{1,17},{2,18},{3,19},{4,20},{5,21},{6,22},{7,23},{8,24},{9,... | collective-permute-start | bytes 1572872 | tf_op jit(solution)/shard_map/ppermute | solution.py:593
  301.2 28.1 %collective-permute-start.43 = (bf16[256,1024]{1,0:T(8,128)(2,1)S(1)}, bf16[256,1024]{1,0:T(8,128)(2,1)S(1)}, u32[]{:S(2)}, u32[]{:S(2)}) collective-permute-start(bf16[256,1024]{1,0:T(8,128)(2,1)S(1)} %add_convert_fusion.1.own_b), channel_id=1, source_target_pairs={{0,8},{1,9},{2,10},{3,11},{4,12},{5,13},{6,14},{7,15},{8,0},{9,1},... | collective-permute-start | bytes 1572872 | tf_op jit(solution)/shard_map/ppermute | solution.py:593
  302.9 26.5 %collective-permute-start.44 = (bf16[128,2048]{1,0:T(8,128)(2,1)S(1)}, bf16[128,2048]{1,0:T(8,128)(2,1)S(1)}, u32[]{:S(2)}, u32[]{:S(2)}) collective-permute-start(bf16[128,2048]{1,0:T(8,128)(2,1)S(1)} %fusion.6), channel_id=1, source_target_pairs={{0,4},{1,5},{2,6},{3,7},{4,0},{5,1},{6,2},{7,3},{8,12},{9,13},{10,... | collective-permute-start | bytes 1572872 | tf_op jit(solution)/shard_map/ppermute | solution.py:593
  331.1 16.8 %collective-permute-start.45 = (bf16[128,2048]{1,0:T(8,128)(2,1)S(1)}, bf16[128,2048]{1,0:T(8,128)(2,1)S(1)}, u32[]{:S(2)}, u32[]{:S(2)}) collective-permute-start(bf16[128,2048]{1,0:T(8,128)(2,1)S(1)} %fusion.5), channel_id=1, source_target_pairs={{0,16},{1,17},{2,18},{3,19},{4,20},{5,21},{6,22},{7,23},{8,24},{9,... | collective-permute-start | bytes 1572872 | tf_op jit(solution)/shard_map/ppermute | solution.py:593
  333.7 14.1 %collective-permute-start.46 = (f32[16,1024]{1,0:T(8,128)S(1)}, f32[16,1024]{1,0:T(8,128)S(1)}, u32[]{:S(2)}, u32[]{:S(2)}) collective-permute-start(f32[16,1024]{1,0:T(8,128)S(1)} %concatenate.34), channel_id=1, source_target_pairs={{0,2},{1,3},{2,0},{3,1},{4,6},{5,7},{6,4},{7,5},{8,10},{9,11},{10,... | collective-permute-start | bytes 196616 | tf_op jit(solution)/shard_map/vectors/ppermute | solution.py:593
  334.7 13.2 %collective-permute-start.47 = (f32[16,1024]{1,0:T(8,128)S(1)}, f32[16,1024]{1,0:T(8,128)S(1)}, u32[]{:S(2)}, u32[]{:S(2)}) collective-permute-start(f32[16,1024]{1,0:T(8,128)S(1)} %concatenate.34), channel_id=1, source_target_pairs={{0,4},{1,5},{2,6},{3,7},{4,0},{5,1},{6,2},{7,3},{8,12},{9,13},{10,... | collective-permute-start | bytes 196616 | tf_op jit(solution)/shard_map/vectors/ppermute | solution.py:593
  336.6 11.2 %collective-permute-start.48 = (f32[16,1024]{1,0:T(8,128)S(1)}, f32[16,1024]{1,0:T(8,128)S(1)}, u32[]{:S(2)}, u32[]{:S(2)}) collective-permute-start(f32[16,1024]{1,0:T(8,128)S(1)} %concatenate.34), channel_id=1, source_target_pairs={{0,6},{1,7},{2,4},{3,5},{4,2},{5,3},{6,0},{7,1},{8,14},{9,15},{10,... | collective-permute-start | bytes 196616 | tf_op jit(solution)/shard_map/vectors/ppermute | solution.py:593
  348.1 11.1 %collective-permute-start.50 = (f32[16,1024]{1,0:T(8,128)S(1)}, f32[16,1024]{1,0:T(8,128)S(1)}, u32[]{:S(2)}, u32[]{:S(2)}) collective-permute-start(f32[16,1024]{1,0:T(8,128)S(1)} %add_add_fusion.1), channel_id=1, source_target_pairs={{0,1},{1,0},{2,3},{3,2},{4,5},{5,4},{6,7},{7,6},{8,9},{9,8},{10,11... | collective-permute-start | bytes 196616 | tf_op jit(solution)/shard_map/vectors/ppermute | solution.py:593
  (54 other events, 564.6 us)

commit v9 on v8

--- a/solution.py
+++ b/solution.py
@@ -26,7 +26,7 @@
 F32 = jnp.float32
 BF16 = jnp.bfloat16
 MIB = 1024 * 1024
-VMEM_NEED = 58
+VMEM_NEED = 51
 
 
 def spec(block, index, single=False):

time: 367 us -> 355 us (0.967)
  Pallas kernels: 237 us -> 226 us
  other arithmetic: 27.5 us -> 18.5 us
  waiting for transfers between devices: 29.7 us -> 35.2 us
    pallas_call x10, Pallas kernels: 185 us -> 177 us  [block_call(): kernel_call(body, grid, [place for _, place in ins], [place for _, place...]
    ppermute x54, waiting for transfers between devices: 29.7 us -> 35.2 us  [move(): return lax.ppermute(value, AXES, pairs)]
  transfers between devices with their start and end apart: 54 -> 54, of which waited for: 9 -> 10; matrix products, arithmetic and copies ran while one was open for 6% -> 4% of each run, Pallas kernels for 65% -> 65%
where the time goes in v9:
time: 355 us; the launch traced here: 349 us
  Pallas kernels  226 us (64%)
  starting transfers between devices  58.6 us (17%)
  waiting for transfers between devices  35.2 us (10%)
  other arithmetic  18.5 us (5%)
  local copies, waits for them, and re-layouts  8.34 us (2%)
    pallas_call x10, Pallas kernels, block_call(): kernel_call(body, grid, [place for _, place in ins], [place for _, place...  177 us
    ppermute x54, starting transfers between devices, move(): return lax.ppermute(value, AXES, pairs)  58.6 us
    ppermute x54, waiting for transfers between devices, move(): return lax.ppermute(value, AXES, pairs)  35.2 us
    pallas_call x2, Pallas kernels, attention(): pl.pallas_call(attn_body, grid=(2, len(pairs)), in_specs=[place for _, pl...  30.9 us
    pallas_call x1, Pallas kernels, adam_mlp(): pl.pallas_call(adam_mlp_body, grid=(4,), in_specs=[scalars()] + [whole((2...  8.7 us
  transfers between devices with their start and end apart: 54, of which 10 were waited for; matrix products, arithmetic and copies ran while one was open for 4% of the time, Pallas kernels for 65%

profile of v9, /device:TPU:0, one launch (start us, length us, event | category | flops | bytes accessed | tf_op | source)
XLA Modules:
  0.0 348.6 jit_solution(5986120478546025220)
XLA Ops:
  0.8 1.4 copy-done
  4.7 3.1 collective-permute-start
  7.7 2.6 collective-permute-start.1
  12.9 1.6 collective-permute-start.2
  15.1 3.8 %fusion.11 = (f32[1024,128]{1,0:T(8,128)S(1)}, f32[1024,128]{1,0:T(8,128)S(1)}, f32[1024,128]{1,0:T(8,128)S(1)}, f32[1024,128]{1,0:T(8,128)S(1)}, f32[1024,128]{1,0:T(8,128)S(1)}, /*index=5*/f32[1024,128]{1,0:T(8,128)S(1)}) fusion(f32[128]{0:T(128)S(1)} %compare_select_fusion.2, f32[1024]{0:T(1024)S(1)} %fusion.26, ...), kind=kLoop, calls=%fused_computation.33 | loop fusion | flops 1048576 | bytes 3154560 | tf_op jit(solution)/shard_map/gather/jit(_where)/select_n | solution.py:557
  19.9 1.4 pad_maximum_fusion
  21.4 2.7 collective-permute-done.refs_1_
  24.1 2.6 collective-permute-done.1.refs_2_
  27.2 1.5 collective-permute-start.6
  29.2 2.5 collective-permute-start.8
  33.9 2.1 prep_mlp.3.refs_0_
  36.0 2.7 collective-permute-done.6.refs_5_
  38.7 7.9 %collective-permute-done.7.refs_6_ = bf16[144,1280]{1,0:T(8,128)(2,1)S(1)} collective-permute-done((bf16[144,1280]{1,0:T(8,128)(2,1)}, bf16[144,1280]{1,0:T(8,128)(2,1)S(1)}, u32[]{:S(2)}, u32[]{:S(2)}) %collective-permute-start.7) | collective-permute-done | bytes 368672 | tf_op jit(solution)/shard_map/gather/ppermute | solution.py:593
  46.6 7.9 %collective-permute-done.9.refs_7_ = bf16[144,1280]{1,0:T(8,128)(2,1)S(1)} collective-permute-done((bf16[144,1280]{1,0:T(8,128)(2,1)}, bf16[144,1280]{1,0:T(8,128)(2,1)S(1)}, u32[]{:S(2)}, u32[]{:S(2)}) %collective-permute-start.9) | collective-permute-done | bytes 368672 | tf_op jit(solution)/shard_map/gather/ppermute | solution.py:593
  54.5 1.5 collective-permute-start.11
  56.5 1.4 collective-permute-start.15
  58.0 1.6 collective-permute-start.14
  59.5 16.7 %qkv.1 = (bf16[2048,256]{1,0:T(8,128)(2,1)}, bf16[2048,256]{1,0:T(8,128)(2,1)}, bf16[2048,256]{1,0:T(8,128)(2,1)}, bf16[2048,512]{1,0:T(8,128)(2,1)}, bf16[2048,...) custom-call(s32[3]{0:T(128)S(1)} %pad_add_fusion.2.ids, ...), custom_call_target="tpu_custom_call" | custom-call | flops 5368709120 | bytes 30000000 | tf_op jit(solution)/shard_map/qkv/qkv/pallas_call | solution.py:644
  77.8 2.1 collective-permute-start.17
  81.1 15.2 %attention.3 = (bf16[2048,256]{1,0:T(8,128)(2,1)S(1)}, bf16[3,2048,256]{2,1,0:T(8,128)(2,1)}) custom-call(bf16[2048,256]{1,0:T(8,128)(2,1)S(1)} %copy-done.14, bf16[2048,256]{1,0:T(8,128)(2,1)} %get-tuple-element.270.k, bf16[2048,256]{1,0:T(8,128)(2,1)} %get-tuple-element.271.v, bf16[2048,512]{1,0:T(8,128)(2,1)} %get-tuple-element.263.d_att.refs_10_, ...), custom_call_target="tpu_custom_call" | custom-call | flops 15000000512 | bytes 5000000 | tf_op jit(solution)/shard_map/attention/attention/pallas_call | solution.py:750
  98.7 15.7 %attention.4 = (bf16[2048,256]{1,0:T(8,128)(2,1)S(1)}, bf16[3,2048,256]{2,1,0:T(8,128)(2,1)}) custom-call(bf16[2048,256]{1,0:T(8,128)(2,1)S(1)} %copy-done.15, bf16[2048,256]{1,0:T(8,128)(2,1)} %get-tuple-element.270.k, bf16[2048,256]{1,0:T(8,128)(2,1)} %get-tuple-element.271.v, ...), custom_call_target="tpu_custom_call", output_to_operand_aliasing={{0}: (9, {}), {1}: (10, {})} | custom-call | flops 15000000512 | bytes 5000000 | tf_op jit(solution)/shard_map/attention/attention/pallas_call | solution.py:750
  114.4 1.6 collective-permute-start.21
  117.7 26.8 %mlp.2 = (bf16[4,256,1024]{2,1,0:T(8,128)(2,1)}, bf16[2,256,1024]{2,1,0:T(8,128)(2,1)}, bf16[2,256,1024]{2,1,0:T(8,128)(2,1)}, bf16[2048,1024]{1,0:T(8,128)(2,1)...) custom-call(s32[3]{0:T(128)S(1)} %pad_add_fusion.2.ids, ...), custom_call_target="tpu_custom_call" | custom-call | flops 17179869184 | bytes 40000000 | tf_op jit(solution)/shard_map/mlp/mlp/pallas_call | solution.py:644
  144.6 1.6 collective-permute-start.24
  146.2 1.8 collective-permute-start.25
  148.0 27.2 %mlp.3 = (bf16[4,256,1024]{2,1,0:T(8,128)(2,1)}, bf16[2,256,1024]{2,1,0:T(8,128)(2,1)}, bf16[2,256,1024]{2,1,0:T(8,128)(2,1)}, bf16[2048,1024]{1,0:T(8,128)(2,1)...) custom-call(s32[3]{0:T(128)S(1)} %pad_add_fusion.2.ids, ...), custom_call_target="tpu_custom_call" | custom-call | flops 17179869184 | bytes 40000000 | tf_op jit(solution)/shard_map/mlp/mlp/pallas_call | solution.py:644
  178.1 1.5 collective-permute-start.28
  180.7 33.7 %attention.5 = (bf16[2048,256]{1,0:T(8,128)(2,1)}, bf16[3,2048,256]{2,1,0:T(8,128)(2,1)}, bf16[1024,768]{1,0:T(8,128)(2,1)}) custom-call(s32[3]{0:T(128)S(1)} %pad_add_fusion.2.ids, bf16[352,1024]{1,0:T(8,128)(2,1)S(1)} %prep_mlp.3.refs_0_, bf16[352,1024]{1,0:T(8,128)(2,1)S(1)} %collective-permute-done.20.refs_1_, ...), custom_call_target="tpu_custom_call" | custom-call | flops 38000001024 | bytes 20000000 | tf_op jit(solution)/shard_map/attention/attention/pallas_call | solution.py:644
  219.2 19.9 %attn_weights.1 = (bf16[4,128,2048]{2,1,0:T(8,128)(2,1)}, bf16[2,128,2048]{2,1,0:T(8,128)(2,1)S(1)}, bf16[2,128,2048]{2,1,0:T(8,128)(2,1)S(1)}, f32[8,1536]{1,0:T(8,128)S(1)}) custom-call(s32[3]{0:T(128)S(1)} %pad_add_fusion.2.ids, bf16[1024,2048]{1,0:T(8,128)(2,1)} %get-tuple-element.283.attn_t, bf16[3,2048,256]{2,1,0:T(8,128)(2,1)} %get-tuple-element.282.grad_a, ...), custom_call_target="tpu_custom_call" | custom-call | flops 8589934592 | bytes 24000000 | tf_op jit(solution)/shard_map/attn_weights/attn_weights/pallas_call | solution.py:644
  239.9 2.3 fusion.7
  242.1 1.9 collective-permute-start.35
  244.0 1.4 fusion.9
  245.5 2.8 collective-permute-start.34
  248.5 22.9 %back.2 = (bf16[2,1024,1024]{2,1,0:T(8,128)(2,1)}, f32[8,1024]{1,0:T(8,128)S(1)}) custom-call(bf16[3,2048,256]{2,1,0:T(8,128)(2,1)} %get-tuple-element.282.grad_a, bf16[3,2048,256]{2,1,0:T(8,128)(2,1)} %get-tuple-element.399.grad_b, bf16[2048,256]{1,0:T(8,128)(2,1)S(1)} %copy-done.12, bf16[2048,256]{1,0:T(8,128)(2,1)S(1)} %copy-done.9, ...), custom_call_target="tpu_custom_call" | custom-call | flops 12884901888 | bytes 40000000 | tf_op jit(solution)/shard_map/back/back/pallas_call | solution.py:644
  271.5 1.6 collective-permute-done.37
  273.1 1.4 fusion.21
  275.8 1.4 fusion.2
  277.2 1.6 collective-permute-start.39
  279.3 3.1 collective-permute-done.38.other.other_a
  282.4 3.8 %adam_down.1 = (f32[512,1024]{1,0:T(8,128)}, f32[512,1024]{1,0:T(8,128)}, f32[512,1024]{1,0:T(8,128)}) custom-call(s32[3]{0:T(128)S(1)} %pad_add_fusion.2.ids, bf16[256,1024]{1,0:T(8,128)(2,1)S(1)} %add_convert_fusion.2.own.own_a, bf16[256,1024]{1,0:T(8,128)(2,1)S(1)} %collective-permute-done.38.other.other_a, f32[512,1024]{1,0:T(8,128)} %refs_3_.2, ...), custom_call_target="tpu_custom_call" | custom-call | bytes 7000000 | tf_op jit(solution)/shard_map/adam_down/pallas_call | solution.py:897
  286.2 4.9 %collective-permute-done.39 = bf16[256,1024]{1,0:T(8,128)(2,1)S(1)} collective-permute-done((bf16[256,1024]{1,0:T(8,128)(2,1)S(1)}, bf16[256,1024]{1,0:T(8,128)(2,1)S(1)}, u32[]{:S(2)}, u32[]{:S(2)}) %collective-permute-start.39) | collective-permute-done | bytes 524320 | tf_op jit(solution)/shard_map/ppermute | solution.py:593
  292.8 2.8 collective-permute-start.44
  295.6 25.7 %back.3 = (bf16[1024,1024]{1,0:T(8,128)(2,1)}, f32[1024,1024]{1,0:T(8,128)}, f32[8,1024]{1,0:T(8,128)S(1)}) custom-call(bf16[3,2048,256]{2,1,0:T(8,128)(2,1)} %get-tuple-element.282.grad_a, bf16[3,2048,256]{2,1,0:T(8,128)(2,1)} %get-tuple-element.399.grad_b, bf16[2048,256]{1,0:T(8,128)(2,1)S(1)} %copy-done.13, bf16[2048,256]{1,0:T(8,128)(2,1)S(1)} %copy-done.10, ...), custom_call_target="tpu_custom_call" | custom-call | flops 12884901888 | bytes 40000000 | tf_op jit(solution)/shard_map/back/back/pallas_call | solution.py:644
  321.7 1.5 collective-permute-start.45
  325.6 2.5 collective-permute-start.48
  328.0 8.7 %adam_mlp.1 = (f32[128,4096]{1,0:T(8,128)}, f32[128,4096]{1,0:T(8,128)}, f32[128,4096]{1,0:T(8,128)}, f32[512,1024]{1,0:T(8,128)}, f32[512,1024]{1,0:T(8,128)}, /*index=5*/f32[512,1024]{1,0:T(8,128)}) custom-call(s32[3]{0:T(128)S(1)} %pad_add_fusion.2.ids, ...), custom_call_target="tpu_custom_call", output_to_operand_aliasing={{3}: (11, {}), {4}: (12, {}), {5}: (13, {})} | custom-call | bytes 21000000 | tf_op jit(solution)/shard_map/vectors/adam_mlp/pallas_call | solution.py:910
  338.8 1.8 collective-permute-start.52
  340.7 5.8 %adam.1 = (f32[128,3072]{1,0:T(8,128)}, f32[128,3072]{1,0:T(8,128)}, f32[128,3072]{1,0:T(8,128)}, f32[128,1024]{1,0:T(8,128)}, f32[128,1024]{1,0:T(8,128)}, /*index=5*/f32[128,1024]{1,0:T(8,128)}) custom-call(s32[3]{0:T(128)S(1)} %pad_add_fusion.2.ids, bf16[128,2048]{1,0:T(8,128)(2,1)S(1)} %add_convert_fusion.own, ...), custom_call_target="tpu_custom_call" | custom-call | bytes 13000000 | tf_op jit(solution)/shard_map/adam/adam/pallas_call | solution.py:1004
  (213 shorter events, 37.0 us)
Async XLA Ops:
  4.7 19.5 %collective-permute-start = (bf16[144,1280]{1,0:T(8,128)(2,1)S(1)}, bf16[144,1280]{1,0:T(8,128)(2,1)S(1)}, u32[]{:S(2)}, u32[]{:S(2)}) collective-permute-start(bf16[144,1280]{1,0:T(8,128)(2,1)S(1)} %prep_attn.1.refs_0_), channel_id=1, source_target_pairs={{0,2},{1,3},{2,0},{3,1},{4,6},{5,7},{6,4},{7,5},{8,10},{9,11},{10,... | collective-permute-start | bytes 1105928 | tf_op jit(solution)/shard_map/gather/ppermute | solution.py:593
  7.7 19.0 %collective-permute-start.1 = (bf16[144,1280]{1,0:T(8,128)(2,1)S(1)}, bf16[144,1280]{1,0:T(8,128)(2,1)}, u32[]{:S(2)}, u32[]{:S(2)}) collective-permute-start(bf16[144,1280]{1,0:T(8,128)(2,1)S(1)} %prep_attn.1.refs_0_), channel_id=1, source_target_pairs={{0,4},{1,5},{2,6},{3,7},{4,0},{5,1},{6,2},{7,3},{8,12},{9,13},{10,... | collective-permute-start | bytes 1105928 | tf_op jit(solution)/shard_map/gather/ppermute | solution.py:593
  10.3 16.4 %collective-permute-start.4 = (bf16[1024,1024]{1,0:T(8,128)(2,1)}, bf16[1024,1024]{1,0:T(8,128)(2,1)}, u32[]{:S(2)}, u32[]{:S(2)}) collective-permute-start(bf16[1024,1024]{1,0:T(8,128)(2,1)} %refs_7_.1), channel_id=1, source_target_pairs={{0,8},{1,9},{2,10},{3,11},{4,12},{5,13},{6,14},{7,15},{8,0},{9,1},... | collective-permute-start | bytes 6291464 | tf_op jit(solution)/shard_map/gather/ppermute | solution.py:593
  10.8 15.9 %collective-permute-start.5 = (bf16[1024,1024]{1,0:T(8,128)(2,1)}, bf16[1024,1024]{1,0:T(8,128)(2,1)}, u32[]{:S(2)}, u32[]{:S(2)}) collective-permute-start(bf16[1024,1024]{1,0:T(8,128)(2,1)} %refs_9_.1), channel_id=1, source_target_pairs={{0,8},{1,9},{2,10},{3,11},{4,12},{5,13},{6,14},{7,15},{8,0},{9,1},... | collective-permute-start | bytes 6291464 | tf_op jit(solution)/shard_map/gather/ppermute | solution.py:593
  12.9 13.9 %collective-permute-start.2 = (bf16[144,1280]{1,0:T(8,128)(2,1)S(1)}, bf16[144,1280]{1,0:T(8,128)(2,1)S(1)}, u32[]{:S(2)}, u32[]{:S(2)}) collective-permute-start(bf16[144,1280]{1,0:T(8,128)(2,1)S(1)} %prep_attn.1.refs_0_), channel_id=1, source_target_pairs={{0,1},{1,0},{2,3},{3,2},{4,5},{5,4},{6,7},{7,6},{8,9},{9,8},{10,11... | collective-permute-start | bytes 1105928 | tf_op jit(solution)/shard_map/gather/ppermute | solution.py:593
  26.8 27.7 %collective-permute-start.10 = (bf16[256,1024]{1,0:T(8,128)(2,1)S(1)}, bf16[256,1024]{1,0:T(8,128)(2,1)S(1)}, u32[]{:S(2)}, u32[]{:S(2)}) collective-permute-start(bf16[256,1024]{1,0:T(8,128)(2,1)S(1)} %prep_mlp.2.refs_0_), channel_id=1, source_target_pairs={{0,4},{1,5},{2,6},{3,7},{4,0},{5,1},{6,2},{7,3},{8,12},{9,13},{10,... | collective-permute-start | bytes 1572872 | tf_op jit(solution)/shard_map/gather/ppermute | solution.py:593
  27.2 11.5 %collective-permute-start.6 = (bf16[144,1280]{1,0:T(8,128)(2,1)S(1)}, bf16[144,1280]{1,0:T(8,128)(2,1)S(1)}, u32[]{:S(2)}, u32[]{:S(2)}) collective-permute-start(bf16[144,1280]{1,0:T(8,128)(2,1)S(1)} %collective-permute-done.refs_1_), channel_id=1, source_target_pairs={{0,1},{1,0},{2,3},{3,2},{4,5},{5,4},{6,7},{7,6},{8,9},{9,8},{10,11... | collective-permute-start | bytes 1105928 | tf_op jit(solution)/shard_map/gather/ppermute | solution.py:593
  28.6 17.9 %collective-permute-start.7 = (bf16[144,1280]{1,0:T(8,128)(2,1)}, bf16[144,1280]{1,0:T(8,128)(2,1)S(1)}, u32[]{:S(2)}, u32[]{:S(2)}) collective-permute-start(bf16[144,1280]{1,0:T(8,128)(2,1)} %collective-permute-done.1.refs_2_), channel_id=1, source_target_pairs={{0,1},{1,0},{2,3},{3,2},{4,5},{5,4},{6,7},{7,6},{8,9},{9,8},{10,11... | collective-permute-start | bytes 1105928 | tf_op jit(solution)/shard_map/gather/ppermute | solution.py:593
  29.2 17.4 %collective-permute-start.8 = (bf16[144,1280]{1,0:T(8,128)(2,1)}, bf16[144,1280]{1,0:T(8,128)(2,1)S(1)}, u32[]{:S(2)}, u32[]{:S(2)}) collective-permute-start(bf16[144,1280]{1,0:T(8,128)(2,1)} %collective-permute-done.1.refs_2_), channel_id=1, source_target_pairs={{0,16},{1,17},{2,18},{3,19},{4,20},{5,21},{6,22},{7,23},{8,24},{9,... | collective-permute-start | bytes 1105928 | tf_op jit(solution)/shard_map/gather/ppermute | solution.py:593
  31.7 22.8 %collective-permute-start.9 = (bf16[144,1280]{1,0:T(8,128)(2,1)}, bf16[144,1280]{1,0:T(8,128)(2,1)S(1)}, u32[]{:S(2)}, u32[]{:S(2)}) collective-permute-start(bf16[144,1280]{1,0:T(8,128)(2,1)} %collective-permute-done.1.refs_2_), channel_id=1, source_target_pairs={{0,17},{1,16},{2,19},{3,18},{4,21},{5,20},{6,23},{7,22},{8,25},{9,... | collective-permute-start | bytes 1105928 | tf_op jit(solution)/shard_map/gather/ppermute | solution.py:593
  54.5 21.7 %collective-permute-start.11 = (bf16[256,1024]{1,0:T(8,128)(2,1)S(1)}, bf16[256,1024]{1,0:T(8,128)(2,1)S(1)}, u32[]{:S(2)}, u32[]{:S(2)}) collective-permute-start(bf16[256,1024]{1,0:T(8,128)(2,1)S(1)} %collective-permute-done.10.refs_2_), channel_id=1, source_target_pairs={{0,1},{1,0},{2,3},{3,2},{4,5},{5,4},{6,7},{7,6},{8,9},{9,8},{10,11... | collective-permute-start | bytes 1572872 | tf_op jit(solution)/shard_map/gather/ppermute | solution.py:593
  56.0 20.6 %collective-permute-start.12 = (bf16[256,1024]{1,0:T(8,128)(2,1)S(1)}, bf16[256,1024]{1,0:T(8,128)(2,1)S(1)}, u32[]{:S(2)}, u32[]{:S(2)}) collective-permute-start(bf16[256,1024]{1,0:T(8,128)(2,1)S(1)} %prep_mlp.2.refs_0_), channel_id=1, source_target_pairs={{0,1},{1,0},{2,3},{3,2},{4,5},{5,4},{6,7},{7,6},{8,9},{9,8},{10,11... | collective-permute-start | bytes 1572872 | tf_op jit(solution)/shard_map/gather/ppermute | solution.py:593
  56.5 20.1 %collective-permute-start.13 = (bf16[256,1024]{1,0:T(8,128)(2,1)S(1)}, bf16[256,1024]{1,0:T(8,128)(2,1)S(1)}, u32[]{:S(2)}, u32[]{:S(2)}) collective-permute-start(bf16[256,1024]{1,0:T(8,128)(2,1)S(1)} %collective-permute-done.10.refs_2_), channel_id=1, source_target_pairs={{0,16},{1,17},{2,18},{3,19},{4,20},{5,21},{6,22},{7,23},{8,24},{9,... | collective-permute-start | bytes 1572872 | tf_op jit(solution)/shard_map/gather/ppermute | solution.py:593
  56.5 39.8 %collective-permute-start.15 = (bf16[256,1024]{1,0:T(8,128)(2,1)S(1)}, bf16[256,1024]{1,0:T(8,128)(2,1)S(1)}, u32[]{:S(2)}, u32[]{:S(2)}) collective-permute-start(bf16[256,1024]{1,0:T(8,128)(2,1)S(1)} %prep_mlp.2.refs_0_), channel_id=1, source_target_pairs={{0,2},{1,3},{2,0},{3,1},{4,6},{5,7},{6,4},{7,5},{8,10},{9,11},{10,... | collective-permute-start | bytes 1572872 | tf_op jit(solution)/shard_map/gather/ppermute | solution.py:593
  58.0 38.4 %collective-permute-start.14 = (bf16[352,1024]{1,0:T(8,128)(2,1)S(1)}, bf16[352,1024]{1,0:T(8,128)(2,1)S(1)}, u32[]{:S(2)}, u32[]{:S(2)}) collective-permute-start(bf16[352,1024]{1,0:T(8,128)(2,1)S(1)} %prep_mlp.3.refs_0_), channel_id=1, source_target_pairs={{0,4},{1,5},{2,6},{3,7},{4,0},{5,1},{6,2},{7,3},{8,12},{9,13},{10,... | collective-permute-start | bytes 2162696 | tf_op jit(solution)/shard_map/gather/ppermute | solution.py:593
  76.6 37.7 %collective-permute-start.16 = (bf16[256,1024]{1,0:T(8,128)(2,1)S(1)}, bf16[256,1024]{1,0:T(8,128)(2,1)S(1)}, u32[]{:S(2)}, u32[]{:S(2)}) collective-permute-start(bf16[256,1024]{1,0:T(8,128)(2,1)S(1)} %collective-permute-done.11.refs_6_), channel_id=1, source_target_pairs={{0,16},{1,17},{2,18},{3,19},{4,20},{5,21},{6,22},{7,23},{8,24},{9,... | collective-permute-start | bytes 1572872 | tf_op jit(solution)/shard_map/gather/ppermute | solution.py:593
  77.8 36.6 %collective-permute-start.17 = (bf16[256,1024]{1,0:T(8,128)(2,1)S(1)}, bf16[256,1024]{1,0:T(8,128)(2,1)S(1)}, u32[]{:S(2)}, u32[]{:S(2)}) collective-permute-start(bf16[256,1024]{1,0:T(8,128)(2,1)S(1)} %prep_mlp.2.refs_0_), channel_id=1, source_target_pairs={{0,3},{1,2},{2,1},{3,0},{4,7},{5,6},{6,5},{7,4},{8,11},{9,10},{10,... | collective-permute-start | bytes 1572872 | tf_op jit(solution)/shard_map/gather/ppermute | solution.py:593
  96.4 18.0 %collective-permute-start.18 = (bf16[352,1024]{1,0:T(8,128)(2,1)S(1)}, bf16[352,1024]{1,0:T(8,128)(2,1)S(1)}, u32[]{:S(2)}, u32[]{:S(2)}) collective-permute-start(bf16[352,1024]{1,0:T(8,128)(2,1)S(1)} %collective-permute-done.14.refs_2_), channel_id=1, source_target_pairs={{0,1},{1,0},{2,3},{3,2},{4,5},{5,4},{6,7},{7,6},{8,9},{9,8},{10,11... | collective-permute-start | bytes 2162696 | tf_op jit(solution)/shard_map/gather/ppermute | solution.py:593
  96.9 17.5 %collective-permute-start.19 = (bf16[352,1024]{1,0:T(8,128)(2,1)S(1)}, bf16[352,1024]{1,0:T(8,128)(2,1)S(1)}, u32[]{:S(2)}, u32[]{:S(2)}) collective-permute-start(bf16[352,1024]{1,0:T(8,128)(2,1)S(1)} %collective-permute-done.14.refs_2_), channel_id=1, source_target_pairs={{0,16},{1,17},{2,18},{3,19},{4,20},{5,21},{6,22},{7,23},{8,24},{9,... | collective-permute-start | bytes 2162696 | tf_op jit(solution)/shard_map/gather/ppermute | solution.py:593
  97.5 16.9 %collective-permute-start.20 = (bf16[352,1024]{1,0:T(8,128)(2,1)S(1)}, bf16[352,1024]{1,0:T(8,128)(2,1)S(1)}, u32[]{:S(2)}, u32[]{:S(2)}) collective-permute-start(bf16[352,1024]{1,0:T(8,128)(2,1)S(1)} %prep_mlp.3.refs_0_), channel_id=1, source_target_pairs={{0,2},{1,3},{2,0},{3,1},{4,6},{5,7},{6,4},{7,5},{8,10},{9,11},{10,... | collective-permute-start | bytes 2162696 | tf_op jit(solution)/shard_map/gather/ppermute | solution.py:593
  114.4 30.0 %collective-permute-start.21 = (bf16[352,1024]{1,0:T(8,128)(2,1)S(1)}, bf16[352,1024]{1,0:T(8,128)(2,1)S(1)}, u32[]{:S(2)}, u32[]{:S(2)}) collective-permute-start(bf16[352,1024]{1,0:T(8,128)(2,1)S(1)} %prep_mlp.3.refs_0_), channel_id=1, source_target_pairs={{0,1},{1,0},{2,3},{3,2},{4,5},{5,4},{6,7},{7,6},{8,9},{9,8},{10,11... | collective-permute-start | bytes 2162696 | tf_op jit(solution)/shard_map/gather/ppermute | solution.py:593
  116.0 28.5 %collective-permute-start.22 = (bf16[352,1024]{1,0:T(8,128)(2,1)S(1)}, bf16[352,1024]{1,0:T(8,128)(2,1)S(1)}, u32[]{:S(2)}, u32[]{:S(2)}) collective-permute-start(bf16[352,1024]{1,0:T(8,128)(2,1)S(1)} %collective-permute-done.20.refs_1_), channel_id=1, source_target_pairs={{0,1},{1,0},{2,3},{3,2},{4,5},{5,4},{6,7},{7,6},{8,9},{9,8},{10,11... | collective-permute-start | bytes 2162696 | tf_op jit(solution)/shard_map/gather/ppermute | solution.py:593
  116.5 28.0 %collective-permute-start.23 = (bf16[352,1024]{1,0:T(8,128)(2,1)S(1)}, bf16[352,1024]{1,0:T(8,128)(2,1)S(1)}, u32[]{:S(2)}, u32[]{:S(2)}) collective-permute-start(bf16[352,1024]{1,0:T(8,128)(2,1)S(1)} %collective-permute-done.18.refs_6_), channel_id=1, source_target_pairs={{0,16},{1,17},{2,18},{3,19},{4,20},{5,21},{6,22},{7,23},{8,24},{9,... | collective-permute-start | bytes 2162696 | tf_op jit(solution)/shard_map/gather/ppermute | solution.py:593
  144.6 30.6 %collective-permute-start.24 = (bf16[2,256,1024]{2,1,0:T(8,128)(2,1)}, bf16[2,256,1024]{2,1,0:T(8,128)(2,1)S(1)}, u32[]{:S(2)}, u32[]{:S(2)}) collective-permute-start(bf16[2,256,1024]{2,1,0:T(8,128)(2,1)} %get-tuple-element.316), channel_id=1, source_target_pairs={{0,1},{1,0},{2,3},{3,2},{4,5},{5,4},{6,7},{7,6},{8,9},{9,8},{10,11... | collective-permute-start | bytes 3145736 | tf_op jit(solution)/shard_map/ppermute | solution.py:593
  146.2 29.0 %collective-permute-start.25 = (bf16[2,256,1024]{2,1,0:T(8,128)(2,1)}, bf16[2,256,1024]{2,1,0:T(8,128)(2,1)S(1)}, u32[]{:S(2)}, u32[]{:S(2)}) collective-permute-start(bf16[2,256,1024]{2,1,0:T(8,128)(2,1)} %get-tuple-element.317), channel_id=1, source_target_pairs={{0,16},{1,17},{2,18},{3,19},{4,20},{5,21},{6,22},{7,23},{8,24},{9,... | collective-permute-start | bytes 3145736 | tf_op jit(solution)/shard_map/ppermute | solution.py:593
  176.4 38.0 %collective-permute-start.26 = (bf16[256,1024]{1,0:T(8,128)(2,1)}, bf16[256,1024]{1,0:T(8,128)(2,1)S(1)}, u32[]{:S(2)}, u32[]{:S(2)}) collective-permute-start(bf16[256,1024]{1,0:T(8,128)(2,1)} %get-tuple-element.463), channel_id=1, source_target_pairs={{0,1},{1,0},{2,3},{3,2},{4,5},{5,4},{6,7},{7,6},{8,9},{9,8},{10,11... | collective-permute-start | bytes 1572872 | tf_op jit(solution)/shard_map/ppermute | solution.py:593
  176.6 37.8 %collective-permute-start.27 = (bf16[256,1024]{1,0:T(8,128)(2,1)S(1)}, bf16[256,1024]{1,0:T(8,128)(2,1)S(1)}, u32[]{:S(2)}, u32[]{:S(2)}) collective-permute-start(bf16[256,1024]{1,0:T(8,128)(2,1)S(1)} %get-tuple-element.462), channel_id=1, source_target_pairs={{0,2},{1,3},{2,0},{3,1},{4,6},{5,7},{6,4},{7,5},{8,10},{9,11},{10,... | collective-permute-start | bytes 1572872 | tf_op jit(solution)/shard_map/ppermute | solution.py:593
  178.1 36.3 %collective-permute-start.28 = (bf16[256,1024]{1,0:T(8,128)(2,1)}, bf16[256,1024]{1,0:T(8,128)(2,1)S(1)}, u32[]{:S(2)}, u32[]{:S(2)}) collective-permute-start(bf16[256,1024]{1,0:T(8,128)(2,1)} %get-tuple-element.464), channel_id=1, source_target_pairs={{0,1},{1,0},{2,3},{3,2},{4,5},{5,4},{6,7},{7,6},{8,9},{9,8},{10,11... | collective-permute-start | bytes 1572872 | tf_op jit(solution)/shard_map/ppermute | solution.py:593
  179.6 34.8 %collective-permute-start.29 = (bf16[2,256,1024]{2,1,0:T(8,128)(2,1)}, bf16[2,256,1024]{2,1,0:T(8,128)(2,1)S(1)}, u32[]{:S(2)}, u32[]{:S(2)}) collective-permute-start(bf16[2,256,1024]{2,1,0:T(8,128)(2,1)} %get-tuple-element.329), channel_id=1, source_target_pairs={{0,16},{1,17},{2,18},{3,19},{4,20},{5,21},{6,22},{7,23},{8,24},{9,... | collective-permute-start | bytes 3145736 | tf_op jit(solution)/shard_map/ppermute | solution.py:593
  214.8 24.2 %collective-permute-start.33 = (bf16[256,1024]{1,0:T(8,128)(2,1)S(1)}, bf16[256,1024]{1,0:T(8,128)(2,1)S(1)}, u32[]{:S(2)}, u32[]{:S(2)}) collective-permute-start(bf16[256,1024]{1,0:T(8,128)(2,1)S(1)} %fusion.3), channel_id=1, source_target_pairs={{0,2},{1,3},{2,0},{3,1},{4,6},{5,7},{6,4},{7,5},{8,10},{9,11},{10,... | collective-permute-start | bytes 1572872 | tf_op jit(solution)/shard_map/ppermute | solution.py:593
  215.8 23.3 %collective-permute-start.32 = (bf16[256,1024]{1,0:T(8,128)(2,1)S(1)}, bf16[256,1024]{1,0:T(8,128)(2,1)S(1)}, u32[]{:S(2)}, u32[]{:S(2)}) collective-permute-start(bf16[256,1024]{1,0:T(8,128)(2,1)S(1)} %fusion.19), channel_id=1, source_target_pairs={{0,1},{1,0},{2,3},{3,2},{4,5},{5,4},{6,7},{7,6},{8,9},{9,8},{10,11... | collective-permute-start | bytes 1572872 | tf_op jit(solution)/shard_map/ppermute | solution.py:593
  216.9 22.2 %collective-permute-start.30 = (bf16[256,1024]{1,0:T(8,128)(2,1)S(1)}, bf16[256,1024]{1,0:T(8,128)(2,1)}, u32[]{:S(2)}, u32[]{:S(2)}) collective-permute-start(bf16[256,1024]{1,0:T(8,128)(2,1)S(1)} %fusion.10), channel_id=1, source_target_pairs={{0,4},{1,5},{2,6},{3,7},{4,0},{5,1},{6,2},{7,3},{8,12},{9,13},{10,... | collective-permute-start | bytes 1572872 | tf_op jit(solution)/shard_map/ppermute | solution.py:593
  218.1 21.0 %collective-permute-start.31 = (bf16[256,1024]{1,0:T(8,128)(2,1)S(1)}, bf16[256,1024]{1,0:T(8,128)(2,1)S(1)}, u32[]{:S(2)}, u32[]{:S(2)}) collective-permute-start(bf16[256,1024]{1,0:T(8,128)(2,1)S(1)} %get-tuple-element.345), channel_id=1, source_target_pairs={{0,1},{1,0},{2,3},{3,2},{4,5},{5,4},{6,7},{7,6},{8,9},{9,8},{10,11... | collective-permute-start | bytes 1572872 | tf_op jit(solution)/shard_map/ppermute | solution.py:593
  242.1 29.3 %collective-permute-start.35 = (bf16[256,1024]{1,0:T(8,128)(2,1)}, bf16[256,1024]{1,0:T(8,128)(2,1)S(1)}, u32[]{:S(2)}, u32[]{:S(2)}) collective-permute-start(bf16[256,1024]{1,0:T(8,128)(2,1)} %fusion.7), channel_id=1, source_target_pairs={{0,4},{1,5},{2,6},{3,7},{4,0},{5,1},{6,2},{7,3},{8,12},{9,13},{10,... | collective-permute-start | bytes 1572872 | tf_op jit(solution)/shard_map/ppermute | solution.py:593
  245.5 26.0 %collective-permute-start.34 = (bf16[256,1024]{1,0:T(8,128)(2,1)S(1)}, bf16[256,1024]{1,0:T(8,128)(2,1)S(1)}, u32[]{:S(2)}, u32[]{:S(2)}) collective-permute-start(bf16[256,1024]{1,0:T(8,128)(2,1)S(1)} %fusion.9), channel_id=1, source_target_pairs={{0,16},{1,17},{2,18},{3,19},{4,20},{5,21},{6,22},{7,23},{8,24},{9,... | collective-permute-start | bytes 1572872 | tf_op jit(solution)/shard_map/ppermute | solution.py:593
  248.2 23.2 %collective-permute-start.36 = (bf16[2,128,2048]{2,1,0:T(8,128)(2,1)S(1)}, bf16[2,128,2048]{2,1,0:T(8,128)(2,1)S(1)}, u32[]{:S(2)}, u32[]{:S(2)}) collective-permute-start(bf16[2,128,2048]{2,1,0:T(8,128)(2,1)S(1)} %get-tuple-element.370), channel_id=1, source_target_pairs={{0,1},{1,0},{2,3},{3,2},{4,5},{5,4},{6,7},{7,6},{8,9},{9,8},{10,11... | collective-permute-start | bytes 3145736 | tf_op jit(solution)/shard_map/ppermute | solution.py:593
  248.4 24.7 %collective-permute-start.37 = (bf16[2,128,2048]{2,1,0:T(8,128)(2,1)S(1)}, bf16[2,128,2048]{2,1,0:T(8,128)(2,1)S(1)}, u32[]{:S(2)}, u32[]{:S(2)}) collective-permute-start(bf16[2,128,2048]{2,1,0:T(8,128)(2,1)S(1)} %get-tuple-element.371), channel_id=1, source_target_pairs={{0,16},{1,17},{2,18},{3,19},{4,20},{5,21},{6,22},{7,23},{8,24},{9,... | collective-permute-start | bytes 3145736 | tf_op jit(solution)/shard_map/ppermute | solution.py:593
  274.4 16.7 %collective-permute-start.42 = (bf16[2,1024,1024]{2,1,0:T(8,128)(2,1)}, bf16[2,1024,1024]{2,1,0:T(8,128)(2,1)}, u32[]{:S(2)}, u32[]{:S(2)}) collective-permute-start(bf16[2,1024,1024]{2,1,0:T(8,128)(2,1)} %get-tuple-element.392), channel_id=1, source_target_pairs={{0,8},{1,9},{2,10},{3,11},{4,12},{5,13},{6,14},{7,15},{8,0},{9,1},... | collective-permute-start | bytes 12582920 | tf_op jit(solution)/shard_map/ppermute | solution.py:593
  274.7 16.4 %collective-permute-start.40 = (bf16[128,2048]{1,0:T(8,128)(2,1)}, bf16[128,2048]{1,0:T(8,128)(2,1)}, u32[]{:S(2)}, u32[]{:S(2)}) collective-permute-start(bf16[128,2048]{1,0:T(8,128)(2,1)} %get-tuple-element.461), channel_id=1, source_target_pairs={{0,1},{1,0},{2,3},{3,2},{4,5},{5,4},{6,7},{7,6},{8,9},{9,8},{10,11... | collective-permute-start | bytes 1572872 | tf_op jit(solution)/shard_map/ppermute | solution.py:593
  275.6 15.5 %collective-permute-start.41 = (bf16[128,2048]{1,0:T(8,128)(2,1)}, bf16[128,2048]{1,0:T(8,128)(2,1)S(1)}, u32[]{:S(2)}, u32[]{:S(2)}) collective-permute-start(bf16[128,2048]{1,0:T(8,128)(2,1)} %get-tuple-element.460), channel_id=1, source_target_pairs={{0,2},{1,3},{2,0},{3,1},{4,6},{5,7},{6,4},{7,5},{8,10},{9,11},{10,... | collective-permute-start | bytes 1572872 | tf_op jit(solution)/shard_map/ppermute | solution.py:593
  277.2 13.9 %collective-permute-start.39 = (bf16[256,1024]{1,0:T(8,128)(2,1)S(1)}, bf16[256,1024]{1,0:T(8,128)(2,1)S(1)}, u32[]{:S(2)}, u32[]{:S(2)}) collective-permute-start(bf16[256,1024]{1,0:T(8,128)(2,1)S(1)} %fusion.2), channel_id=1, source_target_pairs={{0,16},{1,17},{2,18},{3,19},{4,20},{5,21},{6,22},{7,23},{8,24},{9,... | collective-permute-start | bytes 1572872 | tf_op jit(solution)/shard_map/ppermute | solution.py:593
  291.3 30.0 %collective-permute-start.43 = (bf16[256,1024]{1,0:T(8,128)(2,1)S(1)}, bf16[256,1024]{1,0:T(8,128)(2,1)S(1)}, u32[]{:S(2)}, u32[]{:S(2)}) collective-permute-start(bf16[256,1024]{1,0:T(8,128)(2,1)S(1)} %add_convert_fusion.1.own_b), channel_id=1, source_target_pairs={{0,8},{1,9},{2,10},{3,11},{4,12},{5,13},{6,14},{7,15},{8,0},{9,1},... | collective-permute-start | bytes 1572872 | tf_op jit(solution)/shard_map/ppermute | solution.py:593
  292.8 28.6 %collective-permute-start.44 = (bf16[128,2048]{1,0:T(8,128)(2,1)S(1)}, bf16[128,2048]{1,0:T(8,128)(2,1)S(1)}, u32[]{:S(2)}, u32[]{:S(2)}) collective-permute-start(bf16[128,2048]{1,0:T(8,128)(2,1)S(1)} %fusion.6), channel_id=1, source_target_pairs={{0,4},{1,5},{2,6},{3,7},{4,0},{5,1},{6,2},{7,3},{8,12},{9,13},{10,... | collective-permute-start | bytes 1572872 | tf_op jit(solution)/shard_map/ppermute | solution.py:593
  321.7 15.1 %collective-permute-start.45 = (bf16[128,2048]{1,0:T(8,128)(2,1)S(1)}, bf16[128,2048]{1,0:T(8,128)(2,1)S(1)}, u32[]{:S(2)}, u32[]{:S(2)}) collective-permute-start(bf16[128,2048]{1,0:T(8,128)(2,1)S(1)} %fusion.5), channel_id=1, source_target_pairs={{0,16},{1,17},{2,18},{3,19},{4,20},{5,21},{6,22},{7,23},{8,24},{9,... | collective-permute-start | bytes 1572872 | tf_op jit(solution)/shard_map/ppermute | solution.py:593
  323.6 13.2 %collective-permute-start.46 = (f32[16,1024]{1,0:T(8,128)S(1)}, f32[16,1024]{1,0:T(8,128)S(1)}, u32[]{:S(2)}, u32[]{:S(2)}) collective-permute-start(f32[16,1024]{1,0:T(8,128)S(1)} %concatenate.34), channel_id=1, source_target_pairs={{0,2},{1,3},{2,0},{3,1},{4,6},{5,7},{6,4},{7,5},{8,10},{9,11},{10,... | collective-permute-start | bytes 196616 | tf_op jit(solution)/shard_map/vectors/ppermute | solution.py:593
  324.5 12.3 %collective-permute-start.47 = (f32[16,1024]{1,0:T(8,128)S(1)}, f32[16,1024]{1,0:T(8,128)S(1)}, u32[]{:S(2)}, u32[]{:S(2)}) collective-permute-start(f32[16,1024]{1,0:T(8,128)S(1)} %concatenate.34), channel_id=1, source_target_pairs={{0,4},{1,5},{2,6},{3,7},{4,0},{5,1},{6,2},{7,3},{8,12},{9,13},{10,... | collective-permute-start | bytes 196616 | tf_op jit(solution)/shard_map/vectors/ppermute | solution.py:593
  325.6 11.2 %collective-permute-start.48 = (f32[16,1024]{1,0:T(8,128)S(1)}, f32[16,1024]{1,0:T(8,128)S(1)}, u32[]{:S(2)}, u32[]{:S(2)}) collective-permute-start(f32[16,1024]{1,0:T(8,128)S(1)} %concatenate.34), channel_id=1, source_target_pairs={{0,6},{1,7},{2,4},{3,5},{4,2},{5,3},{6,0},{7,1},{8,14},{9,15},{10,... | collective-permute-start | bytes 196616 | tf_op jit(solution)/shard_map/vectors/ppermute | solution.py:593
  337.1 9.3 %collective-permute-start.50 = (f32[16,1024]{1,0:T(8,128)S(1)}, f32[16,1024]{1,0:T(8,128)S(1)}, u32[]{:S(2)}, u32[]{:S(2)}) collective-permute-start(f32[16,1024]{1,0:T(8,128)S(1)} %add_add_fusion.1), channel_id=1, source_target_pairs={{0,1},{1,0},{2,3},{3,2},{4,5},{5,4},{6,7},{7,6},{8,9},{9,8},{10,11... | collective-permute-start | bytes 196616 | tf_op jit(solution)/shard_map/vectors/ppermute | solution.py:593
  (46 other events, 417.7 us)
